TPU v7x, 32 devices: a whole 2x2x4 slice. The times are simulated.
32 devices in a mesh: gx: 8 (over z, y), gy: 4 (over x, core).
Axes of the slice: x: 2, y: 2, z: 4, core: 2. Of those that a mesh axis runs over, the one named last changes fastest.
Arguments:
- template: bfloat16 [256, 128, 256], P('gx', 'gy'), may hold values from -6 to 6
- target_image: bfloat16 [256, 128, 256], P('gx', 'gy'), may hold values from -6 to 6
- velocity: float32 [3, 256, 128, 256], P(None, 'gx', 'gy'), may hold values from -6 to 6
- operators: bfloat16 [64, 3, 32, 32], replicated, may hold values from -1 to 1
- route: int32 [2, 8, 4, 8, 1], P(None, 'gx', 'gy'), may hold values from 0 to 7; in each aligned block of 8 rows (0 to 7, 8 to 15, ..., all dimensions but the last counted through in order) at most 2 rows name the same one
- target_brick: int32 [2, 8, 4, 8], P(None, 'gx', 'gy'), may hold values from 0 to 7
- operator_index: int32 [2, 8, 4, 8], P(None, 'gx', 'gy'), may hold values from 0 to 63
Outputs:
- velocity_grad: float32 [3, 256, 128, 256], P(None, 'gx', 'gy')
- template_grad: bfloat16 [256, 128, 256], P('gx', 'gy')
Inputs may be any that keep to these rules, and one draw needn't show every extreme that they name: `route`: in every step, no device sends more than 2 of its bricks to one destination device, and some device sends exactly 2 to one; the destination keeps the second index.
All inputs are finite; a program needn't handle non-finite values.
Results may differ from a plain program's by a relative error of at most 0.0085.
Values may be sent and summed in bfloat16 or wider, within the bound.
No kernel may reach another device: no remote copies, remote signals or barrier semaphores. Data moves between devices by JAX's collectives and lax.ppermute only.
A program may use at most 128 MiB of HBM per device.

v0:
```python
import functools

import jax
import jax.numpy as jnp
from jax import lax
from jax.experimental import pallas as pl
from jax.experimental.pallas import tpu as pltpu
from jax.sharding import PartitionSpec as P

STEPS = 2
CAP = 2
RIM = 3
F32 = jnp.float32
BF16 = jnp.bfloat16
NT = (((1,), (1,)), ((), ()))
NN = (((1,), (0,)), ((), ()))
TAPS = ((1, 0.75), (2, -0.15), (3, 1.0 / 60.0))


def iota(shape, dim):
    return lax.broadcasted_iota(jnp.int32, shape, dim)


def mm(left, right, dims=NN):
    return lax.dot_general(left, right, dims, preferred_element_type=F32)


def halves(value):
    high = value.astype(BF16)
    return high, (value - high.astype(F32)).astype(BF16)


def table_rows(operators, picks, axis):
    lane = iota((operators.shape[1], 256), 1)
    chosen = jnp.zeros(lane.shape, jnp.int32)
    for b, pick in enumerate(picks):
        chosen = jnp.where(lane // 32 == b, pick, chosen)
    one_hot = (iota(lane.shape, 0) == chosen).astype(F32).astype(BF16)
    found = mm(operators[axis * 1024 : axis * 1024 + 1024, :], one_hot)
    within = iota((32, 256), 1) % 32
    total = jnp.zeros((32, 256), F32)
    for x in range(32):
        total = jnp.where(within == x, found[x * 32 : x * 32 + 32], total)
    return total


def same_block(size, edge):
    return iota((size, size), 0) // edge == iota((size, size), 1) // edge


def identity():
    return (iota((256, 256), 0) == iota((256, 256), 1)).astype(F32).astype(BF16)


def flipped_diagonal(table):
    return jnp.where(same_block(256, 32), jnp.concatenate([table] * 8, axis=0), 0.0).astype(BF16)


def diagonal(table):
    return mm(identity(), flipped_diagonal(table), NT).astype(BF16)


def spread(table):
    copies = (iota((256, 256), 0) % 32 == iota((256, 256), 1) % 32).astype(F32).astype(BF16)
    return mm(flipped_diagonal(table), copies)


def swap_chunks(parts):
    lane = iota(parts[0].shape, 1)
    for bit, shift in ((1, 32), (2, 64)):
        keep = (lane & shift) == 0
        fresh = list(parts)
        for index in range(4):
            if index & bit:
                continue
            one, two = parts[index], parts[index | bit]
            fresh[index] = jnp.where(keep, one, pltpu.roll(two, shift, 1))
            fresh[index | bit] = jnp.where(keep, pltpu.roll(one, 128 - shift, 1), two)
        parts = fresh
    return parts


def swap_brick(block, folded, turned, brick, parts=2):
    slabs = []
    for ph in range(4):
        slabs.append(
            jnp.concatenate(
                [
                    block[(qs // 2) * 32 + ph * 8 : (qs // 2) * 32 + ph * 8 + 8, (qs % 2) * 128 : (qs % 2) * 128 + 128]
                    for qs in range(8)
                ],
                axis=0,
            )
        )
    slabs = swap_chunks(slabs)
    for qh in range(4):
        folded[brick * 4 + qh] = slabs[qh]
    for ps in range(8):
        value = jnp.concatenate(
            [folded[brick * 4 + qh, pl.ds(ps, 8, stride=8), :] for qh in range(4)], axis=0
        )
        for part, half in enumerate(halves(value)[:parts]):
            turned[part * 256 + brick * 32 : part * 256 + brick * 32 + 32, ps * 128 : ps * 128 + 128] = half


def lane_pair(field, g):
    return jnp.concatenate(
        [
            jnp.concatenate([field[b, qs * 32 : qs * 32 + 32, :] for b in range(8)], axis=0)
            for qs in (2 * g, 2 * g + 1)
        ],
        axis=1,
    )


def put_pair(field, g, value):
    for b in range(8):
        for half in range(2):
            rows = slice((2 * g + half) * 32, (2 * g + half) * 32 + 32)
            field[b, rows, :] = value[b * 32 : b * 32 + 32, half * 128 : half * 128 + 128]


def middle_and_last(start, spread_mid, last, folded, turned, flipped):
    mask = same_block(256, 32)
    for brick in range(8):
        rows = spread_mid[brick * 32 : brick * 32 + 32]
        line = jnp.where(mask, jnp.concatenate([rows] * 8, axis=0), 0.0).astype(BF16)
        block = start[brick * 32 : brick * 32 + 32, :]
        block = jnp.concatenate([block[:, g * 256 : g * 256 + 256] for g in range(4)], axis=0)
        high, low = halves(block)
        both = mm(jnp.concatenate([high, low], axis=0), line, NT if flipped else NN)
        swap_brick(both[:128] + both[128:], folded, turned, brick)
    last = jnp.concatenate([last, last], axis=1)
    for g in range(4):
        yield g, mm(last, turned[:, g * 256 : g * 256 + 256]).astype(BF16)


def slot_numbers(route, step):
    own = [route[step, 0, 0, b] for b in range(8)]
    slots = []
    for b in range(8):
        rank = jnp.int32(0)
        for other in range(b):
            rank = rank + (own[other] == own[b]).astype(jnp.int32)
        slots.append((own[b], rank))
    return slots


def fetch(source, target, sem):
    copy = pltpu.make_async_copy(source, target, sem)
    copy.start()
    return copy


def send_quarter(g, bricks, send, slots, sems):
    copies = []
    for b, (place, rank) in enumerate(slots):
        rows = pl.ds(pl.multiple_of(rank * 256 + g * 64, 64), 64)
        copies.append(fetch(bricks.at[b, g * 64 : g * 64 + 64, :], send.at[place, rows, :], sems.at[g, b]))
    return copies


def first_kernel(*refs):
    picks_in, route_in, landing_in, operators, field, send, tables = refs[:7]
    picks, route, landing, table_mem, field_mem, start, folded, turned, out, meta, meta_half, tables_mem, sems, slot_sems = refs[7:]
    told = [fetch(a, b, sems.at[11 + i]) for i, (a, b) in enumerate(((picks_in, picks), (route_in, route), (landing_in, landing)))]
    loads = [fetch(operators, table_mem, sems.at[8]), fetch(field, field_mem, sems.at[9])]
    for copy in told:
        copy.wait()
    meta[...] = jnp.zeros(meta.shape, F32)
    for step in range(STEPS):
        for b, (place, rank) in enumerate(slot_numbers(route, step)):
            value = jnp.full((1, 128), landing[step, 0, 0, b] + 1, jnp.int32).astype(F32)
            meta[place, pl.ds(step * CAP + rank, 1), :] = value
    meta_half[...] = meta[...].astype(BF16)
    told = fetch(meta_half, send.at[:, 512:528, :], sems.at[10])
    chosen = [picks[0, 0, 0, b] for b in range(8)]
    loads[0].wait()
    found = [table_rows(table_mem, chosen, axis) for axis in range(3)]
    for axis in range(3):
        tables_mem[axis] = found[axis].astype(BF16)
    kept = fetch(tables_mem, tables, sems.at[8])
    begin = diagonal(found[2])
    loads[1].wait()
    for g in range(4):
        block = jnp.concatenate(
            [field_mem[qh * 8 + qs] for qs in (2 * g, 2 * g + 1) for qh in range(4)], axis=0
        )
        start[:, g * 256 : g * 256 + 256] = mm(begin, block, NT)
    slots = slot_numbers(route, 0)
    sent = []
    for g, moved in middle_and_last(start, spread(found[1]), diagonal(found[0]), folded, turned, False):
        put_pair(out, g, moved)
        sent += send_quarter(g, out, send, slots, slot_sems)
    for copy in sent + [told, kept]:
        copy.wait()


def second_kernel(route, tables_in, arrived, *refs):
    send, state, landing_out, meta, tables, landing, state_mem, total, start, folded, turned, out, sems, slot_sems = refs[-14:]
    meta[...] = arrived[:, 512:528, :].astype(F32).astype(jnp.int32)[:, 0:8, :]
    told = [fetch(meta, landing, sems.at[9]), fetch(meta, landing_out, sems.at[10])]
    listed = fetch(tables_in, tables, sems.at[11])
    total[...] = jnp.zeros(total.shape, F32)
    told[0].wait()
    gather_sum(0, landing, arrived, total)
    for b in range(8):
        state_mem[b] = total[b].astype(BF16)
    kept = fetch(state_mem, state, sems.at[9])
    listed.wait()
    begin = diagonal(tables[0].astype(F32))
    mid = spread(tables[1].astype(F32))
    end = diagonal(tables[2].astype(F32))
    for g in range(4):
        start[:, g * 256 : g * 256 + 256] = mm(begin, lane_pair(state_mem, g))
    slots = slot_numbers(route, 1)
    sent = []
    for g, moved in middle_and_last(start, mid, end, folded, turned, False):
        put_pair(out, g, moved)
        sent += send_quarter(g, out, send, slots, slot_sems)
    for copy in sent + [kept, told[1]]:
        copy.wait()


def gather_sum(step, landing, arrived, total):
    def add(source, carry):
        for rank in range(CAP):
            brick = landing[source, step * CAP + rank, 0]

            @pl.when(brick > 0)
            def _():
                total[brick - 1] += arrived[source, rank * 256 : rank * 256 + 256, :].astype(F32)

        return carry

    lax.fori_loop(0, arrived.shape[0], add, 0)


def hand_out(step, landing, field, send, sems):
    copies = []
    for source in range(send.shape[0]):
        for rank in range(CAP):
            brick = jnp.maximum(landing[source, step * CAP + rank, 0] - 1, 0)
            target = send.at[source, rank * 256 : rank * 256 + 256, :]
            copies.append(fetch(field.at[brick], target, sems.at[source * CAP + rank]))
    return copies


def third_kernel(landing_in, arrived, target, *refs):
    send, adjoint, arrived_mem, landing, total, adjoint_mem, target_mem, sems, slot_sems = refs[-9:]
    told = fetch(landing_in, landing, sems.at[0])
    load = fetch(arrived, arrived_mem, sems.at[1])
    aim = fetch(target, target_mem, sems.at[2])
    total[...] = jnp.zeros(total.shape, F32)
    told.wait()
    load.wait()
    gather_sum(1, landing, arrived_mem, total)
    aim.wait()
    for b in range(8):
        final = total[b].astype(BF16).astype(F32)
        adjoint_mem[b] = (final - target_mem[b].astype(F32)).astype(BF16)
    sent = hand_out(1, landing, adjoint_mem, send, slot_sems)
    for copy in sent + [fetch(adjoint_mem, adjoint, sems.at[0])]:
        copy.wait()


def pulled_pair(arrived, slots, g):
    tiles = []
    for qs in (2 * g, 2 * g + 1):
        rows = [
            arrived[place, pl.ds(pl.multiple_of(rank * 256 + qs * 32, 32), 32), :] for place, rank in slots
        ]
        tiles.append(jnp.concatenate(rows, axis=0))
    return jnp.concatenate(tiles, axis=1)


def fourth_kernel(route, tables_in, landing_in, arrived, *refs):
    send, adjoint, tables, landing, start, folded, turned, out, sems, slot_sems = refs[-10:]
    listed = fetch(tables_in, tables, sems.at[1])
    told = fetch(landing_in, landing, sems.at[2])
    slots = slot_numbers(route, 1)
    listed.wait()
    begin = flipped_diagonal(tables[2].astype(F32))
    mid = spread(tables[1].astype(F32))
    end = flipped_diagonal(tables[0].astype(F32))
    for g in range(4):
        start[:, g * 256 : g * 256 + 256] = mm(begin, pulled_pair(arrived, slots, g))
    for g, moved in middle_and_last(start, mid, end, folded, turned, True):
        put_pair(out, g, moved)
    told.wait()
    sent = hand_out(0, landing, out, send, slot_sems)
    for copy in sent + [fetch(out, adjoint, sems.at[0])]:
        copy.wait()


def fifth_kernel(route, tables_in, arrived, *refs):
    adjoint, tables, start, folded, turned, out, sems = refs[-7:]
    load = fetch(tables_in, tables, sems.at[0, 7])
    slots = slot_numbers(route, 0)
    load.wait()
    begin = flipped_diagonal(tables[0].astype(F32))
    mid = spread(tables[1].astype(F32))
    end = flipped_diagonal(tables[2].astype(F32))
    for g in range(4):
        start[:, g * 256 : g * 256 + 256] = mm(begin, pulled_pair(arrived, slots, g))
    stored = []
    for g, moved in middle_and_last(start, mid, end, folded, turned, True):
        to_native(moved, g, out)
        for qh in range(4):
            rows = slice(qh * 8 + 2 * g, qh * 8 + 2 * g + 2)
            stored.append(fetch(out.at[rows], adjoint.at[rows], sems.at[g, qh]))
    for copy in stored:
        copy.wait()


def to_native(block, g, field):
    flat = mm(identity(), block, NT).astype(field.dtype)
    for index in range(8):
        x = (index % 4) * 8 + 2 * g + index // 4
        field[x] = flat[index * 32 : index * 32 + 32]


def x_form_to_native(source, folded, turned, field):
    for b in range(8):
        block = source[b].astype(F32)
        block = jnp.concatenate(
            [
                jnp.concatenate([block[g * 64 : g * 64 + 32], block[g * 64 + 32 : g * 64 + 64]], axis=1)
                for g in range(4)
            ],
            axis=0,
        )
        swap_brick(block, folded, turned, b, 1)
    for g in range(4):
        to_native(turned[0:256, g * 256 : g * 256 + 256], g, field)


def tap(offset):
    value = jnp.zeros(offset.shape, F32)
    for step, weight in TAPS:
        value = jnp.where(offset == step, weight, value)
        value = jnp.where(offset == -step, -weight, value)
    return value


def stencils():
    size = 256
    row, col = iota((size, size), 0), iota((size, size), 1)
    along_y = halves(jnp.where(row // 32 == col // 32, tap(col - row), 0.0))
    along_z = halves(tap(row - col))
    row, col = iota((size, 48), 0), iota((size, 48), 1)
    layer = col // 8
    place = jnp.where(layer < RIM, layer - RIM, layer - RIM + 32)
    rim_y = halves(jnp.where(row // 32 == col % 8, tap(place - row % 32), 0.0))
    return along_y, rim_y, along_z


def rim_picker():
    row, col = iota((48, 256), 0), iota((48, 256), 1)
    layer = row // 8
    place = jnp.where(layer < RIM, layer, layer - RIM + 29)
    return ((row % 8 == col // 32) & (place == col % 32)).astype(F32).astype(BF16)


def difference_x(padded, g):
    total = None
    for step, weight in TAPS:
        ahead = padded[pl.ds(8 * g + RIM + step, 8)]
        behind = padded[pl.ds(8 * g + RIM - step, 8)]
        term = weight * (ahead - behind)
        total = term if total is None else total + term
    return total.reshape(256, 256)


def difference_y(parts, rims, along_y, rim_y):
    total = mm(along_y[0], parts[0]) + mm(along_y[1], parts[0])
    if len(parts) > 1:
        total = total + mm(along_y[0], parts[1])
    return total + mm(rim_y[0], rims) + mm(rim_y[1], rims)


def difference_z(parts, along_z):
    total = mm(parts[0], along_z[0]) + mm(parts[0], along_z[1])
    if len(parts) > 1:
        total = total + mm(parts[1], along_z[0])
    return total


def rim_rows(before, after, base, g):
    rows = [before[base + h, (g // 2) * 16 : (g // 2) * 16 + 16, :].astype(F32) for h in range(RIM)]
    rows += [after[base + h, (g // 2) * 16 : (g // 2) * 16 + 16, :].astype(F32) for h in range(RIM)]
    half = (g % 2) * 8
    return jnp.concatenate([value[half : half + 8] for value in rows], axis=0).astype(BF16)


def put_rims(blocks, base, low_y, high_y):
    picker = rim_picker()
    for pair in range(2):
        left, right = mm(picker, blocks[2 * pair]), mm(picker, blocks[2 * pair + 1])
        for layer in range(2 * RIM):
            value = jnp.concatenate(
                [left[layer * 8 : layer * 8 + 8], right[layer * 8 : layer * 8 + 8]], axis=0
            ).astype(BF16)
            target = low_y if layer < RIM else high_y
            target[base + layer % RIM, pair * 16 : pair * 16 + 16, :] = value


def edge_kernel(template, velocity, sent, low_x, high_x, low_y, high_y, field, first_x, last_x, mid_v, sems):
    loads = [
        fetch(template, field, sems.at[0]),
        fetch(velocity.at[0, 0:RIM], first_x, sems.at[1]),
        fetch(velocity.at[0, 29:32], last_x, sems.at[2]),
        fetch(velocity.at[1], mid_v, sems.at[3]),
    ]
    for load in loads:
        load.wait()
    low_x[0:RIM] = field[0:RIM]
    high_x[0:RIM] = field[29:32]
    low_x[RIM : 2 * RIM] = first_x[...].astype(BF16)
    high_x[RIM : 2 * RIM] = last_x[...].astype(BF16)
    put_rims([field[8 * g : 8 * g + 8].reshape(256, 256) for g in range(4)], 0, low_y, high_y)
    put_rims([mid_v[8 * g : 8 * g + 8].astype(BF16).reshape(256, 256) for g in range(4)], RIM, low_y, high_y)


def prepare_kernel(picks, operators, target, edge, target_z, tables):
    chosen = [picks[1, 0, 0, b] for b in range(8)]
    for axis in range(3):
        tables[axis] = table_rows(operators, chosen, axis).astype(BF16)
    for g in range(4):
        block = jnp.concatenate(
            [target[qh * 8 + qs] for qs in (2 * g, 2 * g + 1) for qh in range(4)], axis=0
        )
        put_pair(target_z, g, mm(identity(), block, NT).astype(BF16))


def divergence_kernel(velocity, before_x, after_x, before_y, after_y, sent, divergence, padded):
    along_y, rim_y, along_z = stencils()
    padded[0:RIM] = before_x[RIM : 2 * RIM].astype(F32)
    padded[RIM : RIM + 32] = velocity[0]
    padded[RIM + 32 : 2 * RIM + 32] = after_x[RIM : 2 * RIM].astype(F32)
    for g in range(4):
        along_one = halves(velocity[1, 8 * g : 8 * g + 8].reshape(256, 256))
        along_two = halves(velocity[2, 8 * g : 8 * g + 8].reshape(256, 256))
        total = (
            difference_x(padded, g)
            + difference_y(along_one, rim_rows(before_y, after_y, RIM, g), along_y, rim_y)
            + difference_z(along_two, along_z)
        )
        divergence[8 * g : 8 * g + 8] = total.reshape(8, 32, 256)


def rims_kernel(state, divergence, sent, native, low_x, high_x, low_y, high_y, folded, turned):
    x_form_to_native(state, folded, turned, native)
    low_x[0:RIM] = native[0:RIM]
    high_x[0:RIM] = native[29:32]
    low_x[RIM : 2 * RIM] = divergence[0:RIM].astype(BF16)
    high_x[RIM : 2 * RIM] = divergence[29:32].astype(BF16)
    put_rims([native[8 * g : 8 * g + 8].reshape(256, 256) for g in range(4)], 0, low_y, high_y)
    put_rims(
        [divergence[8 * g : 8 * g + 8].astype(BF16).reshape(256, 256) for g in range(4)], RIM, low_y, high_y
    )


def gradient_kernel(
    template,
    state,
    divergence,
    adjoint_two,
    adjoint_one,
    b0x,
    a0x,
    b0y,
    a0y,
    b1x,
    a1x,
    b1y,
    a1y,
    sent,
    gradient,
    folded,
    turned,
    weight_two,
    weight_one,
    pad_zero,
    pad_one,
    pad_div,
):
    x_form_to_native(adjoint_one, folded, turned, weight_one)
    for g in range(4):
        to_native(lane_pair(adjoint_two, g), g, weight_two)
    along_y, rim_y, along_z = stencils()
    for padded, before, middle, after, base in (
        (pad_zero, b0x, template, a0x, 0),
        (pad_one, b1x, state, a1x, 0),
        (pad_div, b1x, divergence, a1x, RIM),
    ):
        padded[0:RIM] = before[base : base + RIM].astype(F32)
        padded[RIM : RIM + 32] = middle[...].astype(F32)
        padded[RIM + 32 : 2 * RIM + 32] = after[base : base + RIM].astype(F32)
    for g in range(4):
        zero = (template[8 * g : 8 * g + 8].reshape(256, 256),)
        one = (state[8 * g : 8 * g + 8].reshape(256, 256),)
        div = halves(divergence[8 * g : 8 * g + 8].reshape(256, 256))
        weigh_one = 0.5 * weight_one[8 * g : 8 * g + 8].reshape(256, 256)
        weigh_two = 0.5 * weight_two[8 * g : 8 * g + 8].reshape(256, 256)
        for axis in range(3):
            if axis == 0:
                parts = [difference_x(padded, g) for padded in (pad_zero, pad_one, pad_div)]
            elif axis == 1:
                parts = [
                    difference_y(zero, rim_rows(b0y, a0y, 0, g), along_y, rim_y),
                    difference_y(one, rim_rows(b1y, a1y, 0, g), along_y, rim_y),
                    difference_y(div, rim_rows(b1y, a1y, RIM, g), along_y, rim_y),
                ]
            else:
                parts = [difference_z(value, along_z) for value in (zero, one, div)]
            value = weigh_one * parts[0] + weigh_two * parts[1] - 0.25 * parts[2]
            gradient[axis, 8 * g : 8 * g + 8] = value.reshape(8, 32, 256)


SCALAR = pl.BlockSpec(memory_space=pltpu.SMEM)
WHOLE = pl.BlockSpec(memory_space=pltpu.VMEM)
NEAR = pl.BlockSpec(memory_space=pltpu.VMEM)
FAR = pl.BlockSpec(memory_space=pltpu.HBM)
FOLDED = (32, 64, 128)
FLAT = (256, 1024)
NATIVE = (32, 32, 256)
FORM = (8, 256, 128)
TABLES = (3, 32, 256)


def pinned(value, spec):
    if spec is FAR:
        return pltpu.with_memory_space_constraint(value, pltpu.HBM)
    if spec is NEAR:
        return pltpu.with_memory_space_constraint(value, pltpu.VMEM)
    return value


SHORT, LONG = 1 << 20, 1 << 36


def call(kernel, out, in_specs, out_specs, scratch, work=LONG):
    made = pl.pallas_call(
        kernel,
        out_shape=out,
        in_specs=in_specs,
        out_specs=out_specs,
        scratch_shapes=scratch,
        compiler_params=pltpu.CompilerParams(vmem_limit_bytes=24 * 1024 * 1024),
        cost_estimate=pl.CostEstimate(flops=work, bytes_accessed=1024 * 1024, transcendentals=0),
    )

    def apply(*values):
        return made(*[pinned(value, spec) for value, spec in zip(values, in_specs, strict=True)])

    return apply


def like(shape, dtype):
    return jax.ShapeDtypeStruct(shape, dtype)


def far(shape, dtype):
    return pltpu.HBM(shape, dtype)


def neighbours(low_x, high_x, low_y, high_y):
    moved = []
    for low, high, axis in ((low_x, high_x, "gx"), (low_y, high_y, "gy")):
        size = lax.axis_size(axis)
        up = [(i, i + 1) for i in range(size - 1)]
        down = [(i + 1, i) for i in range(size - 1)]
        moved += [lax.ppermute(high, axis, up), lax.ppermute(low, axis, down)]
    return moved


def swap_slots(send):
    return lax.all_to_all(send, "gx", split_axis=0, concat_axis=0, tiled=True)


def shards(template, target_image, velocity, operators, route, target_brick, operator_index):
    peers = lax.axis_size("gx")
    sems = pltpu.SemaphoreType.DMA((16,))
    slot_sems = pltpu.SemaphoreType.DMA((peers * CAP,))
    quarter_sems = pltpu.SemaphoreType.DMA((4, 8))
    turning = [pltpu.VMEM(FLAT, F32), pltpu.VMEM(FOLDED, F32), pltpu.VMEM((512, 1024), BF16)]
    form = pltpu.VMEM(FORM, BF16)
    total = pltpu.VMEM(FORM, F32)
    landed = pltpu.SMEM((peers, 8, 128), jnp.int32)
    slots = far((peers, 512, 128), BF16)
    table_rows_count = operators.shape[1] * operators.shape[2] * operators.shape[3]
    listed = operators.transpose(1, 2, 3, 0).reshape(table_rows_count, operators.shape[0])
    route = route.reshape(route.shape[:4])

    send, tables_zero = call(
        first_kernel,
        [far((peers, 528, 128), BF16), far(TABLES, BF16)],
        [FAR] * 5,
        [FAR, FAR],
        [pltpu.SMEM(route.shape, jnp.int32)] * 3
        + [pltpu.VMEM(listed.shape, BF16), pltpu.VMEM(NATIVE, BF16)]
        + turning
        + [
            form,
            pltpu.VMEM((peers, 16, 128), F32),
            pltpu.VMEM((peers, 16, 128), BF16),
            pltpu.VMEM(TABLES, BF16),
            sems,
            quarter_sems,
        ],
        SHORT,
    )(operator_index, route, target_brick, listed, template)
    arrived = swap_slots(send)

    rim = like((2 * RIM, 32, 256), BF16)
    low_x, high_x, low_y, high_y = call(
        edge_kernel,
        [rim] * 4,
        [FAR] * 3,
        [WHOLE] * 4,
        [pltpu.VMEM(NATIVE, BF16)] + [pltpu.VMEM((RIM, 32, 256), F32)] * 2 + [pltpu.VMEM(NATIVE, F32), sems],
    )(template, velocity, send)
    target_z, tables_one = call(
        prepare_kernel, [far(FORM, BF16), far(TABLES, BF16)], [SCALAR] + [WHOLE] * 3, [WHOLE] * 2, []
    )(operator_index, listed, target_image, low_x)
    b0x, a0x, b0y, a0y = neighbours(low_x, high_x, low_y, high_y)
    send, state_x, landing = call(
        second_kernel,
        [slots, far(FORM, BF16), far((peers, 8, 128), jnp.int32)],
        [SCALAR, FAR, NEAR],
        [FAR] * 3,
        [
            pltpu.VMEM((peers, 8, 128), jnp.int32),
            pltpu.VMEM(TABLES, BF16),
            landed,
            form,
            total,
        ]
        + turning
        + [form, sems, quarter_sems],
        SHORT,
    )(route, tables_one, arrived)
    arrived = swap_slots(send)

    divergence = call(
        divergence_kernel, like(NATIVE, F32), [WHOLE] * 5 + [FAR], WHOLE, [pltpu.VMEM((38, 32, 256), F32)]
    )(velocity, b0x, a0x, b0y, a0y, send)

    state, low_x, high_x, low_y, high_y = call(
        rims_kernel, [far(NATIVE, BF16)] + [rim] * 4, [WHOLE] * 2 + [FAR], [WHOLE] * 5, turning[1:]
    )(state_x, divergence, send)
    send, adjoint_two = call(
        third_kernel,
        [slots, far(FORM, BF16)],
        [FAR, pl.BlockSpec(memory_space=pl.ANY), FAR, FAR],
        [FAR] * 2,
        [pltpu.VMEM((peers, 512, 128), BF16), landed, total, form, form, sems, slot_sems],
        SHORT,
    )(landing, arrived, target_z, state)
    arrived = swap_slots(send)
    b1x, a1x, b1y, a1y = neighbours(low_x, high_x, low_y, high_y)

    send, adjoint_one = call(
        fourth_kernel,
        [slots, far(FORM, BF16)],
        [SCALAR, FAR, FAR, NEAR],
        [FAR] * 2,
        [pltpu.VMEM(TABLES, BF16), landed] + turning + [form, sems, slot_sems],
        SHORT,
    )(route, tables_one, landing, arrived)
    arrived = swap_slots(send)

    gradient = call(
        gradient_kernel,
        far((3,) + NATIVE, F32),
        [WHOLE] * 13 + [FAR],
        WHOLE,
        turning[1:] + [pltpu.VMEM(NATIVE, F32)] * 2 + [pltpu.VMEM((38, 32, 256), F32)] * 3,
    )(template, state, divergence, adjoint_two, adjoint_one, b0x, a0x, b0y, a0y, b1x, a1x, b1y, a1y, send)

    adjoint = call(
        fifth_kernel,
        far(NATIVE, BF16),
        [SCALAR, FAR, NEAR, FAR],
        FAR,
        [pltpu.VMEM(TABLES, BF16)] + turning + [pltpu.VMEM(NATIVE, BF16), quarter_sems],
        SHORT,
    )(route, tables_zero, arrived, gradient)
    return gradient, adjoint


def solution(mesh):
    placed = (
        P("gx", "gy", None),
        P("gx", "gy", None),
        P(None, "gx", "gy", None),
        P(),
        P(None, "gx", "gy", None, None),
        P(None, "gx", "gy", None),
        P(None, "gx", "gy", None),
    )
    return jax.shard_map(
        shards,
        mesh=mesh,
        in_specs=placed,
        out_specs=(P(None, "gx", "gy", None), P("gx", "gy", None)),
        check_vma=False,
    )
```

profile of v0, /device:TPU:0, one launch (start us, length us, event | category | flops | bytes accessed | tf_op | source)
XLA Modules:
  0.0 145.8 jit_solution(13492865147678120214)
XLA Ops:
  0.6 5.0 %shard_map.86 = (bf16[8,528,128]{2,1,0:T(8,128)(2,1)}, bf16[3,32,256]{2,1,0:T(8,128)(2,1)}) custom-call(s32[2,1,1,8]{3,2,1,0:T(1,128)} %picks.1, s32[2,1,1,8]{3,2,1,0:T(1,128)} %bitcast.8, s32[2,1,1,8]{3,2,1,0:T(1,128)} %refs_2_.1, bf16[3072,64]{1,0:T(8,128)(2,1)} %bitcast.6, bf16[32,32,256]{2,1,0:T(8,128)(2,1)} %template.3), custom_call_target="tpu_custom_call" | custom-call | flops 1048576 | bytes 1048576 | tf_op jit(solution)/shard_map/pallas_call | solution.py:555
  5.6 7.3 %all-to-all-start = ((bf16[8,528,128]{2,1,0:T(8,128)(2,1)}), bf16[8,528,128]{2,1,0:T(8,128)(2,1)S(1)}, u32[]{:S(2)}, u32[]{:S(2)}) async-start(bf16[8,528,128]{2,1,0:T(8,128)(2,1)} %get-tuple-element.22.sent), calls=%async_computation | async-start | bytes 2162688 | tf_op jit(solution)/shard_map/all_to_all | solution.py:579
  12.9 2.0 %shard_map.87 = (bf16[6,32,256]{2,1,0:T(8,128)(2,1)S(1)}, bf16[6,32,256]{2,1,0:T(8,128)(2,1)S(1)}, bf16[6,32,256]{2,1,0:T(8,128)(2,1)S(1)}, bf16[6,32,256]{2,1,0:T(8,128)(2,1)S(1)}) custom-call(bf16[32,32,256]{2,1,0:T(8,128)(2,1)} %template.3, f32[3,32,32,256]{3,2,1,0:T(8,128)} %velocity.3, bf16[8,528,128]{2,1,0:T(8,128)(2,1)} %get-tuple-element.22.sent), custom_call_target="tpu_custom_call" | custom-call | flops 68719476736 | bytes 1048576 | tf_op jit(solution)/shard_map/pallas_call | solution.py:555
  14.9 3.9 %collective-permute-start = (bf16[6,32,256]{2,1,0:T(8,128)(2,1)S(1)}, bf16[6,32,256]{2,1,0:T(8,128)(2,1)S(1)}, u32[]{:S(2)}, u32[]{:S(2)}) collective-permute-start(bf16[6,32,256]{2,1,0:T(8,128)(2,1)S(1)} %get-tuple-element.26), channel_id=1, source_target_pairs={{0,4},{4,8},{8,12},{12,16},{16,20},{20,24},{24,28},{1,5},{5,9},{9,... | collective-permute-start | bytes 294920 | tf_op jit(solution)/shard_map/ppermute | solution.py:574
  18.8 1.3 collective-permute-start.2
  20.1 1.3 collective-permute-start.3
  22.8 2.0 %shard_map.88 = (bf16[8,256,128]{2,1,0:T(8,128)(2,1)}, bf16[3,32,256]{2,1,0:T(8,128)(2,1)}) custom-call(s32[2,1,1,8]{3,2,1,0:T(1,128)S(1)} %copy-done.4, bf16[3072,64]{1,0:T(8,128)(2,1)S(1)} %bitcast.7, bf16[32,32,256]{2,1,0:T(8,128)(2,1)S(1)} %copy-done.6, bf16[6,32,256]{2,1,0:T(8,128)(2,1)S(1)} %get-tuple-element.23.edge), custom_call_target="tpu_custom_call" | custom-call | flops 68719476736 | bytes 1048576 | tf_op jit(solution)/shard_map/pallas_call | solution.py:555
  24.8 15.6 %all-to-all-done.arrived = bf16[8,528,128]{2,1,0:T(8,128)(2,1)S(1)} async-done(((bf16[8,528,128]{2,1,0:T(8,128)(2,1)}), bf16[8,528,128]{2,1,0:T(8,128)(2,1)S(1)}, u32[]{:S(2)}, u32[]{:S(2)}) %all-to-all-start) | async-done | bytes 1081376 | tf_op jit(solution)/shard_map/all_to_all | solution.py:579
  40.4 4.8 %shard_map.89 = (bf16[8,512,128]{2,1,0:T(8,128)(2,1)}, bf16[8,256,128]{2,1,0:T(8,128)(2,1)}, s32[8,8,128]{2,1,0:T(8,128)}) custom-call(s32[2,1,1,8]{3,2,1,0:T(1,128)S(1)} %bitcast.9, bf16[3,32,256]{2,1,0:T(8,128)(2,1)} %get-tuple-element.24.tables_in, bf16[8,528,128]{2,1,0:T(8,128)(2,1)S(1)} %all-to-all-done.arrived), custom_call_target="tpu_custom_call" | custom-call | flops 1048576 | bytes 1048576 | tf_op jit(solution)/shard_map/pallas_call | solution.py:555
  45.2 3.7 %all-to-all-start.1 = ((bf16[8,512,128]{2,1,0:T(8,128)(2,1)}), bf16[8,512,128]{2,1,0:T(8,128)(2,1)S(1)}, u32[]{:S(2)}, u32[]{:S(2)}) async-start(bf16[8,512,128]{2,1,0:T(8,128)(2,1)} %get-tuple-element.29.sent), calls=%async_computation.1 | async-start | bytes 2097152 | tf_op jit(solution)/shard_map/all_to_all | solution.py:579
  49.0 1.9 %copy-done.5 = f32[3,32,32,256]{3,2,1,0:T(8,128)S(1)} copy-done((f32[3,32,32,256]{3,2,1,0:T(8,128)S(1)}, f32[3,32,32,256]{3,2,1,0:T(8,128)}, u32[]{:S(2)}) %copy-start.5) | copy-done | bytes 3145752
  50.9 1.5 %shard_map.90.divergence = f32[32,32,256]{2,1,0:T(8,128)S(1)} custom-call(f32[3,32,32,256]{3,2,1,0:T(8,128)S(1)} %copy-done.5, bf16[6,32,256]{2,1,0:T(8,128)(2,1)S(1)} %collective-permute-done.before_x.b0x, bf16[6,32,256]{2,1,0:T(8,128)(2,1)S(1)} %collective-permute-done.1.after_x.a0x, bf16[6,32,256]{2,1,0:T(8,128)(2,1)S(1)} %collective-permute-done.2.before_y.b0y, ...), custom_call_target="tpu_custom_call" | custom-call | flops 68719476736 | bytes 1048576 | tf_op jit(solution)/shard_map/pallas_call | solution.py:555
  52.4 1.6 %shard_map.91 = (bf16[32,32,256]{2,1,0:T(8,128)(2,1)}, bf16[6,32,256]{2,1,0:T(8,128)(2,1)S(1)}, bf16[6,32,256]{2,1,0:T(8,128)(2,1)S(1)}, bf16[6,32,256]{2,1,0:T(8,128)(2,1)S(1)}, bf16[6,32,256]{2,1,0:T(8,128)(2,1)S(1)}) custom-call(bf16[8,256,128]{2,1,0:T(8,128)(2,1)S(1)} %copy-done.9, f32[32,32,256]{2,1,0:T(8,128)S(1)} %shard_map.90.divergence, ...), custom_call_target="tpu_custom_call" | custom-call | flops 68719476736 | bytes 1048576 | tf_op jit(solution)/shard_map/pallas_call | solution.py:555
  54.9 19.2 %all-to-all-done.1.arrived = bf16[8,512,128]{2,1,0:T(8,128)(2,1)S(1)} async-done(((bf16[8,512,128]{2,1,0:T(8,128)(2,1)}), bf16[8,512,128]{2,1,0:T(8,128)(2,1)S(1)}, u32[]{:S(2)}, u32[]{:S(2)}) %all-to-all-start.1) | async-done | bytes 1048608 | tf_op jit(solution)/shard_map/all_to_all | solution.py:579
  74.1 3.0 %shard_map.92 = (bf16[8,512,128]{2,1,0:T(8,128)(2,1)}, bf16[8,256,128]{2,1,0:T(8,128)(2,1)}) custom-call(s32[8,8,128]{2,1,0:T(8,128)} %get-tuple-element.31.landing_in, bf16[8,512,128]{2,1,0:T(8,128)(2,1)S(1)} %all-to-all-done.1.arrived, bf16[8,256,128]{2,1,0:T(8,128)(2,1)} %get-tuple-element.32.target, bf16[32,32,256]{2,1,0:T(8,128)(2,1)} %get-tuple-element.30.refs_0_.state), custom_call_target="tpu_custom_call" | custom-call | flops 1048576 | bytes 1048576 | tf_op jit(solution)/shard_map/pallas_call | solution.py:555
  77.1 3.7 %all-to-all-start.2 = ((bf16[8,512,128]{2,1,0:T(8,128)(2,1)}), bf16[8,512,128]{2,1,0:T(8,128)(2,1)S(1)}, u32[]{:S(2)}, u32[]{:S(2)}) async-start(bf16[8,512,128]{2,1,0:T(8,128)(2,1)} %get-tuple-element.34), calls=%async_computation.2 | async-start | bytes 2097152 | tf_op jit(solution)/shard_map/all_to_all | solution.py:579
  80.8 3.8 %collective-permute-start.4 = (bf16[6,32,256]{2,1,0:T(8,128)(2,1)S(1)}, bf16[6,32,256]{2,1,0:T(8,128)(2,1)S(1)}, u32[]{:S(2)}, u32[]{:S(2)}) collective-permute-start(bf16[6,32,256]{2,1,0:T(8,128)(2,1)S(1)} %get-tuple-element.36), channel_id=1, source_target_pairs={{0,4},{4,8},{8,12},{12,16},{16,20},{20,24},{24,28},{1,5},{5,9},{9,... | collective-permute-start | bytes 294920 | tf_op jit(solution)/shard_map/ppermute | solution.py:574
  86.0 1.9 %collective-permute-start.6 = (bf16[6,32,256]{2,1,0:T(8,128)(2,1)S(1)}, bf16[6,32,256]{2,1,0:T(8,128)(2,1)}, u32[]{:S(2)}, u32[]{:S(2)}) collective-permute-start(bf16[6,32,256]{2,1,0:T(8,128)(2,1)S(1)} %get-tuple-element.38), channel_id=1, source_target_pairs={{0,1},{1,2},{2,3},{4,5},{5,6},{6,7},{8,9},{9,10},{10,11},{12,13},{... | collective-permute-start | bytes 294920 | tf_op jit(solution)/shard_map/ppermute | solution.py:574
  89.2 18.4 %all-to-all-done.2.arrived = bf16[8,512,128]{2,1,0:T(8,128)(2,1)S(1)} async-done(((bf16[8,512,128]{2,1,0:T(8,128)(2,1)}), bf16[8,512,128]{2,1,0:T(8,128)(2,1)S(1)}, u32[]{:S(2)}, u32[]{:S(2)}) %all-to-all-start.2) | async-done | bytes 1048608 | tf_op jit(solution)/shard_map/all_to_all | solution.py:579
  107.6 4.4 %shard_map.93 = (bf16[8,512,128]{2,1,0:T(8,128)(2,1)}, bf16[8,256,128]{2,1,0:T(8,128)(2,1)}) custom-call(s32[2,1,1,8]{3,2,1,0:T(1,128)S(1)} %bitcast.10, bf16[3,32,256]{2,1,0:T(8,128)(2,1)} %get-tuple-element.24.tables_in, s32[8,8,128]{2,1,0:T(8,128)} %get-tuple-element.31.landing_in, bf16[8,512,128]{2,1,0:T(8,128)(2,1)S(1)} %all-to-all-done.2.arrived), custom_call_target="tpu_custom_call" | custom-call | flops 1048576 | bytes 1048576 | tf_op jit(solution)/shard_map/pallas_call | solution.py:555
  112.0 3.7 %all-to-all-start.3 = ((bf16[8,512,128]{2,1,0:T(8,128)(2,1)}), bf16[8,512,128]{2,1,0:T(8,128)(2,1)S(1)}, u32[]{:S(2)}, u32[]{:S(2)}) async-start(bf16[8,512,128]{2,1,0:T(8,128)(2,1)} %get-tuple-element.40.sent), calls=%async_computation.3 | async-start | bytes 2097152 | tf_op jit(solution)/shard_map/all_to_all | solution.py:579
  118.1 7.0 %shard_map.94.refs_0_ = f32[3,32,32,256]{3,2,1,0:T(8,128)} custom-call(bf16[32,32,256]{2,1,0:T(8,128)(2,1)S(1)} %copy-done.1, bf16[32,32,256]{2,1,0:T(8,128)(2,1)S(1)} %copy-done.2, f32[32,32,256]{2,1,0:T(8,128)S(1)} %copy-done.11, bf16[8,256,128]{2,1,0:T(8,128)(2,1)S(1)} %copy-done.7, bf16[8,256,128]{2,1,0:T(8,128)(2,1)S(1)} %copy-done.8, ...), custom_call_target="tpu_custom_call" | custom-call | flops 68719476736 | bytes 1048576 | tf_op jit(solution)/shard_map/pallas_call | solution.py:555
  125.1 15.7 %all-to-all-done.3.arrived = bf16[8,512,128]{2,1,0:T(8,128)(2,1)S(1)} async-done(((bf16[8,512,128]{2,1,0:T(8,128)(2,1)}), bf16[8,512,128]{2,1,0:T(8,128)(2,1)S(1)}, u32[]{:S(2)}, u32[]{:S(2)}) %all-to-all-start.3) | async-done | bytes 1048608 | tf_op jit(solution)/shard_map/all_to_all | solution.py:579
  140.8 4.9 %shard_map.95 = bf16[32,32,256]{2,1,0:T(8,128)(2,1)} custom-call(s32[2,1,1,8]{3,2,1,0:T(1,128)S(1)} %bitcast.11, bf16[3,32,256]{2,1,0:T(8,128)(2,1)} %get-tuple-element.41.tables_in, bf16[8,512,128]{2,1,0:T(8,128)(2,1)S(1)} %all-to-all-done.3.arrived, f32[3,32,32,256]{3,2,1,0:T(8,128)} %shard_map.94.refs_0_), custom_call_target="tpu_custom_call" | custom-call | flops 1048576 | bytes 1048576 | tf_op jit(solution)/shard_map/pallas_call | solution.py:555
  (34 shorter events, 7.2 us)
Async XLA Ops:
  5.6 34.8 %all-to-all-start = ((bf16[8,528,128]{2,1,0:T(8,128)(2,1)}), bf16[8,528,128]{2,1,0:T(8,128)(2,1)S(1)}, u32[]{:S(2)}, u32[]{:S(2)}) async-start(bf16[8,528,128]{2,1,0:T(8,128)(2,1)} %get-tuple-element.22.sent), calls=%async_computation | async-start | bytes 2162688 | tf_op jit(solution)/shard_map/all_to_all | solution.py:579
  12.9 9.9 %copy-start = (bf16[64,3,32,32]{0,3,2,1:T(8,128)(2,1)S(1)}, bf16[64,3,32,32]{0,3,2,1:T(8,128)(2,1)}, u32[]{:S(2)}) copy-start(bf16[64,3,32,32]{0,3,2,1:T(8,128)(2,1)} %param.10) | copy-start | bytes 1179652
  12.9 9.9 %copy-start.4 = (s32[2,1,1,8]{3,2,1,0:T(1,128)S(1)}, s32[2,1,1,8]{3,2,1,0:T(1,128)}, u32[]{:S(2)}) copy-start(s32[2,1,1,8]{3,2,1,0:T(1,128)} %picks.1) | copy-start | bytes 196
  12.9 9.9 %copy-start.6 = (bf16[32,32,256]{2,1,0:T(8,128)(2,1)S(1)}, bf16[32,32,256]{2,1,0:T(8,128)(2,1)}, u32[]{:S(2)}) copy-start(bf16[32,32,256]{2,1,0:T(8,128)(2,1)} %target.1) | copy-start | bytes 1572868
  14.9 34.0 %collective-permute-start = (bf16[6,32,256]{2,1,0:T(8,128)(2,1)S(1)}, bf16[6,32,256]{2,1,0:T(8,128)(2,1)S(1)}, u32[]{:S(2)}, u32[]{:S(2)}) collective-permute-start(bf16[6,32,256]{2,1,0:T(8,128)(2,1)S(1)} %get-tuple-element.26), channel_id=1, source_target_pairs={{0,4},{4,8},{8,12},{12,16},{16,20},{20,24},{24,28},{1,5},{5,9},{9,... | collective-permute-start | bytes 294920 | tf_op jit(solution)/shard_map/ppermute | solution.py:574
  18.8 30.1 %collective-permute-start.2 = (bf16[6,32,256]{2,1,0:T(8,128)(2,1)S(1)}, bf16[6,32,256]{2,1,0:T(8,128)(2,1)S(1)}, u32[]{:S(2)}, u32[]{:S(2)}) collective-permute-start(bf16[6,32,256]{2,1,0:T(8,128)(2,1)S(1)} %get-tuple-element.27), channel_id=1, source_target_pairs={{0,1},{1,2},{2,3},{4,5},{5,6},{6,7},{8,9},{9,10},{10,11},{12,13},{... | collective-permute-start | bytes 294920 | tf_op jit(solution)/shard_map/ppermute | solution.py:574
  20.1 28.8 %collective-permute-start.3 = (bf16[6,32,256]{2,1,0:T(8,128)(2,1)S(1)}, bf16[6,32,256]{2,1,0:T(8,128)(2,1)S(1)}, u32[]{:S(2)}, u32[]{:S(2)}) collective-permute-start(bf16[6,32,256]{2,1,0:T(8,128)(2,1)S(1)} %get-tuple-element.28), channel_id=1, source_target_pairs={{1,0},{2,1},{3,2},{5,4},{6,5},{7,6},{9,8},{10,9},{11,10},{13,12},{... | collective-permute-start | bytes 294920 | tf_op jit(solution)/shard_map/ppermute | solution.py:574
  21.4 19.0 %copy-start.3 = (s32[2,1,1,8,1]{3,4,2,1,0:T(1,128)S(1)}, s32[2,1,1,8,1]{3,4,2,1,0:T(1,128)}, u32[]{:S(2)}) copy-start(s32[2,1,1,8,1]{3,4,2,1,0:T(1,128)} %param.11) | copy-start | bytes 196
  21.4 27.5 %collective-permute-start.1 = (bf16[6,32,256]{2,1,0:T(8,128)(2,1)S(1)}, bf16[6,32,256]{2,1,0:T(8,128)(2,1)S(1)}, u32[]{:S(2)}, u32[]{:S(2)}) collective-permute-start(bf16[6,32,256]{2,1,0:T(8,128)(2,1)S(1)} %get-tuple-element.23.edge), channel_id=1, source_target_pairs={{4,0},{8,4},{12,8},{16,12},{20,16},{24,20},{28,24},{5,1},{9,5},{13... | collective-permute-start | bytes 294920 | tf_op jit(solution)/shard_map/ppermute | solution.py:574
  45.2 7.1 %copy-start.9 = (bf16[8,256,128]{2,1,0:T(8,128)(2,1)S(1)}, bf16[8,256,128]{2,1,0:T(8,128)(2,1)}, u32[]{:S(2)}) copy-start(bf16[8,256,128]{2,1,0:T(8,128)(2,1)} %get-tuple-element.25.state) | copy-start | bytes 1572868
  45.2 28.9 %all-to-all-start.1 = ((bf16[8,512,128]{2,1,0:T(8,128)(2,1)}), bf16[8,512,128]{2,1,0:T(8,128)(2,1)S(1)}, u32[]{:S(2)}, u32[]{:S(2)}) async-start(bf16[8,512,128]{2,1,0:T(8,128)(2,1)} %get-tuple-element.29.sent), calls=%async_computation.1 | async-start | bytes 2097152 | tf_op jit(solution)/shard_map/all_to_all | solution.py:579
  49.0 1.9 %copy-start.5 = (f32[3,32,32,256]{3,2,1,0:T(8,128)S(1)}, f32[3,32,32,256]{3,2,1,0:T(8,128)}, u32[]{:S(2)}) copy-start(f32[3,32,32,256]{3,2,1,0:T(8,128)} %velocity.3) | copy-start | bytes 9437188
  53.9 1.0 copy-start.10
  77.1 38.7 %copy-start.1 = (bf16[32,32,256]{2,1,0:T(8,128)(2,1)S(1)}, bf16[32,32,256]{2,1,0:T(8,128)(2,1)}, u32[]{:S(2)}) copy-start(bf16[32,32,256]{2,1,0:T(8,128)(2,1)} %template.3) | copy-start | bytes 1572868
  77.1 38.7 %copy-start.2 = (bf16[32,32,256]{2,1,0:T(8,128)(2,1)S(1)}, bf16[32,32,256]{2,1,0:T(8,128)(2,1)}, u32[]{:S(2)}) copy-start(bf16[32,32,256]{2,1,0:T(8,128)(2,1)} %get-tuple-element.30.refs_0_.state) | copy-start | bytes 1572868
  77.1 38.7 %copy-start.7 = (bf16[8,256,128]{2,1,0:T(8,128)(2,1)S(1)}, bf16[8,256,128]{2,1,0:T(8,128)(2,1)}, u32[]{:S(2)}) copy-start(bf16[8,256,128]{2,1,0:T(8,128)(2,1)} %get-tuple-element.33.adjoint_two) | copy-start | bytes 1572868
  77.1 30.5 %all-to-all-start.2 = ((bf16[8,512,128]{2,1,0:T(8,128)(2,1)}), bf16[8,512,128]{2,1,0:T(8,128)(2,1)S(1)}, u32[]{:S(2)}, u32[]{:S(2)}) async-start(bf16[8,512,128]{2,1,0:T(8,128)(2,1)} %get-tuple-element.34), calls=%async_computation.2 | async-start | bytes 2097152 | tf_op jit(solution)/shard_map/all_to_all | solution.py:579
  80.8 34.9 %collective-permute-start.4 = (bf16[6,32,256]{2,1,0:T(8,128)(2,1)S(1)}, bf16[6,32,256]{2,1,0:T(8,128)(2,1)S(1)}, u32[]{:S(2)}, u32[]{:S(2)}) collective-permute-start(bf16[6,32,256]{2,1,0:T(8,128)(2,1)S(1)} %get-tuple-element.36), channel_id=1, source_target_pairs={{0,4},{4,8},{8,12},{12,16},{16,20},{20,24},{24,28},{1,5},{5,9},{9,... | collective-permute-start | bytes 294920 | tf_op jit(solution)/shard_map/ppermute | solution.py:574
  84.7 31.1 %collective-permute-start.5 = (bf16[6,32,256]{2,1,0:T(8,128)(2,1)S(1)}, bf16[6,32,256]{2,1,0:T(8,128)(2,1)}, u32[]{:S(2)}, u32[]{:S(2)}) collective-permute-start(bf16[6,32,256]{2,1,0:T(8,128)(2,1)S(1)} %get-tuple-element.37), channel_id=1, source_target_pairs={{4,0},{8,4},{12,8},{16,12},{20,16},{24,20},{28,24},{5,1},{9,5},{13... | collective-permute-start | bytes 294920 | tf_op jit(solution)/shard_map/ppermute | solution.py:574
  86.0 29.8 %collective-permute-start.6 = (bf16[6,32,256]{2,1,0:T(8,128)(2,1)S(1)}, bf16[6,32,256]{2,1,0:T(8,128)(2,1)}, u32[]{:S(2)}, u32[]{:S(2)}) collective-permute-start(bf16[6,32,256]{2,1,0:T(8,128)(2,1)S(1)} %get-tuple-element.38), channel_id=1, source_target_pairs={{0,1},{1,2},{2,3},{4,5},{5,6},{6,7},{8,9},{9,10},{10,11},{12,13},{... | collective-permute-start | bytes 294920 | tf_op jit(solution)/shard_map/ppermute | solution.py:574
  87.9 27.9 %collective-permute-start.7 = (bf16[6,32,256]{2,1,0:T(8,128)(2,1)S(1)}, bf16[6,32,256]{2,1,0:T(8,128)(2,1)}, u32[]{:S(2)}, u32[]{:S(2)}) collective-permute-start(bf16[6,32,256]{2,1,0:T(8,128)(2,1)S(1)} %get-tuple-element.39), channel_id=1, source_target_pairs={{1,0},{2,1},{3,2},{5,4},{6,5},{7,6},{9,8},{10,9},{11,10},{13,12},{... | collective-permute-start | bytes 294920 | tf_op jit(solution)/shard_map/ppermute | solution.py:574
  112.0 28.8 %all-to-all-start.3 = ((bf16[8,512,128]{2,1,0:T(8,128)(2,1)}), bf16[8,512,128]{2,1,0:T(8,128)(2,1)S(1)}, u32[]{:S(2)}, u32[]{:S(2)}) async-start(bf16[8,512,128]{2,1,0:T(8,128)(2,1)} %get-tuple-element.40.sent), calls=%async_computation.3 | async-start | bytes 2097152 | tf_op jit(solution)/shard_map/all_to_all | solution.py:579
  115.8 1.0 copy-start.8
  116.9 1.2 copy-start.11
where the time goes:
time: 147 us; the launch traced here: 146 us
  waiting for transfers between devices  68.9 us (47%)
  Pallas kernels  36 us (24%)
  starting transfers between devices  34.6 us (24%)
  local copies, waits for them, and re-layouts  5.17 us (4%)
    all_to_all x4, waiting for transfers between devices, swap_slots(): return lax.all_to_all(send, 'gx', split_axis=0, concat_axis=0, tiled=True)  68.9 us
    pallas_call x10, Pallas kernels, apply(): made(*[pinned(value, spec) for value, spec in zip(values, in_specs, stric...  36 us
    all_to_all x4, starting transfers between devices, swap_slots(): return lax.all_to_all(send, 'gx', split_axis=0, concat_axis=0, tiled=True)  18.4 us
    ppermute x8, starting transfers between devices, neighbours(): moved += [lax.ppermute(high, axis, up), lax.ppermute(low, axis, down)]  16.1 us
    unnamed x24, local copies, waits for them, and re-layouts  5.17 us
  transfers between devices with their start and end apart: 12, of which 4 were waited for; matrix products, arithmetic and copies ran while one was open for 0% of the time, Pallas kernels for 16%

commit v1 on v0

--- a/solution.py
+++ b/solution.py
@@ -152,34 +152,79 @@
     return copy
 
 
-def send_quarter(g, bricks, send, slots, sems):
-    copies = []
-    for b, (place, rank) in enumerate(slots):
-        rows = pl.ds(pl.multiple_of(rank * 256 + g * 64, 64), 64)
-        copies.append(fetch(bricks.at[b, g * 64 : g * 64 + 64, :], send.at[place, rows, :], sems.at[g, b]))
-    return copies
-
-
-def first_kernel(*refs):
-    picks_in, route_in, landing_in, operators, field, send, tables = refs[:7]
-    picks, route, landing, table_mem, field_mem, start, folded, turned, out, meta, meta_half, tables_mem, sems, slot_sems = refs[7:]
-    told = [fetch(a, b, sems.at[11 + i]) for i, (a, b) in enumerate(((picks_in, picks), (route_in, route), (landing_in, landing)))]
-    loads = [fetch(operators, table_mem, sems.at[8]), fetch(field, field_mem, sems.at[9])]
+def put_pieces(stage, g, value, rows):
+    parts = 32 // rows
+    for half in range(2):
+        tile = value[:, half * 128 : half * 128 + 128]
+        for part in range(parts):
+            share = (2 * g + half) * parts + part
+            if parts == 1:
+                stage[share] = tile
+            else:
+                for b in range(8):
+                    at = b * 32 + part * rows
+                    stage[share, b * rows : b * rows + rows, :] = tile[at : at + rows]
+
+
+def pieces_pair(pieces, kind, g, rows):
+    parts = 32 // rows
+    base = kind * 8 * rows
+    tiles = []
+    for tile in (2 * g, 2 * g + 1):
+        if parts == 1:
+            tiles.append(pieces[tile, base : base + 256, :])
+        else:
+            tiles.append(
+                jnp.concatenate(
+                    [
+                        pieces[tile * parts + part, base + b * rows : base + b * rows + rows, :]
+                        for b in range(8)
+                        for part in range(parts)
+                    ],
+                    axis=0,
+                )
+            )
+    return jnp.concatenate(tiles, axis=1)
+
+
+def target_kernel(picks_in, route_in, brick_in, target, send, *refs):
+    picks, route, landing, field, stage, meta, meta_half, sems = refs
+    told = [
+        fetch(source, place, sems.at[index])
+        for index, (source, place) in enumerate(((picks_in, picks), (route_in, route), (brick_in, landing)))
+    ]
+    load = fetch(target, field, sems.at[3])
     for copy in told:
         copy.wait()
+    lane = iota((1, 128), 1)
     meta[...] = jnp.zeros(meta.shape, F32)
-    for step in range(STEPS):
-        for b, (place, rank) in enumerate(slot_numbers(route, step)):
-            value = jnp.full((1, 128), landing[step, 0, 0, b] + 1, jnp.int32).astype(F32)
-            meta[place, pl.ds(step * CAP + rank, 1), :] = value
-    meta_half[...] = meta[...].astype(BF16)
-    told = fetch(meta_half, send.at[:, 512:528, :], sems.at[10])
+    for b in range(8):
+        codes = [route[step, 0, 0, b] * 8 + landing[step, 0, 0, b] for step in range(STEPS)]
+        value = jnp.zeros((1, 128), jnp.int32)
+        for index, number in enumerate(codes + [picks[1, 0, 0, b]]):
+            value = jnp.where(lane == index, number, value)
+        meta[b : b + 1, :] = value.astype(F32)
+    meta_half[...] = jnp.broadcast_to(meta[...].astype(BF16)[None], meta_half.shape)
+    shared = stage.shape[1]
+    sent = [fetch(meta_half, send.at[:, shared : shared + 16, :], sems.at[4])]
+    load.wait()
+    for g in range(4):
+        block = jnp.concatenate(
+            [field[qh * 8 + qs] for qs in (2 * g, 2 * g + 1) for qh in range(4)], axis=0
+        )
+        put_pieces(stage, g, mm(identity(), block, NT).astype(BF16), shared // 8)
+    for copy in sent + [fetch(stage, send.at[:, 0:shared, :], sems.at[5])]:
+        copy.wait()
+
+
+def first_kernel(picks, operators, field, sent, moved_out, tables, table_mem, field_mem, start, folded, turned, out, tables_mem, sems):
+    loads = [fetch(operators, table_mem, sems.at[0]), fetch(field, field_mem, sems.at[1])]
     chosen = [picks[0, 0, 0, b] for b in range(8)]
     loads[0].wait()
     found = [table_rows(table_mem, chosen, axis) for axis in range(3)]
     for axis in range(3):
         tables_mem[axis] = found[axis].astype(BF16)
-    kept = fetch(tables_mem, tables, sems.at[8])
+    kept = fetch(tables_mem, tables, sems.at[0])
     begin = diagonal(found[2])
     loads[1].wait()
     for g in range(4):
@@ -187,128 +232,110 @@
             [field_mem[qh * 8 + qs] for qs in (2 * g, 2 * g + 1) for qh in range(4)], axis=0
         )
         start[:, g * 256 : g * 256 + 256] = mm(begin, block, NT)
-    slots = slot_numbers(route, 0)
-    sent = []
     for g, moved in middle_and_last(start, spread(found[1]), diagonal(found[0]), folded, turned, False):
         put_pair(out, g, moved)
-        sent += send_quarter(g, out, send, slots, slot_sems)
-    for copy in sent + [told, kept]:
+    for copy in [kept, fetch(out, moved_out, sems.at[1])]:
         copy.wait()
 
 
-def second_kernel(route, tables_in, arrived, *refs):
-    send, state, landing_out, meta, tables, landing, state_mem, total, start, folded, turned, out, sems, slot_sems = refs[-14:]
-    meta[...] = arrived[:, 512:528, :].astype(F32).astype(jnp.int32)[:, 0:8, :]
-    told = [fetch(meta, landing, sems.at[9]), fetch(meta, landing_out, sems.at[10])]
-    listed = fetch(tables_in, tables, sems.at[11])
-    total[...] = jnp.zeros(total.shape, F32)
+def second_kernel(route, landing, operators, moved, arrived, *refs):
+    send, tables, codes_out, table_mem, moved_mem, meta_half, meta, codes, start, folded, turned, stage, tables_mem, sems, slot_sems = refs
+    shared = stage.shape[1]
+    heard = fetch(arrived.at[:, shared : shared + 16, :], meta_half, sems.at[0])
+    loads = [fetch(operators, table_mem, sems.at[1]), fetch(moved, moved_mem, sems.at[2])]
+    heard.wait()
+    meta[...] = meta_half[...].astype(F32).astype(jnp.int32)[:, 0:8, :]
+    told = [fetch(meta, codes, sems.at[3]), fetch(meta, codes_out, sems.at[4])]
+    loads[1].wait()
+    sent = []
+    for b, (place, rank) in enumerate(slot_numbers(route, 0)):
+        rows = pl.ds(pl.multiple_of(rank * 256, 256), 256)
+        sent.append(fetch(moved_mem.at[b], send.at[place, rows, :], slot_sems.at[b]))
     told[0].wait()
-    gather_sum(0, landing, arrived, total)
-    for b in range(8):
-        state_mem[b] = total[b].astype(BF16)
-    kept = fetch(state_mem, state, sems.at[9])
-    listed.wait()
-    begin = diagonal(tables[0].astype(F32))
-    mid = spread(tables[1].astype(F32))
-    end = diagonal(tables[2].astype(F32))
-    for g in range(4):
-        start[:, g * 256 : g * 256 + 256] = mm(begin, lane_pair(state_mem, g))
-    slots = slot_numbers(route, 1)
-    sent = []
-    for g, moved in middle_and_last(start, mid, end, folded, turned, False):
-        put_pair(out, g, moved)
-        sent += send_quarter(g, out, send, slots, slot_sems)
+    chosen = [codes[route[0, 0, 0, b], landing[0, 0, 0, b], 2] for b in range(8)]
+    loads[0].wait()
+    found = [table_rows(table_mem, chosen, axis) for axis in range(3)]
+    for axis in range(3):
+        tables_mem[axis] = found[axis].astype(BF16)
+    kept = fetch(tables_mem, tables, sems.at[5])
+    begin = diagonal(found[0])
+    for g in range(4):
+        start[:, g * 256 : g * 256 + 256] = mm(begin, lane_pair(moved_mem, g))
+    for g, value in middle_and_last(start, spread(found[1]), diagonal(found[2]), folded, turned, False):
+        put_pieces(stage, g, value, shared // 8)
+    sent.append(fetch(stage, send.at[:, 512 : 512 + shared, :], sems.at[6]))
     for copy in sent + [kept, told[1]]:
         copy.wait()
 
 
-def gather_sum(step, landing, arrived, total):
+def share_kernel(codes_in, arrived, targets, send, codes, moved, aims, total, stage, sems):
+    peers, shared = moved.shape[0], moved.shape[1]
+    rows = shared // 8
+    loads = [
+        fetch(codes_in, codes, sems.at[0]),
+        fetch(arrived.at[:, 512 : 512 + shared, :], moved, sems.at[1]),
+        fetch(targets.at[:, 0:shared, :], aims, sems.at[2]),
+    ]
+    total[...] = jnp.zeros(total.shape, F32)
+    for load in loads:
+        load.wait()
+
     def add(source, carry):
-        for rank in range(CAP):
-            brick = landing[source, step * CAP + rank, 0]
-
-            @pl.when(brick > 0)
-            def _():
-                total[brick - 1] += arrived[source, rank * 256 : rank * 256 + 256, :].astype(F32)
-
+        for b in range(8):
+            first = codes[source, b, 0]
+            final = codes[first >> 3, first & 7, 1]
+            place = pl.ds(pl.multiple_of((final & 7) * rows, rows), rows)
+            total[final >> 3, place, :] += moved[source, b * rows : b * rows + rows, :].astype(F32)
         return carry
 
-    lax.fori_loop(0, arrived.shape[0], add, 0)
-
-
-def hand_out(step, landing, field, send, sems):
-    copies = []
-    for source in range(send.shape[0]):
-        for rank in range(CAP):
-            brick = jnp.maximum(landing[source, step * CAP + rank, 0] - 1, 0)
-            target = send.at[source, rank * 256 : rank * 256 + 256, :]
-            copies.append(fetch(field.at[brick], target, sems.at[source * CAP + rank]))
-    return copies
-
-
-def third_kernel(landing_in, arrived, target, *refs):
-    send, adjoint, arrived_mem, landing, total, adjoint_mem, target_mem, sems, slot_sems = refs[-9:]
-    told = fetch(landing_in, landing, sems.at[0])
-    load = fetch(arrived, arrived_mem, sems.at[1])
-    aim = fetch(target, target_mem, sems.at[2])
-    total[...] = jnp.zeros(total.shape, F32)
-    told.wait()
-    load.wait()
-    gather_sum(1, landing, arrived_mem, total)
-    aim.wait()
-    for b in range(8):
-        final = total[b].astype(BF16).astype(F32)
-        adjoint_mem[b] = (final - target_mem[b].astype(F32)).astype(BF16)
-    sent = hand_out(1, landing, adjoint_mem, send, slot_sems)
-    for copy in sent + [fetch(adjoint_mem, adjoint, sems.at[0])]:
-        copy.wait()
-
-
-def pulled_pair(arrived, slots, g):
-    tiles = []
-    for qs in (2 * g, 2 * g + 1):
-        rows = [
-            arrived[place, pl.ds(pl.multiple_of(rank * 256 + qs * 32, 32), 32), :] for place, rank in slots
-        ]
-        tiles.append(jnp.concatenate(rows, axis=0))
-    return jnp.concatenate(tiles, axis=1)
-
-
-def fourth_kernel(route, tables_in, landing_in, arrived, *refs):
-    send, adjoint, tables, landing, start, folded, turned, out, sems, slot_sems = refs[-10:]
-    listed = fetch(tables_in, tables, sems.at[1])
-    told = fetch(landing_in, landing, sems.at[2])
-    slots = slot_numbers(route, 1)
-    listed.wait()
-    begin = flipped_diagonal(tables[2].astype(F32))
-    mid = spread(tables[1].astype(F32))
-    end = flipped_diagonal(tables[0].astype(F32))
-    for g in range(4):
-        start[:, g * 256 : g * 256 + 256] = mm(begin, pulled_pair(arrived, slots, g))
+    lax.fori_loop(0, peers, add, 0)
+    for source in range(peers):
+        final = total[source].astype(BF16).astype(F32)
+        stage[source, 0:shared, :] = (final - aims[source].astype(F32)).astype(BF16)
+
+    def give(source, carry):
+        for b in range(8):
+            first = codes[source, b, 0]
+            for kind, code in ((1, codes[source, b, 1]), (2, codes[first >> 3, first & 7, 1])):
+                place = pl.ds(pl.multiple_of((code & 7) * rows, rows), rows)
+                stage[source, kind * shared + b * rows : kind * shared + b * rows + rows, :] = stage[code >> 3, place, :]
+        return carry
+
+    lax.fori_loop(0, peers, give, 0)
+    fetch(stage, send, sems.at[0]).wait()
+
+
+def final_kernel(tables_one_in, tables_far_in, tables_zero_in, arrived, *refs):
+    adjoint_one, adjoint, tables, start, folded, turned, out, later, field, sems, quarter_sems = refs
+    loads = [
+        fetch(source, tables.at[index], sems.at[index])
+        for index, source in enumerate((tables_one_in, tables_far_in, tables_zero_in))
+    ]
+    rows = arrived.shape[1] // 24
+    for load in loads:
+        load.wait()
+    kept = None
+    for index in range(2):
+        begin = flipped_diagonal(tables[index, 2].astype(F32))
+        mid = spread(tables[index, 1].astype(F32))
+        end = flipped_diagonal(tables[index, 0].astype(F32))
+        for g in range(4):
+            start[:, g * 256 : g * 256 + 256] = mm(begin, pieces_pair(arrived, index + 1, g, rows))
+        for g, moved in middle_and_last(start, mid, end, folded, turned, True):
+            put_pair((out, later)[index], g, moved)
+        if index == 0:
+            kept = fetch(out, adjoint_one, sems.at[0])
+    begin = flipped_diagonal(tables[2, 0].astype(F32))
+    mid = spread(tables[2, 1].astype(F32))
+    end = flipped_diagonal(tables[2, 2].astype(F32))
+    for g in range(4):
+        start[:, g * 256 : g * 256 + 256] = mm(begin, lane_pair(later, g))
+    stored = [kept]
     for g, moved in middle_and_last(start, mid, end, folded, turned, True):
-        put_pair(out, g, moved)
-    told.wait()
-    sent = hand_out(0, landing, out, send, slot_sems)
-    for copy in sent + [fetch(out, adjoint, sems.at[0])]:
-        copy.wait()
-
-
-def fifth_kernel(route, tables_in, arrived, *refs):
-    adjoint, tables, start, folded, turned, out, sems = refs[-7:]
-    load = fetch(tables_in, tables, sems.at[0, 7])
-    slots = slot_numbers(route, 0)
-    load.wait()
-    begin = flipped_diagonal(tables[0].astype(F32))
-    mid = spread(tables[1].astype(F32))
-    end = flipped_diagonal(tables[2].astype(F32))
-    for g in range(4):
-        start[:, g * 256 : g * 256 + 256] = mm(begin, pulled_pair(arrived, slots, g))
-    stored = []
-    for g, moved in middle_and_last(start, mid, end, folded, turned, True):
-        to_native(moved, g, out)
+        to_native(moved, g, field)
         for qh in range(4):
-            rows = slice(qh * 8 + 2 * g, qh * 8 + 2 * g + 2)
-            stored.append(fetch(out.at[rows], adjoint.at[rows], sems.at[g, qh]))
+            at = slice(qh * 8 + 2 * g, qh * 8 + 2 * g + 2)
+            stored.append(fetch(field.at[at], adjoint.at[at], quarter_sems.at[g, qh]))
     for copy in stored:
         copy.wait()
 
@@ -422,15 +449,10 @@
     put_rims([mid_v[8 * g : 8 * g + 8].astype(BF16).reshape(256, 256) for g in range(4)], RIM, low_y, high_y)
 
 
-def prepare_kernel(picks, operators, target, edge, target_z, tables):
+def prepare_kernel(picks, operators, edge, tables):
     chosen = [picks[1, 0, 0, b] for b in range(8)]
     for axis in range(3):
         tables[axis] = table_rows(operators, chosen, axis).astype(BF16)
-    for g in range(4):
-        block = jnp.concatenate(
-            [target[qh * 8 + qs] for qs in (2 * g, 2 * g + 1) for qh in range(4)], axis=0
-        )
-        put_pair(target_z, g, mm(identity(), block, NT).astype(BF16))
 
 
 def divergence_kernel(velocity, before_x, after_x, before_y, after_y, sent, divergence, padded):
@@ -449,7 +471,30 @@
         divergence[8 * g : 8 * g + 8] = total.reshape(8, 32, 256)
 
 
-def rims_kernel(state, divergence, sent, native, low_x, high_x, low_y, high_y, folded, turned):
+def rims_kernel(codes_in, arrived, divergence, sent, native, low_x, high_x, low_y, high_y, codes, slots, total, state, folded, turned, sems):
+    loads = [fetch(codes_in, codes, sems.at[0]), fetch(arrived.at[:, 0:512, :], slots, sems.at[1])]
+    total[...] = jnp.zeros(total.shape, F32)
+    for load in loads:
+        load.wait()
+    me = lax.axis_index("gx")
+
+    def add(source, carry):
+        rank = jnp.int32(0)
+        for b in range(8):
+            code = codes[source, b, 0]
+            hit = (code >> 3) == me
+
+            @pl.when(hit)
+            def _():
+                place = pl.ds(pl.multiple_of(rank * 256, 256), 256)
+                total[code & 7] += slots[source, place, :].astype(F32)
+
+            rank = rank + hit.astype(jnp.int32)
+        return carry
+
+    lax.fori_loop(0, slots.shape[0], add, 0)
+    for b in range(8):
+        state[b] = total[b].astype(BF16)
     x_form_to_native(state, folded, turned, native)
     low_x[0:RIM] = native[0:RIM]
     high_x[0:RIM] = native[29:32]
@@ -475,7 +520,6 @@
     a1x,
     b1y,
     a1y,
-    sent,
     gradient,
     folded,
     turned,
@@ -487,7 +531,7 @@
 ):
     x_form_to_native(adjoint_one, folded, turned, weight_one)
     for g in range(4):
-        to_native(lane_pair(adjoint_two, g), g, weight_two)
+        to_native(pieces_pair(adjoint_two, 0, g, adjoint_two.shape[1] // 24), g, weight_two)
     along_y, rim_y, along_z = stencils()
     for padded, before, middle, after, base in (
         (pad_zero, b0x, template, a0x, 0),
@@ -521,6 +565,7 @@
 SCALAR = pl.BlockSpec(memory_space=pltpu.SMEM)
 WHOLE = pl.BlockSpec(memory_space=pltpu.VMEM)
 NEAR = pl.BlockSpec(memory_space=pltpu.VMEM)
+ANYWHERE = pl.BlockSpec(memory_space=pl.ANY)
 FAR = pl.BlockSpec(memory_space=pltpu.HBM)
 FOLDED = (32, 64, 128)
 FLAT = (256, 1024)
@@ -581,36 +626,49 @@
 
 def shards(template, target_image, velocity, operators, route, target_brick, operator_index):
     peers = lax.axis_size("gx")
+    shared = 8 * (256 // peers)
     sems = pltpu.SemaphoreType.DMA((16,))
-    slot_sems = pltpu.SemaphoreType.DMA((peers * CAP,))
-    quarter_sems = pltpu.SemaphoreType.DMA((4, 8))
+    quarter_sems = pltpu.SemaphoreType.DMA((4, 4))
     turning = [pltpu.VMEM(FLAT, F32), pltpu.VMEM(FOLDED, F32), pltpu.VMEM((512, 1024), BF16)]
     form = pltpu.VMEM(FORM, BF16)
-    total = pltpu.VMEM(FORM, F32)
-    landed = pltpu.SMEM((peers, 8, 128), jnp.int32)
-    slots = far((peers, 512, 128), BF16)
+    tables = pltpu.VMEM(TABLES, BF16)
+    codes_mem = pltpu.SMEM((peers, 8, 128), jnp.int32)
+    stage = pltpu.VMEM((peers, shared, 128), BF16)
+    meta_half = pltpu.VMEM((peers, 16, 128), BF16)
     table_rows_count = operators.shape[1] * operators.shape[2] * operators.shape[3]
     listed = operators.transpose(1, 2, 3, 0).reshape(table_rows_count, operators.shape[0])
+    listed_mem = pltpu.VMEM(listed.shape, BF16)
     route = route.reshape(route.shape[:4])
 
-    send, tables_zero = call(
+    send = call(
+        target_kernel,
+        far((peers, shared + 16, 128), BF16),
+        [FAR] * 4,
+        FAR,
+        [pltpu.SMEM(route.shape, jnp.int32)] * 3
+        + [pltpu.VMEM(NATIVE, BF16), stage, pltpu.VMEM((16, 128), F32), meta_half, sems],
+        SHORT,
+    )(operator_index, route, target_brick, target_image)
+    targets = swap_slots(send)
+
+    moved, tables_zero = call(
         first_kernel,
-        [far((peers, 528, 128), BF16), far(TABLES, BF16)],
-        [FAR] * 5,
-        [FAR, FAR],
-        [pltpu.SMEM(route.shape, jnp.int32)] * 3
-        + [pltpu.VMEM(listed.shape, BF16), pltpu.VMEM(NATIVE, BF16)]
+        [far(FORM, BF16), far(TABLES, BF16)],
+        [SCALAR, FAR, FAR, FAR],
+        [FAR] * 2,
+        [listed_mem, pltpu.VMEM(NATIVE, BF16)] + turning + [form, tables, sems],
+    )(operator_index, listed, template, send)
+
+    send, tables_far, codes = call(
+        second_kernel,
+        [far((peers, 512 + shared, 128), BF16), far(TABLES, BF16), far((peers, 8, 128), jnp.int32)],
+        [SCALAR, SCALAR, FAR, FAR, ANYWHERE],
+        [FAR] * 3,
+        [listed_mem, form, meta_half, pltpu.VMEM((peers, 8, 128), jnp.int32), codes_mem]
         + turning
-        + [
-            form,
-            pltpu.VMEM((peers, 16, 128), F32),
-            pltpu.VMEM((peers, 16, 128), BF16),
-            pltpu.VMEM(TABLES, BF16),
-            sems,
-            quarter_sems,
-        ],
+        + [stage, tables, sems, pltpu.SemaphoreType.DMA((8,))],
         SHORT,
-    )(operator_index, route, target_brick, listed, template)
+    )(route, target_brick, listed, moved, targets)
     arrived = swap_slots(send)
 
     rim = like((2 * RIM, 32, 256), BF16)
@@ -621,72 +679,49 @@
         [WHOLE] * 4,
         [pltpu.VMEM(NATIVE, BF16)] + [pltpu.VMEM((RIM, 32, 256), F32)] * 2 + [pltpu.VMEM(NATIVE, F32), sems],
     )(template, velocity, send)
-    target_z, tables_one = call(
-        prepare_kernel, [far(FORM, BF16), far(TABLES, BF16)], [SCALAR] + [WHOLE] * 3, [WHOLE] * 2, []
-    )(operator_index, listed, target_image, low_x)
+    tables_one = call(prepare_kernel, far(TABLES, BF16), [SCALAR] + [WHOLE] * 2, WHOLE, [])(
+        operator_index, listed, low_x
+    )
     b0x, a0x, b0y, a0y = neighbours(low_x, high_x, low_y, high_y)
-    send, state_x, landing = call(
-        second_kernel,
-        [slots, far(FORM, BF16), far((peers, 8, 128), jnp.int32)],
-        [SCALAR, FAR, NEAR],
-        [FAR] * 3,
-        [
-            pltpu.VMEM((peers, 8, 128), jnp.int32),
-            pltpu.VMEM(TABLES, BF16),
-            landed,
-            form,
-            total,
-        ]
-        + turning
-        + [form, sems, quarter_sems],
+
+    send = call(
+        share_kernel,
+        far((peers, 3 * shared, 128), BF16),
+        [FAR, ANYWHERE, ANYWHERE],
+        FAR,
+        [codes_mem, stage, stage, pltpu.VMEM((peers, shared, 128), F32), pltpu.VMEM((peers, 3 * shared, 128), BF16), sems],
         SHORT,
-    )(route, tables_one, arrived)
-    arrived = swap_slots(send)
+    )(codes, arrived, targets)
+    pulled = swap_slots(send)
 
     divergence = call(
         divergence_kernel, like(NATIVE, F32), [WHOLE] * 5 + [FAR], WHOLE, [pltpu.VMEM((38, 32, 256), F32)]
     )(velocity, b0x, a0x, b0y, a0y, send)
-
     state, low_x, high_x, low_y, high_y = call(
-        rims_kernel, [far(NATIVE, BF16)] + [rim] * 4, [WHOLE] * 2 + [FAR], [WHOLE] * 5, turning[1:]
-    )(state_x, divergence, send)
-    send, adjoint_two = call(
-        third_kernel,
-        [slots, far(FORM, BF16)],
-        [FAR, pl.BlockSpec(memory_space=pl.ANY), FAR, FAR],
+        rims_kernel,
+        [like(NATIVE, BF16)] + [rim] * 4,
+        [FAR, ANYWHERE, WHOLE, FAR],
+        [WHOLE] * 5,
+        [codes_mem, pltpu.VMEM((peers, 512, 128), BF16), pltpu.VMEM(FORM, F32), form] + turning[1:] + [sems],
+    )(codes, arrived, divergence, send)
+    b1x, a1x, b1y, a1y = neighbours(low_x, high_x, low_y, high_y)
+
+    adjoint_one, adjoint = call(
+        final_kernel,
+        [far(FORM, BF16), far(NATIVE, BF16)],
+        [FAR, FAR, FAR, NEAR],
         [FAR] * 2,
-        [pltpu.VMEM((peers, 512, 128), BF16), landed, total, form, form, sems, slot_sems],
+        [pltpu.VMEM((3,) + TABLES, BF16)] + turning + [form, form, pltpu.VMEM(NATIVE, BF16), sems, quarter_sems],
         SHORT,
-    )(landing, arrived, target_z, state)
-    arrived = swap_slots(send)
-    b1x, a1x, b1y, a1y = neighbours(low_x, high_x, low_y, high_y)
-
-    send, adjoint_one = call(
-        fourth_kernel,
-        [slots, far(FORM, BF16)],
-        [SCALAR, FAR, FAR, NEAR],
-        [FAR] * 2,
-        [pltpu.VMEM(TABLES, BF16), landed] + turning + [form, sems, slot_sems],
-        SHORT,
-    )(route, tables_one, landing, arrived)
-    arrived = swap_slots(send)
+    )(tables_one, tables_far, tables_zero, pulled)
 
     gradient = call(
         gradient_kernel,
         far((3,) + NATIVE, F32),
-        [WHOLE] * 13 + [FAR],
+        [WHOLE] * 13,
         WHOLE,
         turning[1:] + [pltpu.VMEM(NATIVE, F32)] * 2 + [pltpu.VMEM((38, 32, 256), F32)] * 3,
-    )(template, state, divergence, adjoint_two, adjoint_one, b0x, a0x, b0y, a0y, b1x, a1x, b1y, a1y, send)
-
-    adjoint = call(
-        fifth_kernel,
-        far(NATIVE, BF16),
-        [SCALAR, FAR, NEAR, FAR],
-        FAR,
-        [pltpu.VMEM(TABLES, BF16)] + turning + [pltpu.VMEM(NATIVE, BF16), quarter_sems],
-        SHORT,
-    )(route, tables_zero, arrived, gradient)
+    )(template, state, divergence, pulled, adjoint_one, b0x, a0x, b0y, a0y, b1x, a1x, b1y, a1y)
     return gradient, adjoint
 
 

time: 147 us -> 135 us (0.918)
  waiting for transfers between devices: 68.9 us -> 58.8 us
  Pallas kernels: 36 us -> 40.9 us
  starting transfers between devices: 34.6 us -> 30.8 us
  local copies, waits for them, and re-layouts: 5.17 us -> 2.97 us
    all_to_all x4 -> x3, waiting for transfers between devices: 68.9 us -> 58.8 us  [swap_slots(): return lax.all_to_all(send, 'gx', split_axis=0, concat_axis=0, tiled=True)]
    pallas_call x10, Pallas kernels: 36 us -> 40.9 us  [apply(): made(*[pinned(value, spec) for value, spec in zip(values, in_specs, stric...]
    all_to_all x4 -> x3, starting transfers between devices: 18.4 us -> 15.3 us  [swap_slots(): return lax.all_to_all(send, 'gx', split_axis=0, concat_axis=0, tiled=True)]
    unnamed x24 -> x20, local copies, waits for them, and re-layouts: 5.17 us -> 2.97 us
  transfers between devices with their start and end apart: 12 -> 11, of which waited for: 4 -> 3; matrix products, arithmetic and copies ran while one was open for 0% -> 0% of each run, Pallas kernels for 16% -> 19%
where the time goes in v1:
time: 135 us; the launch traced here: 134 us
  waiting for transfers between devices  58.8 us (44%)
  Pallas kernels  40.9 us (30%)
  starting transfers between devices  30.8 us (23%)
  local copies, waits for them, and re-layouts  2.97 us (2%)
    all_to_all x3, waiting for transfers between devices, swap_slots(): return lax.all_to_all(send, 'gx', split_axis=0, concat_axis=0, tiled=True)  58.8 us
    pallas_call x10, Pallas kernels, apply(): made(*[pinned(value, spec) for value, spec in zip(values, in_specs, stric...  40.9 us
    ppermute x8, starting transfers between devices, neighbours(): moved += [lax.ppermute(high, axis, up), lax.ppermute(low, axis, down)]  15.6 us
    all_to_all x3, starting transfers between devices, swap_slots(): return lax.all_to_all(send, 'gx', split_axis=0, concat_axis=0, tiled=True)  15.3 us
    unnamed x20, local copies, waits for them, and re-layouts  2.97 us
  transfers between devices with their start and end apart: 11, of which 3 were waited for; matrix products, arithmetic and copies ran while one was open for 0% of the time, Pallas kernels for 19%

profile of v1, /device:TPU:0, one launch (start us, length us, event | category | flops | bytes accessed | tf_op | source)
XLA Modules:
  0.0 134.5 jit_solution(3385965902378282714)
XLA Ops:
  0.6 2.3 %shard_map.86.sent = bf16[8,272,128]{2,1,0:T(8,128)(2,1)} custom-call(s32[2,1,1,8]{3,2,1,0:T(1,128)} %picks.3, s32[2,1,1,8]{3,2,1,0:T(1,128)} %bitcast.9, s32[2,1,1,8]{3,2,1,0:T(1,128)} %landing.1, bf16[32,32,256]{2,1,0:T(8,128)(2,1)} %target.1), custom_call_target="tpu_custom_call" | custom-call | flops 1048576 | bytes 1048576 | tf_op jit(solution)/shard_map/pallas_call | solution.py:600
  3.0 7.3 %all-to-all-start = ((bf16[8,272,128]{2,1,0:T(8,128)(2,1)}), bf16[8,272,128]{2,1,0:T(8,128)(2,1)S(1)}, u32[]{:S(2)}, u32[]{:S(2)}) async-start(bf16[8,272,128]{2,1,0:T(8,128)(2,1)} %shard_map.86.sent), calls=%async_computation | async-start | bytes 1114112 | tf_op jit(solution)/shard_map/all_to_all | solution.py:624
  10.3 5.3 %shard_map.87 = (bf16[8,256,128]{2,1,0:T(8,128)(2,1)}, bf16[3,32,256]{2,1,0:T(8,128)(2,1)}) custom-call(s32[2,1,1,8]{3,2,1,0:T(1,128)S(1)} %copy-done.3, bf16[3072,64]{1,0:T(8,128)(2,1)} %bitcast.6, bf16[32,32,256]{2,1,0:T(8,128)(2,1)} %template.3, bf16[8,272,128]{2,1,0:T(8,128)(2,1)} %shard_map.86.sent), custom_call_target="tpu_custom_call" | custom-call | flops 68719476736 | bytes 1048576 | tf_op jit(solution)/shard_map/pallas_call | solution.py:600
  15.6 9.8 %all-to-all-done.arrived.targets = bf16[8,272,128]{2,1,0:T(8,128)(2,1)S(1)} async-done(((bf16[8,272,128]{2,1,0:T(8,128)(2,1)}), bf16[8,272,128]{2,1,0:T(8,128)(2,1)S(1)}, u32[]{:S(2)}, u32[]{:S(2)}) %all-to-all-start) | async-done | bytes 557088 | tf_op jit(solution)/shard_map/all_to_all | solution.py:624
  25.5 5.2 %shard_map.88 = (bf16[8,768,128]{2,1,0:T(8,128)(2,1)}, bf16[3,32,256]{2,1,0:T(8,128)(2,1)}, s32[8,8,128]{2,1,0:T(8,128)}) custom-call(s32[2,1,1,8]{3,2,1,0:T(1,128)S(1)} %bitcast.10, s32[2,1,1,8]{3,2,1,0:T(1,128)S(1)} %copy-done.2, bf16[3072,64]{1,0:T(8,128)(2,1)} %bitcast.7, bf16[8,256,128]{2,1,0:T(8,128)(2,1)} %get-tuple-element.18.moved, ...), custom_call_target="tpu_custom_call" | custom-call | flops 1048576 | bytes 1048576 | tf_op jit(solution)/shard_map/pallas_call | solution.py:600
  30.6 3.6 %all-to-all-start.1 = ((bf16[8,768,128]{2,1,0:T(8,128)(2,1)}), bf16[8,768,128]{2,1,0:T(8,128)(2,1)S(1)}, u32[]{:S(2)}, u32[]{:S(2)}) async-start(bf16[8,768,128]{2,1,0:T(8,128)(2,1)} %get-tuple-element.20.sent), calls=%async_computation.1 | async-start | bytes 3145728 | tf_op jit(solution)/shard_map/all_to_all | solution.py:624
  34.3 1.9 %shard_map.89 = (bf16[6,32,256]{2,1,0:T(8,128)(2,1)S(1)}, bf16[6,32,256]{2,1,0:T(8,128)(2,1)S(1)}, bf16[6,32,256]{2,1,0:T(8,128)(2,1)S(1)}, bf16[6,32,256]{2,1,0:T(8,128)(2,1)S(1)}) custom-call(bf16[32,32,256]{2,1,0:T(8,128)(2,1)} %template.3, f32[3,32,32,256]{3,2,1,0:T(8,128)} %velocity.3, bf16[8,768,128]{2,1,0:T(8,128)(2,1)} %get-tuple-element.20.sent), custom_call_target="tpu_custom_call" | custom-call | flops 68719476736 | bytes 1048576 | tf_op jit(solution)/shard_map/pallas_call | solution.py:600
  36.2 3.9 %collective-permute-start = (bf16[6,32,256]{2,1,0:T(8,128)(2,1)S(1)}, bf16[6,32,256]{2,1,0:T(8,128)(2,1)S(1)}, u32[]{:S(2)}, u32[]{:S(2)}) collective-permute-start(bf16[6,32,256]{2,1,0:T(8,128)(2,1)S(1)} %get-tuple-element.21), channel_id=1, source_target_pairs={{0,4},{4,8},{8,12},{12,16},{16,20},{20,24},{24,28},{1,5},{5,9},{9,... | collective-permute-start | bytes 294920 | tf_op jit(solution)/shard_map/ppermute | solution.py:619
  40.1 1.3 collective-permute-start.1
  41.4 1.3 collective-permute-start.2
  42.7 1.3 collective-permute-start.3
  44.0 28.5 %all-to-all-done.1.arrived = bf16[8,768,128]{2,1,0:T(8,128)(2,1)S(1)} async-done(((bf16[8,768,128]{2,1,0:T(8,128)(2,1)}), bf16[8,768,128]{2,1,0:T(8,128)(2,1)S(1)}, u32[]{:S(2)}, u32[]{:S(2)}) %all-to-all-start.1) | async-done | bytes 1572896 | tf_op jit(solution)/shard_map/all_to_all | solution.py:624
  72.5 3.6 %shard_map.90.sent = bf16[8,768,128]{2,1,0:T(8,128)(2,1)} custom-call(s32[8,8,128]{2,1,0:T(8,128)} %get-tuple-element.19.codes_in, bf16[8,768,128]{2,1,0:T(8,128)(2,1)S(1)} %all-to-all-done.1.arrived, bf16[8,272,128]{2,1,0:T(8,128)(2,1)S(1)} %all-to-all-done.arrived.targets), custom_call_target="tpu_custom_call" | custom-call | flops 1048576 | bytes 1048576 | tf_op jit(solution)/shard_map/pallas_call | solution.py:600
  76.1 4.3 %all-to-all-start.2 = ((bf16[8,768,128]{2,1,0:T(8,128)(2,1)}), bf16[8,768,128]{2,1,0:T(8,128)(2,1)}, u32[]{:S(2)}, u32[]{:S(2)}) async-start(bf16[8,768,128]{2,1,0:T(8,128)(2,1)} %shard_map.90.sent), calls=%async_computation.2 | async-start | bytes 3145728 | tf_op jit(solution)/shard_map/all_to_all | solution.py:624
  80.5 1.9 %copy-done.5 = f32[3,32,32,256]{3,2,1,0:T(8,128)S(1)} copy-done((f32[3,32,32,256]{3,2,1,0:T(8,128)S(1)}, f32[3,32,32,256]{3,2,1,0:T(8,128)}, u32[]{:S(2)}) %copy-start.5) | copy-done | bytes 3145752
  82.4 1.6 %shard_map.91.divergence = f32[32,32,256]{2,1,0:T(8,128)S(1)} custom-call(f32[3,32,32,256]{3,2,1,0:T(8,128)S(1)} %copy-done.5, bf16[6,32,256]{2,1,0:T(8,128)(2,1)S(1)} %collective-permute-done.before_x.b0x, bf16[6,32,256]{2,1,0:T(8,128)(2,1)S(1)} %collective-permute-done.1.after_x.a0x, bf16[6,32,256]{2,1,0:T(8,128)(2,1)S(1)} %collective-permute-done.2.before_y.b0y, ...), custom_call_target="tpu_custom_call" | custom-call | flops 68719476736 | bytes 1048576 | tf_op jit(solution)/shard_map/pallas_call | solution.py:600
  84.0 3.3 %shard_map.92 = (bf16[32,32,256]{2,1,0:T(8,128)(2,1)S(1)}, bf16[6,32,256]{2,1,0:T(8,128)(2,1)S(1)}, bf16[6,32,256]{2,1,0:T(8,128)(2,1)S(1)}, bf16[6,32,256]{2,1,0:T(8,128)(2,1)S(1)}, bf16[6,32,256]{2,1,0:T(8,128)(2,1)S(1)}) custom-call(s32[8,8,128]{2,1,0:T(8,128)} %get-tuple-element.19.codes_in, bf16[8,768,128]{2,1,0:T(8,128)(2,1)S(1)} %all-to-all-done.1.arrived, ...), custom_call_target="tpu_custom_call" | custom-call | flops 68719476736 | bytes 1048576 | tf_op jit(solution)/shard_map/pallas_call | solution.py:600
  87.3 3.7 %collective-permute-start.4 = (bf16[6,32,256]{2,1,0:T(8,128)(2,1)S(1)}, bf16[6,32,256]{2,1,0:T(8,128)(2,1)S(1)}, u32[]{:S(2)}, u32[]{:S(2)}) collective-permute-start(bf16[6,32,256]{2,1,0:T(8,128)(2,1)S(1)} %get-tuple-element.29), channel_id=1, source_target_pairs={{0,4},{4,8},{8,12},{12,16},{16,20},{20,24},{24,28},{1,5},{5,9},{9,... | collective-permute-start | bytes 294920 | tf_op jit(solution)/shard_map/ppermute | solution.py:619
  92.4 1.3 collective-permute-start.6
  93.7 1.5 %collective-permute-start.7 = (bf16[6,32,256]{2,1,0:T(8,128)(2,1)S(1)}, bf16[6,32,256]{2,1,0:T(8,128)(2,1)S(1)}, u32[]{:S(2)}, u32[]{:S(2)}) collective-permute-start(bf16[6,32,256]{2,1,0:T(8,128)(2,1)S(1)} %get-tuple-element.32), channel_id=1, source_target_pairs={{1,0},{2,1},{3,2},{5,4},{6,5},{7,6},{9,8},{10,9},{11,10},{13,12},{... | collective-permute-start | bytes 294920 | tf_op jit(solution)/shard_map/ppermute | solution.py:619
  95.2 1.7 %shard_map.93.tables_one_in = bf16[3,32,256]{2,1,0:T(8,128)(2,1)} custom-call(s32[2,1,1,8]{3,2,1,0:T(1,128)S(1)} %copy-done.4, bf16[3072,64]{1,0:T(8,128)(2,1)S(1)} %bitcast.8, bf16[6,32,256]{2,1,0:T(8,128)(2,1)S(1)} %get-tuple-element.22.edge), custom_call_target="tpu_custom_call" | custom-call | flops 68719476736 | bytes 1048576 | tf_op jit(solution)/shard_map/pallas_call | solution.py:600
  96.9 20.4 %all-to-all-done.2.arrived.adjoint_two = bf16[8,768,128]{2,1,0:T(8,128)(2,1)} async-done(((bf16[8,768,128]{2,1,0:T(8,128)(2,1)}), bf16[8,768,128]{2,1,0:T(8,128)(2,1)}, u32[]{:S(2)}, u32[]{:S(2)}) %all-to-all-start.2) | async-done | bytes 1572896 | tf_op jit(solution)/shard_map/all_to_all | solution.py:624
  117.3 8.7 %shard_map.94 = (bf16[8,256,128]{2,1,0:T(8,128)(2,1)}, bf16[32,32,256]{2,1,0:T(8,128)(2,1)}) custom-call(bf16[3,32,256]{2,1,0:T(8,128)(2,1)} %shard_map.93.tables_one_in, bf16[3,32,256]{2,1,0:T(8,128)(2,1)} %get-tuple-element.26.tables_far_in, bf16[3,32,256]{2,1,0:T(8,128)(2,1)} %get-tuple-element.27.tables_zero_in, ...), custom_call_target="tpu_custom_call" | custom-call | flops 1048576 | bytes 1048576 | tf_op jit(solution)/shard_map/pallas_call | solution.py:600
  127.2 7.3 %shard_map.95 = f32[3,32,32,256]{3,2,1,0:T(8,128)} custom-call(bf16[32,32,256]{2,1,0:T(8,128)(2,1)S(1)} %copy-done.6, bf16[32,32,256]{2,1,0:T(8,128)(2,1)S(1)} %get-tuple-element.25.state, f32[32,32,256]{2,1,0:T(8,128)S(1)} %copy-done.9, bf16[8,768,128]{2,1,0:T(8,128)(2,1)} %all-to-all-done.2.arrived.adjoint_two, bf16[8,256,128]{2,1,0:T(8,128)(2,1)S(1)} %copy-done.7, ...), custom_call_target="tpu_custom_call" | custom-call | flops 68719476736 | bytes 1048576 | tf_op jit(solution)/shard_map/pallas_call | solution.py:600
  (28 shorter events, 2.4 us)
Async XLA Ops:
  0.6 9.6 %copy-start.3 = (s32[2,1,1,8]{3,2,1,0:T(1,128)S(1)}, s32[2,1,1,8]{3,2,1,0:T(1,128)}, u32[]{:S(2)}) copy-start(s32[2,1,1,8]{3,2,1,0:T(1,128)} %picks.3) | copy-start | bytes 196
  3.0 22.5 %all-to-all-start = ((bf16[8,272,128]{2,1,0:T(8,128)(2,1)}), bf16[8,272,128]{2,1,0:T(8,128)(2,1)S(1)}, u32[]{:S(2)}, u32[]{:S(2)}) async-start(bf16[8,272,128]{2,1,0:T(8,128)(2,1)} %shard_map.86.sent), calls=%async_computation | async-start | bytes 1114112 | tf_op jit(solution)/shard_map/all_to_all | solution.py:624
  10.3 15.2 %copy-start.1 = (s32[2,1,1,8,1]{3,4,2,1,0:T(1,128)S(1)}, s32[2,1,1,8,1]{3,4,2,1,0:T(1,128)}, u32[]{:S(2)}) copy-start(s32[2,1,1,8,1]{3,4,2,1,0:T(1,128)} %param.11) | copy-start | bytes 196
  10.3 15.2 %copy-start.2 = (s32[2,1,1,8]{3,2,1,0:T(1,128)S(1)}, s32[2,1,1,8]{3,2,1,0:T(1,128)}, u32[]{:S(2)}) copy-start(s32[2,1,1,8]{3,2,1,0:T(1,128)} %landing.1) | copy-start | bytes 196
  30.6 41.9 %all-to-all-start.1 = ((bf16[8,768,128]{2,1,0:T(8,128)(2,1)}), bf16[8,768,128]{2,1,0:T(8,128)(2,1)S(1)}, u32[]{:S(2)}, u32[]{:S(2)}) async-start(bf16[8,768,128]{2,1,0:T(8,128)(2,1)} %get-tuple-element.20.sent), calls=%async_computation.1 | async-start | bytes 3145728 | tf_op jit(solution)/shard_map/all_to_all | solution.py:624
  36.2 44.3 %collective-permute-start = (bf16[6,32,256]{2,1,0:T(8,128)(2,1)S(1)}, bf16[6,32,256]{2,1,0:T(8,128)(2,1)S(1)}, u32[]{:S(2)}, u32[]{:S(2)}) collective-permute-start(bf16[6,32,256]{2,1,0:T(8,128)(2,1)S(1)} %get-tuple-element.21), channel_id=1, source_target_pairs={{0,4},{4,8},{8,12},{12,16},{16,20},{20,24},{24,28},{1,5},{5,9},{9,... | collective-permute-start | bytes 294920 | tf_op jit(solution)/shard_map/ppermute | solution.py:619
  40.1 40.4 %collective-permute-start.1 = (bf16[6,32,256]{2,1,0:T(8,128)(2,1)S(1)}, bf16[6,32,256]{2,1,0:T(8,128)(2,1)S(1)}, u32[]{:S(2)}, u32[]{:S(2)}) collective-permute-start(bf16[6,32,256]{2,1,0:T(8,128)(2,1)S(1)} %get-tuple-element.22.edge), channel_id=1, source_target_pairs={{4,0},{8,4},{12,8},{16,12},{20,16},{24,20},{28,24},{5,1},{9,5},{13... | collective-permute-start | bytes 294920 | tf_op jit(solution)/shard_map/ppermute | solution.py:619
  41.4 39.1 %collective-permute-start.2 = (bf16[6,32,256]{2,1,0:T(8,128)(2,1)S(1)}, bf16[6,32,256]{2,1,0:T(8,128)(2,1)S(1)}, u32[]{:S(2)}, u32[]{:S(2)}) collective-permute-start(bf16[6,32,256]{2,1,0:T(8,128)(2,1)S(1)} %get-tuple-element.23), channel_id=1, source_target_pairs={{0,1},{1,2},{2,3},{4,5},{5,6},{6,7},{8,9},{9,10},{10,11},{12,13},{... | collective-permute-start | bytes 294920 | tf_op jit(solution)/shard_map/ppermute | solution.py:619
  42.7 37.8 %collective-permute-start.3 = (bf16[6,32,256]{2,1,0:T(8,128)(2,1)S(1)}, bf16[6,32,256]{2,1,0:T(8,128)(2,1)S(1)}, u32[]{:S(2)}, u32[]{:S(2)}) collective-permute-start(bf16[6,32,256]{2,1,0:T(8,128)(2,1)S(1)} %get-tuple-element.24), channel_id=1, source_target_pairs={{1,0},{2,1},{3,2},{5,4},{6,5},{7,6},{9,8},{10,9},{11,10},{13,12},{... | collective-permute-start | bytes 294920 | tf_op jit(solution)/shard_map/ppermute | solution.py:619
  76.1 41.2 %all-to-all-start.2 = ((bf16[8,768,128]{2,1,0:T(8,128)(2,1)}), bf16[8,768,128]{2,1,0:T(8,128)(2,1)}, u32[]{:S(2)}, u32[]{:S(2)}) async-start(bf16[8,768,128]{2,1,0:T(8,128)(2,1)} %shard_map.90.sent), calls=%async_computation.2 | async-start | bytes 3145728 | tf_op jit(solution)/shard_map/all_to_all | solution.py:624
  80.5 1.9 %copy-start.5 = (f32[3,32,32,256]{3,2,1,0:T(8,128)S(1)}, f32[3,32,32,256]{3,2,1,0:T(8,128)}, u32[]{:S(2)}) copy-start(f32[3,32,32,256]{3,2,1,0:T(8,128)} %velocity.3) | copy-start | bytes 9437188
  83.9 3.4 %copy-start.8 = (f32[32,32,256]{2,1,0:T(8,128)}, f32[32,32,256]{2,1,0:T(8,128)S(1)}, u32[]{:S(2)}) copy-start(f32[32,32,256]{2,1,0:T(8,128)S(1)} %shard_map.91.divergence) | copy-start | bytes 3145732
  84.0 11.2 %copy-start = (bf16[64,3,32,32]{0,3,2,1:T(8,128)(2,1)S(1)}, bf16[64,3,32,32]{0,3,2,1:T(8,128)(2,1)}, u32[]{:S(2)}) copy-start(bf16[64,3,32,32]{0,3,2,1:T(8,128)(2,1)} %param.10) | copy-start | bytes 1179652
  84.0 11.2 %copy-start.4 = (s32[2,1,1,8]{3,2,1,0:T(1,128)S(1)}, s32[2,1,1,8]{3,2,1,0:T(1,128)}, u32[]{:S(2)}) copy-start(s32[2,1,1,8]{3,2,1,0:T(1,128)} %picks.3) | copy-start | bytes 196
  87.3 38.7 %collective-permute-start.4 = (bf16[6,32,256]{2,1,0:T(8,128)(2,1)S(1)}, bf16[6,32,256]{2,1,0:T(8,128)(2,1)S(1)}, u32[]{:S(2)}, u32[]{:S(2)}) collective-permute-start(bf16[6,32,256]{2,1,0:T(8,128)(2,1)S(1)} %get-tuple-element.29), channel_id=1, source_target_pairs={{0,4},{4,8},{8,12},{12,16},{16,20},{20,24},{24,28},{1,5},{5,9},{9,... | collective-permute-start | bytes 294920 | tf_op jit(solution)/shard_map/ppermute | solution.py:619
  91.1 35.0 %collective-permute-start.5 = (bf16[6,32,256]{2,1,0:T(8,128)(2,1)S(1)}, bf16[6,32,256]{2,1,0:T(8,128)(2,1)S(1)}, u32[]{:S(2)}, u32[]{:S(2)}) collective-permute-start(bf16[6,32,256]{2,1,0:T(8,128)(2,1)S(1)} %get-tuple-element.30), channel_id=1, source_target_pairs={{4,0},{8,4},{12,8},{16,12},{20,16},{24,20},{28,24},{5,1},{9,5},{13... | collective-permute-start | bytes 294920 | tf_op jit(solution)/shard_map/ppermute | solution.py:619
  92.4 33.8 %collective-permute-start.6 = (bf16[6,32,256]{2,1,0:T(8,128)(2,1)S(1)}, bf16[6,32,256]{2,1,0:T(8,128)(2,1)S(1)}, u32[]{:S(2)}, u32[]{:S(2)}) collective-permute-start(bf16[6,32,256]{2,1,0:T(8,128)(2,1)S(1)} %get-tuple-element.31), channel_id=1, source_target_pairs={{0,1},{1,2},{2,3},{4,5},{5,6},{6,7},{8,9},{9,10},{10,11},{12,13},{... | collective-permute-start | bytes 294920 | tf_op jit(solution)/shard_map/ppermute | solution.py:619
  93.7 32.5 %collective-permute-start.7 = (bf16[6,32,256]{2,1,0:T(8,128)(2,1)S(1)}, bf16[6,32,256]{2,1,0:T(8,128)(2,1)S(1)}, u32[]{:S(2)}, u32[]{:S(2)}) collective-permute-start(bf16[6,32,256]{2,1,0:T(8,128)(2,1)S(1)} %get-tuple-element.32), channel_id=1, source_target_pairs={{1,0},{2,1},{3,2},{5,4},{6,5},{7,6},{9,8},{10,9},{11,10},{13,12},{... | collective-permute-start | bytes 294920 | tf_op jit(solution)/shard_map/ppermute | solution.py:619
  96.9 29.2 %copy-start.6 = (bf16[32,32,256]{2,1,0:T(8,128)(2,1)S(1)}, bf16[32,32,256]{2,1,0:T(8,128)(2,1)}, u32[]{:S(2)}) copy-start(bf16[32,32,256]{2,1,0:T(8,128)(2,1)} %template.3) | copy-start | bytes 1572868
  117.3 8.8 %copy-start.9 = (f32[32,32,256]{2,1,0:T(8,128)S(1)}, f32[32,32,256]{2,1,0:T(8,128)}, u32[]{:S(2)}) copy-start(f32[32,32,256]{2,1,0:T(8,128)} %copy-done.8) | copy-start | bytes 3145732
  126.1 1.0 copy-start.7

commit v2 on v1

--- a/solution.py
+++ b/solution.py
@@ -30,12 +30,17 @@
     return high, (value - high.astype(F32)).astype(BF16)
 
 
-def table_rows(operators, picks, axis):
-    lane = iota((operators.shape[1], 256), 1)
+def on_lanes(picks):
+    lane = iota((1, 256), 1)
     chosen = jnp.zeros(lane.shape, jnp.int32)
     for b, pick in enumerate(picks):
         chosen = jnp.where(lane // 32 == b, pick, chosen)
-    one_hot = (iota(lane.shape, 0) == chosen).astype(F32).astype(BF16)
+    return chosen
+
+
+def table_rows(operators, chosen, axis):
+    shape = (operators.shape[1], 256)
+    one_hot = (iota(shape, 0) == jnp.broadcast_to(chosen, shape)).astype(F32).astype(BF16)
     found = mm(operators[axis * 1024 : axis * 1024 + 1024, :], one_hot)
     within = iota((32, 256), 1) % 32
     total = jnp.zeros((32, 256), F32)
@@ -201,9 +206,10 @@
     for b in range(8):
         codes = [route[step, 0, 0, b] * 8 + landing[step, 0, 0, b] for step in range(STEPS)]
         value = jnp.zeros((1, 128), jnp.int32)
-        for index, number in enumerate(codes + [picks[1, 0, 0, b]]):
+        for index, number in enumerate(codes):
             value = jnp.where(lane == index, number, value)
         meta[b : b + 1, :] = value.astype(F32)
+        meta[8 + b : 9 + b, :] = jnp.full((1, 128), picks[1, 0, 0, b], jnp.int32).astype(F32)
     meta_half[...] = jnp.broadcast_to(meta[...].astype(BF16)[None], meta_half.shape)
     shared = stage.shape[1]
     sent = [fetch(meta_half, send.at[:, shared : shared + 16, :], sems.at[4])]
@@ -219,7 +225,7 @@
 
 def first_kernel(picks, operators, field, sent, moved_out, tables, table_mem, field_mem, start, folded, turned, out, tables_mem, sems):
     loads = [fetch(operators, table_mem, sems.at[0]), fetch(field, field_mem, sems.at[1])]
-    chosen = [picks[0, 0, 0, b] for b in range(8)]
+    chosen = on_lanes([picks[0, 0, 0, b] for b in range(8)])
     loads[0].wait()
     found = [table_rows(table_mem, chosen, axis) for axis in range(3)]
     for axis in range(3):
@@ -244,15 +250,24 @@
     heard = fetch(arrived.at[:, shared : shared + 16, :], meta_half, sems.at[0])
     loads = [fetch(operators, table_mem, sems.at[1]), fetch(moved, moved_mem, sems.at[2])]
     heard.wait()
-    meta[...] = meta_half[...].astype(F32).astype(jnp.int32)[:, 0:8, :]
-    told = [fetch(meta, codes, sems.at[3]), fetch(meta, codes_out, sems.at[4])]
+    meta[...] = meta_half[...].astype(F32)
+    codes[...] = meta[:, 0:8, :].astype(jnp.int32)
+    told = fetch(codes, codes_out, sems.at[3])
+    lane = iota((1, 128), 1) // 32
+    chosen = []
+    for part in range(2):
+        row = jnp.zeros((1, 128), F32)
+        for b in range(4):
+            own = part * 4 + b
+            found = meta[route[0, 0, 0, own], pl.ds(8 + landing[0, 0, 0, own], 1), :]
+            row = jnp.where(lane == b, found, row)
+        chosen.append(row)
+    chosen = jnp.concatenate(chosen, axis=1).astype(jnp.int32)
     loads[1].wait()
     sent = []
     for b, (place, rank) in enumerate(slot_numbers(route, 0)):
         rows = pl.ds(pl.multiple_of(rank * 256, 256), 256)
         sent.append(fetch(moved_mem.at[b], send.at[place, rows, :], slot_sems.at[b]))
-    told[0].wait()
-    chosen = [codes[route[0, 0, 0, b], landing[0, 0, 0, b], 2] for b in range(8)]
     loads[0].wait()
     found = [table_rows(table_mem, chosen, axis) for axis in range(3)]
     for axis in range(3):
@@ -264,11 +279,11 @@
     for g, value in middle_and_last(start, spread(found[1]), diagonal(found[2]), folded, turned, False):
         put_pieces(stage, g, value, shared // 8)
     sent.append(fetch(stage, send.at[:, 512 : 512 + shared, :], sems.at[6]))
-    for copy in sent + [kept, told[1]]:
+    for copy in sent + [kept, told]:
         copy.wait()
 
 
-def share_kernel(codes_in, arrived, targets, send, codes, moved, aims, total, stage, sems):
+def share_kernel(codes_in, arrived, targets, send, codes, moved, aims, total, stage, sems, chunk_sems):
     peers, shared = moved.shape[0], moved.shape[1]
     rows = shared // 8
     loads = [
@@ -292,45 +307,72 @@
     for source in range(peers):
         final = total[source].astype(BF16).astype(F32)
         stage[source, 0:shared, :] = (final - aims[source].astype(F32)).astype(BF16)
+    sent = []
+    for source in range(peers):
+        for b in range(8):
+            code = codes[source, b, 1]
+            place = pl.ds(pl.multiple_of((code & 7) * rows, rows), rows)
+            stage[source, shared + b * rows : shared + b * rows + rows, :] = stage[code >> 3, place, :]
+        sent.append(fetch(stage.at[source], send.at[source], chunk_sems.at[source]))
+    for copy in sent:
+        copy.wait()
+
+
+def composed_kernel(codes_in, shares, edge, send, codes, own, stage, sems):
+    peers, shared = own.shape[0], own.shape[1]
+    rows = shared // 8
+    loads = [fetch(codes_in, codes, sems.at[0]), fetch(shares.at[:, 0:shared, :], own, sems.at[1])]
+    for load in loads:
+        load.wait()
 
     def give(source, carry):
         for b in range(8):
             first = codes[source, b, 0]
-            for kind, code in ((1, codes[source, b, 1]), (2, codes[first >> 3, first & 7, 1])):
-                place = pl.ds(pl.multiple_of((code & 7) * rows, rows), rows)
-                stage[source, kind * shared + b * rows : kind * shared + b * rows + rows, :] = stage[code >> 3, place, :]
+            code = codes[first >> 3, first & 7, 1]
+            place = pl.ds(pl.multiple_of((code & 7) * rows, rows), rows)
+            stage[source, b * rows : b * rows + rows, :] = own[code >> 3, place, :]
         return carry
 
     lax.fori_loop(0, peers, give, 0)
     fetch(stage, send, sems.at[0]).wait()
 
 
-def final_kernel(tables_one_in, tables_far_in, tables_zero_in, arrived, *refs):
-    adjoint_one, adjoint, tables, start, folded, turned, out, later, field, sems, quarter_sems = refs
+def adjoint_kernel(tables_in, arrived, *refs):
+    adjoint, tables, start, folded, turned, sems = refs
+    load = fetch(tables_in, tables, sems.at[0])
+    rows = arrived.shape[1] // 16
+    load.wait()
+    begin = flipped_diagonal(tables[2].astype(F32))
+    mid = spread(tables[1].astype(F32))
+    end = flipped_diagonal(tables[0].astype(F32))
+    for g in range(4):
+        start[:, g * 256 : g * 256 + 256] = mm(begin, pieces_pair(arrived, 1, g, rows))
+    for g, moved in middle_and_last(start, mid, end, folded, turned, True):
+        put_pair(adjoint, g, moved)
+
+
+def final_kernel(tables_far_in, tables_zero_in, gradient, arrived, *refs):
+    adjoint, tables, start, folded, turned, later, field, sems, quarter_sems = refs
     loads = [
         fetch(source, tables.at[index], sems.at[index])
-        for index, source in enumerate((tables_one_in, tables_far_in, tables_zero_in))
+        for index, source in enumerate((tables_far_in, tables_zero_in))
     ]
-    rows = arrived.shape[1] // 24
+    rows = arrived.shape[1] // 8
     for load in loads:
         load.wait()
-    kept = None
-    for index in range(2):
-        begin = flipped_diagonal(tables[index, 2].astype(F32))
-        mid = spread(tables[index, 1].astype(F32))
-        end = flipped_diagonal(tables[index, 0].astype(F32))
-        for g in range(4):
-            start[:, g * 256 : g * 256 + 256] = mm(begin, pieces_pair(arrived, index + 1, g, rows))
-        for g, moved in middle_and_last(start, mid, end, folded, turned, True):
-            put_pair((out, later)[index], g, moved)
-        if index == 0:
-            kept = fetch(out, adjoint_one, sems.at[0])
-    begin = flipped_diagonal(tables[2, 0].astype(F32))
-    mid = spread(tables[2, 1].astype(F32))
-    end = flipped_diagonal(tables[2, 2].astype(F32))
+    begin = flipped_diagonal(tables[0, 2].astype(F32))
+    mid = spread(tables[0, 1].astype(F32))
+    end = flipped_diagonal(tables[0, 0].astype(F32))
+    for g in range(4):
+        start[:, g * 256 : g * 256 + 256] = mm(begin, pieces_pair(arrived, 0, g, rows))
+    for g, moved in middle_and_last(start, mid, end, folded, turned, True):
+        put_pair(later, g, moved)
+    begin = flipped_diagonal(tables[1, 0].astype(F32))
+    mid = spread(tables[1, 1].astype(F32))
+    end = flipped_diagonal(tables[1, 2].astype(F32))
     for g in range(4):
         start[:, g * 256 : g * 256 + 256] = mm(begin, lane_pair(later, g))
-    stored = [kept]
+    stored = []
     for g, moved in middle_and_last(start, mid, end, folded, turned, True):
         to_native(moved, g, field)
         for qh in range(4):
@@ -450,7 +492,7 @@
 
 
 def prepare_kernel(picks, operators, edge, tables):
-    chosen = [picks[1, 0, 0, b] for b in range(8)]
+    chosen = on_lanes([picks[1, 0, 0, b] for b in range(8)])
     for axis in range(3):
         tables[axis] = table_rows(operators, chosen, axis).astype(BF16)
 
@@ -531,7 +573,7 @@
 ):
     x_form_to_native(adjoint_one, folded, turned, weight_one)
     for g in range(4):
-        to_native(pieces_pair(adjoint_two, 0, g, adjoint_two.shape[1] // 24), g, weight_two)
+        to_native(pieces_pair(adjoint_two, 0, g, adjoint_two.shape[1] // 16), g, weight_two)
     along_y, rim_y, along_z = stencils()
     for padded, before, middle, after, base in (
         (pad_zero, b0x, template, a0x, 0),
@@ -664,7 +706,7 @@
         [far((peers, 512 + shared, 128), BF16), far(TABLES, BF16), far((peers, 8, 128), jnp.int32)],
         [SCALAR, SCALAR, FAR, FAR, ANYWHERE],
         [FAR] * 3,
-        [listed_mem, form, meta_half, pltpu.VMEM((peers, 8, 128), jnp.int32), codes_mem]
+        [listed_mem, form, meta_half, pltpu.VMEM((peers, 16, 128), F32), pltpu.VMEM((peers, 8, 128), jnp.int32)]
         + turning
         + [stage, tables, sems, pltpu.SemaphoreType.DMA((8,))],
         SHORT,
@@ -686,14 +728,14 @@
 
     send = call(
         share_kernel,
-        far((peers, 3 * shared, 128), BF16),
+        far((peers, 2 * shared, 128), BF16),
         [FAR, ANYWHERE, ANYWHERE],
         FAR,
-        [codes_mem, stage, stage, pltpu.VMEM((peers, shared, 128), F32), pltpu.VMEM((peers, 3 * shared, 128), BF16), sems],
+        [codes_mem, stage, stage, pltpu.VMEM((peers, shared, 128), F32), pltpu.VMEM((peers, 2 * shared, 128), BF16)]
+        + [sems, pltpu.SemaphoreType.DMA((peers,))],
         SHORT,
     )(codes, arrived, targets)
     pulled = swap_slots(send)
-
     divergence = call(
         divergence_kernel, like(NATIVE, F32), [WHOLE] * 5 + [FAR], WHOLE, [pltpu.VMEM((38, 32, 256), F32)]
     )(velocity, b0x, a0x, b0y, a0y, send)
@@ -705,16 +747,15 @@
         [codes_mem, pltpu.VMEM((peers, 512, 128), BF16), pltpu.VMEM(FORM, F32), form] + turning[1:] + [sems],
     )(codes, arrived, divergence, send)
     b1x, a1x, b1y, a1y = neighbours(low_x, high_x, low_y, high_y)
-
-    adjoint_one, adjoint = call(
-        final_kernel,
-        [far(FORM, BF16), far(NATIVE, BF16)],
-        [FAR, FAR, FAR, NEAR],
-        [FAR] * 2,
-        [pltpu.VMEM((3,) + TABLES, BF16)] + turning + [form, form, pltpu.VMEM(NATIVE, BF16), sems, quarter_sems],
-        SHORT,
-    )(tables_one, tables_far, tables_zero, pulled)
-
+    composed = call(
+        composed_kernel, far((peers, shared, 128), BF16), [FAR, FAR, WHOLE], FAR, [codes_mem, stage, stage, sems]
+    )(codes, send, low_x)
+
+    composed = swap_slots(composed)
+
+    adjoint_one = call(
+        adjoint_kernel, like(FORM, BF16), [FAR, NEAR], WHOLE, [tables] + turning + [sems]
+    )(tables_one, pulled)
     gradient = call(
         gradient_kernel,
         far((3,) + NATIVE, F32),
@@ -722,6 +763,15 @@
         WHOLE,
         turning[1:] + [pltpu.VMEM(NATIVE, F32)] * 2 + [pltpu.VMEM((38, 32, 256), F32)] * 3,
     )(template, state, divergence, pulled, adjoint_one, b0x, a0x, b0y, a0y, b1x, a1x, b1y, a1y)
+
+    adjoint = call(
+        final_kernel,
+        far(NATIVE, BF16),
+        [FAR, FAR, FAR, NEAR],
+        FAR,
+        [pltpu.VMEM((2,) + TABLES, BF16)] + turning + [form, pltpu.VMEM(NATIVE, BF16), sems, quarter_sems],
+        SHORT,
+    )(tables_far, tables_zero, gradient, composed)
     return gradient, adjoint
 
 

time: 135 us -> 130 us (0.963)
  waiting for transfers between devices: 58.8 us -> 46.3 us
  starting transfers between devices: 30.8 us -> 35.1 us
  Pallas kernels: 40.9 us -> 43.3 us
    all_to_all x3 -> x4, waiting for transfers between devices: 58.8 us -> 46.3 us  [swap_slots(): return lax.all_to_all(send, 'gx', split_axis=0, concat_axis=0, tiled=True)]
    all_to_all x3 -> x4, starting transfers between devices: 15.3 us -> 18.9 us  [swap_slots(): return lax.all_to_all(send, 'gx', split_axis=0, concat_axis=0, tiled=True)]
    pallas_call x10 -> x12, Pallas kernels: 40.9 us -> 43.3 us  [apply(): made(*[pinned(value, spec) for value, spec in zip(values, in_specs, stric...]
    unnamed x20 -> x18, local copies, waits for them, and re-layouts: 2.97 us -> 2.59 us
  transfers between devices with their start and end apart: 11 -> 12, of which waited for: 3 -> 4; matrix products, arithmetic and copies ran while one was open for 0% -> 0% of each run, Pallas kernels for 19% -> 23%
where the time goes in v2:
time: 130 us; the launch traced here: 128 us
  waiting for transfers between devices  46.3 us (36%)
  Pallas kernels  43.3 us (33%)
  starting transfers between devices  35.1 us (27%)
  local copies, waits for them, and re-layouts  2.59 us (2%)
    all_to_all x4, waiting for transfers between devices, swap_slots(): return lax.all_to_all(send, 'gx', split_axis=0, concat_axis=0, tiled=True)  46.3 us
    pallas_call x12, Pallas kernels, apply(): made(*[pinned(value, spec) for value, spec in zip(values, in_specs, stric...  43.3 us
    all_to_all x4, starting transfers between devices, swap_slots(): return lax.all_to_all(send, 'gx', split_axis=0, concat_axis=0, tiled=True)  18.9 us
    ppermute x8, starting transfers between devices, neighbours(): moved += [lax.ppermute(high, axis, up), lax.ppermute(low, axis, down)]  16.2 us
  transfers between devices with their start and end apart: 12, of which 4 were waited for; matrix products, arithmetic and copies ran while one was open for 0% of the time, Pallas kernels for 23%

profile of v2, /device:TPU:0, one launch (start us, length us, event | category | flops | bytes accessed | tf_op | source)
XLA Modules:
  0.0 128.4 jit_solution(5429950918129832660)
XLA Ops:
  0.6 2.3 %shard_map.86.sent = bf16[8,272,128]{2,1,0:T(8,128)(2,1)} custom-call(s32[2,1,1,8]{3,2,1,0:T(1,128)} %picks.3, s32[2,1,1,8]{3,2,1,0:T(1,128)} %bitcast.9, s32[2,1,1,8]{3,2,1,0:T(1,128)} %landing.1, bf16[32,32,256]{2,1,0:T(8,128)(2,1)} %target.1), custom_call_target="tpu_custom_call" | custom-call | flops 1048576 | bytes 1048576 | tf_op jit(solution)/shard_map/pallas_call | solution.py:642
  3.0 7.3 %all-to-all-start = ((bf16[8,272,128]{2,1,0:T(8,128)(2,1)}), bf16[8,272,128]{2,1,0:T(8,128)(2,1)S(1)}, u32[]{:S(2)}, u32[]{:S(2)}) async-start(bf16[8,272,128]{2,1,0:T(8,128)(2,1)} %shard_map.86.sent), calls=%async_computation | async-start | bytes 1114112 | tf_op jit(solution)/shard_map/all_to_all | solution.py:666
  10.9 5.3 %shard_map.87 = (bf16[8,256,128]{2,1,0:T(8,128)(2,1)}, bf16[3,32,256]{2,1,0:T(8,128)(2,1)}) custom-call(s32[2,1,1,8]{3,2,1,0:T(1,128)S(1)} %copy-done.3, bf16[3072,64]{1,0:T(8,128)(2,1)} %bitcast.6, bf16[32,32,256]{2,1,0:T(8,128)(2,1)} %template.3, bf16[8,272,128]{2,1,0:T(8,128)(2,1)} %shard_map.86.sent), custom_call_target="tpu_custom_call" | custom-call | flops 68719476736 | bytes 1048576 | tf_op jit(solution)/shard_map/pallas_call | solution.py:642
  16.3 9.2 %all-to-all-done.arrived.targets = bf16[8,272,128]{2,1,0:T(8,128)(2,1)S(1)} async-done(((bf16[8,272,128]{2,1,0:T(8,128)(2,1)}), bf16[8,272,128]{2,1,0:T(8,128)(2,1)S(1)}, u32[]{:S(2)}, u32[]{:S(2)}) %all-to-all-start) | async-done | bytes 557088 | tf_op jit(solution)/shard_map/all_to_all | solution.py:666
  25.4 5.1 %shard_map.88 = (bf16[8,768,128]{2,1,0:T(8,128)(2,1)}, bf16[3,32,256]{2,1,0:T(8,128)(2,1)}, s32[8,8,128]{2,1,0:T(8,128)}) custom-call(s32[2,1,1,8]{3,2,1,0:T(1,128)S(1)} %bitcast.10, s32[2,1,1,8]{3,2,1,0:T(1,128)S(1)} %copy-done.2, bf16[3072,64]{1,0:T(8,128)(2,1)} %bitcast.7, bf16[8,256,128]{2,1,0:T(8,128)(2,1)} %get-tuple-element.16.moved, ...), custom_call_target="tpu_custom_call" | custom-call | flops 1048576 | bytes 1048576 | tf_op jit(solution)/shard_map/pallas_call | solution.py:642
  30.6 3.6 %all-to-all-start.1 = ((bf16[8,768,128]{2,1,0:T(8,128)(2,1)}), bf16[8,768,128]{2,1,0:T(8,128)(2,1)S(1)}, u32[]{:S(2)}, u32[]{:S(2)}) async-start(bf16[8,768,128]{2,1,0:T(8,128)(2,1)} %get-tuple-element.18.sent), calls=%async_computation.1 | async-start | bytes 3145728 | tf_op jit(solution)/shard_map/all_to_all | solution.py:666
  34.2 1.9 %shard_map.89 = (bf16[6,32,256]{2,1,0:T(8,128)(2,1)S(1)}, bf16[6,32,256]{2,1,0:T(8,128)(2,1)S(1)}, bf16[6,32,256]{2,1,0:T(8,128)(2,1)S(1)}, bf16[6,32,256]{2,1,0:T(8,128)(2,1)S(1)}) custom-call(bf16[32,32,256]{2,1,0:T(8,128)(2,1)} %template.3, f32[3,32,32,256]{3,2,1,0:T(8,128)} %velocity.3, bf16[8,768,128]{2,1,0:T(8,128)(2,1)} %get-tuple-element.18.sent), custom_call_target="tpu_custom_call" | custom-call | flops 68719476736 | bytes 1048576 | tf_op jit(solution)/shard_map/pallas_call | solution.py:642
  36.2 3.9 %collective-permute-start = (bf16[6,32,256]{2,1,0:T(8,128)(2,1)S(1)}, bf16[6,32,256]{2,1,0:T(8,128)(2,1)S(1)}, u32[]{:S(2)}, u32[]{:S(2)}) collective-permute-start(bf16[6,32,256]{2,1,0:T(8,128)(2,1)S(1)} %get-tuple-element.19), channel_id=1, source_target_pairs={{0,4},{4,8},{8,12},{12,16},{16,20},{20,24},{24,28},{1,5},{5,9},{9,... | collective-permute-start | bytes 294920 | tf_op jit(solution)/shard_map/ppermute | solution.py:661
  40.1 1.3 %collective-permute-start.2 = (bf16[6,32,256]{2,1,0:T(8,128)(2,1)S(1)}, bf16[6,32,256]{2,1,0:T(8,128)(2,1)S(1)}, u32[]{:S(2)}, u32[]{:S(2)}) collective-permute-start(bf16[6,32,256]{2,1,0:T(8,128)(2,1)S(1)} %get-tuple-element.21), channel_id=1, source_target_pairs={{0,1},{1,2},{2,3},{4,5},{5,6},{6,7},{8,9},{9,10},{10,11},{12,13},{... | collective-permute-start | bytes 294920 | tf_op jit(solution)/shard_map/ppermute | solution.py:661
  44.0 1.7 %shard_map.93.tables_in = bf16[3,32,256]{2,1,0:T(8,128)(2,1)} custom-call(s32[2,1,1,8]{3,2,1,0:T(1,128)S(1)} %copy-done.4, bf16[3072,64]{1,0:T(8,128)(2,1)S(1)} %bitcast.8, bf16[6,32,256]{2,1,0:T(8,128)(2,1)S(1)} %get-tuple-element.20.edge), custom_call_target="tpu_custom_call" | custom-call | flops 68719476736 | bytes 1048576 | tf_op jit(solution)/shard_map/pallas_call | solution.py:642
  45.8 26.7 %all-to-all-done.1.arrived = bf16[8,768,128]{2,1,0:T(8,128)(2,1)S(1)} async-done(((bf16[8,768,128]{2,1,0:T(8,128)(2,1)}), bf16[8,768,128]{2,1,0:T(8,128)(2,1)S(1)}, u32[]{:S(2)}, u32[]{:S(2)}) %all-to-all-start.1) | async-done | bytes 1572896 | tf_op jit(solution)/shard_map/all_to_all | solution.py:666
  72.5 3.0 %shard_map.90.sent.shares = bf16[8,512,128]{2,1,0:T(8,128)(2,1)} custom-call(s32[8,8,128]{2,1,0:T(8,128)} %get-tuple-element.17.codes_in, bf16[8,768,128]{2,1,0:T(8,128)(2,1)S(1)} %all-to-all-done.1.arrived, bf16[8,272,128]{2,1,0:T(8,128)(2,1)S(1)} %all-to-all-done.arrived.targets), custom_call_target="tpu_custom_call" | custom-call | flops 1048576 | bytes 1048576 | tf_op jit(solution)/shard_map/pallas_call | solution.py:642
  75.4 4.3 %all-to-all-start.2 = ((bf16[8,512,128]{2,1,0:T(8,128)(2,1)}), bf16[8,512,128]{2,1,0:T(8,128)(2,1)}, u32[]{:S(2)}, u32[]{:S(2)}) async-start(bf16[8,512,128]{2,1,0:T(8,128)(2,1)} %shard_map.90.sent.shares), calls=%async_computation.2 | async-start | bytes 2097152 | tf_op jit(solution)/shard_map/all_to_all | solution.py:666
  79.8 1.9 %copy-done.5 = f32[3,32,32,256]{3,2,1,0:T(8,128)S(1)} copy-done((f32[3,32,32,256]{3,2,1,0:T(8,128)S(1)}, f32[3,32,32,256]{3,2,1,0:T(8,128)}, u32[]{:S(2)}) %copy-start.5) | copy-done | bytes 3145752
  81.7 1.5 %shard_map.91.divergence = f32[32,32,256]{2,1,0:T(8,128)S(1)} custom-call(f32[3,32,32,256]{3,2,1,0:T(8,128)S(1)} %copy-done.5, bf16[6,32,256]{2,1,0:T(8,128)(2,1)S(1)} %collective-permute-done.before_x.b0x, bf16[6,32,256]{2,1,0:T(8,128)(2,1)S(1)} %collective-permute-done.1.after_x.a0x, bf16[6,32,256]{2,1,0:T(8,128)(2,1)S(1)} %collective-permute-done.2.before_y.b0y, ...), custom_call_target="tpu_custom_call" | custom-call | flops 68719476736 | bytes 1048576 | tf_op jit(solution)/shard_map/pallas_call | solution.py:642
  83.2 3.1 %shard_map.92 = (bf16[32,32,256]{2,1,0:T(8,128)(2,1)S(1)}, bf16[6,32,256]{2,1,0:T(8,128)(2,1)S(1)}, bf16[6,32,256]{2,1,0:T(8,128)(2,1)S(1)}, bf16[6,32,256]{2,1,0:T(8,128)(2,1)S(1)}, bf16[6,32,256]{2,1,0:T(8,128)(2,1)S(1)}) custom-call(s32[8,8,128]{2,1,0:T(8,128)} %get-tuple-element.17.codes_in, bf16[8,768,128]{2,1,0:T(8,128)(2,1)S(1)} %all-to-all-done.1.arrived, ...), custom_call_target="tpu_custom_call" | custom-call | flops 68719476736 | bytes 1048576 | tf_op jit(solution)/shard_map/pallas_call | solution.py:642
  86.3 2.5 %shard_map.96 = bf16[8,256,128]{2,1,0:T(8,128)(2,1)} custom-call(s32[8,8,128]{2,1,0:T(8,128)} %get-tuple-element.17.codes_in, bf16[8,512,128]{2,1,0:T(8,128)(2,1)} %shard_map.90.sent.shares, bf16[6,32,256]{2,1,0:T(8,128)(2,1)S(1)} %get-tuple-element.25.edge), custom_call_target="tpu_custom_call" | custom-call | flops 68719476736 | bytes 1048576 | tf_op jit(solution)/shard_map/pallas_call | solution.py:642
  90.0 4.6 %collective-permute-start.4 = (bf16[6,32,256]{2,1,0:T(8,128)(2,1)S(1)}, bf16[6,32,256]{2,1,0:T(8,128)(2,1)S(1)}, u32[]{:S(2)}, u32[]{:S(2)}) collective-permute-start(bf16[6,32,256]{2,1,0:T(8,128)(2,1)S(1)} %get-tuple-element.24), channel_id=1, source_target_pairs={{0,4},{4,8},{8,12},{12,16},{16,20},{20,24},{24,28},{1,5},{5,9},{9,... | collective-permute-start | bytes 294920 | tf_op jit(solution)/shard_map/ppermute | solution.py:661
  97.2 8.2 %all-to-all-done.2.arrived.adjoint_two = bf16[8,512,128]{2,1,0:T(8,128)(2,1)} async-done(((bf16[8,512,128]{2,1,0:T(8,128)(2,1)}), bf16[8,512,128]{2,1,0:T(8,128)(2,1)}, u32[]{:S(2)}, u32[]{:S(2)}) %all-to-all-start.2) | async-done | bytes 1048608 | tf_op jit(solution)/shard_map/all_to_all | solution.py:666
  105.4 3.7 %all-to-all-start.3 = ((bf16[8,256,128]{2,1,0:T(8,128)(2,1)}), bf16[8,256,128]{2,1,0:T(8,128)(2,1)S(1)}, u32[]{:S(2)}, u32[]{:S(2)}) async-start(bf16[8,256,128]{2,1,0:T(8,128)(2,1)} %shard_map.96), calls=%async_computation.3 | async-start | bytes 1048576 | tf_op jit(solution)/shard_map/all_to_all | solution.py:666
  109.1 3.9 %shard_map.94.adjoint_one = bf16[8,256,128]{2,1,0:T(8,128)(2,1)S(1)} custom-call(bf16[3,32,256]{2,1,0:T(8,128)(2,1)} %shard_map.93.tables_in, bf16[8,512,128]{2,1,0:T(8,128)(2,1)} %all-to-all-done.2.arrived.adjoint_two), custom_call_target="tpu_custom_call" | custom-call | flops 68719476736 | bytes 1048576 | tf_op jit(solution)/shard_map/pallas_call | solution.py:642
  113.0 7.1 %shard_map.95.gradient = f32[3,32,32,256]{3,2,1,0:T(8,128)} custom-call(bf16[32,32,256]{2,1,0:T(8,128)(2,1)S(1)} %copy-done.6, bf16[32,32,256]{2,1,0:T(8,128)(2,1)S(1)} %get-tuple-element.23.state, f32[32,32,256]{2,1,0:T(8,128)S(1)} %copy-done.8, bf16[8,512,128]{2,1,0:T(8,128)(2,1)} %all-to-all-done.2.arrived.adjoint_two, ...), custom_call_target="tpu_custom_call" | custom-call | flops 68719476736 | bytes 1048576 | tf_op jit(solution)/shard_map/pallas_call | solution.py:642
  120.2 2.3 %all-to-all-done.3.arrived = bf16[8,256,128]{2,1,0:T(8,128)(2,1)S(1)} async-done(((bf16[8,256,128]{2,1,0:T(8,128)(2,1)}), bf16[8,256,128]{2,1,0:T(8,128)(2,1)S(1)}, u32[]{:S(2)}, u32[]{:S(2)}) %all-to-all-start.3) | async-done | bytes 524320 | tf_op jit(solution)/shard_map/all_to_all | solution.py:666
  122.5 5.8 %shard_map.97 = bf16[32,32,256]{2,1,0:T(8,128)(2,1)} custom-call(bf16[3,32,256]{2,1,0:T(8,128)(2,1)} %get-tuple-element.28.tables_far_in, bf16[3,32,256]{2,1,0:T(8,128)(2,1)} %get-tuple-element.29.tables_zero_in, f32[3,32,32,256]{3,2,1,0:T(8,128)} %shard_map.95.gradient, bf16[8,256,128]{2,1,0:T(8,128)(2,1)S(1)} %all-to-all-done.3.arrived), custom_call_target="tpu_custom_call" | custom-call | flops 1048576 | bytes 1048576 | tf_op jit(solution)/shard_map/pallas_call | solution.py:642
  (30 shorter events, 7.2 us)
Async XLA Ops:
  3.0 22.5 %all-to-all-start = ((bf16[8,272,128]{2,1,0:T(8,128)(2,1)}), bf16[8,272,128]{2,1,0:T(8,128)(2,1)S(1)}, u32[]{:S(2)}, u32[]{:S(2)}) async-start(bf16[8,272,128]{2,1,0:T(8,128)(2,1)} %shard_map.86.sent), calls=%async_computation | async-start | bytes 1114112 | tf_op jit(solution)/shard_map/all_to_all | solution.py:666
  10.2 0.7 copy-start.3
  10.9 14.5 %copy-start.1 = (s32[2,1,1,8,1]{3,4,2,1,0:T(1,128)S(1)}, s32[2,1,1,8,1]{3,4,2,1,0:T(1,128)}, u32[]{:S(2)}) copy-start(s32[2,1,1,8,1]{3,4,2,1,0:T(1,128)} %param.11) | copy-start | bytes 196
  10.9 14.5 %copy-start.2 = (s32[2,1,1,8]{3,2,1,0:T(1,128)S(1)}, s32[2,1,1,8]{3,2,1,0:T(1,128)}, u32[]{:S(2)}) copy-start(s32[2,1,1,8]{3,2,1,0:T(1,128)} %landing.1) | copy-start | bytes 196
  30.6 41.9 %all-to-all-start.1 = ((bf16[8,768,128]{2,1,0:T(8,128)(2,1)}), bf16[8,768,128]{2,1,0:T(8,128)(2,1)S(1)}, u32[]{:S(2)}, u32[]{:S(2)}) async-start(bf16[8,768,128]{2,1,0:T(8,128)(2,1)} %get-tuple-element.18.sent), calls=%async_computation.1 | async-start | bytes 3145728 | tf_op jit(solution)/shard_map/all_to_all | solution.py:666
  34.2 9.8 %copy-start = (bf16[64,3,32,32]{0,3,2,1:T(8,128)(2,1)S(1)}, bf16[64,3,32,32]{0,3,2,1:T(8,128)(2,1)}, u32[]{:S(2)}) copy-start(bf16[64,3,32,32]{0,3,2,1:T(8,128)(2,1)} %param.10) | copy-start | bytes 1179652
  34.2 9.8 %copy-start.4 = (s32[2,1,1,8]{3,2,1,0:T(1,128)S(1)}, s32[2,1,1,8]{3,2,1,0:T(1,128)}, u32[]{:S(2)}) copy-start(s32[2,1,1,8]{3,2,1,0:T(1,128)} %picks.3) | copy-start | bytes 196
  36.2 43.5 %collective-permute-start = (bf16[6,32,256]{2,1,0:T(8,128)(2,1)S(1)}, bf16[6,32,256]{2,1,0:T(8,128)(2,1)S(1)}, u32[]{:S(2)}, u32[]{:S(2)}) collective-permute-start(bf16[6,32,256]{2,1,0:T(8,128)(2,1)S(1)} %get-tuple-element.19), channel_id=1, source_target_pairs={{0,4},{4,8},{8,12},{12,16},{16,20},{20,24},{24,28},{1,5},{5,9},{9,... | collective-permute-start | bytes 294920 | tf_op jit(solution)/shard_map/ppermute | solution.py:661
  40.1 39.6 %collective-permute-start.2 = (bf16[6,32,256]{2,1,0:T(8,128)(2,1)S(1)}, bf16[6,32,256]{2,1,0:T(8,128)(2,1)S(1)}, u32[]{:S(2)}, u32[]{:S(2)}) collective-permute-start(bf16[6,32,256]{2,1,0:T(8,128)(2,1)S(1)} %get-tuple-element.21), channel_id=1, source_target_pairs={{0,1},{1,2},{2,3},{4,5},{5,6},{6,7},{8,9},{9,10},{10,11},{12,13},{... | collective-permute-start | bytes 294920 | tf_op jit(solution)/shard_map/ppermute | solution.py:661
  41.4 38.3 %collective-permute-start.3 = (bf16[6,32,256]{2,1,0:T(8,128)(2,1)S(1)}, bf16[6,32,256]{2,1,0:T(8,128)(2,1)S(1)}, u32[]{:S(2)}, u32[]{:S(2)}) collective-permute-start(bf16[6,32,256]{2,1,0:T(8,128)(2,1)S(1)} %get-tuple-element.22), channel_id=1, source_target_pairs={{1,0},{2,1},{3,2},{5,4},{6,5},{7,6},{9,8},{10,9},{11,10},{13,12},{... | collective-permute-start | bytes 294920 | tf_op jit(solution)/shard_map/ppermute | solution.py:661
  42.7 37.0 %collective-permute-start.1 = (bf16[6,32,256]{2,1,0:T(8,128)(2,1)S(1)}, bf16[6,32,256]{2,1,0:T(8,128)(2,1)S(1)}, u32[]{:S(2)}, u32[]{:S(2)}) collective-permute-start(bf16[6,32,256]{2,1,0:T(8,128)(2,1)S(1)} %get-tuple-element.20.edge), channel_id=1, source_target_pairs={{4,0},{8,4},{12,8},{16,12},{20,16},{24,20},{28,24},{5,1},{9,5},{13... | collective-permute-start | bytes 294920 | tf_op jit(solution)/shard_map/ppermute | solution.py:661
  75.4 29.9 %all-to-all-start.2 = ((bf16[8,512,128]{2,1,0:T(8,128)(2,1)}), bf16[8,512,128]{2,1,0:T(8,128)(2,1)}, u32[]{:S(2)}, u32[]{:S(2)}) async-start(bf16[8,512,128]{2,1,0:T(8,128)(2,1)} %shard_map.90.sent.shares), calls=%async_computation.2 | async-start | bytes 2097152 | tf_op jit(solution)/shard_map/all_to_all | solution.py:666
  79.8 1.9 %copy-start.5 = (f32[3,32,32,256]{3,2,1,0:T(8,128)S(1)}, f32[3,32,32,256]{3,2,1,0:T(8,128)}, u32[]{:S(2)}) copy-start(f32[3,32,32,256]{3,2,1,0:T(8,128)} %velocity.3) | copy-start | bytes 9437188
  83.1 3.1 %copy-start.7 = (f32[32,32,256]{2,1,0:T(8,128)}, f32[32,32,256]{2,1,0:T(8,128)S(1)}, u32[]{:S(2)}) copy-start(f32[32,32,256]{2,1,0:T(8,128)S(1)} %shard_map.91.divergence) | copy-start | bytes 3145732
  88.7 24.3 %collective-permute-start.5 = (bf16[6,32,256]{2,1,0:T(8,128)(2,1)S(1)}, bf16[6,32,256]{2,1,0:T(8,128)(2,1)S(1)}, u32[]{:S(2)}, u32[]{:S(2)}) collective-permute-start(bf16[6,32,256]{2,1,0:T(8,128)(2,1)S(1)} %get-tuple-element.25.edge), channel_id=1, source_target_pairs={{4,0},{8,4},{12,8},{16,12},{20,16},{24,20},{28,24},{5,1},{9,5},{13... | collective-permute-start | bytes 294920 | tf_op jit(solution)/shard_map/ppermute | solution.py:661
  90.0 22.9 %collective-permute-start.4 = (bf16[6,32,256]{2,1,0:T(8,128)(2,1)S(1)}, bf16[6,32,256]{2,1,0:T(8,128)(2,1)S(1)}, u32[]{:S(2)}, u32[]{:S(2)}) collective-permute-start(bf16[6,32,256]{2,1,0:T(8,128)(2,1)S(1)} %get-tuple-element.24), channel_id=1, source_target_pairs={{0,4},{4,8},{8,12},{12,16},{16,20},{20,24},{24,28},{1,5},{5,9},{9,... | collective-permute-start | bytes 294920 | tf_op jit(solution)/shard_map/ppermute | solution.py:661
  94.6 18.4 %collective-permute-start.6 = (bf16[6,32,256]{2,1,0:T(8,128)(2,1)S(1)}, bf16[6,32,256]{2,1,0:T(8,128)(2,1)S(1)}, u32[]{:S(2)}, u32[]{:S(2)}) collective-permute-start(bf16[6,32,256]{2,1,0:T(8,128)(2,1)S(1)} %get-tuple-element.26), channel_id=1, source_target_pairs={{0,1},{1,2},{2,3},{4,5},{5,6},{6,7},{8,9},{9,10},{10,11},{12,13},{... | collective-permute-start | bytes 294920 | tf_op jit(solution)/shard_map/ppermute | solution.py:661
  95.9 17.1 %collective-permute-start.7 = (bf16[6,32,256]{2,1,0:T(8,128)(2,1)S(1)}, bf16[6,32,256]{2,1,0:T(8,128)(2,1)S(1)}, u32[]{:S(2)}, u32[]{:S(2)}) collective-permute-start(bf16[6,32,256]{2,1,0:T(8,128)(2,1)S(1)} %get-tuple-element.27), channel_id=1, source_target_pairs={{1,0},{2,1},{3,2},{5,4},{6,5},{7,6},{9,8},{10,9},{11,10},{13,12},{... | collective-permute-start | bytes 294920 | tf_op jit(solution)/shard_map/ppermute | solution.py:661
  105.4 17.1 %all-to-all-start.3 = ((bf16[8,256,128]{2,1,0:T(8,128)(2,1)}), bf16[8,256,128]{2,1,0:T(8,128)(2,1)S(1)}, u32[]{:S(2)}, u32[]{:S(2)}) async-start(bf16[8,256,128]{2,1,0:T(8,128)(2,1)} %shard_map.96), calls=%async_computation.3 | async-start | bytes 1048576 | tf_op jit(solution)/shard_map/all_to_all | solution.py:666
  109.1 4.0 %copy-start.6 = (bf16[32,32,256]{2,1,0:T(8,128)(2,1)S(1)}, bf16[32,32,256]{2,1,0:T(8,128)(2,1)}, u32[]{:S(2)}) copy-start(bf16[32,32,256]{2,1,0:T(8,128)(2,1)} %template.3) | copy-start | bytes 1572868
  109.1 4.0 %copy-start.8 = (f32[32,32,256]{2,1,0:T(8,128)S(1)}, f32[32,32,256]{2,1,0:T(8,128)}, u32[]{:S(2)}) copy-start(f32[32,32,256]{2,1,0:T(8,128)} %copy-done.7) | copy-start | bytes 3145732

commit v3 on v2

--- a/solution.py
+++ b/solution.py
@@ -192,35 +192,38 @@
     return jnp.concatenate(tiles, axis=1)
 
 
-def target_kernel(picks_in, route_in, brick_in, target, send, *refs):
-    picks, route, landing, field, stage, meta, meta_half, sems = refs
+def tell_kernel(picks_in, route_in, brick_in, send, picks, route, landing, meta, meta_half, sems):
     told = [
         fetch(source, place, sems.at[index])
         for index, (source, place) in enumerate(((picks_in, picks), (route_in, route), (brick_in, landing)))
     ]
-    load = fetch(target, field, sems.at[3])
     for copy in told:
         copy.wait()
     lane = iota((1, 128), 1)
     meta[...] = jnp.zeros(meta.shape, F32)
+    value = jnp.zeros((1, 128), jnp.int32)
     for b in range(8):
-        codes = [route[step, 0, 0, b] * 8 + landing[step, 0, 0, b] for step in range(STEPS)]
-        value = jnp.zeros((1, 128), jnp.int32)
-        for index, number in enumerate(codes):
-            value = jnp.where(lane == index, number, value)
-        meta[b : b + 1, :] = value.astype(F32)
+        for step in range(STEPS):
+            code = route[step, 0, 0, b] * 8 + landing[step, 0, 0, b]
+            value = jnp.where(lane == 2 * b + step, code, value)
         meta[8 + b : 9 + b, :] = jnp.full((1, 128), picks[1, 0, 0, b], jnp.int32).astype(F32)
+    meta[0:1, :] = value.astype(F32)
     meta_half[...] = jnp.broadcast_to(meta[...].astype(BF16)[None], meta_half.shape)
-    shared = stage.shape[1]
-    sent = [fetch(meta_half, send.at[:, shared : shared + 16, :], sems.at[4])]
-    load.wait()
+    fetch(meta_half, send, sems.at[0]).wait()
+
+
+def target_kernel(target, told, send, field, stage, sems):
+    fetch(target, field, sems.at[0]).wait()
     for g in range(4):
         block = jnp.concatenate(
             [field[qh * 8 + qs] for qs in (2 * g, 2 * g + 1) for qh in range(4)], axis=0
         )
-        put_pieces(stage, g, mm(identity(), block, NT).astype(BF16), shared // 8)
-    for copy in sent + [fetch(stage, send.at[:, 0:shared, :], sems.at[5])]:
-        copy.wait()
+        put_pieces(stage, g, mm(identity(), block, NT).astype(BF16), stage.shape[1] // 8)
+    fetch(stage, send, sems.at[0]).wait()
+
+
+def pass_kernel(send, targets, same):
+    del send, targets, same
 
 
 def first_kernel(picks, operators, field, sent, moved_out, tables, table_mem, field_mem, start, folded, turned, out, tables_mem, sems):
@@ -247,11 +250,12 @@
 def second_kernel(route, landing, operators, moved, arrived, *refs):
     send, tables, codes_out, table_mem, moved_mem, meta_half, meta, codes, start, folded, turned, stage, tables_mem, sems, slot_sems = refs
     shared = stage.shape[1]
-    heard = fetch(arrived.at[:, shared : shared + 16, :], meta_half, sems.at[0])
+    heard = fetch(arrived, meta_half, sems.at[0])
     loads = [fetch(operators, table_mem, sems.at[1]), fetch(moved, moved_mem, sems.at[2])]
     heard.wait()
     meta[...] = meta_half[...].astype(F32)
-    codes[...] = meta[:, 0:8, :].astype(jnp.int32)
+    for source in range(meta.shape[0]):
+        codes[source : source + 1, :] = meta[source, 0:1, :].astype(jnp.int32)
     told = fetch(codes, codes_out, sems.at[3])
     lane = iota((1, 128), 1) // 32
     chosen = []
@@ -283,34 +287,29 @@
         copy.wait()
 
 
-def share_kernel(codes_in, arrived, targets, send, codes, moved, aims, total, stage, sems, chunk_sems):
-    peers, shared = moved.shape[0], moved.shape[1]
+def share_kernel(plan_in, arrived, targets, send, plan, total, stage, sems, chunk_sems):
+    peers, shared = targets.shape[0], targets.shape[1]
     rows = shared // 8
-    loads = [
-        fetch(codes_in, codes, sems.at[0]),
-        fetch(arrived.at[:, 512 : 512 + shared, :], moved, sems.at[1]),
-        fetch(targets.at[:, 0:shared, :], aims, sems.at[2]),
-    ]
+    load = fetch(plan_in, plan, sems.at[0])
     total[...] = jnp.zeros(total.shape, F32)
-    for load in loads:
-        load.wait()
+    load.wait()
 
     def add(source, carry):
         for b in range(8):
-            first = codes[source, b, 0]
-            final = codes[first >> 3, first & 7, 1]
+            final = plan[source, 8 + b]
             place = pl.ds(pl.multiple_of((final & 7) * rows, rows), rows)
-            total[final >> 3, place, :] += moved[source, b * rows : b * rows + rows, :].astype(F32)
+            at = 512 + b * rows
+            total[final >> 3, place, :] += arrived[source, at : at + rows, :].astype(F32)
         return carry
 
     lax.fori_loop(0, peers, add, 0)
     for source in range(peers):
         final = total[source].astype(BF16).astype(F32)
-        stage[source, 0:shared, :] = (final - aims[source].astype(F32)).astype(BF16)
+        stage[source, 0:shared, :] = (final - targets[source].astype(F32)).astype(BF16)
     sent = []
     for source in range(peers):
         for b in range(8):
-            code = codes[source, b, 1]
+            code = plan[source, b]
             place = pl.ds(pl.multiple_of((code & 7) * rows, rows), rows)
             stage[source, shared + b * rows : shared + b * rows + rows, :] = stage[code >> 3, place, :]
         sent.append(fetch(stage.at[source], send.at[source], chunk_sems.at[source]))
@@ -318,17 +317,16 @@
         copy.wait()
 
 
-def composed_kernel(codes_in, shares, edge, send, codes, own, stage, sems):
+def composed_kernel(plan_in, shares, edge, send, plan, own, stage, sems):
     peers, shared = own.shape[0], own.shape[1]
     rows = shared // 8
-    loads = [fetch(codes_in, codes, sems.at[0]), fetch(shares.at[:, 0:shared, :], own, sems.at[1])]
+    loads = [fetch(plan_in, plan, sems.at[0]), fetch(shares.at[:, 0:shared, :], own, sems.at[1])]
     for load in loads:
         load.wait()
 
     def give(source, carry):
         for b in range(8):
-            first = codes[source, b, 0]
-            code = codes[first >> 3, first & 7, 1]
+            code = plan[source, 8 + b]
             place = pl.ds(pl.multiple_of((code & 7) * rows, rows), rows)
             stage[source, b * rows : b * rows + rows, :] = own[code >> 3, place, :]
         return carry
@@ -351,25 +349,19 @@
         put_pair(adjoint, g, moved)
 
 
-def final_kernel(tables_far_in, tables_zero_in, gradient, arrived, *refs):
-    adjoint, tables, start, folded, turned, later, field, sems, quarter_sems = refs
-    loads = [
-        fetch(source, tables.at[index], sems.at[index])
-        for index, source in enumerate((tables_far_in, tables_zero_in))
-    ]
+def final_kernel(tables_far, tables_zero, gradient, arrived, *refs):
+    adjoint, start, folded, turned, later, field, quarter_sems = refs
     rows = arrived.shape[1] // 8
-    for load in loads:
-        load.wait()
-    begin = flipped_diagonal(tables[0, 2].astype(F32))
-    mid = spread(tables[0, 1].astype(F32))
-    end = flipped_diagonal(tables[0, 0].astype(F32))
+    begin = flipped_diagonal(tables_far[2].astype(F32))
+    mid = spread(tables_far[1].astype(F32))
+    end = flipped_diagonal(tables_far[0].astype(F32))
     for g in range(4):
         start[:, g * 256 : g * 256 + 256] = mm(begin, pieces_pair(arrived, 0, g, rows))
     for g, moved in middle_and_last(start, mid, end, folded, turned, True):
         put_pair(later, g, moved)
-    begin = flipped_diagonal(tables[1, 0].astype(F32))
-    mid = spread(tables[1, 1].astype(F32))
-    end = flipped_diagonal(tables[1, 2].astype(F32))
+    begin = flipped_diagonal(tables_zero[0].astype(F32))
+    mid = spread(tables_zero[1].astype(F32))
+    end = flipped_diagonal(tables_zero[2].astype(F32))
     for g in range(4):
         start[:, g * 256 : g * 256 + 256] = mm(begin, lane_pair(later, g))
     stored = []
@@ -491,10 +483,22 @@
     put_rims([mid_v[8 * g : 8 * g + 8].astype(BF16).reshape(256, 256) for g in range(4)], RIM, low_y, high_y)
 
 
-def prepare_kernel(picks, operators, edge, tables):
+def prepare_kernel(picks, codes_in, operators, edge, tables, plan_out, codes, plan, sems):
+    load = fetch(codes_in, codes, sems.at[0])
     chosen = on_lanes([picks[1, 0, 0, b] for b in range(8)])
     for axis in range(3):
         tables[axis] = table_rows(operators, chosen, axis).astype(BF16)
+    load.wait()
+
+    def row(source, carry):
+        for b in range(8):
+            first = codes[source, 2 * b]
+            plan[source, b] = codes[source, 2 * b + 1]
+            plan[source, 8 + b] = codes[first >> 3, 2 * (first & 7) + 1]
+        return carry
+
+    lax.fori_loop(0, codes.shape[0], row, 0)
+    fetch(plan, plan_out, sems.at[0]).wait()
 
 
 def divergence_kernel(velocity, before_x, after_x, before_y, after_y, sent, divergence, padded):
@@ -523,7 +527,7 @@
     def add(source, carry):
         rank = jnp.int32(0)
         for b in range(8):
-            code = codes[source, b, 0]
+            code = codes[source, 2 * b]
             hit = (code >> 3) == me
 
             @pl.when(hit)
@@ -674,7 +678,7 @@
     turning = [pltpu.VMEM(FLAT, F32), pltpu.VMEM(FOLDED, F32), pltpu.VMEM((512, 1024), BF16)]
     form = pltpu.VMEM(FORM, BF16)
     tables = pltpu.VMEM(TABLES, BF16)
-    codes_mem = pltpu.SMEM((peers, 8, 128), jnp.int32)
+    routes_mem = pltpu.SMEM((peers, 128), jnp.int32)
     stage = pltpu.VMEM((peers, shared, 128), BF16)
     meta_half = pltpu.VMEM((peers, 16, 128), BF16)
     table_rows_count = operators.shape[1] * operators.shape[2] * operators.shape[3]
@@ -682,15 +686,18 @@
     listed_mem = pltpu.VMEM(listed.shape, BF16)
     route = route.reshape(route.shape[:4])
 
+    told = call(
+        tell_kernel,
+        far((peers, 16, 128), BF16),
+        [FAR] * 3,
+        FAR,
+        [pltpu.SMEM(route.shape, jnp.int32)] * 3 + [pltpu.VMEM((16, 128), F32), meta_half, sems],
+        SHORT,
+    )(operator_index, route, target_brick)
+    heard = swap_slots(told)
     send = call(
-        target_kernel,
-        far((peers, shared + 16, 128), BF16),
-        [FAR] * 4,
-        FAR,
-        [pltpu.SMEM(route.shape, jnp.int32)] * 3
-        + [pltpu.VMEM(NATIVE, BF16), stage, pltpu.VMEM((16, 128), F32), meta_half, sems],
-        SHORT,
-    )(operator_index, route, target_brick, target_image)
+        target_kernel, far((peers, shared, 128), BF16), [FAR, FAR], FAR, [pltpu.VMEM(NATIVE, BF16), stage, sems]
+    )(target_image, told)
     targets = swap_slots(send)
 
     moved, tables_zero = call(
@@ -700,17 +707,23 @@
         [FAR] * 2,
         [listed_mem, pltpu.VMEM(NATIVE, BF16)] + turning + [form, tables, sems],
     )(operator_index, listed, template, send)
-
     send, tables_far, codes = call(
         second_kernel,
-        [far((peers, 512 + shared, 128), BF16), far(TABLES, BF16), far((peers, 8, 128), jnp.int32)],
+        [far((peers, 512 + shared, 128), BF16), far(TABLES, BF16), far((peers, 128), jnp.int32)],
         [SCALAR, SCALAR, FAR, FAR, ANYWHERE],
         [FAR] * 3,
-        [listed_mem, form, meta_half, pltpu.VMEM((peers, 16, 128), F32), pltpu.VMEM((peers, 8, 128), jnp.int32)]
+        [listed_mem, form, meta_half, pltpu.VMEM((peers, 16, 128), F32), pltpu.VMEM((peers, 128), jnp.int32)]
         + turning
         + [stage, tables, sems, pltpu.SemaphoreType.DMA((8,))],
-        SHORT,
-    )(route, target_brick, listed, moved, targets)
+    )(route, target_brick, listed, moved, heard)
+    send = pl.pallas_call(
+        pass_kernel,
+        out_shape=far(send.shape, BF16),
+        in_specs=[FAR, ANYWHERE],
+        out_specs=FAR,
+        input_output_aliases={0: 0},
+        cost_estimate=pl.CostEstimate(flops=SHORT, bytes_accessed=1024, transcendentals=0),
+    )(pinned(send, FAR), targets)
     arrived = swap_slots(send)
 
     rim = like((2 * RIM, 32, 256), BF16)
@@ -721,21 +734,26 @@
         [WHOLE] * 4,
         [pltpu.VMEM(NATIVE, BF16)] + [pltpu.VMEM((RIM, 32, 256), F32)] * 2 + [pltpu.VMEM(NATIVE, F32), sems],
     )(template, velocity, send)
-    tables_one = call(prepare_kernel, far(TABLES, BF16), [SCALAR] + [WHOLE] * 2, WHOLE, [])(
-        operator_index, listed, low_x
-    )
+    tables_one, plan = call(
+        prepare_kernel,
+        [far(TABLES, BF16), far((peers, 128), jnp.int32)],
+        [SCALAR, FAR, WHOLE, WHOLE],
+        [WHOLE, FAR],
+        [routes_mem, routes_mem, sems],
+    )(operator_index, codes, listed, low_x)
     b0x, a0x, b0y, a0y = neighbours(low_x, high_x, low_y, high_y)
 
     send = call(
         share_kernel,
         far((peers, 2 * shared, 128), BF16),
-        [FAR, ANYWHERE, ANYWHERE],
+        [FAR, WHOLE, WHOLE],
         FAR,
-        [codes_mem, stage, stage, pltpu.VMEM((peers, shared, 128), F32), pltpu.VMEM((peers, 2 * shared, 128), BF16)]
+        [routes_mem, pltpu.VMEM((peers, shared, 128), F32), pltpu.VMEM((peers, 2 * shared, 128), BF16)]
         + [sems, pltpu.SemaphoreType.DMA((peers,))],
         SHORT,
-    )(codes, arrived, targets)
+    )(plan, arrived, targets)
     pulled = swap_slots(send)
+
     divergence = call(
         divergence_kernel, like(NATIVE, F32), [WHOLE] * 5 + [FAR], WHOLE, [pltpu.VMEM((38, 32, 256), F32)]
     )(velocity, b0x, a0x, b0y, a0y, send)
@@ -744,12 +762,12 @@
         [like(NATIVE, BF16)] + [rim] * 4,
         [FAR, ANYWHERE, WHOLE, FAR],
         [WHOLE] * 5,
-        [codes_mem, pltpu.VMEM((peers, 512, 128), BF16), pltpu.VMEM(FORM, F32), form] + turning[1:] + [sems],
+        [routes_mem, pltpu.VMEM((peers, 512, 128), BF16), pltpu.VMEM(FORM, F32), form] + turning[1:] + [sems],
     )(codes, arrived, divergence, send)
     b1x, a1x, b1y, a1y = neighbours(low_x, high_x, low_y, high_y)
     composed = call(
-        composed_kernel, far((peers, shared, 128), BF16), [FAR, FAR, WHOLE], FAR, [codes_mem, stage, stage, sems]
-    )(codes, send, low_x)
+        composed_kernel, far((peers, shared, 128), BF16), [FAR, FAR, WHOLE], FAR, [routes_mem, stage, stage, sems]
+    )(plan, send, low_x)
 
     composed = swap_slots(composed)
 
@@ -767,9 +785,9 @@
     adjoint = call(
         final_kernel,
         far(NATIVE, BF16),
-        [FAR, FAR, FAR, NEAR],
+        [WHOLE, WHOLE, FAR, NEAR],
         FAR,
-        [pltpu.VMEM((2,) + TABLES, BF16)] + turning + [form, pltpu.VMEM(NATIVE, BF16), sems, quarter_sems],
+        turning + [form, pltpu.VMEM(NATIVE, BF16), quarter_sems],
         SHORT,
     )(tables_far, tables_zero, gradient, composed)
     return gradient, adjoint

time: 130 us -> 135 us (1.038)
  starting transfers between devices: 35.1 us -> 41.1 us
  waiting for transfers between devices: 46.3 us -> 44.4 us
    all_to_all x4 -> x5, starting transfers between devices: 18.9 us -> 24.9 us  [swap_slots(): return lax.all_to_all(send, 'gx', split_axis=0, concat_axis=0, tiled=True)]
    all_to_all x4 -> x5, waiting for transfers between devices: 46.3 us -> 44.4 us  [swap_slots(): return lax.all_to_all(send, 'gx', split_axis=0, concat_axis=0, tiled=True)]
    pallas_call x12 -> x13, Pallas kernels: 43.3 us -> 44.4 us  [apply(): made(*[pinned(value, spec) for value, spec in zip(values, in_specs, stric...]
    unnamed x18 -> x24, local copies, waits for them, and re-layouts: 2.59 us -> 2.73 us
  transfers between devices with their start and end apart: 12 -> 13, of which waited for: 4 -> 4; matrix products, arithmetic and copies ran while one was open for 0% -> 0% of each run, Pallas kernels for 23% -> 28%
where the time goes in v3:
time: 135 us; the launch traced here: 134 us
  Pallas kernels  44.4 us (33%)
  waiting for transfers between devices  44.4 us (33%)
  starting transfers between devices  41.1 us (30%)
  local copies, waits for them, and re-layouts  2.73 us (2%)
    pallas_call x13, Pallas kernels, apply(): made(*[pinned(value, spec) for value, spec in zip(values, in_specs, stric...  44.4 us
    all_to_all x5, waiting for transfers between devices, swap_slots(): return lax.all_to_all(send, 'gx', split_axis=0, concat_axis=0, tiled=True)  44.4 us
    all_to_all x5, starting transfers between devices, swap_slots(): return lax.all_to_all(send, 'gx', split_axis=0, concat_axis=0, tiled=True)  24.9 us
    ppermute x8, starting transfers between devices, neighbours(): moved += [lax.ppermute(high, axis, up), lax.ppermute(low, axis, down)]  16.2 us
    unnamed x24, local copies, waits for them, and re-layouts  2.73 us
  transfers between devices with their start and end apart: 13, of which 4 were waited for; matrix products, arithmetic and copies ran while one was open for 0% of the time, Pallas kernels for 28%

profile of v3, /device:TPU:0, one launch (start us, length us, event | category | flops | bytes accessed | tf_op | source)
XLA Modules:
  0.0 133.8 jit_solution(4459786852859912340)
XLA Ops:
  0.6 1.5 %shard_map.86.told = bf16[8,16,128]{2,1,0:T(8,128)(2,1)} custom-call(s32[2,1,1,8]{3,2,1,0:T(1,128)} %picks.3, s32[2,1,1,8]{3,2,1,0:T(1,128)} %bitcast.6, s32[2,1,1,8]{3,2,1,0:T(1,128)} %landing.1), custom_call_target="tpu_custom_call" | custom-call | flops 1048576 | bytes 1048576 | tf_op jit(solution)/shard_map/pallas_call | solution.py:646
  2.1 7.3 %all-to-all-start = ((bf16[8,16,128]{2,1,0:T(8,128)(2,1)}), bf16[8,16,128]{2,1,0:T(8,128)(2,1)S(1)}, u32[]{:S(2)}, u32[]{:S(2)}) async-start(bf16[8,16,128]{2,1,0:T(8,128)(2,1)} %shard_map.86.told), calls=%async_computation | async-start | bytes 65536 | tf_op jit(solution)/shard_map/all_to_all | solution.py:670
  9.4 2.3 %shard_map.87.sent = bf16[8,256,128]{2,1,0:T(8,128)(2,1)} custom-call(bf16[32,32,256]{2,1,0:T(8,128)(2,1)} %target.1, bf16[8,16,128]{2,1,0:T(8,128)(2,1)} %shard_map.86.told), custom_call_target="tpu_custom_call" | custom-call | flops 68719476736 | bytes 1048576 | tf_op jit(solution)/shard_map/pallas_call | solution.py:646
  11.8 5.3 %shard_map.88 = (bf16[8,256,128]{2,1,0:T(8,128)(2,1)}, bf16[3,32,256]{2,1,0:T(8,128)(2,1)}) custom-call(s32[2,1,1,8]{3,2,1,0:T(1,128)S(1)} %copy-done.6, bf16[3072,64]{1,0:T(8,128)(2,1)} %bitcast.8, bf16[32,32,256]{2,1,0:T(8,128)(2,1)} %template.3, bf16[8,256,128]{2,1,0:T(8,128)(2,1)} %shard_map.87.sent), custom_call_target="tpu_custom_call" | custom-call | flops 68719476736 | bytes 1048576 | tf_op jit(solution)/shard_map/pallas_call | solution.py:646
  17.1 6.0 %all-to-all-start.1 = ((bf16[8,256,128]{2,1,0:T(8,128)(2,1)}), bf16[8,256,128]{2,1,0:T(8,128)(2,1)S(1)}, u32[]{:S(2)}, u32[]{:S(2)}) async-start(bf16[8,256,128]{2,1,0:T(8,128)(2,1)} %shard_map.87.sent), calls=%async_computation.1 | async-start | bytes 1048576 | tf_op jit(solution)/shard_map/all_to_all | solution.py:670
  23.2 5.2 %shard_map.89 = (bf16[8,768,128]{2,1,0:T(8,128)(2,1)}, bf16[3,32,256]{2,1,0:T(8,128)(2,1)}, s32[8,128]{1,0:T(8,128)}) custom-call(s32[2,1,1,8]{3,2,1,0:T(1,128)S(1)} %bitcast.7, s32[2,1,1,8]{3,2,1,0:T(1,128)S(1)} %copy-done.5, bf16[3072,64]{1,0:T(8,128)(2,1)} %bitcast.9, bf16[8,256,128]{2,1,0:T(8,128)(2,1)} %get-tuple-element.18.moved, ...), custom_call_target="tpu_custom_call" | custom-call | flops 68719476736 | bytes 1048576 | tf_op jit(solution)/shard_map/pallas_call | solution.py:646
  28.3 8.8 %all-to-all-done.1.targets = bf16[8,256,128]{2,1,0:T(8,128)(2,1)S(1)} async-done(((bf16[8,256,128]{2,1,0:T(8,128)(2,1)}), bf16[8,256,128]{2,1,0:T(8,128)(2,1)S(1)}, u32[]{:S(2)}, u32[]{:S(2)}) %all-to-all-start.1) | async-done | bytes 524320 | tf_op jit(solution)/shard_map/all_to_all | solution.py:670
  37.9 3.6 %all-to-all-start.2 = ((bf16[8,768,128]{2,1,0:T(8,128)(2,1)}), bf16[8,768,128]{2,1,0:T(8,128)(2,1)S(1)}, u32[]{:S(2)}, u32[]{:S(2)}) async-start(bf16[8,768,128]{2,1,0:T(8,128)(2,1)} %shard_map.90.sent), calls=%async_computation.2 | async-start | bytes 3145728 | tf_op jit(solution)/shard_map/all_to_all | solution.py:670
  41.6 1.9 %shard_map.91 = (bf16[6,32,256]{2,1,0:T(8,128)(2,1)S(1)}, bf16[6,32,256]{2,1,0:T(8,128)(2,1)S(1)}, bf16[6,32,256]{2,1,0:T(8,128)(2,1)S(1)}, bf16[6,32,256]{2,1,0:T(8,128)(2,1)S(1)}) custom-call(bf16[32,32,256]{2,1,0:T(8,128)(2,1)} %template.3, f32[3,32,32,256]{3,2,1,0:T(8,128)} %velocity.3, bf16[8,768,128]{2,1,0:T(8,128)(2,1)} %shard_map.90.sent), custom_call_target="tpu_custom_call" | custom-call | flops 68719476736 | bytes 1048576 | tf_op jit(solution)/shard_map/pallas_call | solution.py:646
  43.5 3.9 %collective-permute-start = (bf16[6,32,256]{2,1,0:T(8,128)(2,1)S(1)}, bf16[6,32,256]{2,1,0:T(8,128)(2,1)S(1)}, u32[]{:S(2)}, u32[]{:S(2)}) collective-permute-start(bf16[6,32,256]{2,1,0:T(8,128)(2,1)S(1)} %get-tuple-element.21), channel_id=1, source_target_pairs={{0,4},{4,8},{8,12},{12,16},{16,20},{20,24},{24,28},{1,5},{5,9},{9,... | collective-permute-start | bytes 294920 | tf_op jit(solution)/shard_map/ppermute | solution.py:665
  51.4 3.4 %shard_map.92 = (bf16[3,32,256]{2,1,0:T(8,128)(2,1)}, s32[8,128]{1,0:T(8,128)}) custom-call(s32[2,1,1,8]{3,2,1,0:T(1,128)S(1)} %copy-done.6, s32[8,128]{1,0:T(8,128)} %get-tuple-element.19.codes_in, bf16[3072,64]{1,0:T(8,128)(2,1)S(1)} %bitcast.10, bf16[6,32,256]{2,1,0:T(8,128)(2,1)S(1)} %get-tuple-element.22.edge), custom_call_target="tpu_custom_call" | custom-call | flops 68719476736 | bytes 1048576 | tf_op jit(solution)/shard_map/pallas_call | solution.py:646
  54.8 24.5 %all-to-all-done.2.arrived = bf16[8,768,128]{2,1,0:T(8,128)(2,1)S(1)} async-done(((bf16[8,768,128]{2,1,0:T(8,128)(2,1)}), bf16[8,768,128]{2,1,0:T(8,128)(2,1)S(1)}, u32[]{:S(2)}, u32[]{:S(2)}) %all-to-all-start.2) | async-done | bytes 1572896 | tf_op jit(solution)/shard_map/all_to_all | solution.py:670
  79.3 2.4 %shard_map.93.sent.shares = bf16[8,512,128]{2,1,0:T(8,128)(2,1)} custom-call(s32[8,128]{1,0:T(8,128)} %get-tuple-element.25.plan_in, bf16[8,768,128]{2,1,0:T(8,128)(2,1)S(1)} %all-to-all-done.2.arrived, bf16[8,256,128]{2,1,0:T(8,128)(2,1)S(1)} %copy-done.1), custom_call_target="tpu_custom_call" | custom-call | flops 1048576 | bytes 1048576 | tf_op jit(solution)/shard_map/pallas_call | solution.py:646
  81.7 4.3 %all-to-all-start.3 = ((bf16[8,512,128]{2,1,0:T(8,128)(2,1)}), bf16[8,512,128]{2,1,0:T(8,128)(2,1)}, u32[]{:S(2)}, u32[]{:S(2)}) async-start(bf16[8,512,128]{2,1,0:T(8,128)(2,1)} %shard_map.93.sent.shares), calls=%async_computation.3 | async-start | bytes 2097152 | tf_op jit(solution)/shard_map/all_to_all | solution.py:670
  86.1 1.9 %copy-done.7 = f32[3,32,32,256]{3,2,1,0:T(8,128)S(1)} copy-done((f32[3,32,32,256]{3,2,1,0:T(8,128)S(1)}, f32[3,32,32,256]{3,2,1,0:T(8,128)}, u32[]{:S(2)}) %copy-start.7) | copy-done | bytes 3145752
  89.4 2.7 %shard_map.95 = (bf16[32,32,256]{2,1,0:T(8,128)(2,1)S(1)}, bf16[6,32,256]{2,1,0:T(8,128)(2,1)S(1)}, bf16[6,32,256]{2,1,0:T(8,128)(2,1)S(1)}, bf16[6,32,256]{2,1,0:T(8,128)(2,1)S(1)}, bf16[6,32,256]{2,1,0:T(8,128)(2,1)S(1)}) custom-call(s32[8,128]{1,0:T(8,128)} %get-tuple-element.19.codes_in, bf16[8,768,128]{2,1,0:T(8,128)(2,1)S(1)} %all-to-all-done.2.arrived, ...), custom_call_target="tpu_custom_call" | custom-call | flops 68719476736 | bytes 1048576 | tf_op jit(solution)/shard_map/pallas_call | solution.py:646
  92.2 2.2 %shard_map.98 = bf16[8,256,128]{2,1,0:T(8,128)(2,1)} custom-call(s32[8,128]{1,0:T(8,128)} %get-tuple-element.25.plan_in, bf16[8,512,128]{2,1,0:T(8,128)(2,1)} %shard_map.93.sent.shares, bf16[6,32,256]{2,1,0:T(8,128)(2,1)S(1)} %get-tuple-element.29.edge), custom_call_target="tpu_custom_call" | custom-call | flops 68719476736 | bytes 1048576 | tf_op jit(solution)/shard_map/pallas_call | solution.py:646
  95.7 4.6 %collective-permute-start.4 = (bf16[6,32,256]{2,1,0:T(8,128)(2,1)S(1)}, bf16[6,32,256]{2,1,0:T(8,128)(2,1)S(1)}, u32[]{:S(2)}, u32[]{:S(2)}) collective-permute-start(bf16[6,32,256]{2,1,0:T(8,128)(2,1)S(1)} %get-tuple-element.28), channel_id=1, source_target_pairs={{0,4},{4,8},{8,12},{12,16},{16,20},{20,24},{24,28},{1,5},{5,9},{9,... | collective-permute-start | bytes 294920 | tf_op jit(solution)/shard_map/ppermute | solution.py:665
  102.8 8.9 %all-to-all-done.3.arrived.adjoint_two = bf16[8,512,128]{2,1,0:T(8,128)(2,1)} async-done(((bf16[8,512,128]{2,1,0:T(8,128)(2,1)}), bf16[8,512,128]{2,1,0:T(8,128)(2,1)}, u32[]{:S(2)}, u32[]{:S(2)}) %all-to-all-start.3) | async-done | bytes 1048608 | tf_op jit(solution)/shard_map/all_to_all | solution.py:670
  111.7 3.7 %all-to-all-start.4 = ((bf16[8,256,128]{2,1,0:T(8,128)(2,1)}), bf16[8,256,128]{2,1,0:T(8,128)(2,1)S(1)}, u32[]{:S(2)}, u32[]{:S(2)}) async-start(bf16[8,256,128]{2,1,0:T(8,128)(2,1)} %shard_map.98), calls=%async_computation.4 | async-start | bytes 1048576 | tf_op jit(solution)/shard_map/all_to_all | solution.py:670
  115.4 3.9 %shard_map.96.adjoint_one = bf16[8,256,128]{2,1,0:T(8,128)(2,1)S(1)} custom-call(bf16[3,32,256]{2,1,0:T(8,128)(2,1)} %get-tuple-element.27.tables_in, bf16[8,512,128]{2,1,0:T(8,128)(2,1)} %all-to-all-done.3.arrived.adjoint_two), custom_call_target="tpu_custom_call" | custom-call | flops 68719476736 | bytes 1048576 | tf_op jit(solution)/shard_map/pallas_call | solution.py:646
  119.4 7.2 %shard_map.97.gradient = f32[3,32,32,256]{3,2,1,0:T(8,128)} custom-call(bf16[32,32,256]{2,1,0:T(8,128)(2,1)S(1)} %copy-done.9, bf16[32,32,256]{2,1,0:T(8,128)(2,1)S(1)} %get-tuple-element.26.state, f32[32,32,256]{2,1,0:T(8,128)S(1)} %copy-done.11, bf16[8,512,128]{2,1,0:T(8,128)(2,1)} %all-to-all-done.3.arrived.adjoint_two, ...), custom_call_target="tpu_custom_call" | custom-call | flops 68719476736 | bytes 1048576 | tf_op jit(solution)/shard_map/pallas_call | solution.py:646
  126.6 2.2 %all-to-all-done.4.arrived = bf16[8,256,128]{2,1,0:T(8,128)(2,1)S(1)} async-done(((bf16[8,256,128]{2,1,0:T(8,128)(2,1)}), bf16[8,256,128]{2,1,0:T(8,128)(2,1)S(1)}, u32[]{:S(2)}, u32[]{:S(2)}) %all-to-all-start.4) | async-done | bytes 524320 | tf_op jit(solution)/shard_map/all_to_all | solution.py:670
  128.8 4.9 %shard_map.99 = bf16[32,32,256]{2,1,0:T(8,128)(2,1)} custom-call(bf16[3,32,256]{2,1,0:T(8,128)(2,1)S(1)} %copy-done.3, bf16[3,32,256]{2,1,0:T(8,128)(2,1)S(1)} %copy-done.2, f32[3,32,32,256]{3,2,1,0:T(8,128)} %shard_map.97.gradient, bf16[8,256,128]{2,1,0:T(8,128)(2,1)S(1)} %all-to-all-done.4.arrived), custom_call_target="tpu_custom_call" | custom-call | flops 1048576 | bytes 1048576 | tf_op jit(solution)/shard_map/pallas_call | solution.py:646
  (40 shorter events, 10.1 us)
Async XLA Ops:
  2.1 15.0 %all-to-all-start = ((bf16[8,16,128]{2,1,0:T(8,128)(2,1)}), bf16[8,16,128]{2,1,0:T(8,128)(2,1)S(1)}, u32[]{:S(2)}, u32[]{:S(2)}) async-start(bf16[8,16,128]{2,1,0:T(8,128)(2,1)} %shard_map.86.told), calls=%async_computation | async-start | bytes 65536 | tf_op jit(solution)/shard_map/all_to_all | solution.py:670
  9.4 2.3 %copy-start.6 = (s32[2,1,1,8]{3,2,1,0:T(1,128)S(1)}, s32[2,1,1,8]{3,2,1,0:T(1,128)}, u32[]{:S(2)}) copy-start(s32[2,1,1,8]{3,2,1,0:T(1,128)} %picks.3) | copy-start | bytes 196
  11.8 11.4 %copy-start.4 = (s32[2,1,1,8,1]{3,4,2,1,0:T(1,128)S(1)}, s32[2,1,1,8,1]{3,4,2,1,0:T(1,128)}, u32[]{:S(2)}) copy-start(s32[2,1,1,8,1]{3,4,2,1,0:T(1,128)} %param.11) | copy-start | bytes 196
  11.8 11.4 %copy-start.5 = (s32[2,1,1,8]{3,2,1,0:T(1,128)S(1)}, s32[2,1,1,8]{3,2,1,0:T(1,128)}, u32[]{:S(2)}) copy-start(s32[2,1,1,8]{3,2,1,0:T(1,128)} %landing.1) | copy-start | bytes 196
  17.1 20.0 %all-to-all-start.1 = ((bf16[8,256,128]{2,1,0:T(8,128)(2,1)}), bf16[8,256,128]{2,1,0:T(8,128)(2,1)S(1)}, u32[]{:S(2)}, u32[]{:S(2)}) async-start(bf16[8,256,128]{2,1,0:T(8,128)(2,1)} %shard_map.87.sent), calls=%async_computation.1 | async-start | bytes 1048576 | tf_op jit(solution)/shard_map/all_to_all | solution.py:670
  37.9 41.4 %all-to-all-start.2 = ((bf16[8,768,128]{2,1,0:T(8,128)(2,1)}), bf16[8,768,128]{2,1,0:T(8,128)(2,1)S(1)}, u32[]{:S(2)}, u32[]{:S(2)}) async-start(bf16[8,768,128]{2,1,0:T(8,128)(2,1)} %shard_map.90.sent), calls=%async_computation.2 | async-start | bytes 3145728 | tf_op jit(solution)/shard_map/all_to_all | solution.py:670
  41.6 9.8 %copy-start.8 = (bf16[64,3,32,32]{0,3,2,1:T(8,128)(2,1)S(1)}, bf16[64,3,32,32]{0,3,2,1:T(8,128)(2,1)}, u32[]{:S(2)}) copy-start(bf16[64,3,32,32]{0,3,2,1:T(8,128)(2,1)} %param.10) | copy-start | bytes 1179652
  43.5 42.5 %collective-permute-start = (bf16[6,32,256]{2,1,0:T(8,128)(2,1)S(1)}, bf16[6,32,256]{2,1,0:T(8,128)(2,1)S(1)}, u32[]{:S(2)}, u32[]{:S(2)}) collective-permute-start(bf16[6,32,256]{2,1,0:T(8,128)(2,1)S(1)} %get-tuple-element.21), channel_id=1, source_target_pairs={{0,4},{4,8},{8,12},{12,16},{16,20},{20,24},{24,28},{1,5},{5,9},{9,... | collective-permute-start | bytes 294920 | tf_op jit(solution)/shard_map/ppermute | solution.py:665
  47.5 38.6 %collective-permute-start.2 = (bf16[6,32,256]{2,1,0:T(8,128)(2,1)S(1)}, bf16[6,32,256]{2,1,0:T(8,128)(2,1)S(1)}, u32[]{:S(2)}, u32[]{:S(2)}) collective-permute-start(bf16[6,32,256]{2,1,0:T(8,128)(2,1)S(1)} %get-tuple-element.23), channel_id=1, source_target_pairs={{0,1},{1,2},{2,3},{4,5},{5,6},{6,7},{8,9},{9,10},{10,11},{12,13},{... | collective-permute-start | bytes 294920 | tf_op jit(solution)/shard_map/ppermute | solution.py:665
  48.8 37.3 %collective-permute-start.3 = (bf16[6,32,256]{2,1,0:T(8,128)(2,1)S(1)}, bf16[6,32,256]{2,1,0:T(8,128)(2,1)S(1)}, u32[]{:S(2)}, u32[]{:S(2)}) collective-permute-start(bf16[6,32,256]{2,1,0:T(8,128)(2,1)S(1)} %get-tuple-element.24), channel_id=1, source_target_pairs={{1,0},{2,1},{3,2},{5,4},{6,5},{7,6},{9,8},{10,9},{11,10},{13,12},{... | collective-permute-start | bytes 294920 | tf_op jit(solution)/shard_map/ppermute | solution.py:665
  50.1 36.0 %collective-permute-start.1 = (bf16[6,32,256]{2,1,0:T(8,128)(2,1)S(1)}, bf16[6,32,256]{2,1,0:T(8,128)(2,1)S(1)}, u32[]{:S(2)}, u32[]{:S(2)}) collective-permute-start(bf16[6,32,256]{2,1,0:T(8,128)(2,1)S(1)} %get-tuple-element.22.edge), channel_id=1, source_target_pairs={{4,0},{8,4},{12,8},{16,12},{20,16},{24,20},{28,24},{5,1},{9,5},{13... | collective-permute-start | bytes 294920 | tf_op jit(solution)/shard_map/ppermute | solution.py:665
  51.4 28.0 %copy-start.1 = (bf16[8,256,128]{2,1,0:T(8,128)(2,1)S(1)}, bf16[8,256,128]{2,1,0:T(8,128)(2,1)}, u32[]{:S(2)}) copy-start(bf16[8,256,128]{2,1,0:T(8,128)(2,1)} %copy-done) | copy-start | bytes 1572868
  81.7 29.9 %all-to-all-start.3 = ((bf16[8,512,128]{2,1,0:T(8,128)(2,1)}), bf16[8,512,128]{2,1,0:T(8,128)(2,1)}, u32[]{:S(2)}, u32[]{:S(2)}) async-start(bf16[8,512,128]{2,1,0:T(8,128)(2,1)} %shard_map.93.sent.shares), calls=%async_computation.3 | async-start | bytes 2097152 | tf_op jit(solution)/shard_map/all_to_all | solution.py:670
  86.0 1.9 %copy-start.7 = (f32[3,32,32,256]{3,2,1,0:T(8,128)S(1)}, f32[3,32,32,256]{3,2,1,0:T(8,128)}, u32[]{:S(2)}) copy-start(f32[3,32,32,256]{3,2,1,0:T(8,128)} %velocity.3) | copy-start | bytes 9437188
  89.4 2.8 %copy-start.10 = (f32[32,32,256]{2,1,0:T(8,128)}, f32[32,32,256]{2,1,0:T(8,128)S(1)}, u32[]{:S(2)}) copy-start(f32[32,32,256]{2,1,0:T(8,128)S(1)} %shard_map.94.divergence) | copy-start | bytes 3145732
  94.4 25.0 %collective-permute-start.5 = (bf16[6,32,256]{2,1,0:T(8,128)(2,1)S(1)}, bf16[6,32,256]{2,1,0:T(8,128)(2,1)S(1)}, u32[]{:S(2)}, u32[]{:S(2)}) collective-permute-start(bf16[6,32,256]{2,1,0:T(8,128)(2,1)S(1)} %get-tuple-element.29.edge), channel_id=1, source_target_pairs={{4,0},{8,4},{12,8},{16,12},{20,16},{24,20},{28,24},{5,1},{9,5},{13... | collective-permute-start | bytes 294920 | tf_op jit(solution)/shard_map/ppermute | solution.py:665
  95.7 23.6 %collective-permute-start.4 = (bf16[6,32,256]{2,1,0:T(8,128)(2,1)S(1)}, bf16[6,32,256]{2,1,0:T(8,128)(2,1)S(1)}, u32[]{:S(2)}, u32[]{:S(2)}) collective-permute-start(bf16[6,32,256]{2,1,0:T(8,128)(2,1)S(1)} %get-tuple-element.28), channel_id=1, source_target_pairs={{0,4},{4,8},{8,12},{12,16},{16,20},{20,24},{24,28},{1,5},{5,9},{9,... | collective-permute-start | bytes 294920 | tf_op jit(solution)/shard_map/ppermute | solution.py:665
  100.2 19.1 %collective-permute-start.6 = (bf16[6,32,256]{2,1,0:T(8,128)(2,1)S(1)}, bf16[6,32,256]{2,1,0:T(8,128)(2,1)S(1)}, u32[]{:S(2)}, u32[]{:S(2)}) collective-permute-start(bf16[6,32,256]{2,1,0:T(8,128)(2,1)S(1)} %get-tuple-element.30), channel_id=1, source_target_pairs={{0,1},{1,2},{2,3},{4,5},{5,6},{6,7},{8,9},{9,10},{10,11},{12,13},{... | collective-permute-start | bytes 294920 | tf_op jit(solution)/shard_map/ppermute | solution.py:665
  101.5 17.8 %collective-permute-start.7 = (bf16[6,32,256]{2,1,0:T(8,128)(2,1)S(1)}, bf16[6,32,256]{2,1,0:T(8,128)(2,1)S(1)}, u32[]{:S(2)}, u32[]{:S(2)}) collective-permute-start(bf16[6,32,256]{2,1,0:T(8,128)(2,1)S(1)} %get-tuple-element.31), channel_id=1, source_target_pairs={{1,0},{2,1},{3,2},{5,4},{6,5},{7,6},{9,8},{10,9},{11,10},{13,12},{... | collective-permute-start | bytes 294920 | tf_op jit(solution)/shard_map/ppermute | solution.py:665
  111.7 17.1 %all-to-all-start.4 = ((bf16[8,256,128]{2,1,0:T(8,128)(2,1)}), bf16[8,256,128]{2,1,0:T(8,128)(2,1)S(1)}, u32[]{:S(2)}, u32[]{:S(2)}) async-start(bf16[8,256,128]{2,1,0:T(8,128)(2,1)} %shard_map.98), calls=%async_computation.4 | async-start | bytes 1048576 | tf_op jit(solution)/shard_map/all_to_all | solution.py:670
  115.4 4.0 %copy-start.9 = (bf16[32,32,256]{2,1,0:T(8,128)(2,1)S(1)}, bf16[32,32,256]{2,1,0:T(8,128)(2,1)}, u32[]{:S(2)}) copy-start(bf16[32,32,256]{2,1,0:T(8,128)(2,1)} %template.3) | copy-start | bytes 1572868
  115.4 4.0 %copy-start.11 = (f32[32,32,256]{2,1,0:T(8,128)S(1)}, f32[32,32,256]{2,1,0:T(8,128)}, u32[]{:S(2)}) copy-start(f32[32,32,256]{2,1,0:T(8,128)} %copy-done.10) | copy-start | bytes 3145732
  119.3 9.4 %copy-start.2 = (bf16[3,32,256]{2,1,0:T(8,128)(2,1)S(1)}, bf16[3,32,256]{2,1,0:T(8,128)(2,1)}, u32[]{:S(2)}) copy-start(bf16[3,32,256]{2,1,0:T(8,128)(2,1)} %get-tuple-element.33.tables_zero) | copy-start | bytes 147460
  119.3 9.4 %copy-start.3 = (bf16[3,32,256]{2,1,0:T(8,128)(2,1)S(1)}, bf16[3,32,256]{2,1,0:T(8,128)(2,1)}, u32[]{:S(2)}) copy-start(bf16[3,32,256]{2,1,0:T(8,128)(2,1)} %get-tuple-element.32.tables_far) | copy-start | bytes 147460
  (1 other events, 0.8 us)

commit v4 on v3

--- a/solution.py
+++ b/solution.py
@@ -192,11 +192,13 @@
     return jnp.concatenate(tiles, axis=1)
 
 
-def tell_kernel(picks_in, route_in, brick_in, send, picks, route, landing, meta, meta_half, sems):
+def target_kernel(picks_in, route_in, brick_in, target, send, *refs):
+    picks, route, landing, field, stage, meta, meta_half, sems = refs
     told = [
         fetch(source, place, sems.at[index])
         for index, (source, place) in enumerate(((picks_in, picks), (route_in, route), (brick_in, landing)))
     ]
+    load = fetch(target, field, sems.at[3])
     for copy in told:
         copy.wait()
     lane = iota((1, 128), 1)
@@ -209,21 +211,16 @@
         meta[8 + b : 9 + b, :] = jnp.full((1, 128), picks[1, 0, 0, b], jnp.int32).astype(F32)
     meta[0:1, :] = value.astype(F32)
     meta_half[...] = jnp.broadcast_to(meta[...].astype(BF16)[None], meta_half.shape)
-    fetch(meta_half, send, sems.at[0]).wait()
-
-
-def target_kernel(target, told, send, field, stage, sems):
-    fetch(target, field, sems.at[0]).wait()
+    shared = stage.shape[1]
+    sent = [fetch(meta_half, send.at[:, shared : shared + 16, :], sems.at[4])]
+    load.wait()
     for g in range(4):
         block = jnp.concatenate(
             [field[qh * 8 + qs] for qs in (2 * g, 2 * g + 1) for qh in range(4)], axis=0
         )
-        put_pieces(stage, g, mm(identity(), block, NT).astype(BF16), stage.shape[1] // 8)
-    fetch(stage, send, sems.at[0]).wait()
-
-
-def pass_kernel(send, targets, same):
-    del send, targets, same
+        put_pieces(stage, g, mm(identity(), block, NT).astype(BF16), shared // 8)
+    for copy in sent + [fetch(stage, send.at[:, 0:shared, :], sems.at[5])]:
+        copy.wait()
 
 
 def first_kernel(picks, operators, field, sent, moved_out, tables, table_mem, field_mem, start, folded, turned, out, tables_mem, sems):
@@ -250,7 +247,7 @@
 def second_kernel(route, landing, operators, moved, arrived, *refs):
     send, tables, codes_out, table_mem, moved_mem, meta_half, meta, codes, start, folded, turned, stage, tables_mem, sems, slot_sems = refs
     shared = stage.shape[1]
-    heard = fetch(arrived, meta_half, sems.at[0])
+    heard = fetch(arrived.at[:, shared : shared + 16, :], meta_half, sems.at[0])
     loads = [fetch(operators, table_mem, sems.at[1]), fetch(moved, moved_mem, sems.at[2])]
     heard.wait()
     meta[...] = meta_half[...].astype(F32)
@@ -288,7 +285,7 @@
 
 
 def share_kernel(plan_in, arrived, targets, send, plan, total, stage, sems, chunk_sems):
-    peers, shared = targets.shape[0], targets.shape[1]
+    peers, shared = total.shape[0], total.shape[1]
     rows = shared // 8
     load = fetch(plan_in, plan, sems.at[0])
     total[...] = jnp.zeros(total.shape, F32)
@@ -305,7 +302,7 @@
     lax.fori_loop(0, peers, add, 0)
     for source in range(peers):
         final = total[source].astype(BF16).astype(F32)
-        stage[source, 0:shared, :] = (final - targets[source].astype(F32)).astype(BF16)
+        stage[source, 0:shared, :] = (final - targets[source, 0:shared, :].astype(F32)).astype(BF16)
     sent = []
     for source in range(peers):
         for b in range(8):
@@ -686,18 +683,15 @@
     listed_mem = pltpu.VMEM(listed.shape, BF16)
     route = route.reshape(route.shape[:4])
 
-    told = call(
-        tell_kernel,
-        far((peers, 16, 128), BF16),
-        [FAR] * 3,
+    send = call(
+        target_kernel,
+        far((peers, shared + 16, 128), BF16),
+        [FAR] * 4,
         FAR,
-        [pltpu.SMEM(route.shape, jnp.int32)] * 3 + [pltpu.VMEM((16, 128), F32), meta_half, sems],
+        [pltpu.SMEM(route.shape, jnp.int32)] * 3
+        + [pltpu.VMEM(NATIVE, BF16), stage, pltpu.VMEM((16, 128), F32), meta_half, sems],
         SHORT,
-    )(operator_index, route, target_brick)
-    heard = swap_slots(told)
-    send = call(
-        target_kernel, far((peers, shared, 128), BF16), [FAR, FAR], FAR, [pltpu.VMEM(NATIVE, BF16), stage, sems]
-    )(target_image, told)
+    )(operator_index, route, target_brick, target_image)
     targets = swap_slots(send)
 
     moved, tables_zero = call(
@@ -715,15 +709,8 @@
         [listed_mem, form, meta_half, pltpu.VMEM((peers, 16, 128), F32), pltpu.VMEM((peers, 128), jnp.int32)]
         + turning
         + [stage, tables, sems, pltpu.SemaphoreType.DMA((8,))],
-    )(route, target_brick, listed, moved, heard)
-    send = pl.pallas_call(
-        pass_kernel,
-        out_shape=far(send.shape, BF16),
-        in_specs=[FAR, ANYWHERE],
-        out_specs=FAR,
-        input_output_aliases={0: 0},
-        cost_estimate=pl.CostEstimate(flops=SHORT, bytes_accessed=1024, transcendentals=0),
-    )(pinned(send, FAR), targets)
+        SHORT,
+    )(route, target_brick, listed, moved, targets)
     arrived = swap_slots(send)
 
     rim = like((2 * RIM, 32, 256), BF16)

time: 135 us -> 128 us (0.948)
  starting transfers between devices: 41.1 us -> 35.1 us
  Pallas kernels: 44.4 us -> 42.8 us
    all_to_all x5 -> x4, starting transfers between devices: 24.9 us -> 18.9 us  [swap_slots(): return lax.all_to_all(send, 'gx', split_axis=0, concat_axis=0, tiled=True)]
    pallas_call x13 -> x12, Pallas kernels: 44.4 us -> 42.8 us  [apply(): made(*[pinned(value, spec) for value, spec in zip(values, in_specs, stric...]
    all_to_all x5 -> x4, waiting for transfers between devices: 44.4 us -> 45.3 us  [swap_slots(): return lax.all_to_all(send, 'gx', split_axis=0, concat_axis=0, tiled=True)]
    unnamed x24 -> x22, local copies, waits for them, and re-layouts: 2.73 us -> 2.6 us
  transfers between devices with their start and end apart: 13 -> 12, of which waited for: 4 -> 4; matrix products, arithmetic and copies ran while one was open for 0% -> 0% of each run, Pallas kernels for 28% -> 24%
where the time goes in v4:
time: 128 us; the launch traced here: 127 us
  waiting for transfers between devices  45.3 us (35%)
  Pallas kernels  42.8 us (33%)
  starting transfers between devices  35.1 us (27%)
  local copies, waits for them, and re-layouts  2.6 us (2%)
    all_to_all x4, waiting for transfers between devices, swap_slots(): return lax.all_to_all(send, 'gx', split_axis=0, concat_axis=0, tiled=True)  45.3 us
    pallas_call x12, Pallas kernels, apply(): made(*[pinned(value, spec) for value, spec in zip(values, in_specs, stric...  42.8 us
    all_to_all x4, starting transfers between devices, swap_slots(): return lax.all_to_all(send, 'gx', split_axis=0, concat_axis=0, tiled=True)  18.9 us
    ppermute x8, starting transfers between devices, neighbours(): moved += [lax.ppermute(high, axis, up), lax.ppermute(low, axis, down)]  16.2 us
    unnamed x22, local copies, waits for them, and re-layouts  2.6 us
  transfers between devices with their start and end apart: 12, of which 4 were waited for; matrix products, arithmetic and copies ran while one was open for 0% of the time, Pallas kernels for 24%

profile of v4, /device:TPU:0, one launch (start us, length us, event | category | flops | bytes accessed | tf_op | source)
XLA Modules:
  0.0 126.9 jit_solution(1097059442338831902)
XLA Ops:
  0.6 2.3 %shard_map.86.sent = bf16[8,272,128]{2,1,0:T(8,128)(2,1)} custom-call(s32[2,1,1,8]{3,2,1,0:T(1,128)} %picks.3, s32[2,1,1,8]{3,2,1,0:T(1,128)} %bitcast.9, s32[2,1,1,8]{3,2,1,0:T(1,128)} %landing.1, bf16[32,32,256]{2,1,0:T(8,128)(2,1)} %target.1), custom_call_target="tpu_custom_call" | custom-call | flops 1048576 | bytes 1048576 | tf_op jit(solution)/shard_map/pallas_call | solution.py:643
  3.0 7.3 %all-to-all-start = ((bf16[8,272,128]{2,1,0:T(8,128)(2,1)}), bf16[8,272,128]{2,1,0:T(8,128)(2,1)S(1)}, u32[]{:S(2)}, u32[]{:S(2)}) async-start(bf16[8,272,128]{2,1,0:T(8,128)(2,1)} %shard_map.86.sent), calls=%async_computation | async-start | bytes 1114112 | tf_op jit(solution)/shard_map/all_to_all | solution.py:667
  10.9 5.3 %shard_map.87 = (bf16[8,256,128]{2,1,0:T(8,128)(2,1)}, bf16[3,32,256]{2,1,0:T(8,128)(2,1)}) custom-call(s32[2,1,1,8]{3,2,1,0:T(1,128)S(1)} %copy-done.5, bf16[3072,64]{1,0:T(8,128)(2,1)} %bitcast.6, bf16[32,32,256]{2,1,0:T(8,128)(2,1)} %template.3, bf16[8,272,128]{2,1,0:T(8,128)(2,1)} %shard_map.86.sent), custom_call_target="tpu_custom_call" | custom-call | flops 68719476736 | bytes 1048576 | tf_op jit(solution)/shard_map/pallas_call | solution.py:643
  16.3 9.2 %all-to-all-done.arrived.targets = bf16[8,272,128]{2,1,0:T(8,128)(2,1)S(1)} async-done(((bf16[8,272,128]{2,1,0:T(8,128)(2,1)}), bf16[8,272,128]{2,1,0:T(8,128)(2,1)S(1)}, u32[]{:S(2)}, u32[]{:S(2)}) %all-to-all-start) | async-done | bytes 557088 | tf_op jit(solution)/shard_map/all_to_all | solution.py:667
  25.4 5.1 %shard_map.88 = (bf16[8,768,128]{2,1,0:T(8,128)(2,1)}, bf16[3,32,256]{2,1,0:T(8,128)(2,1)}, s32[8,128]{1,0:T(8,128)}) custom-call(s32[2,1,1,8]{3,2,1,0:T(1,128)S(1)} %bitcast.10, s32[2,1,1,8]{3,2,1,0:T(1,128)S(1)} %copy-done.4, bf16[3072,64]{1,0:T(8,128)(2,1)} %bitcast.7, bf16[8,256,128]{2,1,0:T(8,128)(2,1)} %get-tuple-element.18.moved, ...), custom_call_target="tpu_custom_call" | custom-call | flops 1048576 | bytes 1048576 | tf_op jit(solution)/shard_map/pallas_call | solution.py:643
  30.6 3.6 %all-to-all-start.1 = ((bf16[8,768,128]{2,1,0:T(8,128)(2,1)}), bf16[8,768,128]{2,1,0:T(8,128)(2,1)S(1)}, u32[]{:S(2)}, u32[]{:S(2)}) async-start(bf16[8,768,128]{2,1,0:T(8,128)(2,1)} %get-tuple-element.20.sent), calls=%async_computation.1 | async-start | bytes 3145728 | tf_op jit(solution)/shard_map/all_to_all | solution.py:667
  34.2 1.9 %shard_map.89 = (bf16[6,32,256]{2,1,0:T(8,128)(2,1)S(1)}, bf16[6,32,256]{2,1,0:T(8,128)(2,1)S(1)}, bf16[6,32,256]{2,1,0:T(8,128)(2,1)S(1)}, bf16[6,32,256]{2,1,0:T(8,128)(2,1)S(1)}) custom-call(bf16[32,32,256]{2,1,0:T(8,128)(2,1)} %template.3, f32[3,32,32,256]{3,2,1,0:T(8,128)} %velocity.3, bf16[8,768,128]{2,1,0:T(8,128)(2,1)} %get-tuple-element.20.sent), custom_call_target="tpu_custom_call" | custom-call | flops 68719476736 | bytes 1048576 | tf_op jit(solution)/shard_map/pallas_call | solution.py:643
  36.2 3.9 %collective-permute-start = (bf16[6,32,256]{2,1,0:T(8,128)(2,1)S(1)}, bf16[6,32,256]{2,1,0:T(8,128)(2,1)S(1)}, u32[]{:S(2)}, u32[]{:S(2)}) collective-permute-start(bf16[6,32,256]{2,1,0:T(8,128)(2,1)S(1)} %get-tuple-element.21), channel_id=1, source_target_pairs={{0,4},{4,8},{8,12},{12,16},{16,20},{20,24},{24,28},{1,5},{5,9},{9,... | collective-permute-start | bytes 294920 | tf_op jit(solution)/shard_map/ppermute | solution.py:662
  40.1 1.3 %collective-permute-start.2 = (bf16[6,32,256]{2,1,0:T(8,128)(2,1)S(1)}, bf16[6,32,256]{2,1,0:T(8,128)(2,1)S(1)}, u32[]{:S(2)}, u32[]{:S(2)}) collective-permute-start(bf16[6,32,256]{2,1,0:T(8,128)(2,1)S(1)} %get-tuple-element.23), channel_id=1, source_target_pairs={{0,1},{1,2},{2,3},{4,5},{5,6},{6,7},{8,9},{9,10},{10,11},{12,13},{... | collective-permute-start | bytes 294920 | tf_op jit(solution)/shard_map/ppermute | solution.py:662
  44.0 3.4 %shard_map.90 = (bf16[3,32,256]{2,1,0:T(8,128)(2,1)}, s32[8,128]{1,0:T(8,128)}) custom-call(s32[2,1,1,8]{3,2,1,0:T(1,128)S(1)} %copy-done.6, s32[8,128]{1,0:T(8,128)} %get-tuple-element.19.codes_in, bf16[3072,64]{1,0:T(8,128)(2,1)S(1)} %bitcast.8, bf16[6,32,256]{2,1,0:T(8,128)(2,1)S(1)} %get-tuple-element.22.edge), custom_call_target="tpu_custom_call" | custom-call | flops 68719476736 | bytes 1048576 | tf_op jit(solution)/shard_map/pallas_call | solution.py:643
  47.5 25.0 %all-to-all-done.1.arrived = bf16[8,768,128]{2,1,0:T(8,128)(2,1)S(1)} async-done(((bf16[8,768,128]{2,1,0:T(8,128)(2,1)}), bf16[8,768,128]{2,1,0:T(8,128)(2,1)S(1)}, u32[]{:S(2)}, u32[]{:S(2)}) %all-to-all-start.1) | async-done | bytes 1572896 | tf_op jit(solution)/shard_map/all_to_all | solution.py:667
  72.5 2.4 %shard_map.91.sent.shares = bf16[8,512,128]{2,1,0:T(8,128)(2,1)} custom-call(s32[8,128]{1,0:T(8,128)} %get-tuple-element.25.plan_in, bf16[8,768,128]{2,1,0:T(8,128)(2,1)S(1)} %all-to-all-done.1.arrived, bf16[8,272,128]{2,1,0:T(8,128)(2,1)S(1)} %all-to-all-done.arrived.targets), custom_call_target="tpu_custom_call" | custom-call | flops 1048576 | bytes 1048576 | tf_op jit(solution)/shard_map/pallas_call | solution.py:643
  74.9 4.3 %all-to-all-start.2 = ((bf16[8,512,128]{2,1,0:T(8,128)(2,1)}), bf16[8,512,128]{2,1,0:T(8,128)(2,1)}, u32[]{:S(2)}, u32[]{:S(2)}) async-start(bf16[8,512,128]{2,1,0:T(8,128)(2,1)} %shard_map.91.sent.shares), calls=%async_computation.2 | async-start | bytes 2097152 | tf_op jit(solution)/shard_map/all_to_all | solution.py:667
  79.2 1.9 %copy-done.7 = f32[3,32,32,256]{3,2,1,0:T(8,128)S(1)} copy-done((f32[3,32,32,256]{3,2,1,0:T(8,128)S(1)}, f32[3,32,32,256]{3,2,1,0:T(8,128)}, u32[]{:S(2)}) %copy-start.7) | copy-done | bytes 3145752
  81.1 1.5 %shard_map.92.divergence = f32[32,32,256]{2,1,0:T(8,128)S(1)} custom-call(f32[3,32,32,256]{3,2,1,0:T(8,128)S(1)} %copy-done.7, bf16[6,32,256]{2,1,0:T(8,128)(2,1)S(1)} %collective-permute-done.before_x.b0x, bf16[6,32,256]{2,1,0:T(8,128)(2,1)S(1)} %collective-permute-done.1.after_x.a0x, bf16[6,32,256]{2,1,0:T(8,128)(2,1)S(1)} %collective-permute-done.2.before_y.b0y, ...), custom_call_target="tpu_custom_call" | custom-call | flops 68719476736 | bytes 1048576 | tf_op jit(solution)/shard_map/pallas_call | solution.py:643
  82.6 2.7 %shard_map.93 = (bf16[32,32,256]{2,1,0:T(8,128)(2,1)S(1)}, bf16[6,32,256]{2,1,0:T(8,128)(2,1)S(1)}, bf16[6,32,256]{2,1,0:T(8,128)(2,1)S(1)}, bf16[6,32,256]{2,1,0:T(8,128)(2,1)S(1)}, bf16[6,32,256]{2,1,0:T(8,128)(2,1)S(1)}) custom-call(s32[8,128]{1,0:T(8,128)} %get-tuple-element.19.codes_in, bf16[8,768,128]{2,1,0:T(8,128)(2,1)S(1)} %all-to-all-done.1.arrived, ...), custom_call_target="tpu_custom_call" | custom-call | flops 68719476736 | bytes 1048576 | tf_op jit(solution)/shard_map/pallas_call | solution.py:643
  85.3 2.2 %shard_map.96 = bf16[8,256,128]{2,1,0:T(8,128)(2,1)} custom-call(s32[8,128]{1,0:T(8,128)} %get-tuple-element.25.plan_in, bf16[8,512,128]{2,1,0:T(8,128)(2,1)} %shard_map.91.sent.shares, bf16[6,32,256]{2,1,0:T(8,128)(2,1)S(1)} %get-tuple-element.29.edge), custom_call_target="tpu_custom_call" | custom-call | flops 68719476736 | bytes 1048576 | tf_op jit(solution)/shard_map/pallas_call | solution.py:643
  88.8 4.6 %collective-permute-start.4 = (bf16[6,32,256]{2,1,0:T(8,128)(2,1)S(1)}, bf16[6,32,256]{2,1,0:T(8,128)(2,1)S(1)}, u32[]{:S(2)}, u32[]{:S(2)}) collective-permute-start(bf16[6,32,256]{2,1,0:T(8,128)(2,1)S(1)} %get-tuple-element.28), channel_id=1, source_target_pairs={{0,4},{4,8},{8,12},{12,16},{16,20},{20,24},{24,28},{1,5},{5,9},{9,... | collective-permute-start | bytes 294920 | tf_op jit(solution)/shard_map/ppermute | solution.py:662
  95.9 8.8 %all-to-all-done.2.arrived.adjoint_two = bf16[8,512,128]{2,1,0:T(8,128)(2,1)} async-done(((bf16[8,512,128]{2,1,0:T(8,128)(2,1)}), bf16[8,512,128]{2,1,0:T(8,128)(2,1)}, u32[]{:S(2)}, u32[]{:S(2)}) %all-to-all-start.2) | async-done | bytes 1048608 | tf_op jit(solution)/shard_map/all_to_all | solution.py:667
  104.8 3.7 %all-to-all-start.3 = ((bf16[8,256,128]{2,1,0:T(8,128)(2,1)}), bf16[8,256,128]{2,1,0:T(8,128)(2,1)S(1)}, u32[]{:S(2)}, u32[]{:S(2)}) async-start(bf16[8,256,128]{2,1,0:T(8,128)(2,1)} %shard_map.96), calls=%async_computation.3 | async-start | bytes 1048576 | tf_op jit(solution)/shard_map/all_to_all | solution.py:667
  108.5 3.9 %shard_map.94.adjoint_one = bf16[8,256,128]{2,1,0:T(8,128)(2,1)S(1)} custom-call(bf16[3,32,256]{2,1,0:T(8,128)(2,1)} %get-tuple-element.27.tables_in, bf16[8,512,128]{2,1,0:T(8,128)(2,1)} %all-to-all-done.2.arrived.adjoint_two), custom_call_target="tpu_custom_call" | custom-call | flops 68719476736 | bytes 1048576 | tf_op jit(solution)/shard_map/pallas_call | solution.py:643
  112.5 7.1 %shard_map.95.gradient = f32[3,32,32,256]{3,2,1,0:T(8,128)} custom-call(bf16[32,32,256]{2,1,0:T(8,128)(2,1)S(1)} %copy-done.8, bf16[32,32,256]{2,1,0:T(8,128)(2,1)S(1)} %get-tuple-element.26.state, f32[32,32,256]{2,1,0:T(8,128)S(1)} %copy-done.10, bf16[8,512,128]{2,1,0:T(8,128)(2,1)} %all-to-all-done.2.arrived.adjoint_two, ...), custom_call_target="tpu_custom_call" | custom-call | flops 68719476736 | bytes 1048576 | tf_op jit(solution)/shard_map/pallas_call | solution.py:643
  119.6 2.3 %all-to-all-done.3.arrived = bf16[8,256,128]{2,1,0:T(8,128)(2,1)S(1)} async-done(((bf16[8,256,128]{2,1,0:T(8,128)(2,1)}), bf16[8,256,128]{2,1,0:T(8,128)(2,1)S(1)}, u32[]{:S(2)}, u32[]{:S(2)}) %all-to-all-start.3) | async-done | bytes 524320 | tf_op jit(solution)/shard_map/all_to_all | solution.py:667
  121.9 4.8 %shard_map.97 = bf16[32,32,256]{2,1,0:T(8,128)(2,1)} custom-call(bf16[3,32,256]{2,1,0:T(8,128)(2,1)S(1)} %copy-done.2, bf16[3,32,256]{2,1,0:T(8,128)(2,1)S(1)} %copy-done.1, f32[3,32,32,256]{3,2,1,0:T(8,128)} %shard_map.95.gradient, bf16[8,256,128]{2,1,0:T(8,128)(2,1)S(1)} %all-to-all-done.3.arrived), custom_call_target="tpu_custom_call" | custom-call | flops 1048576 | bytes 1048576 | tf_op jit(solution)/shard_map/pallas_call | solution.py:643
  (34 shorter events, 7.2 us)
Async XLA Ops:
  3.0 22.5 %all-to-all-start = ((bf16[8,272,128]{2,1,0:T(8,128)(2,1)}), bf16[8,272,128]{2,1,0:T(8,128)(2,1)S(1)}, u32[]{:S(2)}, u32[]{:S(2)}) async-start(bf16[8,272,128]{2,1,0:T(8,128)(2,1)} %shard_map.86.sent), calls=%async_computation | async-start | bytes 1114112 | tf_op jit(solution)/shard_map/all_to_all | solution.py:667
  10.2 0.7 copy-start.5
  10.9 14.5 %copy-start.3 = (s32[2,1,1,8,1]{3,4,2,1,0:T(1,128)S(1)}, s32[2,1,1,8,1]{3,4,2,1,0:T(1,128)}, u32[]{:S(2)}) copy-start(s32[2,1,1,8,1]{3,4,2,1,0:T(1,128)} %param.11) | copy-start | bytes 196
  10.9 14.5 %copy-start.4 = (s32[2,1,1,8]{3,2,1,0:T(1,128)S(1)}, s32[2,1,1,8]{3,2,1,0:T(1,128)}, u32[]{:S(2)}) copy-start(s32[2,1,1,8]{3,2,1,0:T(1,128)} %landing.1) | copy-start | bytes 196
  30.6 41.9 %all-to-all-start.1 = ((bf16[8,768,128]{2,1,0:T(8,128)(2,1)}), bf16[8,768,128]{2,1,0:T(8,128)(2,1)S(1)}, u32[]{:S(2)}, u32[]{:S(2)}) async-start(bf16[8,768,128]{2,1,0:T(8,128)(2,1)} %get-tuple-element.20.sent), calls=%async_computation.1 | async-start | bytes 3145728 | tf_op jit(solution)/shard_map/all_to_all | solution.py:667
  34.2 9.8 %copy-start = (bf16[64,3,32,32]{0,3,2,1:T(8,128)(2,1)S(1)}, bf16[64,3,32,32]{0,3,2,1:T(8,128)(2,1)}, u32[]{:S(2)}) copy-start(bf16[64,3,32,32]{0,3,2,1:T(8,128)(2,1)} %param.10) | copy-start | bytes 1179652
  34.2 9.8 %copy-start.6 = (s32[2,1,1,8]{3,2,1,0:T(1,128)S(1)}, s32[2,1,1,8]{3,2,1,0:T(1,128)}, u32[]{:S(2)}) copy-start(s32[2,1,1,8]{3,2,1,0:T(1,128)} %picks.3) | copy-start | bytes 196
  36.2 42.9 %collective-permute-start = (bf16[6,32,256]{2,1,0:T(8,128)(2,1)S(1)}, bf16[6,32,256]{2,1,0:T(8,128)(2,1)S(1)}, u32[]{:S(2)}, u32[]{:S(2)}) collective-permute-start(bf16[6,32,256]{2,1,0:T(8,128)(2,1)S(1)} %get-tuple-element.21), channel_id=1, source_target_pairs={{0,4},{4,8},{8,12},{12,16},{16,20},{20,24},{24,28},{1,5},{5,9},{9,... | collective-permute-start | bytes 294920 | tf_op jit(solution)/shard_map/ppermute | solution.py:662
  40.1 39.0 %collective-permute-start.2 = (bf16[6,32,256]{2,1,0:T(8,128)(2,1)S(1)}, bf16[6,32,256]{2,1,0:T(8,128)(2,1)S(1)}, u32[]{:S(2)}, u32[]{:S(2)}) collective-permute-start(bf16[6,32,256]{2,1,0:T(8,128)(2,1)S(1)} %get-tuple-element.23), channel_id=1, source_target_pairs={{0,1},{1,2},{2,3},{4,5},{5,6},{6,7},{8,9},{9,10},{10,11},{12,13},{... | collective-permute-start | bytes 294920 | tf_op jit(solution)/shard_map/ppermute | solution.py:662
  41.4 37.7 %collective-permute-start.3 = (bf16[6,32,256]{2,1,0:T(8,128)(2,1)S(1)}, bf16[6,32,256]{2,1,0:T(8,128)(2,1)S(1)}, u32[]{:S(2)}, u32[]{:S(2)}) collective-permute-start(bf16[6,32,256]{2,1,0:T(8,128)(2,1)S(1)} %get-tuple-element.24), channel_id=1, source_target_pairs={{1,0},{2,1},{3,2},{5,4},{6,5},{7,6},{9,8},{10,9},{11,10},{13,12},{... | collective-permute-start | bytes 294920 | tf_op jit(solution)/shard_map/ppermute | solution.py:662
  42.7 36.4 %collective-permute-start.1 = (bf16[6,32,256]{2,1,0:T(8,128)(2,1)S(1)}, bf16[6,32,256]{2,1,0:T(8,128)(2,1)S(1)}, u32[]{:S(2)}, u32[]{:S(2)}) collective-permute-start(bf16[6,32,256]{2,1,0:T(8,128)(2,1)S(1)} %get-tuple-element.22.edge), channel_id=1, source_target_pairs={{4,0},{8,4},{12,8},{16,12},{20,16},{24,20},{28,24},{5,1},{9,5},{13... | collective-permute-start | bytes 294920 | tf_op jit(solution)/shard_map/ppermute | solution.py:662
  74.9 29.9 %all-to-all-start.2 = ((bf16[8,512,128]{2,1,0:T(8,128)(2,1)}), bf16[8,512,128]{2,1,0:T(8,128)(2,1)}, u32[]{:S(2)}, u32[]{:S(2)}) async-start(bf16[8,512,128]{2,1,0:T(8,128)(2,1)} %shard_map.91.sent.shares), calls=%async_computation.2 | async-start | bytes 2097152 | tf_op jit(solution)/shard_map/all_to_all | solution.py:667
  79.2 1.9 %copy-start.7 = (f32[3,32,32,256]{3,2,1,0:T(8,128)S(1)}, f32[3,32,32,256]{3,2,1,0:T(8,128)}, u32[]{:S(2)}) copy-start(f32[3,32,32,256]{3,2,1,0:T(8,128)} %velocity.3) | copy-start | bytes 9437188
  82.5 2.8 %copy-start.9 = (f32[32,32,256]{2,1,0:T(8,128)}, f32[32,32,256]{2,1,0:T(8,128)S(1)}, u32[]{:S(2)}) copy-start(f32[32,32,256]{2,1,0:T(8,128)S(1)} %shard_map.92.divergence) | copy-start | bytes 3145732
  87.5 24.9 %collective-permute-start.5 = (bf16[6,32,256]{2,1,0:T(8,128)(2,1)S(1)}, bf16[6,32,256]{2,1,0:T(8,128)(2,1)S(1)}, u32[]{:S(2)}, u32[]{:S(2)}) collective-permute-start(bf16[6,32,256]{2,1,0:T(8,128)(2,1)S(1)} %get-tuple-element.29.edge), channel_id=1, source_target_pairs={{4,0},{8,4},{12,8},{16,12},{20,16},{24,20},{28,24},{5,1},{9,5},{13... | collective-permute-start | bytes 294920 | tf_op jit(solution)/shard_map/ppermute | solution.py:662
  88.8 23.6 %collective-permute-start.4 = (bf16[6,32,256]{2,1,0:T(8,128)(2,1)S(1)}, bf16[6,32,256]{2,1,0:T(8,128)(2,1)S(1)}, u32[]{:S(2)}, u32[]{:S(2)}) collective-permute-start(bf16[6,32,256]{2,1,0:T(8,128)(2,1)S(1)} %get-tuple-element.28), channel_id=1, source_target_pairs={{0,4},{4,8},{8,12},{12,16},{16,20},{20,24},{24,28},{1,5},{5,9},{9,... | collective-permute-start | bytes 294920 | tf_op jit(solution)/shard_map/ppermute | solution.py:662
  93.3 19.1 %collective-permute-start.6 = (bf16[6,32,256]{2,1,0:T(8,128)(2,1)S(1)}, bf16[6,32,256]{2,1,0:T(8,128)(2,1)S(1)}, u32[]{:S(2)}, u32[]{:S(2)}) collective-permute-start(bf16[6,32,256]{2,1,0:T(8,128)(2,1)S(1)} %get-tuple-element.30), channel_id=1, source_target_pairs={{0,1},{1,2},{2,3},{4,5},{5,6},{6,7},{8,9},{9,10},{10,11},{12,13},{... | collective-permute-start | bytes 294920 | tf_op jit(solution)/shard_map/ppermute | solution.py:662
  94.6 17.8 %collective-permute-start.7 = (bf16[6,32,256]{2,1,0:T(8,128)(2,1)S(1)}, bf16[6,32,256]{2,1,0:T(8,128)(2,1)S(1)}, u32[]{:S(2)}, u32[]{:S(2)}) collective-permute-start(bf16[6,32,256]{2,1,0:T(8,128)(2,1)S(1)} %get-tuple-element.31), channel_id=1, source_target_pairs={{1,0},{2,1},{3,2},{5,4},{6,5},{7,6},{9,8},{10,9},{11,10},{13,12},{... | collective-permute-start | bytes 294920 | tf_op jit(solution)/shard_map/ppermute | solution.py:662
  104.8 17.1 %all-to-all-start.3 = ((bf16[8,256,128]{2,1,0:T(8,128)(2,1)}), bf16[8,256,128]{2,1,0:T(8,128)(2,1)S(1)}, u32[]{:S(2)}, u32[]{:S(2)}) async-start(bf16[8,256,128]{2,1,0:T(8,128)(2,1)} %shard_map.96), calls=%async_computation.3 | async-start | bytes 1048576 | tf_op jit(solution)/shard_map/all_to_all | solution.py:667
  108.5 4.0 %copy-start.8 = (bf16[32,32,256]{2,1,0:T(8,128)(2,1)S(1)}, bf16[32,32,256]{2,1,0:T(8,128)(2,1)}, u32[]{:S(2)}) copy-start(bf16[32,32,256]{2,1,0:T(8,128)(2,1)} %template.3) | copy-start | bytes 1572868
  108.5 4.0 %copy-start.10 = (f32[32,32,256]{2,1,0:T(8,128)S(1)}, f32[32,32,256]{2,1,0:T(8,128)}, u32[]{:S(2)}) copy-start(f32[32,32,256]{2,1,0:T(8,128)} %copy-done.9) | copy-start | bytes 3145732
  112.4 9.4 %copy-start.1 = (bf16[3,32,256]{2,1,0:T(8,128)(2,1)S(1)}, bf16[3,32,256]{2,1,0:T(8,128)(2,1)}, u32[]{:S(2)}) copy-start(bf16[3,32,256]{2,1,0:T(8,128)(2,1)} %get-tuple-element.33.tables_zero) | copy-start | bytes 147460
  112.5 9.4 %copy-start.2 = (bf16[3,32,256]{2,1,0:T(8,128)(2,1)S(1)}, bf16[3,32,256]{2,1,0:T(8,128)(2,1)}, u32[]{:S(2)}) copy-start(bf16[3,32,256]{2,1,0:T(8,128)(2,1)} %get-tuple-element.32.tables_far) | copy-start | bytes 147460

commit v5 on v4

--- a/solution.py
+++ b/solution.py
@@ -169,6 +169,12 @@
                 for b in range(8):
                     at = b * 32 + part * rows
                     stage[share, b * rows : b * rows + rows, :] = tile[at : at + rows]
+
+
+def send_pieces(stage, send, base, g, sem):
+    count = stage.shape[0] // 4
+    shares = slice(g * count, g * count + count)
+    return fetch(stage.at[shares], send.at[shares, base : base + stage.shape[1], :], sem)
 
 
 def pieces_pair(pieces, kind, g, rows):
@@ -219,11 +225,12 @@
             [field[qh * 8 + qs] for qs in (2 * g, 2 * g + 1) for qh in range(4)], axis=0
         )
         put_pieces(stage, g, mm(identity(), block, NT).astype(BF16), shared // 8)
-    for copy in sent + [fetch(stage, send.at[:, 0:shared, :], sems.at[5])]:
+        sent.append(send_pieces(stage, send, 0, g, sems.at[5 + g]))
+    for copy in sent:
         copy.wait()
 
 
-def first_kernel(picks, operators, field, sent, moved_out, tables, table_mem, field_mem, start, folded, turned, out, tables_mem, sems):
+def first_kernel(picks, operators, field, sent, moved_out, tables, table_mem, field_mem, start, folded, turned, tables_mem, sems):
     loads = [fetch(operators, table_mem, sems.at[0]), fetch(field, field_mem, sems.at[1])]
     chosen = on_lanes([picks[0, 0, 0, b] for b in range(8)])
     loads[0].wait()
@@ -239,21 +246,21 @@
         )
         start[:, g * 256 : g * 256 + 256] = mm(begin, block, NT)
     for g, moved in middle_and_last(start, spread(found[1]), diagonal(found[0]), folded, turned, False):
-        put_pair(out, g, moved)
-    for copy in [kept, fetch(out, moved_out, sems.at[1])]:
-        copy.wait()
+        put_pair(moved_out, g, moved)
+    kept.wait()
 
 
 def second_kernel(route, landing, operators, moved, arrived, *refs):
-    send, tables, codes_out, table_mem, moved_mem, meta_half, meta, codes, start, folded, turned, stage, tables_mem, sems, slot_sems = refs
+    send, tables, codes_out, meta, codes, start, folded, turned, stage, tables_mem, sems, slot_sems = refs
     shared = stage.shape[1]
-    heard = fetch(arrived.at[:, shared : shared + 16, :], meta_half, sems.at[0])
-    loads = [fetch(operators, table_mem, sems.at[1]), fetch(moved, moved_mem, sems.at[2])]
-    heard.wait()
-    meta[...] = meta_half[...].astype(F32)
+    sent = []
+    for b, (place, rank) in enumerate(slot_numbers(route, 0)):
+        rows = pl.ds(pl.multiple_of(rank * 256, 256), 256)
+        sent.append(fetch(moved.at[b], send.at[place, rows, :], slot_sems.at[b]))
+    meta[...] = arrived[:, shared : shared + 16, :].astype(F32)
     for source in range(meta.shape[0]):
         codes[source : source + 1, :] = meta[source, 0:1, :].astype(jnp.int32)
-    told = fetch(codes, codes_out, sems.at[3])
+    sent.append(fetch(codes, codes_out, sems.at[0]))
     lane = iota((1, 128), 1) // 32
     chosen = []
     for part in range(2):
@@ -264,23 +271,17 @@
             row = jnp.where(lane == b, found, row)
         chosen.append(row)
     chosen = jnp.concatenate(chosen, axis=1).astype(jnp.int32)
-    loads[1].wait()
-    sent = []
-    for b, (place, rank) in enumerate(slot_numbers(route, 0)):
-        rows = pl.ds(pl.multiple_of(rank * 256, 256), 256)
-        sent.append(fetch(moved_mem.at[b], send.at[place, rows, :], slot_sems.at[b]))
-    loads[0].wait()
-    found = [table_rows(table_mem, chosen, axis) for axis in range(3)]
+    found = [table_rows(operators, chosen, axis) for axis in range(3)]
     for axis in range(3):
         tables_mem[axis] = found[axis].astype(BF16)
-    kept = fetch(tables_mem, tables, sems.at[5])
+    sent.append(fetch(tables_mem, tables, sems.at[1]))
     begin = diagonal(found[0])
     for g in range(4):
-        start[:, g * 256 : g * 256 + 256] = mm(begin, lane_pair(moved_mem, g))
+        start[:, g * 256 : g * 256 + 256] = mm(begin, lane_pair(moved, g))
     for g, value in middle_and_last(start, spread(found[1]), diagonal(found[2]), folded, turned, False):
         put_pieces(stage, g, value, shared // 8)
-    sent.append(fetch(stage, send.at[:, 512 : 512 + shared, :], sems.at[6]))
-    for copy in sent + [kept, told]:
+        sent.append(send_pieces(stage, send, 512, g, sems.at[2 + g]))
+    for copy in sent:
         copy.wait()
 
 
@@ -696,17 +697,17 @@
 
     moved, tables_zero = call(
         first_kernel,
-        [far(FORM, BF16), far(TABLES, BF16)],
+        [like(FORM, BF16), far(TABLES, BF16)],
         [SCALAR, FAR, FAR, FAR],
-        [FAR] * 2,
-        [listed_mem, pltpu.VMEM(NATIVE, BF16)] + turning + [form, tables, sems],
+        [WHOLE, FAR],
+        [listed_mem, pltpu.VMEM(NATIVE, BF16)] + turning + [tables, sems],
     )(operator_index, listed, template, send)
     send, tables_far, codes = call(
         second_kernel,
         [far((peers, 512 + shared, 128), BF16), far(TABLES, BF16), far((peers, 128), jnp.int32)],
-        [SCALAR, SCALAR, FAR, FAR, ANYWHERE],
+        [SCALAR, SCALAR, WHOLE, WHOLE, WHOLE],
         [FAR] * 3,
-        [listed_mem, form, meta_half, pltpu.VMEM((peers, 16, 128), F32), pltpu.VMEM((peers, 128), jnp.int32)]
+        [pltpu.VMEM((peers, 16, 128), F32), pltpu.VMEM((peers, 128), jnp.int32)]
         + turning
         + [stage, tables, sems, pltpu.SemaphoreType.DMA((8,))],
         SHORT,

time: 128 us -> 126 us (0.984)
  Pallas kernels: 42.8 us -> 41 us
    pallas_call x12, Pallas kernels: 42.8 us -> 41 us  [apply(): made(*[pinned(value, spec) for value, spec in zip(values, in_specs, stric...]
where the time goes in v5:
time: 126 us; the launch traced here: 125 us
  waiting for transfers between devices  45.6 us (36%)
  Pallas kernels  41 us (33%)
  starting transfers between devices  35.1 us (28%)
  local copies, waits for them, and re-layouts  2.6 us (2%)
    all_to_all x4, waiting for transfers between devices, swap_slots(): return lax.all_to_all(send, 'gx', split_axis=0, concat_axis=0, tiled=True)  45.6 us
    pallas_call x12, Pallas kernels, apply(): made(*[pinned(value, spec) for value, spec in zip(values, in_specs, stric...  41 us
    all_to_all x4, starting transfers between devices, swap_slots(): return lax.all_to_all(send, 'gx', split_axis=0, concat_axis=0, tiled=True)  18.9 us
    ppermute x8, starting transfers between devices, neighbours(): moved += [lax.ppermute(high, axis, up), lax.ppermute(low, axis, down)]  16.2 us
    unnamed x22, local copies, waits for them, and re-layouts  2.6 us
  transfers between devices with their start and end apart: 12, of which 4 were waited for; matrix products, arithmetic and copies ran while one was open for 0% of the time, Pallas kernels for 24%

profile of v5, /device:TPU:0, one launch (start us, length us, event | category | flops | bytes accessed | tf_op | source)
XLA Modules:
  0.0 125.4 jit_solution(8381329818923203185)
XLA Ops:
  0.6 2.2 %shard_map.86.sent = bf16[8,272,128]{2,1,0:T(8,128)(2,1)} custom-call(s32[2,1,1,8]{3,2,1,0:T(1,128)} %picks.3, s32[2,1,1,8]{3,2,1,0:T(1,128)} %bitcast.9, s32[2,1,1,8]{3,2,1,0:T(1,128)} %landing.1, bf16[32,32,256]{2,1,0:T(8,128)(2,1)} %target.1), custom_call_target="tpu_custom_call" | custom-call | flops 1048576 | bytes 1048576 | tf_op jit(solution)/shard_map/pallas_call | solution.py:644
  2.9 7.3 %all-to-all-start = ((bf16[8,272,128]{2,1,0:T(8,128)(2,1)}), bf16[8,272,128]{2,1,0:T(8,128)(2,1)S(1)}, u32[]{:S(2)}, u32[]{:S(2)}) async-start(bf16[8,272,128]{2,1,0:T(8,128)(2,1)} %shard_map.86.sent), calls=%async_computation | async-start | bytes 1114112 | tf_op jit(solution)/shard_map/all_to_all | solution.py:668
  10.9 4.5 %shard_map.87 = (bf16[8,256,128]{2,1,0:T(8,128)(2,1)S(1)}, bf16[3,32,256]{2,1,0:T(8,128)(2,1)}) custom-call(s32[2,1,1,8]{3,2,1,0:T(1,128)S(1)} %copy-done.5, bf16[3072,64]{1,0:T(8,128)(2,1)} %bitcast.6, bf16[32,32,256]{2,1,0:T(8,128)(2,1)} %template.3, bf16[8,272,128]{2,1,0:T(8,128)(2,1)} %shard_map.86.sent), custom_call_target="tpu_custom_call" | custom-call | flops 68719476736 | bytes 1048576 | tf_op jit(solution)/shard_map/pallas_call | solution.py:644
  15.4 10.0 %all-to-all-done.arrived.targets = bf16[8,272,128]{2,1,0:T(8,128)(2,1)S(1)} async-done(((bf16[8,272,128]{2,1,0:T(8,128)(2,1)}), bf16[8,272,128]{2,1,0:T(8,128)(2,1)S(1)}, u32[]{:S(2)}, u32[]{:S(2)}) %all-to-all-start) | async-done | bytes 557088 | tf_op jit(solution)/shard_map/all_to_all | solution.py:668
  25.4 3.8 %shard_map.88 = (bf16[8,768,128]{2,1,0:T(8,128)(2,1)}, bf16[3,32,256]{2,1,0:T(8,128)(2,1)}, s32[8,128]{1,0:T(8,128)}) custom-call(s32[2,1,1,8]{3,2,1,0:T(1,128)S(1)} %bitcast.10, s32[2,1,1,8]{3,2,1,0:T(1,128)S(1)} %copy-done.4, bf16[3072,64]{1,0:T(8,128)(2,1)S(1)} %bitcast.7, bf16[8,256,128]{2,1,0:T(8,128)(2,1)S(1)} %get-tuple-element.18.moved, ...), custom_call_target="tpu_custom_call" | custom-call | flops 1048576 | bytes 1048576 | tf_op jit(solution)/shard_map/pallas_call | solution.py:644
  29.1 3.6 %all-to-all-start.1 = ((bf16[8,768,128]{2,1,0:T(8,128)(2,1)}), bf16[8,768,128]{2,1,0:T(8,128)(2,1)S(1)}, u32[]{:S(2)}, u32[]{:S(2)}) async-start(bf16[8,768,128]{2,1,0:T(8,128)(2,1)} %get-tuple-element.20.sent), calls=%async_computation.1 | async-start | bytes 3145728 | tf_op jit(solution)/shard_map/all_to_all | solution.py:668
  32.8 2.5 %shard_map.89 = (bf16[6,32,256]{2,1,0:T(8,128)(2,1)S(1)}, bf16[6,32,256]{2,1,0:T(8,128)(2,1)}, bf16[6,32,256]{2,1,0:T(8,128)(2,1)S(1)}, bf16[6,32,256]{2,1,0:T(8,128)(2,1)}) custom-call(bf16[32,32,256]{2,1,0:T(8,128)(2,1)} %template.3, f32[3,32,32,256]{3,2,1,0:T(8,128)} %velocity.3, bf16[8,768,128]{2,1,0:T(8,128)(2,1)} %get-tuple-element.20.sent), custom_call_target="tpu_custom_call" | custom-call | flops 68719476736 | bytes 1048576 | tf_op jit(solution)/shard_map/pallas_call | solution.py:644
  35.3 3.9 %collective-permute-start = (bf16[6,32,256]{2,1,0:T(8,128)(2,1)}, bf16[6,32,256]{2,1,0:T(8,128)(2,1)S(1)}, u32[]{:S(2)}, u32[]{:S(2)}) collective-permute-start(bf16[6,32,256]{2,1,0:T(8,128)(2,1)} %get-tuple-element.21), channel_id=1, source_target_pairs={{0,4},{4,8},{8,12},{12,16},{16,20},{20,24},{24,28},{1,5},{5,9},{9,... | collective-permute-start | bytes 294920 | tf_op jit(solution)/shard_map/ppermute | solution.py:663
  43.2 3.4 %shard_map.90 = (bf16[3,32,256]{2,1,0:T(8,128)(2,1)}, s32[8,128]{1,0:T(8,128)}) custom-call(s32[2,1,1,8]{3,2,1,0:T(1,128)S(1)} %copy-done.6, s32[8,128]{1,0:T(8,128)} %get-tuple-element.19.codes_in, bf16[3072,64]{1,0:T(8,128)(2,1)S(1)} %bitcast.8, bf16[6,32,256]{2,1,0:T(8,128)(2,1)S(1)} %get-tuple-element.22.edge), custom_call_target="tpu_custom_call" | custom-call | flops 68719476736 | bytes 1048576 | tf_op jit(solution)/shard_map/pallas_call | solution.py:644
  46.6 24.4 %all-to-all-done.1.arrived = bf16[8,768,128]{2,1,0:T(8,128)(2,1)S(1)} async-done(((bf16[8,768,128]{2,1,0:T(8,128)(2,1)}), bf16[8,768,128]{2,1,0:T(8,128)(2,1)S(1)}, u32[]{:S(2)}, u32[]{:S(2)}) %all-to-all-start.1) | async-done | bytes 1572896 | tf_op jit(solution)/shard_map/all_to_all | solution.py:668
  71.0 2.4 %shard_map.91.sent.shares = bf16[8,512,128]{2,1,0:T(8,128)(2,1)} custom-call(s32[8,128]{1,0:T(8,128)} %get-tuple-element.25.plan_in, bf16[8,768,128]{2,1,0:T(8,128)(2,1)S(1)} %all-to-all-done.1.arrived, bf16[8,272,128]{2,1,0:T(8,128)(2,1)S(1)} %all-to-all-done.arrived.targets), custom_call_target="tpu_custom_call" | custom-call | flops 1048576 | bytes 1048576 | tf_op jit(solution)/shard_map/pallas_call | solution.py:644
  73.4 4.3 %all-to-all-start.2 = ((bf16[8,512,128]{2,1,0:T(8,128)(2,1)}), bf16[8,512,128]{2,1,0:T(8,128)(2,1)}, u32[]{:S(2)}, u32[]{:S(2)}) async-start(bf16[8,512,128]{2,1,0:T(8,128)(2,1)} %shard_map.91.sent.shares), calls=%async_computation.2 | async-start | bytes 2097152 | tf_op jit(solution)/shard_map/all_to_all | solution.py:668
  77.7 1.9 %copy-done.7 = f32[3,32,32,256]{3,2,1,0:T(8,128)S(1)} copy-done((f32[3,32,32,256]{3,2,1,0:T(8,128)S(1)}, f32[3,32,32,256]{3,2,1,0:T(8,128)}, u32[]{:S(2)}) %copy-start.7) | copy-done | bytes 3145752
  79.6 1.5 %shard_map.92.divergence = f32[32,32,256]{2,1,0:T(8,128)S(1)} custom-call(f32[3,32,32,256]{3,2,1,0:T(8,128)S(1)} %copy-done.7, bf16[6,32,256]{2,1,0:T(8,128)(2,1)S(1)} %collective-permute-done.before_x.b0x, bf16[6,32,256]{2,1,0:T(8,128)(2,1)S(1)} %collective-permute-done.1.after_x.a0x, bf16[6,32,256]{2,1,0:T(8,128)(2,1)S(1)} %collective-permute-done.2.before_y.b0y, ...), custom_call_target="tpu_custom_call" | custom-call | flops 68719476736 | bytes 1048576 | tf_op jit(solution)/shard_map/pallas_call | solution.py:644
  81.1 2.6 %shard_map.93 = (bf16[32,32,256]{2,1,0:T(8,128)(2,1)S(1)}, bf16[6,32,256]{2,1,0:T(8,128)(2,1)S(1)}, bf16[6,32,256]{2,1,0:T(8,128)(2,1)S(1)}, bf16[6,32,256]{2,1,0:T(8,128)(2,1)S(1)}, bf16[6,32,256]{2,1,0:T(8,128)(2,1)S(1)}) custom-call(s32[8,128]{1,0:T(8,128)} %get-tuple-element.19.codes_in, bf16[8,768,128]{2,1,0:T(8,128)(2,1)S(1)} %all-to-all-done.1.arrived, ...), custom_call_target="tpu_custom_call" | custom-call | flops 68719476736 | bytes 1048576 | tf_op jit(solution)/shard_map/pallas_call | solution.py:644
  83.8 2.2 %shard_map.96 = bf16[8,256,128]{2,1,0:T(8,128)(2,1)} custom-call(s32[8,128]{1,0:T(8,128)} %get-tuple-element.25.plan_in, bf16[8,512,128]{2,1,0:T(8,128)(2,1)} %shard_map.91.sent.shares, bf16[6,32,256]{2,1,0:T(8,128)(2,1)S(1)} %get-tuple-element.29.edge), custom_call_target="tpu_custom_call" | custom-call | flops 68719476736 | bytes 1048576 | tf_op jit(solution)/shard_map/pallas_call | solution.py:644
  87.2 4.6 %collective-permute-start.4 = (bf16[6,32,256]{2,1,0:T(8,128)(2,1)S(1)}, bf16[6,32,256]{2,1,0:T(8,128)(2,1)S(1)}, u32[]{:S(2)}, u32[]{:S(2)}) collective-permute-start(bf16[6,32,256]{2,1,0:T(8,128)(2,1)S(1)} %get-tuple-element.28), channel_id=1, source_target_pairs={{0,4},{4,8},{8,12},{12,16},{16,20},{20,24},{24,28},{1,5},{5,9},{9,... | collective-permute-start | bytes 294920 | tf_op jit(solution)/shard_map/ppermute | solution.py:663
  91.8 1.3 %collective-permute-start.6 = (bf16[6,32,256]{2,1,0:T(8,128)(2,1)S(1)}, bf16[6,32,256]{2,1,0:T(8,128)(2,1)S(1)}, u32[]{:S(2)}, u32[]{:S(2)}) collective-permute-start(bf16[6,32,256]{2,1,0:T(8,128)(2,1)S(1)} %get-tuple-element.30), channel_id=1, source_target_pairs={{0,1},{1,2},{2,3},{4,5},{5,6},{6,7},{8,9},{9,10},{10,11},{12,13},{... | collective-permute-start | bytes 294920 | tf_op jit(solution)/shard_map/ppermute | solution.py:663
  94.4 8.9 %all-to-all-done.2.arrived.adjoint_two = bf16[8,512,128]{2,1,0:T(8,128)(2,1)} async-done(((bf16[8,512,128]{2,1,0:T(8,128)(2,1)}), bf16[8,512,128]{2,1,0:T(8,128)(2,1)}, u32[]{:S(2)}, u32[]{:S(2)}) %all-to-all-start.2) | async-done | bytes 1048608 | tf_op jit(solution)/shard_map/all_to_all | solution.py:668
  103.3 3.7 %all-to-all-start.3 = ((bf16[8,256,128]{2,1,0:T(8,128)(2,1)}), bf16[8,256,128]{2,1,0:T(8,128)(2,1)S(1)}, u32[]{:S(2)}, u32[]{:S(2)}) async-start(bf16[8,256,128]{2,1,0:T(8,128)(2,1)} %shard_map.96), calls=%async_computation.3 | async-start | bytes 1048576 | tf_op jit(solution)/shard_map/all_to_all | solution.py:668
  107.1 3.9 %shard_map.94.adjoint_one = bf16[8,256,128]{2,1,0:T(8,128)(2,1)S(1)} custom-call(bf16[3,32,256]{2,1,0:T(8,128)(2,1)} %get-tuple-element.27.tables_in, bf16[8,512,128]{2,1,0:T(8,128)(2,1)} %all-to-all-done.2.arrived.adjoint_two), custom_call_target="tpu_custom_call" | custom-call | flops 68719476736 | bytes 1048576 | tf_op jit(solution)/shard_map/pallas_call | solution.py:644
  111.0 7.1 %shard_map.95.gradient = f32[3,32,32,256]{3,2,1,0:T(8,128)} custom-call(bf16[32,32,256]{2,1,0:T(8,128)(2,1)S(1)} %copy-done.8, bf16[32,32,256]{2,1,0:T(8,128)(2,1)S(1)} %get-tuple-element.26.state, f32[32,32,256]{2,1,0:T(8,128)S(1)} %copy-done.10, bf16[8,512,128]{2,1,0:T(8,128)(2,1)} %all-to-all-done.2.arrived.adjoint_two, ...), custom_call_target="tpu_custom_call" | custom-call | flops 68719476736 | bytes 1048576 | tf_op jit(solution)/shard_map/pallas_call | solution.py:644
  118.2 2.3 %all-to-all-done.3.arrived = bf16[8,256,128]{2,1,0:T(8,128)(2,1)S(1)} async-done(((bf16[8,256,128]{2,1,0:T(8,128)(2,1)}), bf16[8,256,128]{2,1,0:T(8,128)(2,1)S(1)}, u32[]{:S(2)}, u32[]{:S(2)}) %all-to-all-start.3) | async-done | bytes 524320 | tf_op jit(solution)/shard_map/all_to_all | solution.py:668
  120.4 4.8 %shard_map.97 = bf16[32,32,256]{2,1,0:T(8,128)(2,1)} custom-call(bf16[3,32,256]{2,1,0:T(8,128)(2,1)S(1)} %copy-done.2, bf16[3,32,256]{2,1,0:T(8,128)(2,1)S(1)} %copy-done.1, f32[3,32,32,256]{3,2,1,0:T(8,128)} %shard_map.95.gradient, bf16[8,256,128]{2,1,0:T(8,128)(2,1)S(1)} %all-to-all-done.3.arrived), custom_call_target="tpu_custom_call" | custom-call | flops 1048576 | bytes 1048576 | tf_op jit(solution)/shard_map/pallas_call | solution.py:644
  (34 shorter events, 7.2 us)
Async XLA Ops:
  2.9 22.5 %all-to-all-start = ((bf16[8,272,128]{2,1,0:T(8,128)(2,1)}), bf16[8,272,128]{2,1,0:T(8,128)(2,1)S(1)}, u32[]{:S(2)}, u32[]{:S(2)}) async-start(bf16[8,272,128]{2,1,0:T(8,128)(2,1)} %shard_map.86.sent), calls=%async_computation | async-start | bytes 1114112 | tf_op jit(solution)/shard_map/all_to_all | solution.py:668
  10.2 0.7 copy-start.5
  10.8 14.5 %copy-start = (bf16[64,3,32,32]{0,3,2,1:T(8,128)(2,1)S(1)}, bf16[64,3,32,32]{0,3,2,1:T(8,128)(2,1)}, u32[]{:S(2)}) copy-start(bf16[64,3,32,32]{0,3,2,1:T(8,128)(2,1)} %param.10) | copy-start | bytes 1179652
  10.8 14.5 %copy-start.3 = (s32[2,1,1,8,1]{3,4,2,1,0:T(1,128)S(1)}, s32[2,1,1,8,1]{3,4,2,1,0:T(1,128)}, u32[]{:S(2)}) copy-start(s32[2,1,1,8,1]{3,4,2,1,0:T(1,128)} %param.11) | copy-start | bytes 196
  10.8 14.5 %copy-start.4 = (s32[2,1,1,8]{3,2,1,0:T(1,128)S(1)}, s32[2,1,1,8]{3,2,1,0:T(1,128)}, u32[]{:S(2)}) copy-start(s32[2,1,1,8]{3,2,1,0:T(1,128)} %landing.1) | copy-start | bytes 196
  29.1 41.9 %all-to-all-start.1 = ((bf16[8,768,128]{2,1,0:T(8,128)(2,1)}), bf16[8,768,128]{2,1,0:T(8,128)(2,1)S(1)}, u32[]{:S(2)}, u32[]{:S(2)}) async-start(bf16[8,768,128]{2,1,0:T(8,128)(2,1)} %get-tuple-element.20.sent), calls=%async_computation.1 | async-start | bytes 3145728 | tf_op jit(solution)/shard_map/all_to_all | solution.py:668
  32.8 10.4 %copy-start.6 = (s32[2,1,1,8]{3,2,1,0:T(1,128)S(1)}, s32[2,1,1,8]{3,2,1,0:T(1,128)}, u32[]{:S(2)}) copy-start(s32[2,1,1,8]{3,2,1,0:T(1,128)} %picks.3) | copy-start | bytes 196
  35.3 42.4 %collective-permute-start = (bf16[6,32,256]{2,1,0:T(8,128)(2,1)}, bf16[6,32,256]{2,1,0:T(8,128)(2,1)S(1)}, u32[]{:S(2)}, u32[]{:S(2)}) collective-permute-start(bf16[6,32,256]{2,1,0:T(8,128)(2,1)} %get-tuple-element.21), channel_id=1, source_target_pairs={{0,4},{4,8},{8,12},{12,16},{16,20},{20,24},{24,28},{1,5},{5,9},{9,... | collective-permute-start | bytes 294920 | tf_op jit(solution)/shard_map/ppermute | solution.py:663
  39.2 38.5 %collective-permute-start.2 = (bf16[6,32,256]{2,1,0:T(8,128)(2,1)}, bf16[6,32,256]{2,1,0:T(8,128)(2,1)S(1)}, u32[]{:S(2)}, u32[]{:S(2)}) collective-permute-start(bf16[6,32,256]{2,1,0:T(8,128)(2,1)} %get-tuple-element.23), channel_id=1, source_target_pairs={{0,1},{1,2},{2,3},{4,5},{5,6},{6,7},{8,9},{9,10},{10,11},{12,13},{... | collective-permute-start | bytes 294920 | tf_op jit(solution)/shard_map/ppermute | solution.py:663
  40.5 37.2 %collective-permute-start.3 = (bf16[6,32,256]{2,1,0:T(8,128)(2,1)S(1)}, bf16[6,32,256]{2,1,0:T(8,128)(2,1)S(1)}, u32[]{:S(2)}, u32[]{:S(2)}) collective-permute-start(bf16[6,32,256]{2,1,0:T(8,128)(2,1)S(1)} %get-tuple-element.24), channel_id=1, source_target_pairs={{1,0},{2,1},{3,2},{5,4},{6,5},{7,6},{9,8},{10,9},{11,10},{13,12},{... | collective-permute-start | bytes 294920 | tf_op jit(solution)/shard_map/ppermute | solution.py:663
  41.8 35.9 %collective-permute-start.1 = (bf16[6,32,256]{2,1,0:T(8,128)(2,1)S(1)}, bf16[6,32,256]{2,1,0:T(8,128)(2,1)S(1)}, u32[]{:S(2)}, u32[]{:S(2)}) collective-permute-start(bf16[6,32,256]{2,1,0:T(8,128)(2,1)S(1)} %get-tuple-element.22.edge), channel_id=1, source_target_pairs={{4,0},{8,4},{12,8},{16,12},{20,16},{24,20},{28,24},{5,1},{9,5},{13... | collective-permute-start | bytes 294920 | tf_op jit(solution)/shard_map/ppermute | solution.py:663
  73.4 29.9 %all-to-all-start.2 = ((bf16[8,512,128]{2,1,0:T(8,128)(2,1)}), bf16[8,512,128]{2,1,0:T(8,128)(2,1)}, u32[]{:S(2)}, u32[]{:S(2)}) async-start(bf16[8,512,128]{2,1,0:T(8,128)(2,1)} %shard_map.91.sent.shares), calls=%async_computation.2 | async-start | bytes 2097152 | tf_op jit(solution)/shard_map/all_to_all | solution.py:668
  77.7 1.9 %copy-start.7 = (f32[3,32,32,256]{3,2,1,0:T(8,128)S(1)}, f32[3,32,32,256]{3,2,1,0:T(8,128)}, u32[]{:S(2)}) copy-start(f32[3,32,32,256]{3,2,1,0:T(8,128)} %velocity.3) | copy-start | bytes 9437188
  81.1 2.7 %copy-start.9 = (f32[32,32,256]{2,1,0:T(8,128)}, f32[32,32,256]{2,1,0:T(8,128)S(1)}, u32[]{:S(2)}) copy-start(f32[32,32,256]{2,1,0:T(8,128)S(1)} %shard_map.92.divergence) | copy-start | bytes 3145732
  85.9 25.0 %collective-permute-start.5 = (bf16[6,32,256]{2,1,0:T(8,128)(2,1)S(1)}, bf16[6,32,256]{2,1,0:T(8,128)(2,1)S(1)}, u32[]{:S(2)}, u32[]{:S(2)}) collective-permute-start(bf16[6,32,256]{2,1,0:T(8,128)(2,1)S(1)} %get-tuple-element.29.edge), channel_id=1, source_target_pairs={{4,0},{8,4},{12,8},{16,12},{20,16},{24,20},{28,24},{5,1},{9,5},{13... | collective-permute-start | bytes 294920 | tf_op jit(solution)/shard_map/ppermute | solution.py:663
  87.2 23.7 %collective-permute-start.4 = (bf16[6,32,256]{2,1,0:T(8,128)(2,1)S(1)}, bf16[6,32,256]{2,1,0:T(8,128)(2,1)S(1)}, u32[]{:S(2)}, u32[]{:S(2)}) collective-permute-start(bf16[6,32,256]{2,1,0:T(8,128)(2,1)S(1)} %get-tuple-element.28), channel_id=1, source_target_pairs={{0,4},{4,8},{8,12},{12,16},{16,20},{20,24},{24,28},{1,5},{5,9},{9,... | collective-permute-start | bytes 294920 | tf_op jit(solution)/shard_map/ppermute | solution.py:663
  91.8 19.2 %collective-permute-start.6 = (bf16[6,32,256]{2,1,0:T(8,128)(2,1)S(1)}, bf16[6,32,256]{2,1,0:T(8,128)(2,1)S(1)}, u32[]{:S(2)}, u32[]{:S(2)}) collective-permute-start(bf16[6,32,256]{2,1,0:T(8,128)(2,1)S(1)} %get-tuple-element.30), channel_id=1, source_target_pairs={{0,1},{1,2},{2,3},{4,5},{5,6},{6,7},{8,9},{9,10},{10,11},{12,13},{... | collective-permute-start | bytes 294920 | tf_op jit(solution)/shard_map/ppermute | solution.py:663
  93.1 17.9 %collective-permute-start.7 = (bf16[6,32,256]{2,1,0:T(8,128)(2,1)S(1)}, bf16[6,32,256]{2,1,0:T(8,128)(2,1)S(1)}, u32[]{:S(2)}, u32[]{:S(2)}) collective-permute-start(bf16[6,32,256]{2,1,0:T(8,128)(2,1)S(1)} %get-tuple-element.31), channel_id=1, source_target_pairs={{1,0},{2,1},{3,2},{5,4},{6,5},{7,6},{9,8},{10,9},{11,10},{13,12},{... | collective-permute-start | bytes 294920 | tf_op jit(solution)/shard_map/ppermute | solution.py:663
  103.3 17.1 %all-to-all-start.3 = ((bf16[8,256,128]{2,1,0:T(8,128)(2,1)}), bf16[8,256,128]{2,1,0:T(8,128)(2,1)S(1)}, u32[]{:S(2)}, u32[]{:S(2)}) async-start(bf16[8,256,128]{2,1,0:T(8,128)(2,1)} %shard_map.96), calls=%async_computation.3 | async-start | bytes 1048576 | tf_op jit(solution)/shard_map/all_to_all | solution.py:668
  107.0 4.0 %copy-start.8 = (bf16[32,32,256]{2,1,0:T(8,128)(2,1)S(1)}, bf16[32,32,256]{2,1,0:T(8,128)(2,1)}, u32[]{:S(2)}) copy-start(bf16[32,32,256]{2,1,0:T(8,128)(2,1)} %template.3) | copy-start | bytes 1572868
  107.0 4.0 %copy-start.10 = (f32[32,32,256]{2,1,0:T(8,128)S(1)}, f32[32,32,256]{2,1,0:T(8,128)}, u32[]{:S(2)}) copy-start(f32[32,32,256]{2,1,0:T(8,128)} %copy-done.9) | copy-start | bytes 3145732
  111.0 9.4 %copy-start.1 = (bf16[3,32,256]{2,1,0:T(8,128)(2,1)S(1)}, bf16[3,32,256]{2,1,0:T(8,128)(2,1)}, u32[]{:S(2)}) copy-start(bf16[3,32,256]{2,1,0:T(8,128)(2,1)} %get-tuple-element.33.tables_zero) | copy-start | bytes 147460
  111.0 9.4 %copy-start.2 = (bf16[3,32,256]{2,1,0:T(8,128)(2,1)S(1)}, bf16[3,32,256]{2,1,0:T(8,128)(2,1)}, u32[]{:S(2)}) copy-start(bf16[3,32,256]{2,1,0:T(8,128)(2,1)} %get-tuple-element.32.tables_far) | copy-start | bytes 147460

commit v6 on v5

--- a/solution.py
+++ b/solution.py
@@ -14,6 +14,7 @@
 BF16 = jnp.bfloat16
 NT = (((1,), (1,)), ((), ()))
 NN = (((1,), (0,)), ((), ()))
+TN = (((0,), (0,)), ((), ()))
 TAPS = ((1, 0.75), (2, -0.15), (3, 1.0 / 60.0))
 
 
@@ -125,7 +126,7 @@
             field[b, rows, :] = value[b * 32 : b * 32 + 32, half * 128 : half * 128 + 128]
 
 
-def middle_and_last(start, spread_mid, last, folded, turned, flipped):
+def middle(start, spread_mid, folded, turned, flipped):
     mask = same_block(256, 32)
     for brick in range(8):
         rows = spread_mid[brick * 32 : brick * 32 + 32]
@@ -135,6 +136,10 @@
         high, low = halves(block)
         both = mm(jnp.concatenate([high, low], axis=0), line, NT if flipped else NN)
         swap_brick(both[:128] + both[128:], folded, turned, brick)
+
+
+def middle_and_last(start, spread_mid, last, folded, turned, flipped):
+    middle(start, spread_mid, folded, turned, flipped)
     last = jnp.concatenate([last, last], axis=1)
     for g in range(4):
         yield g, mm(last, turned[:, g * 256 : g * 256 + 256]).astype(BF16)
@@ -359,12 +364,16 @@
         put_pair(later, g, moved)
     begin = flipped_diagonal(tables_zero[0].astype(F32))
     mid = spread(tables_zero[1].astype(F32))
-    end = flipped_diagonal(tables_zero[2].astype(F32))
+    end = diagonal(tables_zero[2].astype(F32))
+    end = jnp.concatenate([end, end], axis=0)
     for g in range(4):
         start[:, g * 256 : g * 256 + 256] = mm(begin, lane_pair(later, g))
     stored = []
-    for g, moved in middle_and_last(start, mid, end, folded, turned, True):
-        to_native(moved, g, field)
+    middle(start, mid, folded, turned, True)
+    for g in range(4):
+        flat = mm(turned[:, g * 256 : g * 256 + 256], end, TN).astype(BF16)
+        for index in range(8):
+            field[(index % 4) * 8 + 2 * g + index // 4] = flat[index * 32 : index * 32 + 32]
         for qh in range(4):
             at = slice(qh * 8 + 2 * g, qh * 8 + 2 * g + 2)
             stored.append(fetch(field.at[at], adjoint.at[at], quarter_sems.at[g, qh]))

time: 126 us -> 125 us (level)
  no operation moved by 1% of the time
where the time goes in v6:
time: 125 us
  waiting for transfers between devices  45.6 us (36%)
  Pallas kernels  40.2 us (32%)
  starting transfers between devices  35.1 us (28%)
  local copies, waits for them, and re-layouts  2.6 us (2%)
    all_to_all x4, waiting for transfers between devices, swap_slots(): return lax.all_to_all(send, 'gx', split_axis=0, concat_axis=0, tiled=True)  45.6 us
    pallas_call x12, Pallas kernels, apply(): made(*[pinned(value, spec) for value, spec in zip(values, in_specs, stric...  40.2 us
    all_to_all x4, starting transfers between devices, swap_slots(): return lax.all_to_all(send, 'gx', split_axis=0, concat_axis=0, tiled=True)  18.9 us
    ppermute x8, starting transfers between devices, neighbours(): moved += [lax.ppermute(high, axis, up), lax.ppermute(low, axis, down)]  16.2 us
    unnamed x22, local copies, waits for them, and re-layouts  2.6 us
  transfers between devices with their start and end apart: 12, of which 4 were waited for; matrix products, arithmetic and copies ran while one was open for 0% of the time, Pallas kernels for 24%

profile of v6, /device:TPU:0, one launch (start us, length us, event | category | flops | bytes accessed | tf_op | source)
XLA Modules:
  0.0 124.6 jit_solution(11639092939782615540)
XLA Ops:
  0.6 2.2 %shard_map.86.sent = bf16[8,272,128]{2,1,0:T(8,128)(2,1)} custom-call(s32[2,1,1,8]{3,2,1,0:T(1,128)} %picks.3, s32[2,1,1,8]{3,2,1,0:T(1,128)} %bitcast.9, s32[2,1,1,8]{3,2,1,0:T(1,128)} %landing.1, bf16[32,32,256]{2,1,0:T(8,128)(2,1)} %target.1), custom_call_target="tpu_custom_call" | custom-call | flops 1048576 | bytes 1048576 | tf_op jit(solution)/shard_map/pallas_call | solution.py:653
  2.9 7.3 %all-to-all-start = ((bf16[8,272,128]{2,1,0:T(8,128)(2,1)}), bf16[8,272,128]{2,1,0:T(8,128)(2,1)S(1)}, u32[]{:S(2)}, u32[]{:S(2)}) async-start(bf16[8,272,128]{2,1,0:T(8,128)(2,1)} %shard_map.86.sent), calls=%async_computation | async-start | bytes 1114112 | tf_op jit(solution)/shard_map/all_to_all | solution.py:677
  10.9 4.5 %shard_map.87 = (bf16[8,256,128]{2,1,0:T(8,128)(2,1)S(1)}, bf16[3,32,256]{2,1,0:T(8,128)(2,1)}) custom-call(s32[2,1,1,8]{3,2,1,0:T(1,128)S(1)} %copy-done.5, bf16[3072,64]{1,0:T(8,128)(2,1)} %bitcast.6, bf16[32,32,256]{2,1,0:T(8,128)(2,1)} %template.3, bf16[8,272,128]{2,1,0:T(8,128)(2,1)} %shard_map.86.sent), custom_call_target="tpu_custom_call" | custom-call | flops 68719476736 | bytes 1048576 | tf_op jit(solution)/shard_map/pallas_call | solution.py:653
  15.4 10.0 %all-to-all-done.arrived.targets = bf16[8,272,128]{2,1,0:T(8,128)(2,1)S(1)} async-done(((bf16[8,272,128]{2,1,0:T(8,128)(2,1)}), bf16[8,272,128]{2,1,0:T(8,128)(2,1)S(1)}, u32[]{:S(2)}, u32[]{:S(2)}) %all-to-all-start) | async-done | bytes 557088 | tf_op jit(solution)/shard_map/all_to_all | solution.py:677
  25.4 3.8 %shard_map.88 = (bf16[8,768,128]{2,1,0:T(8,128)(2,1)}, bf16[3,32,256]{2,1,0:T(8,128)(2,1)}, s32[8,128]{1,0:T(8,128)}) custom-call(s32[2,1,1,8]{3,2,1,0:T(1,128)S(1)} %bitcast.10, s32[2,1,1,8]{3,2,1,0:T(1,128)S(1)} %copy-done.4, bf16[3072,64]{1,0:T(8,128)(2,1)S(1)} %bitcast.7, bf16[8,256,128]{2,1,0:T(8,128)(2,1)S(1)} %get-tuple-element.18.moved, ...), custom_call_target="tpu_custom_call" | custom-call | flops 1048576 | bytes 1048576 | tf_op jit(solution)/shard_map/pallas_call | solution.py:653
  29.1 3.6 %all-to-all-start.1 = ((bf16[8,768,128]{2,1,0:T(8,128)(2,1)}), bf16[8,768,128]{2,1,0:T(8,128)(2,1)S(1)}, u32[]{:S(2)}, u32[]{:S(2)}) async-start(bf16[8,768,128]{2,1,0:T(8,128)(2,1)} %get-tuple-element.20.sent), calls=%async_computation.1 | async-start | bytes 3145728 | tf_op jit(solution)/shard_map/all_to_all | solution.py:677
  32.8 2.5 %shard_map.89 = (bf16[6,32,256]{2,1,0:T(8,128)(2,1)S(1)}, bf16[6,32,256]{2,1,0:T(8,128)(2,1)}, bf16[6,32,256]{2,1,0:T(8,128)(2,1)S(1)}, bf16[6,32,256]{2,1,0:T(8,128)(2,1)}) custom-call(bf16[32,32,256]{2,1,0:T(8,128)(2,1)} %template.3, f32[3,32,32,256]{3,2,1,0:T(8,128)} %velocity.3, bf16[8,768,128]{2,1,0:T(8,128)(2,1)} %get-tuple-element.20.sent), custom_call_target="tpu_custom_call" | custom-call | flops 68719476736 | bytes 1048576 | tf_op jit(solution)/shard_map/pallas_call | solution.py:653
  35.3 3.9 %collective-permute-start = (bf16[6,32,256]{2,1,0:T(8,128)(2,1)}, bf16[6,32,256]{2,1,0:T(8,128)(2,1)S(1)}, u32[]{:S(2)}, u32[]{:S(2)}) collective-permute-start(bf16[6,32,256]{2,1,0:T(8,128)(2,1)} %get-tuple-element.21), channel_id=1, source_target_pairs={{0,4},{4,8},{8,12},{12,16},{16,20},{20,24},{24,28},{1,5},{5,9},{9,... | collective-permute-start | bytes 294920 | tf_op jit(solution)/shard_map/ppermute | solution.py:672
  43.2 3.4 %shard_map.90 = (bf16[3,32,256]{2,1,0:T(8,128)(2,1)}, s32[8,128]{1,0:T(8,128)}) custom-call(s32[2,1,1,8]{3,2,1,0:T(1,128)S(1)} %copy-done.6, s32[8,128]{1,0:T(8,128)} %get-tuple-element.19.codes_in, bf16[3072,64]{1,0:T(8,128)(2,1)S(1)} %bitcast.8, bf16[6,32,256]{2,1,0:T(8,128)(2,1)S(1)} %get-tuple-element.22.edge), custom_call_target="tpu_custom_call" | custom-call | flops 68719476736 | bytes 1048576 | tf_op jit(solution)/shard_map/pallas_call | solution.py:653
  46.6 24.4 %all-to-all-done.1.arrived = bf16[8,768,128]{2,1,0:T(8,128)(2,1)S(1)} async-done(((bf16[8,768,128]{2,1,0:T(8,128)(2,1)}), bf16[8,768,128]{2,1,0:T(8,128)(2,1)S(1)}, u32[]{:S(2)}, u32[]{:S(2)}) %all-to-all-start.1) | async-done | bytes 1572896 | tf_op jit(solution)/shard_map/all_to_all | solution.py:677
  71.0 2.4 %shard_map.91.sent.shares = bf16[8,512,128]{2,1,0:T(8,128)(2,1)} custom-call(s32[8,128]{1,0:T(8,128)} %get-tuple-element.25.plan_in, bf16[8,768,128]{2,1,0:T(8,128)(2,1)S(1)} %all-to-all-done.1.arrived, bf16[8,272,128]{2,1,0:T(8,128)(2,1)S(1)} %all-to-all-done.arrived.targets), custom_call_target="tpu_custom_call" | custom-call | flops 1048576 | bytes 1048576 | tf_op jit(solution)/shard_map/pallas_call | solution.py:653
  73.4 4.3 %all-to-all-start.2 = ((bf16[8,512,128]{2,1,0:T(8,128)(2,1)}), bf16[8,512,128]{2,1,0:T(8,128)(2,1)}, u32[]{:S(2)}, u32[]{:S(2)}) async-start(bf16[8,512,128]{2,1,0:T(8,128)(2,1)} %shard_map.91.sent.shares), calls=%async_computation.2 | async-start | bytes 2097152 | tf_op jit(solution)/shard_map/all_to_all | solution.py:677
  77.7 1.9 %copy-done.7 = f32[3,32,32,256]{3,2,1,0:T(8,128)S(1)} copy-done((f32[3,32,32,256]{3,2,1,0:T(8,128)S(1)}, f32[3,32,32,256]{3,2,1,0:T(8,128)}, u32[]{:S(2)}) %copy-start.7) | copy-done | bytes 3145752
  79.6 1.5 %shard_map.92.divergence = f32[32,32,256]{2,1,0:T(8,128)S(1)} custom-call(f32[3,32,32,256]{3,2,1,0:T(8,128)S(1)} %copy-done.7, bf16[6,32,256]{2,1,0:T(8,128)(2,1)S(1)} %collective-permute-done.before_x.b0x, bf16[6,32,256]{2,1,0:T(8,128)(2,1)S(1)} %collective-permute-done.1.after_x.a0x, bf16[6,32,256]{2,1,0:T(8,128)(2,1)S(1)} %collective-permute-done.2.before_y.b0y, ...), custom_call_target="tpu_custom_call" | custom-call | flops 68719476736 | bytes 1048576 | tf_op jit(solution)/shard_map/pallas_call | solution.py:653
  81.1 2.6 %shard_map.93 = (bf16[32,32,256]{2,1,0:T(8,128)(2,1)S(1)}, bf16[6,32,256]{2,1,0:T(8,128)(2,1)S(1)}, bf16[6,32,256]{2,1,0:T(8,128)(2,1)S(1)}, bf16[6,32,256]{2,1,0:T(8,128)(2,1)S(1)}, bf16[6,32,256]{2,1,0:T(8,128)(2,1)S(1)}) custom-call(s32[8,128]{1,0:T(8,128)} %get-tuple-element.19.codes_in, bf16[8,768,128]{2,1,0:T(8,128)(2,1)S(1)} %all-to-all-done.1.arrived, ...), custom_call_target="tpu_custom_call" | custom-call | flops 68719476736 | bytes 1048576 | tf_op jit(solution)/shard_map/pallas_call | solution.py:653
  83.8 2.2 %shard_map.96 = bf16[8,256,128]{2,1,0:T(8,128)(2,1)} custom-call(s32[8,128]{1,0:T(8,128)} %get-tuple-element.25.plan_in, bf16[8,512,128]{2,1,0:T(8,128)(2,1)} %shard_map.91.sent.shares, bf16[6,32,256]{2,1,0:T(8,128)(2,1)S(1)} %get-tuple-element.29.edge), custom_call_target="tpu_custom_call" | custom-call | flops 68719476736 | bytes 1048576 | tf_op jit(solution)/shard_map/pallas_call | solution.py:653
  87.2 4.6 %collective-permute-start.4 = (bf16[6,32,256]{2,1,0:T(8,128)(2,1)S(1)}, bf16[6,32,256]{2,1,0:T(8,128)(2,1)S(1)}, u32[]{:S(2)}, u32[]{:S(2)}) collective-permute-start(bf16[6,32,256]{2,1,0:T(8,128)(2,1)S(1)} %get-tuple-element.28), channel_id=1, source_target_pairs={{0,4},{4,8},{8,12},{12,16},{16,20},{20,24},{24,28},{1,5},{5,9},{9,... | collective-permute-start | bytes 294920 | tf_op jit(solution)/shard_map/ppermute | solution.py:672
  91.8 1.3 %collective-permute-start.6 = (bf16[6,32,256]{2,1,0:T(8,128)(2,1)S(1)}, bf16[6,32,256]{2,1,0:T(8,128)(2,1)S(1)}, u32[]{:S(2)}, u32[]{:S(2)}) collective-permute-start(bf16[6,32,256]{2,1,0:T(8,128)(2,1)S(1)} %get-tuple-element.30), channel_id=1, source_target_pairs={{0,1},{1,2},{2,3},{4,5},{5,6},{6,7},{8,9},{9,10},{10,11},{12,13},{... | collective-permute-start | bytes 294920 | tf_op jit(solution)/shard_map/ppermute | solution.py:672
  94.4 8.9 %all-to-all-done.2.arrived.adjoint_two = bf16[8,512,128]{2,1,0:T(8,128)(2,1)} async-done(((bf16[8,512,128]{2,1,0:T(8,128)(2,1)}), bf16[8,512,128]{2,1,0:T(8,128)(2,1)}, u32[]{:S(2)}, u32[]{:S(2)}) %all-to-all-start.2) | async-done | bytes 1048608 | tf_op jit(solution)/shard_map/all_to_all | solution.py:677
  103.3 3.7 %all-to-all-start.3 = ((bf16[8,256,128]{2,1,0:T(8,128)(2,1)}), bf16[8,256,128]{2,1,0:T(8,128)(2,1)S(1)}, u32[]{:S(2)}, u32[]{:S(2)}) async-start(bf16[8,256,128]{2,1,0:T(8,128)(2,1)} %shard_map.96), calls=%async_computation.3 | async-start | bytes 1048576 | tf_op jit(solution)/shard_map/all_to_all | solution.py:677
  107.0 3.9 %shard_map.94.adjoint_one = bf16[8,256,128]{2,1,0:T(8,128)(2,1)S(1)} custom-call(bf16[3,32,256]{2,1,0:T(8,128)(2,1)} %get-tuple-element.27.tables_in, bf16[8,512,128]{2,1,0:T(8,128)(2,1)} %all-to-all-done.2.arrived.adjoint_two), custom_call_target="tpu_custom_call" | custom-call | flops 68719476736 | bytes 1048576 | tf_op jit(solution)/shard_map/pallas_call | solution.py:653
  111.0 7.1 %shard_map.95.gradient = f32[3,32,32,256]{3,2,1,0:T(8,128)} custom-call(bf16[32,32,256]{2,1,0:T(8,128)(2,1)S(1)} %copy-done.8, bf16[32,32,256]{2,1,0:T(8,128)(2,1)S(1)} %get-tuple-element.26.state, f32[32,32,256]{2,1,0:T(8,128)S(1)} %copy-done.10, bf16[8,512,128]{2,1,0:T(8,128)(2,1)} %all-to-all-done.2.arrived.adjoint_two, ...), custom_call_target="tpu_custom_call" | custom-call | flops 68719476736 | bytes 1048576 | tf_op jit(solution)/shard_map/pallas_call | solution.py:653
  118.2 2.3 %all-to-all-done.3.arrived = bf16[8,256,128]{2,1,0:T(8,128)(2,1)S(1)} async-done(((bf16[8,256,128]{2,1,0:T(8,128)(2,1)}), bf16[8,256,128]{2,1,0:T(8,128)(2,1)S(1)}, u32[]{:S(2)}, u32[]{:S(2)}) %all-to-all-start.3) | async-done | bytes 524320 | tf_op jit(solution)/shard_map/all_to_all | solution.py:677
  120.4 4.0 %shard_map.97 = bf16[32,32,256]{2,1,0:T(8,128)(2,1)} custom-call(bf16[3,32,256]{2,1,0:T(8,128)(2,1)S(1)} %copy-done.2, bf16[3,32,256]{2,1,0:T(8,128)(2,1)S(1)} %copy-done.1, f32[3,32,32,256]{3,2,1,0:T(8,128)} %shard_map.95.gradient, bf16[8,256,128]{2,1,0:T(8,128)(2,1)S(1)} %all-to-all-done.3.arrived), custom_call_target="tpu_custom_call" | custom-call | flops 1048576 | bytes 1048576 | tf_op jit(solution)/shard_map/pallas_call | solution.py:653
  (34 shorter events, 7.2 us)
Async XLA Ops:
  2.9 22.5 %all-to-all-start = ((bf16[8,272,128]{2,1,0:T(8,128)(2,1)}), bf16[8,272,128]{2,1,0:T(8,128)(2,1)S(1)}, u32[]{:S(2)}, u32[]{:S(2)}) async-start(bf16[8,272,128]{2,1,0:T(8,128)(2,1)} %shard_map.86.sent), calls=%async_computation | async-start | bytes 1114112 | tf_op jit(solution)/shard_map/all_to_all | solution.py:677
  10.2 0.7 copy-start.5
  10.8 14.5 %copy-start = (bf16[64,3,32,32]{0,3,2,1:T(8,128)(2,1)S(1)}, bf16[64,3,32,32]{0,3,2,1:T(8,128)(2,1)}, u32[]{:S(2)}) copy-start(bf16[64,3,32,32]{0,3,2,1:T(8,128)(2,1)} %param.10) | copy-start | bytes 1179652
  10.8 14.5 %copy-start.3 = (s32[2,1,1,8,1]{3,4,2,1,0:T(1,128)S(1)}, s32[2,1,1,8,1]{3,4,2,1,0:T(1,128)}, u32[]{:S(2)}) copy-start(s32[2,1,1,8,1]{3,4,2,1,0:T(1,128)} %param.11) | copy-start | bytes 196
  10.8 14.5 %copy-start.4 = (s32[2,1,1,8]{3,2,1,0:T(1,128)S(1)}, s32[2,1,1,8]{3,2,1,0:T(1,128)}, u32[]{:S(2)}) copy-start(s32[2,1,1,8]{3,2,1,0:T(1,128)} %landing.1) | copy-start | bytes 196
  29.1 41.9 %all-to-all-start.1 = ((bf16[8,768,128]{2,1,0:T(8,128)(2,1)}), bf16[8,768,128]{2,1,0:T(8,128)(2,1)S(1)}, u32[]{:S(2)}, u32[]{:S(2)}) async-start(bf16[8,768,128]{2,1,0:T(8,128)(2,1)} %get-tuple-element.20.sent), calls=%async_computation.1 | async-start | bytes 3145728 | tf_op jit(solution)/shard_map/all_to_all | solution.py:677
  32.8 10.4 %copy-start.6 = (s32[2,1,1,8]{3,2,1,0:T(1,128)S(1)}, s32[2,1,1,8]{3,2,1,0:T(1,128)}, u32[]{:S(2)}) copy-start(s32[2,1,1,8]{3,2,1,0:T(1,128)} %picks.3) | copy-start | bytes 196
  35.3 42.4 %collective-permute-start = (bf16[6,32,256]{2,1,0:T(8,128)(2,1)}, bf16[6,32,256]{2,1,0:T(8,128)(2,1)S(1)}, u32[]{:S(2)}, u32[]{:S(2)}) collective-permute-start(bf16[6,32,256]{2,1,0:T(8,128)(2,1)} %get-tuple-element.21), channel_id=1, source_target_pairs={{0,4},{4,8},{8,12},{12,16},{16,20},{20,24},{24,28},{1,5},{5,9},{9,... | collective-permute-start | bytes 294920 | tf_op jit(solution)/shard_map/ppermute | solution.py:672
  39.3 38.4 %collective-permute-start.2 = (bf16[6,32,256]{2,1,0:T(8,128)(2,1)}, bf16[6,32,256]{2,1,0:T(8,128)(2,1)S(1)}, u32[]{:S(2)}, u32[]{:S(2)}) collective-permute-start(bf16[6,32,256]{2,1,0:T(8,128)(2,1)} %get-tuple-element.23), channel_id=1, source_target_pairs={{0,1},{1,2},{2,3},{4,5},{5,6},{6,7},{8,9},{9,10},{10,11},{12,13},{... | collective-permute-start | bytes 294920 | tf_op jit(solution)/shard_map/ppermute | solution.py:672
  40.6 37.2 %collective-permute-start.3 = (bf16[6,32,256]{2,1,0:T(8,128)(2,1)S(1)}, bf16[6,32,256]{2,1,0:T(8,128)(2,1)S(1)}, u32[]{:S(2)}, u32[]{:S(2)}) collective-permute-start(bf16[6,32,256]{2,1,0:T(8,128)(2,1)S(1)} %get-tuple-element.24), channel_id=1, source_target_pairs={{1,0},{2,1},{3,2},{5,4},{6,5},{7,6},{9,8},{10,9},{11,10},{13,12},{... | collective-permute-start | bytes 294920 | tf_op jit(solution)/shard_map/ppermute | solution.py:672
  41.9 35.9 %collective-permute-start.1 = (bf16[6,32,256]{2,1,0:T(8,128)(2,1)S(1)}, bf16[6,32,256]{2,1,0:T(8,128)(2,1)S(1)}, u32[]{:S(2)}, u32[]{:S(2)}) collective-permute-start(bf16[6,32,256]{2,1,0:T(8,128)(2,1)S(1)} %get-tuple-element.22.edge), channel_id=1, source_target_pairs={{4,0},{8,4},{12,8},{16,12},{20,16},{24,20},{28,24},{5,1},{9,5},{13... | collective-permute-start | bytes 294920 | tf_op jit(solution)/shard_map/ppermute | solution.py:672
  73.4 29.9 %all-to-all-start.2 = ((bf16[8,512,128]{2,1,0:T(8,128)(2,1)}), bf16[8,512,128]{2,1,0:T(8,128)(2,1)}, u32[]{:S(2)}, u32[]{:S(2)}) async-start(bf16[8,512,128]{2,1,0:T(8,128)(2,1)} %shard_map.91.sent.shares), calls=%async_computation.2 | async-start | bytes 2097152 | tf_op jit(solution)/shard_map/all_to_all | solution.py:677
  77.7 1.9 %copy-start.7 = (f32[3,32,32,256]{3,2,1,0:T(8,128)S(1)}, f32[3,32,32,256]{3,2,1,0:T(8,128)}, u32[]{:S(2)}) copy-start(f32[3,32,32,256]{3,2,1,0:T(8,128)} %velocity.3) | copy-start | bytes 9437188
  81.1 2.7 %copy-start.9 = (f32[32,32,256]{2,1,0:T(8,128)}, f32[32,32,256]{2,1,0:T(8,128)S(1)}, u32[]{:S(2)}) copy-start(f32[32,32,256]{2,1,0:T(8,128)S(1)} %shard_map.92.divergence) | copy-start | bytes 3145732
  85.9 25.0 %collective-permute-start.5 = (bf16[6,32,256]{2,1,0:T(8,128)(2,1)S(1)}, bf16[6,32,256]{2,1,0:T(8,128)(2,1)S(1)}, u32[]{:S(2)}, u32[]{:S(2)}) collective-permute-start(bf16[6,32,256]{2,1,0:T(8,128)(2,1)S(1)} %get-tuple-element.29.edge), channel_id=1, source_target_pairs={{4,0},{8,4},{12,8},{16,12},{20,16},{24,20},{28,24},{5,1},{9,5},{13... | collective-permute-start | bytes 294920 | tf_op jit(solution)/shard_map/ppermute | solution.py:672
  87.2 23.7 %collective-permute-start.4 = (bf16[6,32,256]{2,1,0:T(8,128)(2,1)S(1)}, bf16[6,32,256]{2,1,0:T(8,128)(2,1)S(1)}, u32[]{:S(2)}, u32[]{:S(2)}) collective-permute-start(bf16[6,32,256]{2,1,0:T(8,128)(2,1)S(1)} %get-tuple-element.28), channel_id=1, source_target_pairs={{0,4},{4,8},{8,12},{12,16},{16,20},{20,24},{24,28},{1,5},{5,9},{9,... | collective-permute-start | bytes 294920 | tf_op jit(solution)/shard_map/ppermute | solution.py:672
  91.8 19.2 %collective-permute-start.6 = (bf16[6,32,256]{2,1,0:T(8,128)(2,1)S(1)}, bf16[6,32,256]{2,1,0:T(8,128)(2,1)S(1)}, u32[]{:S(2)}, u32[]{:S(2)}) collective-permute-start(bf16[6,32,256]{2,1,0:T(8,128)(2,1)S(1)} %get-tuple-element.30), channel_id=1, source_target_pairs={{0,1},{1,2},{2,3},{4,5},{5,6},{6,7},{8,9},{9,10},{10,11},{12,13},{... | collective-permute-start | bytes 294920 | tf_op jit(solution)/shard_map/ppermute | solution.py:672
  93.1 17.9 %collective-permute-start.7 = (bf16[6,32,256]{2,1,0:T(8,128)(2,1)S(1)}, bf16[6,32,256]{2,1,0:T(8,128)(2,1)S(1)}, u32[]{:S(2)}, u32[]{:S(2)}) collective-permute-start(bf16[6,32,256]{2,1,0:T(8,128)(2,1)S(1)} %get-tuple-element.31), channel_id=1, source_target_pairs={{1,0},{2,1},{3,2},{5,4},{6,5},{7,6},{9,8},{10,9},{11,10},{13,12},{... | collective-permute-start | bytes 294920 | tf_op jit(solution)/shard_map/ppermute | solution.py:672
  103.3 17.1 %all-to-all-start.3 = ((bf16[8,256,128]{2,1,0:T(8,128)(2,1)}), bf16[8,256,128]{2,1,0:T(8,128)(2,1)S(1)}, u32[]{:S(2)}, u32[]{:S(2)}) async-start(bf16[8,256,128]{2,1,0:T(8,128)(2,1)} %shard_map.96), calls=%async_computation.3 | async-start | bytes 1048576 | tf_op jit(solution)/shard_map/all_to_all | solution.py:677
  107.0 4.0 %copy-start.8 = (bf16[32,32,256]{2,1,0:T(8,128)(2,1)S(1)}, bf16[32,32,256]{2,1,0:T(8,128)(2,1)}, u32[]{:S(2)}) copy-start(bf16[32,32,256]{2,1,0:T(8,128)(2,1)} %template.3) | copy-start | bytes 1572868
  107.0 4.0 %copy-start.10 = (f32[32,32,256]{2,1,0:T(8,128)S(1)}, f32[32,32,256]{2,1,0:T(8,128)}, u32[]{:S(2)}) copy-start(f32[32,32,256]{2,1,0:T(8,128)} %copy-done.9) | copy-start | bytes 3145732
  111.0 9.4 %copy-start.1 = (bf16[3,32,256]{2,1,0:T(8,128)(2,1)S(1)}, bf16[3,32,256]{2,1,0:T(8,128)(2,1)}, u32[]{:S(2)}) copy-start(bf16[3,32,256]{2,1,0:T(8,128)(2,1)} %get-tuple-element.33.tables_zero) | copy-start | bytes 147460
  111.0 9.4 %copy-start.2 = (bf16[3,32,256]{2,1,0:T(8,128)(2,1)S(1)}, bf16[3,32,256]{2,1,0:T(8,128)(2,1)}, u32[]{:S(2)}) copy-start(bf16[3,32,256]{2,1,0:T(8,128)(2,1)} %get-tuple-element.32.tables_far) | copy-start | bytes 147460

commit v7 on v6

--- a/solution.py
+++ b/solution.py
@@ -126,23 +126,23 @@
             field[b, rows, :] = value[b * 32 : b * 32 + 32, half * 128 : half * 128 + 128]
 
 
-def middle(start, spread_mid, folded, turned, flipped):
+def middle(start, spread_mid, folded, turned, flipped, parts):
     mask = same_block(256, 32)
     for brick in range(8):
         rows = spread_mid[brick * 32 : brick * 32 + 32]
         line = jnp.where(mask, jnp.concatenate([rows] * 8, axis=0), 0.0).astype(BF16)
         block = start[brick * 32 : brick * 32 + 32, :]
         block = jnp.concatenate([block[:, g * 256 : g * 256 + 256] for g in range(4)], axis=0)
-        high, low = halves(block)
-        both = mm(jnp.concatenate([high, low], axis=0), line, NT if flipped else NN)
-        swap_brick(both[:128] + both[128:], folded, turned, brick)
-
-
-def middle_and_last(start, spread_mid, last, folded, turned, flipped):
-    middle(start, spread_mid, folded, turned, flipped)
-    last = jnp.concatenate([last, last], axis=1)
-    for g in range(4):
-        yield g, mm(last, turned[:, g * 256 : g * 256 + 256]).astype(BF16)
+        held = jnp.concatenate(halves(block)[:parts], axis=0)
+        both = mm(held, line, NT if flipped else NN)
+        swap_brick(both if parts == 1 else both[:128] + both[128:], folded, turned, brick, parts)
+
+
+def middle_and_last(start, spread_mid, last, folded, turned, flipped, parts=2):
+    middle(start, spread_mid, folded, turned, flipped, parts)
+    last = jnp.concatenate([last] * parts, axis=1)
+    for g in range(4):
+        yield g, mm(last, turned[0 : parts * 256, g * 256 : g * 256 + 256]).astype(BF16)
 
 
 def slot_numbers(route, step):
@@ -283,7 +283,7 @@
     begin = diagonal(found[0])
     for g in range(4):
         start[:, g * 256 : g * 256 + 256] = mm(begin, lane_pair(moved, g))
-    for g, value in middle_and_last(start, spread(found[1]), diagonal(found[2]), folded, turned, False):
+    for g, value in middle_and_last(start, spread(found[1]), diagonal(found[2]), folded, turned, False, 1):
         put_pieces(stage, g, value, shared // 8)
         sent.append(send_pieces(stage, send, 512, g, sems.at[2 + g]))
     for copy in sent:
@@ -360,18 +360,17 @@
     end = flipped_diagonal(tables_far[0].astype(F32))
     for g in range(4):
         start[:, g * 256 : g * 256 + 256] = mm(begin, pieces_pair(arrived, 0, g, rows))
-    for g, moved in middle_and_last(start, mid, end, folded, turned, True):
+    for g, moved in middle_and_last(start, mid, end, folded, turned, True, 1):
         put_pair(later, g, moved)
     begin = flipped_diagonal(tables_zero[0].astype(F32))
     mid = spread(tables_zero[1].astype(F32))
     end = diagonal(tables_zero[2].astype(F32))
-    end = jnp.concatenate([end, end], axis=0)
     for g in range(4):
         start[:, g * 256 : g * 256 + 256] = mm(begin, lane_pair(later, g))
     stored = []
-    middle(start, mid, folded, turned, True)
-    for g in range(4):
-        flat = mm(turned[:, g * 256 : g * 256 + 256], end, TN).astype(BF16)
+    middle(start, mid, folded, turned, True, 1)
+    for g in range(4):
+        flat = mm(turned[0:256, g * 256 : g * 256 + 256], end, TN).astype(BF16)
         for index in range(8):
             field[(index % 4) * 8 + 2 * g + index // 4] = flat[index * 32 : index * 32 + 32]
         for qh in range(4):

time: 125 us -> 125 us (level)
  no operation moved by 1% of the time
where the time goes in v7:
time: 125 us; the launch traced here: 124 us
  waiting for transfers between devices  45.6 us (36%)
  Pallas kernels  39.6 us (32%)
  starting transfers between devices  35.1 us (28%)
  local copies, waits for them, and re-layouts  2.6 us (2%)
    all_to_all x4, waiting for transfers between devices, swap_slots(): return lax.all_to_all(send, 'gx', split_axis=0, concat_axis=0, tiled=True)  45.6 us
    pallas_call x12, Pallas kernels, apply(): made(*[pinned(value, spec) for value, spec in zip(values, in_specs, stric...  39.6 us
    all_to_all x4, starting transfers between devices, swap_slots(): return lax.all_to_all(send, 'gx', split_axis=0, concat_axis=0, tiled=True)  18.9 us
    ppermute x8, starting transfers between devices, neighbours(): moved += [lax.ppermute(high, axis, up), lax.ppermute(low, axis, down)]  16.2 us
    unnamed x22, local copies, waits for them, and re-layouts  2.6 us
  transfers between devices with their start and end apart: 12, of which 4 were waited for; matrix products, arithmetic and copies ran while one was open for 0% of the time, Pallas kernels for 24%

profile of v7, /device:TPU:0, one launch (start us, length us, event | category | flops | bytes accessed | tf_op | source)
XLA Modules:
  0.0 124.0 jit_solution(17643521878832112085)
XLA Ops:
  0.6 2.2 %shard_map.86.sent = bf16[8,272,128]{2,1,0:T(8,128)(2,1)} custom-call(s32[2,1,1,8]{3,2,1,0:T(1,128)} %picks.3, s32[2,1,1,8]{3,2,1,0:T(1,128)} %bitcast.9, s32[2,1,1,8]{3,2,1,0:T(1,128)} %landing.1, bf16[32,32,256]{2,1,0:T(8,128)(2,1)} %target.1), custom_call_target="tpu_custom_call" | custom-call | flops 1048576 | bytes 1048576 | tf_op jit(solution)/shard_map/pallas_call | solution.py:652
  2.9 7.3 %all-to-all-start = ((bf16[8,272,128]{2,1,0:T(8,128)(2,1)}), bf16[8,272,128]{2,1,0:T(8,128)(2,1)S(1)}, u32[]{:S(2)}, u32[]{:S(2)}) async-start(bf16[8,272,128]{2,1,0:T(8,128)(2,1)} %shard_map.86.sent), calls=%async_computation | async-start | bytes 1114112 | tf_op jit(solution)/shard_map/all_to_all | solution.py:676
  10.9 4.5 %shard_map.87 = (bf16[8,256,128]{2,1,0:T(8,128)(2,1)S(1)}, bf16[3,32,256]{2,1,0:T(8,128)(2,1)}) custom-call(s32[2,1,1,8]{3,2,1,0:T(1,128)S(1)} %copy-done.5, bf16[3072,64]{1,0:T(8,128)(2,1)} %bitcast.6, bf16[32,32,256]{2,1,0:T(8,128)(2,1)} %template.3, bf16[8,272,128]{2,1,0:T(8,128)(2,1)} %shard_map.86.sent), custom_call_target="tpu_custom_call" | custom-call | flops 68719476736 | bytes 1048576 | tf_op jit(solution)/shard_map/pallas_call | solution.py:652
  15.4 10.0 %all-to-all-done.arrived.targets = bf16[8,272,128]{2,1,0:T(8,128)(2,1)S(1)} async-done(((bf16[8,272,128]{2,1,0:T(8,128)(2,1)}), bf16[8,272,128]{2,1,0:T(8,128)(2,1)S(1)}, u32[]{:S(2)}, u32[]{:S(2)}) %all-to-all-start) | async-done | bytes 557088 | tf_op jit(solution)/shard_map/all_to_all | solution.py:676
  25.4 3.6 %shard_map.88 = (bf16[8,768,128]{2,1,0:T(8,128)(2,1)}, bf16[3,32,256]{2,1,0:T(8,128)(2,1)}, s32[8,128]{1,0:T(8,128)}) custom-call(s32[2,1,1,8]{3,2,1,0:T(1,128)S(1)} %bitcast.10, s32[2,1,1,8]{3,2,1,0:T(1,128)S(1)} %copy-done.4, bf16[3072,64]{1,0:T(8,128)(2,1)S(1)} %bitcast.7, bf16[8,256,128]{2,1,0:T(8,128)(2,1)S(1)} %get-tuple-element.18.moved, ...), custom_call_target="tpu_custom_call" | custom-call | flops 1048576 | bytes 1048576 | tf_op jit(solution)/shard_map/pallas_call | solution.py:652
  29.0 3.6 %all-to-all-start.1 = ((bf16[8,768,128]{2,1,0:T(8,128)(2,1)}), bf16[8,768,128]{2,1,0:T(8,128)(2,1)S(1)}, u32[]{:S(2)}, u32[]{:S(2)}) async-start(bf16[8,768,128]{2,1,0:T(8,128)(2,1)} %get-tuple-element.20.sent), calls=%async_computation.1 | async-start | bytes 3145728 | tf_op jit(solution)/shard_map/all_to_all | solution.py:676
  32.6 2.5 %shard_map.89 = (bf16[6,32,256]{2,1,0:T(8,128)(2,1)S(1)}, bf16[6,32,256]{2,1,0:T(8,128)(2,1)}, bf16[6,32,256]{2,1,0:T(8,128)(2,1)S(1)}, bf16[6,32,256]{2,1,0:T(8,128)(2,1)}) custom-call(bf16[32,32,256]{2,1,0:T(8,128)(2,1)} %template.3, f32[3,32,32,256]{3,2,1,0:T(8,128)} %velocity.3, bf16[8,768,128]{2,1,0:T(8,128)(2,1)} %get-tuple-element.20.sent), custom_call_target="tpu_custom_call" | custom-call | flops 68719476736 | bytes 1048576 | tf_op jit(solution)/shard_map/pallas_call | solution.py:652
  35.1 3.9 %collective-permute-start = (bf16[6,32,256]{2,1,0:T(8,128)(2,1)}, bf16[6,32,256]{2,1,0:T(8,128)(2,1)S(1)}, u32[]{:S(2)}, u32[]{:S(2)}) collective-permute-start(bf16[6,32,256]{2,1,0:T(8,128)(2,1)} %get-tuple-element.21), channel_id=1, source_target_pairs={{0,4},{4,8},{8,12},{12,16},{16,20},{20,24},{24,28},{1,5},{5,9},{9,... | collective-permute-start | bytes 294920 | tf_op jit(solution)/shard_map/ppermute | solution.py:671
  43.0 3.4 %shard_map.90 = (bf16[3,32,256]{2,1,0:T(8,128)(2,1)}, s32[8,128]{1,0:T(8,128)}) custom-call(s32[2,1,1,8]{3,2,1,0:T(1,128)S(1)} %copy-done.6, s32[8,128]{1,0:T(8,128)} %get-tuple-element.19.codes_in, bf16[3072,64]{1,0:T(8,128)(2,1)S(1)} %bitcast.8, bf16[6,32,256]{2,1,0:T(8,128)(2,1)S(1)} %get-tuple-element.22.edge), custom_call_target="tpu_custom_call" | custom-call | flops 68719476736 | bytes 1048576 | tf_op jit(solution)/shard_map/pallas_call | solution.py:652
  46.4 24.4 %all-to-all-done.1.arrived = bf16[8,768,128]{2,1,0:T(8,128)(2,1)S(1)} async-done(((bf16[8,768,128]{2,1,0:T(8,128)(2,1)}), bf16[8,768,128]{2,1,0:T(8,128)(2,1)S(1)}, u32[]{:S(2)}, u32[]{:S(2)}) %all-to-all-start.1) | async-done | bytes 1572896 | tf_op jit(solution)/shard_map/all_to_all | solution.py:676
  70.8 2.4 %shard_map.91.sent.shares = bf16[8,512,128]{2,1,0:T(8,128)(2,1)} custom-call(s32[8,128]{1,0:T(8,128)} %get-tuple-element.25.plan_in, bf16[8,768,128]{2,1,0:T(8,128)(2,1)S(1)} %all-to-all-done.1.arrived, bf16[8,272,128]{2,1,0:T(8,128)(2,1)S(1)} %all-to-all-done.arrived.targets), custom_call_target="tpu_custom_call" | custom-call | flops 1048576 | bytes 1048576 | tf_op jit(solution)/shard_map/pallas_call | solution.py:652
  73.2 4.3 %all-to-all-start.2 = ((bf16[8,512,128]{2,1,0:T(8,128)(2,1)}), bf16[8,512,128]{2,1,0:T(8,128)(2,1)}, u32[]{:S(2)}, u32[]{:S(2)}) async-start(bf16[8,512,128]{2,1,0:T(8,128)(2,1)} %shard_map.91.sent.shares), calls=%async_computation.2 | async-start | bytes 2097152 | tf_op jit(solution)/shard_map/all_to_all | solution.py:676
  77.6 1.9 %copy-done.7 = f32[3,32,32,256]{3,2,1,0:T(8,128)S(1)} copy-done((f32[3,32,32,256]{3,2,1,0:T(8,128)S(1)}, f32[3,32,32,256]{3,2,1,0:T(8,128)}, u32[]{:S(2)}) %copy-start.7) | copy-done | bytes 3145752
  79.5 1.5 %shard_map.92.divergence = f32[32,32,256]{2,1,0:T(8,128)S(1)} custom-call(f32[3,32,32,256]{3,2,1,0:T(8,128)S(1)} %copy-done.7, bf16[6,32,256]{2,1,0:T(8,128)(2,1)S(1)} %collective-permute-done.before_x.b0x, bf16[6,32,256]{2,1,0:T(8,128)(2,1)S(1)} %collective-permute-done.1.after_x.a0x, bf16[6,32,256]{2,1,0:T(8,128)(2,1)S(1)} %collective-permute-done.2.before_y.b0y, ...), custom_call_target="tpu_custom_call" | custom-call | flops 68719476736 | bytes 1048576 | tf_op jit(solution)/shard_map/pallas_call | solution.py:652
  80.9 2.7 %shard_map.93 = (bf16[32,32,256]{2,1,0:T(8,128)(2,1)S(1)}, bf16[6,32,256]{2,1,0:T(8,128)(2,1)S(1)}, bf16[6,32,256]{2,1,0:T(8,128)(2,1)S(1)}, bf16[6,32,256]{2,1,0:T(8,128)(2,1)S(1)}, bf16[6,32,256]{2,1,0:T(8,128)(2,1)S(1)}) custom-call(s32[8,128]{1,0:T(8,128)} %get-tuple-element.19.codes_in, bf16[8,768,128]{2,1,0:T(8,128)(2,1)S(1)} %all-to-all-done.1.arrived, ...), custom_call_target="tpu_custom_call" | custom-call | flops 68719476736 | bytes 1048576 | tf_op jit(solution)/shard_map/pallas_call | solution.py:652
  83.6 2.2 %shard_map.96 = bf16[8,256,128]{2,1,0:T(8,128)(2,1)} custom-call(s32[8,128]{1,0:T(8,128)} %get-tuple-element.25.plan_in, bf16[8,512,128]{2,1,0:T(8,128)(2,1)} %shard_map.91.sent.shares, bf16[6,32,256]{2,1,0:T(8,128)(2,1)S(1)} %get-tuple-element.29.edge), custom_call_target="tpu_custom_call" | custom-call | flops 68719476736 | bytes 1048576 | tf_op jit(solution)/shard_map/pallas_call | solution.py:652
  87.1 4.6 %collective-permute-start.4 = (bf16[6,32,256]{2,1,0:T(8,128)(2,1)S(1)}, bf16[6,32,256]{2,1,0:T(8,128)(2,1)S(1)}, u32[]{:S(2)}, u32[]{:S(2)}) collective-permute-start(bf16[6,32,256]{2,1,0:T(8,128)(2,1)S(1)} %get-tuple-element.28), channel_id=1, source_target_pairs={{0,4},{4,8},{8,12},{12,16},{16,20},{20,24},{24,28},{1,5},{5,9},{9,... | collective-permute-start | bytes 294920 | tf_op jit(solution)/shard_map/ppermute | solution.py:671
  91.6 1.3 %collective-permute-start.6 = (bf16[6,32,256]{2,1,0:T(8,128)(2,1)S(1)}, bf16[6,32,256]{2,1,0:T(8,128)(2,1)S(1)}, u32[]{:S(2)}, u32[]{:S(2)}) collective-permute-start(bf16[6,32,256]{2,1,0:T(8,128)(2,1)S(1)} %get-tuple-element.30), channel_id=1, source_target_pairs={{0,1},{1,2},{2,3},{4,5},{5,6},{6,7},{8,9},{9,10},{10,11},{12,13},{... | collective-permute-start | bytes 294920 | tf_op jit(solution)/shard_map/ppermute | solution.py:671
  94.2 8.9 %all-to-all-done.2.arrived.adjoint_two = bf16[8,512,128]{2,1,0:T(8,128)(2,1)} async-done(((bf16[8,512,128]{2,1,0:T(8,128)(2,1)}), bf16[8,512,128]{2,1,0:T(8,128)(2,1)}, u32[]{:S(2)}, u32[]{:S(2)}) %all-to-all-start.2) | async-done | bytes 1048608 | tf_op jit(solution)/shard_map/all_to_all | solution.py:676
  103.2 3.7 %all-to-all-start.3 = ((bf16[8,256,128]{2,1,0:T(8,128)(2,1)}), bf16[8,256,128]{2,1,0:T(8,128)(2,1)S(1)}, u32[]{:S(2)}, u32[]{:S(2)}) async-start(bf16[8,256,128]{2,1,0:T(8,128)(2,1)} %shard_map.96), calls=%async_computation.3 | async-start | bytes 1048576 | tf_op jit(solution)/shard_map/all_to_all | solution.py:676
  106.9 3.9 %shard_map.94.adjoint_one = bf16[8,256,128]{2,1,0:T(8,128)(2,1)S(1)} custom-call(bf16[3,32,256]{2,1,0:T(8,128)(2,1)} %get-tuple-element.27.tables_in, bf16[8,512,128]{2,1,0:T(8,128)(2,1)} %all-to-all-done.2.arrived.adjoint_two), custom_call_target="tpu_custom_call" | custom-call | flops 68719476736 | bytes 1048576 | tf_op jit(solution)/shard_map/pallas_call | solution.py:652
  110.9 7.1 %shard_map.95.gradient = f32[3,32,32,256]{3,2,1,0:T(8,128)} custom-call(bf16[32,32,256]{2,1,0:T(8,128)(2,1)S(1)} %copy-done.8, bf16[32,32,256]{2,1,0:T(8,128)(2,1)S(1)} %get-tuple-element.26.state, f32[32,32,256]{2,1,0:T(8,128)S(1)} %copy-done.10, bf16[8,512,128]{2,1,0:T(8,128)(2,1)} %all-to-all-done.2.arrived.adjoint_two, ...), custom_call_target="tpu_custom_call" | custom-call | flops 68719476736 | bytes 1048576 | tf_op jit(solution)/shard_map/pallas_call | solution.py:652
  118.0 2.3 %all-to-all-done.3.arrived = bf16[8,256,128]{2,1,0:T(8,128)(2,1)S(1)} async-done(((bf16[8,256,128]{2,1,0:T(8,128)(2,1)}), bf16[8,256,128]{2,1,0:T(8,128)(2,1)S(1)}, u32[]{:S(2)}, u32[]{:S(2)}) %all-to-all-start.3) | async-done | bytes 524320 | tf_op jit(solution)/shard_map/all_to_all | solution.py:676
  120.3 3.6 %shard_map.97 = bf16[32,32,256]{2,1,0:T(8,128)(2,1)} custom-call(bf16[3,32,256]{2,1,0:T(8,128)(2,1)S(1)} %copy-done.2, bf16[3,32,256]{2,1,0:T(8,128)(2,1)S(1)} %copy-done.1, f32[3,32,32,256]{3,2,1,0:T(8,128)} %shard_map.95.gradient, bf16[8,256,128]{2,1,0:T(8,128)(2,1)S(1)} %all-to-all-done.3.arrived), custom_call_target="tpu_custom_call" | custom-call | flops 1048576 | bytes 1048576 | tf_op jit(solution)/shard_map/pallas_call | solution.py:652
  (34 shorter events, 7.2 us)
Async XLA Ops:
  2.9 22.5 %all-to-all-start = ((bf16[8,272,128]{2,1,0:T(8,128)(2,1)}), bf16[8,272,128]{2,1,0:T(8,128)(2,1)S(1)}, u32[]{:S(2)}, u32[]{:S(2)}) async-start(bf16[8,272,128]{2,1,0:T(8,128)(2,1)} %shard_map.86.sent), calls=%async_computation | async-start | bytes 1114112 | tf_op jit(solution)/shard_map/all_to_all | solution.py:676
  10.2 0.7 copy-start.5
  10.8 14.5 %copy-start = (bf16[64,3,32,32]{0,3,2,1:T(8,128)(2,1)S(1)}, bf16[64,3,32,32]{0,3,2,1:T(8,128)(2,1)}, u32[]{:S(2)}) copy-start(bf16[64,3,32,32]{0,3,2,1:T(8,128)(2,1)} %param.10) | copy-start | bytes 1179652
  10.8 14.5 %copy-start.3 = (s32[2,1,1,8,1]{3,4,2,1,0:T(1,128)S(1)}, s32[2,1,1,8,1]{3,4,2,1,0:T(1,128)}, u32[]{:S(2)}) copy-start(s32[2,1,1,8,1]{3,4,2,1,0:T(1,128)} %param.11) | copy-start | bytes 196
  10.8 14.5 %copy-start.4 = (s32[2,1,1,8]{3,2,1,0:T(1,128)S(1)}, s32[2,1,1,8]{3,2,1,0:T(1,128)}, u32[]{:S(2)}) copy-start(s32[2,1,1,8]{3,2,1,0:T(1,128)} %landing.1) | copy-start | bytes 196
  29.0 41.9 %all-to-all-start.1 = ((bf16[8,768,128]{2,1,0:T(8,128)(2,1)}), bf16[8,768,128]{2,1,0:T(8,128)(2,1)S(1)}, u32[]{:S(2)}, u32[]{:S(2)}) async-start(bf16[8,768,128]{2,1,0:T(8,128)(2,1)} %get-tuple-element.20.sent), calls=%async_computation.1 | async-start | bytes 3145728 | tf_op jit(solution)/shard_map/all_to_all | solution.py:676
  32.6 10.4 %copy-start.6 = (s32[2,1,1,8]{3,2,1,0:T(1,128)S(1)}, s32[2,1,1,8]{3,2,1,0:T(1,128)}, u32[]{:S(2)}) copy-start(s32[2,1,1,8]{3,2,1,0:T(1,128)} %picks.3) | copy-start | bytes 196
  35.1 42.4 %collective-permute-start = (bf16[6,32,256]{2,1,0:T(8,128)(2,1)}, bf16[6,32,256]{2,1,0:T(8,128)(2,1)S(1)}, u32[]{:S(2)}, u32[]{:S(2)}) collective-permute-start(bf16[6,32,256]{2,1,0:T(8,128)(2,1)} %get-tuple-element.21), channel_id=1, source_target_pairs={{0,4},{4,8},{8,12},{12,16},{16,20},{20,24},{24,28},{1,5},{5,9},{9,... | collective-permute-start | bytes 294920 | tf_op jit(solution)/shard_map/ppermute | solution.py:671
  39.1 38.5 %collective-permute-start.2 = (bf16[6,32,256]{2,1,0:T(8,128)(2,1)}, bf16[6,32,256]{2,1,0:T(8,128)(2,1)S(1)}, u32[]{:S(2)}, u32[]{:S(2)}) collective-permute-start(bf16[6,32,256]{2,1,0:T(8,128)(2,1)} %get-tuple-element.23), channel_id=1, source_target_pairs={{0,1},{1,2},{2,3},{4,5},{5,6},{6,7},{8,9},{9,10},{10,11},{12,13},{... | collective-permute-start | bytes 294920 | tf_op jit(solution)/shard_map/ppermute | solution.py:671
  40.4 37.2 %collective-permute-start.3 = (bf16[6,32,256]{2,1,0:T(8,128)(2,1)S(1)}, bf16[6,32,256]{2,1,0:T(8,128)(2,1)S(1)}, u32[]{:S(2)}, u32[]{:S(2)}) collective-permute-start(bf16[6,32,256]{2,1,0:T(8,128)(2,1)S(1)} %get-tuple-element.24), channel_id=1, source_target_pairs={{1,0},{2,1},{3,2},{5,4},{6,5},{7,6},{9,8},{10,9},{11,10},{13,12},{... | collective-permute-start | bytes 294920 | tf_op jit(solution)/shard_map/ppermute | solution.py:671
  41.7 35.9 %collective-permute-start.1 = (bf16[6,32,256]{2,1,0:T(8,128)(2,1)S(1)}, bf16[6,32,256]{2,1,0:T(8,128)(2,1)S(1)}, u32[]{:S(2)}, u32[]{:S(2)}) collective-permute-start(bf16[6,32,256]{2,1,0:T(8,128)(2,1)S(1)} %get-tuple-element.22.edge), channel_id=1, source_target_pairs={{4,0},{8,4},{12,8},{16,12},{20,16},{24,20},{28,24},{5,1},{9,5},{13... | collective-permute-start | bytes 294920 | tf_op jit(solution)/shard_map/ppermute | solution.py:671
  73.2 29.9 %all-to-all-start.2 = ((bf16[8,512,128]{2,1,0:T(8,128)(2,1)}), bf16[8,512,128]{2,1,0:T(8,128)(2,1)}, u32[]{:S(2)}, u32[]{:S(2)}) async-start(bf16[8,512,128]{2,1,0:T(8,128)(2,1)} %shard_map.91.sent.shares), calls=%async_computation.2 | async-start | bytes 2097152 | tf_op jit(solution)/shard_map/all_to_all | solution.py:676
  77.6 1.9 %copy-start.7 = (f32[3,32,32,256]{3,2,1,0:T(8,128)S(1)}, f32[3,32,32,256]{3,2,1,0:T(8,128)}, u32[]{:S(2)}) copy-start(f32[3,32,32,256]{3,2,1,0:T(8,128)} %velocity.3) | copy-start | bytes 9437188
  80.9 2.7 %copy-start.9 = (f32[32,32,256]{2,1,0:T(8,128)}, f32[32,32,256]{2,1,0:T(8,128)S(1)}, u32[]{:S(2)}) copy-start(f32[32,32,256]{2,1,0:T(8,128)S(1)} %shard_map.92.divergence) | copy-start | bytes 3145732
  85.8 25.0 %collective-permute-start.5 = (bf16[6,32,256]{2,1,0:T(8,128)(2,1)S(1)}, bf16[6,32,256]{2,1,0:T(8,128)(2,1)S(1)}, u32[]{:S(2)}, u32[]{:S(2)}) collective-permute-start(bf16[6,32,256]{2,1,0:T(8,128)(2,1)S(1)} %get-tuple-element.29.edge), channel_id=1, source_target_pairs={{4,0},{8,4},{12,8},{16,12},{20,16},{24,20},{28,24},{5,1},{9,5},{13... | collective-permute-start | bytes 294920 | tf_op jit(solution)/shard_map/ppermute | solution.py:671
  87.1 23.7 %collective-permute-start.4 = (bf16[6,32,256]{2,1,0:T(8,128)(2,1)S(1)}, bf16[6,32,256]{2,1,0:T(8,128)(2,1)S(1)}, u32[]{:S(2)}, u32[]{:S(2)}) collective-permute-start(bf16[6,32,256]{2,1,0:T(8,128)(2,1)S(1)} %get-tuple-element.28), channel_id=1, source_target_pairs={{0,4},{4,8},{8,12},{12,16},{16,20},{20,24},{24,28},{1,5},{5,9},{9,... | collective-permute-start | bytes 294920 | tf_op jit(solution)/shard_map/ppermute | solution.py:671
  91.6 19.1 %collective-permute-start.6 = (bf16[6,32,256]{2,1,0:T(8,128)(2,1)S(1)}, bf16[6,32,256]{2,1,0:T(8,128)(2,1)S(1)}, u32[]{:S(2)}, u32[]{:S(2)}) collective-permute-start(bf16[6,32,256]{2,1,0:T(8,128)(2,1)S(1)} %get-tuple-element.30), channel_id=1, source_target_pairs={{0,1},{1,2},{2,3},{4,5},{5,6},{6,7},{8,9},{9,10},{10,11},{12,13},{... | collective-permute-start | bytes 294920 | tf_op jit(solution)/shard_map/ppermute | solution.py:671
  92.9 17.8 %collective-permute-start.7 = (bf16[6,32,256]{2,1,0:T(8,128)(2,1)S(1)}, bf16[6,32,256]{2,1,0:T(8,128)(2,1)S(1)}, u32[]{:S(2)}, u32[]{:S(2)}) collective-permute-start(bf16[6,32,256]{2,1,0:T(8,128)(2,1)S(1)} %get-tuple-element.31), channel_id=1, source_target_pairs={{1,0},{2,1},{3,2},{5,4},{6,5},{7,6},{9,8},{10,9},{11,10},{13,12},{... | collective-permute-start | bytes 294920 | tf_op jit(solution)/shard_map/ppermute | solution.py:671
  103.2 17.1 %all-to-all-start.3 = ((bf16[8,256,128]{2,1,0:T(8,128)(2,1)}), bf16[8,256,128]{2,1,0:T(8,128)(2,1)S(1)}, u32[]{:S(2)}, u32[]{:S(2)}) async-start(bf16[8,256,128]{2,1,0:T(8,128)(2,1)} %shard_map.96), calls=%async_computation.3 | async-start | bytes 1048576 | tf_op jit(solution)/shard_map/all_to_all | solution.py:676
  106.9 4.0 %copy-start.8 = (bf16[32,32,256]{2,1,0:T(8,128)(2,1)S(1)}, bf16[32,32,256]{2,1,0:T(8,128)(2,1)}, u32[]{:S(2)}) copy-start(bf16[32,32,256]{2,1,0:T(8,128)(2,1)} %template.3) | copy-start | bytes 1572868
  106.9 4.0 %copy-start.10 = (f32[32,32,256]{2,1,0:T(8,128)S(1)}, f32[32,32,256]{2,1,0:T(8,128)}, u32[]{:S(2)}) copy-start(f32[32,32,256]{2,1,0:T(8,128)} %copy-done.9) | copy-start | bytes 3145732
  110.8 9.4 %copy-start.1 = (bf16[3,32,256]{2,1,0:T(8,128)(2,1)S(1)}, bf16[3,32,256]{2,1,0:T(8,128)(2,1)}, u32[]{:S(2)}) copy-start(bf16[3,32,256]{2,1,0:T(8,128)(2,1)} %get-tuple-element.33.tables_zero) | copy-start | bytes 147460
  110.8 9.4 %copy-start.2 = (bf16[3,32,256]{2,1,0:T(8,128)(2,1)S(1)}, bf16[3,32,256]{2,1,0:T(8,128)(2,1)}, u32[]{:S(2)}) copy-start(bf16[3,32,256]{2,1,0:T(8,128)(2,1)} %get-tuple-element.32.tables_far) | copy-start | bytes 147460

commit v8 on v7

--- a/solution.py
+++ b/solution.py
@@ -229,7 +229,7 @@
         block = jnp.concatenate(
             [field[qh * 8 + qs] for qs in (2 * g, 2 * g + 1) for qh in range(4)], axis=0
         )
-        put_pieces(stage, g, mm(identity(), block, NT).astype(BF16), shared // 8)
+        put_pieces(stage, g, block.T, shared // 8)
         sent.append(send_pieces(stage, send, 0, g, sems.at[5 + g]))
     for copy in sent:
         copy.wait()
@@ -381,7 +381,7 @@
 
 
 def to_native(block, g, field):
-    flat = mm(identity(), block, NT).astype(field.dtype)
+    flat = block.T.astype(field.dtype)
     for index in range(8):
         x = (index % 4) * 8 + 2 * g + index // 4
         field[x] = flat[index * 32 : index * 32 + 32]

time: 125 us -> 125 us (level)
  no operation moved by 1% of the time
where the time goes in v8:
time: 125 us; the launch traced here: 124 us
  waiting for transfers between devices  45.6 us (36%)
  Pallas kernels  39.5 us (32%)
  starting transfers between devices  35.1 us (28%)
  local copies, waits for them, and re-layouts  2.6 us (2%)
    all_to_all x4, waiting for transfers between devices, swap_slots(): return lax.all_to_all(send, 'gx', split_axis=0, concat_axis=0, tiled=True)  45.6 us
    pallas_call x12, Pallas kernels, apply(): made(*[pinned(value, spec) for value, spec in zip(values, in_specs, stric...  39.5 us
    all_to_all x4, starting transfers between devices, swap_slots(): return lax.all_to_all(send, 'gx', split_axis=0, concat_axis=0, tiled=True)  18.9 us
    ppermute x8, starting transfers between devices, neighbours(): moved += [lax.ppermute(high, axis, up), lax.ppermute(low, axis, down)]  16.2 us
    unnamed x22, local copies, waits for them, and re-layouts  2.6 us
  transfers between devices with their start and end apart: 12, of which 4 were waited for; matrix products, arithmetic and copies ran while one was open for 0% of the time, Pallas kernels for 24%

profile of v8, /device:TPU:0, one launch (start us, length us, event | category | flops | bytes accessed | tf_op | source)
XLA Modules:
  0.0 123.9 jit_solution(3323756856880567507)
XLA Ops:
  0.6 2.1 %shard_map.86.sent = bf16[8,272,128]{2,1,0:T(8,128)(2,1)} custom-call(s32[2,1,1,8]{3,2,1,0:T(1,128)} %picks.3, s32[2,1,1,8]{3,2,1,0:T(1,128)} %bitcast.9, s32[2,1,1,8]{3,2,1,0:T(1,128)} %landing.1, bf16[32,32,256]{2,1,0:T(8,128)(2,1)} %target.1), custom_call_target="tpu_custom_call" | custom-call | flops 1048576 | bytes 1048576 | tf_op jit(solution)/shard_map/pallas_call | solution.py:652
  2.7 7.3 %all-to-all-start = ((bf16[8,272,128]{2,1,0:T(8,128)(2,1)}), bf16[8,272,128]{2,1,0:T(8,128)(2,1)S(1)}, u32[]{:S(2)}, u32[]{:S(2)}) async-start(bf16[8,272,128]{2,1,0:T(8,128)(2,1)} %shard_map.86.sent), calls=%async_computation | async-start | bytes 1114112 | tf_op jit(solution)/shard_map/all_to_all | solution.py:676
  10.7 4.5 %shard_map.87 = (bf16[8,256,128]{2,1,0:T(8,128)(2,1)S(1)}, bf16[3,32,256]{2,1,0:T(8,128)(2,1)}) custom-call(s32[2,1,1,8]{3,2,1,0:T(1,128)S(1)} %copy-done.5, bf16[3072,64]{1,0:T(8,128)(2,1)} %bitcast.6, bf16[32,32,256]{2,1,0:T(8,128)(2,1)} %template.3, bf16[8,272,128]{2,1,0:T(8,128)(2,1)} %shard_map.86.sent), custom_call_target="tpu_custom_call" | custom-call | flops 68719476736 | bytes 1048576 | tf_op jit(solution)/shard_map/pallas_call | solution.py:652
  15.2 10.0 %all-to-all-done.arrived.targets = bf16[8,272,128]{2,1,0:T(8,128)(2,1)S(1)} async-done(((bf16[8,272,128]{2,1,0:T(8,128)(2,1)}), bf16[8,272,128]{2,1,0:T(8,128)(2,1)S(1)}, u32[]{:S(2)}, u32[]{:S(2)}) %all-to-all-start) | async-done | bytes 557088 | tf_op jit(solution)/shard_map/all_to_all | solution.py:676
  25.2 3.6 %shard_map.88 = (bf16[8,768,128]{2,1,0:T(8,128)(2,1)}, bf16[3,32,256]{2,1,0:T(8,128)(2,1)}, s32[8,128]{1,0:T(8,128)}) custom-call(s32[2,1,1,8]{3,2,1,0:T(1,128)S(1)} %bitcast.10, s32[2,1,1,8]{3,2,1,0:T(1,128)S(1)} %copy-done.4, bf16[3072,64]{1,0:T(8,128)(2,1)S(1)} %bitcast.7, bf16[8,256,128]{2,1,0:T(8,128)(2,1)S(1)} %get-tuple-element.18.moved, ...), custom_call_target="tpu_custom_call" | custom-call | flops 1048576 | bytes 1048576 | tf_op jit(solution)/shard_map/pallas_call | solution.py:652
  28.8 3.6 %all-to-all-start.1 = ((bf16[8,768,128]{2,1,0:T(8,128)(2,1)}), bf16[8,768,128]{2,1,0:T(8,128)(2,1)S(1)}, u32[]{:S(2)}, u32[]{:S(2)}) async-start(bf16[8,768,128]{2,1,0:T(8,128)(2,1)} %get-tuple-element.20.sent), calls=%async_computation.1 | async-start | bytes 3145728 | tf_op jit(solution)/shard_map/all_to_all | solution.py:676
  32.4 2.5 %shard_map.89 = (bf16[6,32,256]{2,1,0:T(8,128)(2,1)S(1)}, bf16[6,32,256]{2,1,0:T(8,128)(2,1)}, bf16[6,32,256]{2,1,0:T(8,128)(2,1)S(1)}, bf16[6,32,256]{2,1,0:T(8,128)(2,1)}) custom-call(bf16[32,32,256]{2,1,0:T(8,128)(2,1)} %template.3, f32[3,32,32,256]{3,2,1,0:T(8,128)} %velocity.3, bf16[8,768,128]{2,1,0:T(8,128)(2,1)} %get-tuple-element.20.sent), custom_call_target="tpu_custom_call" | custom-call | flops 68719476736 | bytes 1048576 | tf_op jit(solution)/shard_map/pallas_call | solution.py:652
  35.0 3.9 %collective-permute-start = (bf16[6,32,256]{2,1,0:T(8,128)(2,1)}, bf16[6,32,256]{2,1,0:T(8,128)(2,1)S(1)}, u32[]{:S(2)}, u32[]{:S(2)}) collective-permute-start(bf16[6,32,256]{2,1,0:T(8,128)(2,1)} %get-tuple-element.21), channel_id=1, source_target_pairs={{0,4},{4,8},{8,12},{12,16},{16,20},{20,24},{24,28},{1,5},{5,9},{9,... | collective-permute-start | bytes 294920 | tf_op jit(solution)/shard_map/ppermute | solution.py:671
  42.8 3.4 %shard_map.90 = (bf16[3,32,256]{2,1,0:T(8,128)(2,1)}, s32[8,128]{1,0:T(8,128)}) custom-call(s32[2,1,1,8]{3,2,1,0:T(1,128)S(1)} %copy-done.6, s32[8,128]{1,0:T(8,128)} %get-tuple-element.19.codes_in, bf16[3072,64]{1,0:T(8,128)(2,1)S(1)} %bitcast.8, bf16[6,32,256]{2,1,0:T(8,128)(2,1)S(1)} %get-tuple-element.22.edge), custom_call_target="tpu_custom_call" | custom-call | flops 68719476736 | bytes 1048576 | tf_op jit(solution)/shard_map/pallas_call | solution.py:652
  46.3 24.4 %all-to-all-done.1.arrived = bf16[8,768,128]{2,1,0:T(8,128)(2,1)S(1)} async-done(((bf16[8,768,128]{2,1,0:T(8,128)(2,1)}), bf16[8,768,128]{2,1,0:T(8,128)(2,1)S(1)}, u32[]{:S(2)}, u32[]{:S(2)}) %all-to-all-start.1) | async-done | bytes 1572896 | tf_op jit(solution)/shard_map/all_to_all | solution.py:676
  70.7 2.4 %shard_map.91.sent.shares = bf16[8,512,128]{2,1,0:T(8,128)(2,1)} custom-call(s32[8,128]{1,0:T(8,128)} %get-tuple-element.25.plan_in, bf16[8,768,128]{2,1,0:T(8,128)(2,1)S(1)} %all-to-all-done.1.arrived, bf16[8,272,128]{2,1,0:T(8,128)(2,1)S(1)} %all-to-all-done.arrived.targets), custom_call_target="tpu_custom_call" | custom-call | flops 1048576 | bytes 1048576 | tf_op jit(solution)/shard_map/pallas_call | solution.py:652
  73.1 4.3 %all-to-all-start.2 = ((bf16[8,512,128]{2,1,0:T(8,128)(2,1)}), bf16[8,512,128]{2,1,0:T(8,128)(2,1)}, u32[]{:S(2)}, u32[]{:S(2)}) async-start(bf16[8,512,128]{2,1,0:T(8,128)(2,1)} %shard_map.91.sent.shares), calls=%async_computation.2 | async-start | bytes 2097152 | tf_op jit(solution)/shard_map/all_to_all | solution.py:676
  77.4 1.9 %copy-done.7 = f32[3,32,32,256]{3,2,1,0:T(8,128)S(1)} copy-done((f32[3,32,32,256]{3,2,1,0:T(8,128)S(1)}, f32[3,32,32,256]{3,2,1,0:T(8,128)}, u32[]{:S(2)}) %copy-start.7) | copy-done | bytes 3145752
  79.3 1.5 %shard_map.92.divergence = f32[32,32,256]{2,1,0:T(8,128)S(1)} custom-call(f32[3,32,32,256]{3,2,1,0:T(8,128)S(1)} %copy-done.7, bf16[6,32,256]{2,1,0:T(8,128)(2,1)S(1)} %collective-permute-done.before_x.b0x, bf16[6,32,256]{2,1,0:T(8,128)(2,1)S(1)} %collective-permute-done.1.after_x.a0x, bf16[6,32,256]{2,1,0:T(8,128)(2,1)S(1)} %collective-permute-done.2.before_y.b0y, ...), custom_call_target="tpu_custom_call" | custom-call | flops 68719476736 | bytes 1048576 | tf_op jit(solution)/shard_map/pallas_call | solution.py:652
  80.8 2.7 %shard_map.93 = (bf16[32,32,256]{2,1,0:T(8,128)(2,1)S(1)}, bf16[6,32,256]{2,1,0:T(8,128)(2,1)S(1)}, bf16[6,32,256]{2,1,0:T(8,128)(2,1)S(1)}, bf16[6,32,256]{2,1,0:T(8,128)(2,1)S(1)}, bf16[6,32,256]{2,1,0:T(8,128)(2,1)S(1)}) custom-call(s32[8,128]{1,0:T(8,128)} %get-tuple-element.19.codes_in, bf16[8,768,128]{2,1,0:T(8,128)(2,1)S(1)} %all-to-all-done.1.arrived, ...), custom_call_target="tpu_custom_call" | custom-call | flops 68719476736 | bytes 1048576 | tf_op jit(solution)/shard_map/pallas_call | solution.py:652
  83.5 2.2 %shard_map.96 = bf16[8,256,128]{2,1,0:T(8,128)(2,1)} custom-call(s32[8,128]{1,0:T(8,128)} %get-tuple-element.25.plan_in, bf16[8,512,128]{2,1,0:T(8,128)(2,1)} %shard_map.91.sent.shares, bf16[6,32,256]{2,1,0:T(8,128)(2,1)S(1)} %get-tuple-element.29.edge), custom_call_target="tpu_custom_call" | custom-call | flops 68719476736 | bytes 1048576 | tf_op jit(solution)/shard_map/pallas_call | solution.py:652
  87.0 4.6 %collective-permute-start.4 = (bf16[6,32,256]{2,1,0:T(8,128)(2,1)S(1)}, bf16[6,32,256]{2,1,0:T(8,128)(2,1)S(1)}, u32[]{:S(2)}, u32[]{:S(2)}) collective-permute-start(bf16[6,32,256]{2,1,0:T(8,128)(2,1)S(1)} %get-tuple-element.28), channel_id=1, source_target_pairs={{0,4},{4,8},{8,12},{12,16},{16,20},{20,24},{24,28},{1,5},{5,9},{9,... | collective-permute-start | bytes 294920 | tf_op jit(solution)/shard_map/ppermute | solution.py:671
  91.6 1.3 %collective-permute-start.6 = (bf16[6,32,256]{2,1,0:T(8,128)(2,1)S(1)}, bf16[6,32,256]{2,1,0:T(8,128)(2,1)S(1)}, u32[]{:S(2)}, u32[]{:S(2)}) collective-permute-start(bf16[6,32,256]{2,1,0:T(8,128)(2,1)S(1)} %get-tuple-element.30), channel_id=1, source_target_pairs={{0,1},{1,2},{2,3},{4,5},{5,6},{6,7},{8,9},{9,10},{10,11},{12,13},{... | collective-permute-start | bytes 294920 | tf_op jit(solution)/shard_map/ppermute | solution.py:671
  94.2 8.9 %all-to-all-done.2.arrived.adjoint_two = bf16[8,512,128]{2,1,0:T(8,128)(2,1)} async-done(((bf16[8,512,128]{2,1,0:T(8,128)(2,1)}), bf16[8,512,128]{2,1,0:T(8,128)(2,1)}, u32[]{:S(2)}, u32[]{:S(2)}) %all-to-all-start.2) | async-done | bytes 1048608 | tf_op jit(solution)/shard_map/all_to_all | solution.py:676
  103.0 3.7 %all-to-all-start.3 = ((bf16[8,256,128]{2,1,0:T(8,128)(2,1)}), bf16[8,256,128]{2,1,0:T(8,128)(2,1)S(1)}, u32[]{:S(2)}, u32[]{:S(2)}) async-start(bf16[8,256,128]{2,1,0:T(8,128)(2,1)} %shard_map.96), calls=%async_computation.3 | async-start | bytes 1048576 | tf_op jit(solution)/shard_map/all_to_all | solution.py:676
  106.7 3.9 %shard_map.94.adjoint_one = bf16[8,256,128]{2,1,0:T(8,128)(2,1)S(1)} custom-call(bf16[3,32,256]{2,1,0:T(8,128)(2,1)} %get-tuple-element.27.tables_in, bf16[8,512,128]{2,1,0:T(8,128)(2,1)} %all-to-all-done.2.arrived.adjoint_two), custom_call_target="tpu_custom_call" | custom-call | flops 68719476736 | bytes 1048576 | tf_op jit(solution)/shard_map/pallas_call | solution.py:652
  110.7 7.0 %shard_map.95.gradient = f32[3,32,32,256]{3,2,1,0:T(8,128)} custom-call(bf16[32,32,256]{2,1,0:T(8,128)(2,1)S(1)} %copy-done.8, bf16[32,32,256]{2,1,0:T(8,128)(2,1)S(1)} %get-tuple-element.26.state, f32[32,32,256]{2,1,0:T(8,128)S(1)} %copy-done.10, bf16[8,512,128]{2,1,0:T(8,128)(2,1)} %all-to-all-done.2.arrived.adjoint_two, ...), custom_call_target="tpu_custom_call" | custom-call | flops 68719476736 | bytes 1048576 | tf_op jit(solution)/shard_map/pallas_call | solution.py:652
  117.7 2.4 %all-to-all-done.3.arrived = bf16[8,256,128]{2,1,0:T(8,128)(2,1)S(1)} async-done(((bf16[8,256,128]{2,1,0:T(8,128)(2,1)}), bf16[8,256,128]{2,1,0:T(8,128)(2,1)S(1)}, u32[]{:S(2)}, u32[]{:S(2)}) %all-to-all-start.3) | async-done | bytes 524320 | tf_op jit(solution)/shard_map/all_to_all | solution.py:676
  120.1 3.6 %shard_map.97 = bf16[32,32,256]{2,1,0:T(8,128)(2,1)} custom-call(bf16[3,32,256]{2,1,0:T(8,128)(2,1)S(1)} %copy-done.2, bf16[3,32,256]{2,1,0:T(8,128)(2,1)S(1)} %copy-done.1, f32[3,32,32,256]{3,2,1,0:T(8,128)} %shard_map.95.gradient, bf16[8,256,128]{2,1,0:T(8,128)(2,1)S(1)} %all-to-all-done.3.arrived), custom_call_target="tpu_custom_call" | custom-call | flops 1048576 | bytes 1048576 | tf_op jit(solution)/shard_map/pallas_call | solution.py:652
  (34 shorter events, 7.2 us)
Async XLA Ops:
  2.7 22.5 %all-to-all-start = ((bf16[8,272,128]{2,1,0:T(8,128)(2,1)}), bf16[8,272,128]{2,1,0:T(8,128)(2,1)S(1)}, u32[]{:S(2)}, u32[]{:S(2)}) async-start(bf16[8,272,128]{2,1,0:T(8,128)(2,1)} %shard_map.86.sent), calls=%async_computation | async-start | bytes 1114112 | tf_op jit(solution)/shard_map/all_to_all | solution.py:676
  10.0 0.7 copy-start.5
  10.7 14.5 %copy-start = (bf16[64,3,32,32]{0,3,2,1:T(8,128)(2,1)S(1)}, bf16[64,3,32,32]{0,3,2,1:T(8,128)(2,1)}, u32[]{:S(2)}) copy-start(bf16[64,3,32,32]{0,3,2,1:T(8,128)(2,1)} %param.10) | copy-start | bytes 1179652
  10.7 14.5 %copy-start.3 = (s32[2,1,1,8,1]{3,4,2,1,0:T(1,128)S(1)}, s32[2,1,1,8,1]{3,4,2,1,0:T(1,128)}, u32[]{:S(2)}) copy-start(s32[2,1,1,8,1]{3,4,2,1,0:T(1,128)} %param.11) | copy-start | bytes 196
  10.7 14.5 %copy-start.4 = (s32[2,1,1,8]{3,2,1,0:T(1,128)S(1)}, s32[2,1,1,8]{3,2,1,0:T(1,128)}, u32[]{:S(2)}) copy-start(s32[2,1,1,8]{3,2,1,0:T(1,128)} %landing.1) | copy-start | bytes 196
  28.8 41.9 %all-to-all-start.1 = ((bf16[8,768,128]{2,1,0:T(8,128)(2,1)}), bf16[8,768,128]{2,1,0:T(8,128)(2,1)S(1)}, u32[]{:S(2)}, u32[]{:S(2)}) async-start(bf16[8,768,128]{2,1,0:T(8,128)(2,1)} %get-tuple-element.20.sent), calls=%async_computation.1 | async-start | bytes 3145728 | tf_op jit(solution)/shard_map/all_to_all | solution.py:676
  32.4 10.4 %copy-start.6 = (s32[2,1,1,8]{3,2,1,0:T(1,128)S(1)}, s32[2,1,1,8]{3,2,1,0:T(1,128)}, u32[]{:S(2)}) copy-start(s32[2,1,1,8]{3,2,1,0:T(1,128)} %picks.3) | copy-start | bytes 196
  35.0 42.4 %collective-permute-start = (bf16[6,32,256]{2,1,0:T(8,128)(2,1)}, bf16[6,32,256]{2,1,0:T(8,128)(2,1)S(1)}, u32[]{:S(2)}, u32[]{:S(2)}) collective-permute-start(bf16[6,32,256]{2,1,0:T(8,128)(2,1)} %get-tuple-element.21), channel_id=1, source_target_pairs={{0,4},{4,8},{8,12},{12,16},{16,20},{20,24},{24,28},{1,5},{5,9},{9,... | collective-permute-start | bytes 294920 | tf_op jit(solution)/shard_map/ppermute | solution.py:671
  38.9 38.4 %collective-permute-start.2 = (bf16[6,32,256]{2,1,0:T(8,128)(2,1)}, bf16[6,32,256]{2,1,0:T(8,128)(2,1)S(1)}, u32[]{:S(2)}, u32[]{:S(2)}) collective-permute-start(bf16[6,32,256]{2,1,0:T(8,128)(2,1)} %get-tuple-element.23), channel_id=1, source_target_pairs={{0,1},{1,2},{2,3},{4,5},{5,6},{6,7},{8,9},{9,10},{10,11},{12,13},{... | collective-permute-start | bytes 294920 | tf_op jit(solution)/shard_map/ppermute | solution.py:671
  40.2 37.2 %collective-permute-start.3 = (bf16[6,32,256]{2,1,0:T(8,128)(2,1)S(1)}, bf16[6,32,256]{2,1,0:T(8,128)(2,1)S(1)}, u32[]{:S(2)}, u32[]{:S(2)}) collective-permute-start(bf16[6,32,256]{2,1,0:T(8,128)(2,1)S(1)} %get-tuple-element.24), channel_id=1, source_target_pairs={{1,0},{2,1},{3,2},{5,4},{6,5},{7,6},{9,8},{10,9},{11,10},{13,12},{... | collective-permute-start | bytes 294920 | tf_op jit(solution)/shard_map/ppermute | solution.py:671
  41.5 35.9 %collective-permute-start.1 = (bf16[6,32,256]{2,1,0:T(8,128)(2,1)S(1)}, bf16[6,32,256]{2,1,0:T(8,128)(2,1)S(1)}, u32[]{:S(2)}, u32[]{:S(2)}) collective-permute-start(bf16[6,32,256]{2,1,0:T(8,128)(2,1)S(1)} %get-tuple-element.22.edge), channel_id=1, source_target_pairs={{4,0},{8,4},{12,8},{16,12},{20,16},{24,20},{28,24},{5,1},{9,5},{13... | collective-permute-start | bytes 294920 | tf_op jit(solution)/shard_map/ppermute | solution.py:671
  73.1 29.9 %all-to-all-start.2 = ((bf16[8,512,128]{2,1,0:T(8,128)(2,1)}), bf16[8,512,128]{2,1,0:T(8,128)(2,1)}, u32[]{:S(2)}, u32[]{:S(2)}) async-start(bf16[8,512,128]{2,1,0:T(8,128)(2,1)} %shard_map.91.sent.shares), calls=%async_computation.2 | async-start | bytes 2097152 | tf_op jit(solution)/shard_map/all_to_all | solution.py:676
  77.4 1.9 %copy-start.7 = (f32[3,32,32,256]{3,2,1,0:T(8,128)S(1)}, f32[3,32,32,256]{3,2,1,0:T(8,128)}, u32[]{:S(2)}) copy-start(f32[3,32,32,256]{3,2,1,0:T(8,128)} %velocity.3) | copy-start | bytes 9437188
  80.8 2.8 %copy-start.9 = (f32[32,32,256]{2,1,0:T(8,128)}, f32[32,32,256]{2,1,0:T(8,128)S(1)}, u32[]{:S(2)}) copy-start(f32[32,32,256]{2,1,0:T(8,128)S(1)} %shard_map.92.divergence) | copy-start | bytes 3145732
  85.7 25.0 %collective-permute-start.5 = (bf16[6,32,256]{2,1,0:T(8,128)(2,1)S(1)}, bf16[6,32,256]{2,1,0:T(8,128)(2,1)S(1)}, u32[]{:S(2)}, u32[]{:S(2)}) collective-permute-start(bf16[6,32,256]{2,1,0:T(8,128)(2,1)S(1)} %get-tuple-element.29.edge), channel_id=1, source_target_pairs={{4,0},{8,4},{12,8},{16,12},{20,16},{24,20},{28,24},{5,1},{9,5},{13... | collective-permute-start | bytes 294920 | tf_op jit(solution)/shard_map/ppermute | solution.py:671
  87.0 23.6 %collective-permute-start.4 = (bf16[6,32,256]{2,1,0:T(8,128)(2,1)S(1)}, bf16[6,32,256]{2,1,0:T(8,128)(2,1)S(1)}, u32[]{:S(2)}, u32[]{:S(2)}) collective-permute-start(bf16[6,32,256]{2,1,0:T(8,128)(2,1)S(1)} %get-tuple-element.28), channel_id=1, source_target_pairs={{0,4},{4,8},{8,12},{12,16},{16,20},{20,24},{24,28},{1,5},{5,9},{9,... | collective-permute-start | bytes 294920 | tf_op jit(solution)/shard_map/ppermute | solution.py:671
  91.6 19.1 %collective-permute-start.6 = (bf16[6,32,256]{2,1,0:T(8,128)(2,1)S(1)}, bf16[6,32,256]{2,1,0:T(8,128)(2,1)S(1)}, u32[]{:S(2)}, u32[]{:S(2)}) collective-permute-start(bf16[6,32,256]{2,1,0:T(8,128)(2,1)S(1)} %get-tuple-element.30), channel_id=1, source_target_pairs={{0,1},{1,2},{2,3},{4,5},{5,6},{6,7},{8,9},{9,10},{10,11},{12,13},{... | collective-permute-start | bytes 294920 | tf_op jit(solution)/shard_map/ppermute | solution.py:671
  92.9 17.8 %collective-permute-start.7 = (bf16[6,32,256]{2,1,0:T(8,128)(2,1)S(1)}, bf16[6,32,256]{2,1,0:T(8,128)(2,1)S(1)}, u32[]{:S(2)}, u32[]{:S(2)}) collective-permute-start(bf16[6,32,256]{2,1,0:T(8,128)(2,1)S(1)} %get-tuple-element.31), channel_id=1, source_target_pairs={{1,0},{2,1},{3,2},{5,4},{6,5},{7,6},{9,8},{10,9},{11,10},{13,12},{... | collective-permute-start | bytes 294920 | tf_op jit(solution)/shard_map/ppermute | solution.py:671
  103.0 17.1 %all-to-all-start.3 = ((bf16[8,256,128]{2,1,0:T(8,128)(2,1)}), bf16[8,256,128]{2,1,0:T(8,128)(2,1)S(1)}, u32[]{:S(2)}, u32[]{:S(2)}) async-start(bf16[8,256,128]{2,1,0:T(8,128)(2,1)} %shard_map.96), calls=%async_computation.3 | async-start | bytes 1048576 | tf_op jit(solution)/shard_map/all_to_all | solution.py:676
  106.7 4.0 %copy-start.8 = (bf16[32,32,256]{2,1,0:T(8,128)(2,1)S(1)}, bf16[32,32,256]{2,1,0:T(8,128)(2,1)}, u32[]{:S(2)}) copy-start(bf16[32,32,256]{2,1,0:T(8,128)(2,1)} %template.3) | copy-start | bytes 1572868
  106.7 4.0 %copy-start.10 = (f32[32,32,256]{2,1,0:T(8,128)S(1)}, f32[32,32,256]{2,1,0:T(8,128)}, u32[]{:S(2)}) copy-start(f32[32,32,256]{2,1,0:T(8,128)} %copy-done.9) | copy-start | bytes 3145732
  110.7 9.4 %copy-start.1 = (bf16[3,32,256]{2,1,0:T(8,128)(2,1)S(1)}, bf16[3,32,256]{2,1,0:T(8,128)(2,1)}, u32[]{:S(2)}) copy-start(bf16[3,32,256]{2,1,0:T(8,128)(2,1)} %get-tuple-element.33.tables_zero) | copy-start | bytes 147460
  110.7 9.4 %copy-start.2 = (bf16[3,32,256]{2,1,0:T(8,128)(2,1)S(1)}, bf16[3,32,256]{2,1,0:T(8,128)(2,1)}, u32[]{:S(2)}) copy-start(bf16[3,32,256]{2,1,0:T(8,128)(2,1)} %get-tuple-element.32.tables_far) | copy-start | bytes 147460

commit v9 on v8

--- a/solution.py
+++ b/solution.py
@@ -249,7 +249,7 @@
         block = jnp.concatenate(
             [field_mem[qh * 8 + qs] for qs in (2 * g, 2 * g + 1) for qh in range(4)], axis=0
         )
-        start[:, g * 256 : g * 256 + 256] = mm(begin, block, NT)
+        start[:, g * 256 : g * 256 + 256] = mm(begin, block, NT).astype(start.dtype)
     for g, moved in middle_and_last(start, spread(found[1]), diagonal(found[0]), folded, turned, False):
         put_pair(moved_out, g, moved)
     kept.wait()
@@ -282,7 +282,7 @@
     sent.append(fetch(tables_mem, tables, sems.at[1]))
     begin = diagonal(found[0])
     for g in range(4):
-        start[:, g * 256 : g * 256 + 256] = mm(begin, lane_pair(moved, g))
+        start[:, g * 256 : g * 256 + 256] = mm(begin, lane_pair(moved, g)).astype(start.dtype)
     for g, value in middle_and_last(start, spread(found[1]), diagonal(found[2]), folded, turned, False, 1):
         put_pieces(stage, g, value, shared // 8)
         sent.append(send_pieces(stage, send, 512, g, sems.at[2 + g]))
@@ -290,12 +290,10 @@
         copy.wait()
 
 
-def share_kernel(plan_in, arrived, targets, send, plan, total, stage, sems, chunk_sems):
+def share_kernel(plan, arrived, targets, send, total, stage, chunk_sems):
     peers, shared = total.shape[0], total.shape[1]
     rows = shared // 8
-    load = fetch(plan_in, plan, sems.at[0])
     total[...] = jnp.zeros(total.shape, F32)
-    load.wait()
 
     def add(source, carry):
         for b in range(8):
@@ -347,7 +345,7 @@
     mid = spread(tables[1].astype(F32))
     end = flipped_diagonal(tables[0].astype(F32))
     for g in range(4):
-        start[:, g * 256 : g * 256 + 256] = mm(begin, pieces_pair(arrived, 1, g, rows))
+        start[:, g * 256 : g * 256 + 256] = mm(begin, pieces_pair(arrived, 1, g, rows)).astype(start.dtype)
     for g, moved in middle_and_last(start, mid, end, folded, turned, True):
         put_pair(adjoint, g, moved)
 
@@ -359,14 +357,14 @@
     mid = spread(tables_far[1].astype(F32))
     end = flipped_diagonal(tables_far[0].astype(F32))
     for g in range(4):
-        start[:, g * 256 : g * 256 + 256] = mm(begin, pieces_pair(arrived, 0, g, rows))
+        start[:, g * 256 : g * 256 + 256] = mm(begin, pieces_pair(arrived, 0, g, rows)).astype(start.dtype)
     for g, moved in middle_and_last(start, mid, end, folded, turned, True, 1):
         put_pair(later, g, moved)
     begin = flipped_diagonal(tables_zero[0].astype(F32))
     mid = spread(tables_zero[1].astype(F32))
     end = diagonal(tables_zero[2].astype(F32))
     for g in range(4):
-        start[:, g * 256 : g * 256 + 256] = mm(begin, lane_pair(later, g))
+        start[:, g * 256 : g * 256 + 256] = mm(begin, lane_pair(later, g)).astype(start.dtype)
     stored = []
     middle(start, mid, folded, turned, True, 1)
     for g in range(4):
@@ -715,8 +713,8 @@
         [far((peers, 512 + shared, 128), BF16), far(TABLES, BF16), far((peers, 128), jnp.int32)],
         [SCALAR, SCALAR, WHOLE, WHOLE, WHOLE],
         [FAR] * 3,
-        [pltpu.VMEM((peers, 16, 128), F32), pltpu.VMEM((peers, 128), jnp.int32)]
-        + turning
+        [pltpu.VMEM((peers, 16, 128), F32), pltpu.VMEM((peers, 128), jnp.int32), pltpu.VMEM(FLAT, BF16)]
+        + turning[1:]
         + [stage, tables, sems, pltpu.SemaphoreType.DMA((8,))],
         SHORT,
     )(route, target_brick, listed, moved, targets)
@@ -742,10 +740,10 @@
     send = call(
         share_kernel,
         far((peers, 2 * shared, 128), BF16),
-        [FAR, WHOLE, WHOLE],
+        [SCALAR, WHOLE, WHOLE],
         FAR,
-        [routes_mem, pltpu.VMEM((peers, shared, 128), F32), pltpu.VMEM((peers, 2 * shared, 128), BF16)]
-        + [sems, pltpu.SemaphoreType.DMA((peers,))],
+        [pltpu.VMEM((peers, shared, 128), F32), pltpu.VMEM((peers, 2 * shared, 128), BF16)]
+        + [pltpu.SemaphoreType.DMA((peers,))],
         SHORT,
     )(plan, arrived, targets)
     pulled = swap_slots(send)
@@ -783,7 +781,7 @@
         far(NATIVE, BF16),
         [WHOLE, WHOLE, FAR, NEAR],
         FAR,
-        turning + [form, pltpu.VMEM(NATIVE, BF16), quarter_sems],
+        [pltpu.VMEM(FLAT, BF16)] + turning[1:] + [form, pltpu.VMEM(NATIVE, BF16), quarter_sems],
         SHORT,
     )(tables_far, tables_zero, gradient, composed)
     return gradient, adjoint

time: 125 us -> 125 us (level)
    unnamed x22 -> x24, local copies, waits for them, and re-layouts: 2.6 us -> 3.27 us
where the time goes in v9:
time: 125 us; the launch traced here: 124 us
  waiting for transfers between devices  45.6 us (36%)
  Pallas kernels  39.3 us (31%)
  starting transfers between devices  35.1 us (28%)
  local copies, waits for them, and re-layouts  3.27 us (3%)
    all_to_all x4, waiting for transfers between devices, swap_slots(): return lax.all_to_all(send, 'gx', split_axis=0, concat_axis=0, tiled=True)  45.6 us
    pallas_call x12, Pallas kernels, apply(): made(*[pinned(value, spec) for value, spec in zip(values, in_specs, stric...  39.3 us
    all_to_all x4, starting transfers between devices, swap_slots(): return lax.all_to_all(send, 'gx', split_axis=0, concat_axis=0, tiled=True)  18.9 us
    ppermute x8, starting transfers between devices, neighbours(): moved += [lax.ppermute(high, axis, up), lax.ppermute(low, axis, down)]  16.2 us
    unnamed x24, local copies, waits for them, and re-layouts  3.27 us
  transfers between devices with their start and end apart: 12, of which 4 were waited for; matrix products, arithmetic and copies ran while one was open for 0% of the time, Pallas kernels for 24%

profile of v9, /device:TPU:0, one launch (start us, length us, event | category | flops | bytes accessed | tf_op | source)
XLA Modules:
  0.0 124.4 jit_solution(7764294631836384409)
XLA Ops:
  0.6 2.1 %shard_map.86.sent = bf16[8,272,128]{2,1,0:T(8,128)(2,1)} custom-call(s32[2,1,1,8]{3,2,1,0:T(1,128)} %picks.3, s32[2,1,1,8]{3,2,1,0:T(1,128)} %bitcast.9, s32[2,1,1,8]{3,2,1,0:T(1,128)} %landing.1, bf16[32,32,256]{2,1,0:T(8,128)(2,1)} %target.1), custom_call_target="tpu_custom_call" | custom-call | flops 1048576 | bytes 1048576 | tf_op jit(solution)/shard_map/pallas_call | solution.py:650
  2.7 7.3 %all-to-all-start = ((bf16[8,272,128]{2,1,0:T(8,128)(2,1)}), bf16[8,272,128]{2,1,0:T(8,128)(2,1)S(1)}, u32[]{:S(2)}, u32[]{:S(2)}) async-start(bf16[8,272,128]{2,1,0:T(8,128)(2,1)} %shard_map.86.sent), calls=%async_computation | async-start | bytes 1114112 | tf_op jit(solution)/shard_map/all_to_all | solution.py:674
  10.7 4.5 %shard_map.87 = (bf16[8,256,128]{2,1,0:T(8,128)(2,1)S(1)}, bf16[3,32,256]{2,1,0:T(8,128)(2,1)}) custom-call(s32[2,1,1,8]{3,2,1,0:T(1,128)S(1)} %copy-done.6, bf16[3072,64]{1,0:T(8,128)(2,1)} %bitcast.6, bf16[32,32,256]{2,1,0:T(8,128)(2,1)} %template.3, bf16[8,272,128]{2,1,0:T(8,128)(2,1)} %shard_map.86.sent), custom_call_target="tpu_custom_call" | custom-call | flops 68719476736 | bytes 1048576 | tf_op jit(solution)/shard_map/pallas_call | solution.py:650
  15.2 10.0 %all-to-all-done.arrived.targets = bf16[8,272,128]{2,1,0:T(8,128)(2,1)S(1)} async-done(((bf16[8,272,128]{2,1,0:T(8,128)(2,1)}), bf16[8,272,128]{2,1,0:T(8,128)(2,1)S(1)}, u32[]{:S(2)}, u32[]{:S(2)}) %all-to-all-start) | async-done | bytes 557088 | tf_op jit(solution)/shard_map/all_to_all | solution.py:674
  25.2 3.6 %shard_map.88 = (bf16[8,768,128]{2,1,0:T(8,128)(2,1)}, bf16[3,32,256]{2,1,0:T(8,128)(2,1)}, s32[8,128]{1,0:T(8,128)}) custom-call(s32[2,1,1,8]{3,2,1,0:T(1,128)S(1)} %bitcast.10, s32[2,1,1,8]{3,2,1,0:T(1,128)S(1)} %copy-done.5, bf16[3072,64]{1,0:T(8,128)(2,1)S(1)} %bitcast.7, bf16[8,256,128]{2,1,0:T(8,128)(2,1)S(1)} %get-tuple-element.18.moved, ...), custom_call_target="tpu_custom_call" | custom-call | flops 1048576 | bytes 1048576 | tf_op jit(solution)/shard_map/pallas_call | solution.py:650
  28.8 3.6 %all-to-all-start.1 = ((bf16[8,768,128]{2,1,0:T(8,128)(2,1)}), bf16[8,768,128]{2,1,0:T(8,128)(2,1)S(1)}, u32[]{:S(2)}, u32[]{:S(2)}) async-start(bf16[8,768,128]{2,1,0:T(8,128)(2,1)} %get-tuple-element.20.sent), calls=%async_computation.1 | async-start | bytes 3145728 | tf_op jit(solution)/shard_map/all_to_all | solution.py:674
  32.4 2.5 %shard_map.89 = (bf16[6,32,256]{2,1,0:T(8,128)(2,1)S(1)}, bf16[6,32,256]{2,1,0:T(8,128)(2,1)}, bf16[6,32,256]{2,1,0:T(8,128)(2,1)S(1)}, bf16[6,32,256]{2,1,0:T(8,128)(2,1)}) custom-call(bf16[32,32,256]{2,1,0:T(8,128)(2,1)} %template.3, f32[3,32,32,256]{3,2,1,0:T(8,128)} %velocity.3, bf16[8,768,128]{2,1,0:T(8,128)(2,1)} %get-tuple-element.20.sent), custom_call_target="tpu_custom_call" | custom-call | flops 68719476736 | bytes 1048576 | tf_op jit(solution)/shard_map/pallas_call | solution.py:650
  35.0 3.9 %collective-permute-start = (bf16[6,32,256]{2,1,0:T(8,128)(2,1)}, bf16[6,32,256]{2,1,0:T(8,128)(2,1)S(1)}, u32[]{:S(2)}, u32[]{:S(2)}) collective-permute-start(bf16[6,32,256]{2,1,0:T(8,128)(2,1)} %get-tuple-element.21), channel_id=1, source_target_pairs={{0,4},{4,8},{8,12},{12,16},{16,20},{20,24},{24,28},{1,5},{5,9},{9,... | collective-permute-start | bytes 294920 | tf_op jit(solution)/shard_map/ppermute | solution.py:669
  42.8 3.4 %shard_map.90 = (bf16[3,32,256]{2,1,0:T(8,128)(2,1)}, s32[8,128]{1,0:T(8,128)}) custom-call(s32[2,1,1,8]{3,2,1,0:T(1,128)S(1)} %copy-done.7, s32[8,128]{1,0:T(8,128)} %get-tuple-element.19.codes_in, bf16[3072,64]{1,0:T(8,128)(2,1)S(1)} %bitcast.8, bf16[6,32,256]{2,1,0:T(8,128)(2,1)S(1)} %get-tuple-element.22.edge), custom_call_target="tpu_custom_call" | custom-call | flops 68719476736 | bytes 1048576 | tf_op jit(solution)/shard_map/pallas_call | solution.py:650
  46.3 24.4 %all-to-all-done.1.arrived = bf16[8,768,128]{2,1,0:T(8,128)(2,1)S(1)} async-done(((bf16[8,768,128]{2,1,0:T(8,128)(2,1)}), bf16[8,768,128]{2,1,0:T(8,128)(2,1)S(1)}, u32[]{:S(2)}, u32[]{:S(2)}) %all-to-all-start.1) | async-done | bytes 1572896 | tf_op jit(solution)/shard_map/all_to_all | solution.py:674
  71.4 2.2 %shard_map.91.sent.shares = bf16[8,512,128]{2,1,0:T(8,128)(2,1)} custom-call(s32[8,128]{1,0:T(8,128)S(1)} %copy-done.3, bf16[8,768,128]{2,1,0:T(8,128)(2,1)S(1)} %all-to-all-done.1.arrived, bf16[8,272,128]{2,1,0:T(8,128)(2,1)S(1)} %all-to-all-done.arrived.targets), custom_call_target="tpu_custom_call" | custom-call | flops 1048576 | bytes 1048576 | tf_op jit(solution)/shard_map/pallas_call | solution.py:650
  73.6 4.3 %all-to-all-start.2 = ((bf16[8,512,128]{2,1,0:T(8,128)(2,1)}), bf16[8,512,128]{2,1,0:T(8,128)(2,1)}, u32[]{:S(2)}, u32[]{:S(2)}) async-start(bf16[8,512,128]{2,1,0:T(8,128)(2,1)} %shard_map.91.sent.shares), calls=%async_computation.2 | async-start | bytes 2097152 | tf_op jit(solution)/shard_map/all_to_all | solution.py:674
  77.9 1.9 %copy-done.8 = f32[3,32,32,256]{3,2,1,0:T(8,128)S(1)} copy-done((f32[3,32,32,256]{3,2,1,0:T(8,128)S(1)}, f32[3,32,32,256]{3,2,1,0:T(8,128)}, u32[]{:S(2)}) %copy-start.8) | copy-done | bytes 3145752
  79.8 1.5 %shard_map.92.divergence = f32[32,32,256]{2,1,0:T(8,128)S(1)} custom-call(f32[3,32,32,256]{3,2,1,0:T(8,128)S(1)} %copy-done.8, bf16[6,32,256]{2,1,0:T(8,128)(2,1)S(1)} %collective-permute-done.before_x.b0x, bf16[6,32,256]{2,1,0:T(8,128)(2,1)S(1)} %collective-permute-done.1.after_x.a0x, bf16[6,32,256]{2,1,0:T(8,128)(2,1)S(1)} %collective-permute-done.2.before_y.b0y, ...), custom_call_target="tpu_custom_call" | custom-call | flops 68719476736 | bytes 1048576 | tf_op jit(solution)/shard_map/pallas_call | solution.py:650
  81.3 2.7 %shard_map.93 = (bf16[32,32,256]{2,1,0:T(8,128)(2,1)S(1)}, bf16[6,32,256]{2,1,0:T(8,128)(2,1)S(1)}, bf16[6,32,256]{2,1,0:T(8,128)(2,1)S(1)}, bf16[6,32,256]{2,1,0:T(8,128)(2,1)S(1)}, bf16[6,32,256]{2,1,0:T(8,128)(2,1)S(1)}) custom-call(s32[8,128]{1,0:T(8,128)} %get-tuple-element.19.codes_in, bf16[8,768,128]{2,1,0:T(8,128)(2,1)S(1)} %all-to-all-done.1.arrived, ...), custom_call_target="tpu_custom_call" | custom-call | flops 68719476736 | bytes 1048576 | tf_op jit(solution)/shard_map/pallas_call | solution.py:650
  84.0 2.2 %shard_map.96 = bf16[8,256,128]{2,1,0:T(8,128)(2,1)} custom-call(s32[8,128]{1,0:T(8,128)} %get-tuple-element.25.plan.plan_in, bf16[8,512,128]{2,1,0:T(8,128)(2,1)} %shard_map.91.sent.shares, bf16[6,32,256]{2,1,0:T(8,128)(2,1)S(1)} %get-tuple-element.29.edge), custom_call_target="tpu_custom_call" | custom-call | flops 68719476736 | bytes 1048576 | tf_op jit(solution)/shard_map/pallas_call | solution.py:650
  87.5 4.6 %collective-permute-start.4 = (bf16[6,32,256]{2,1,0:T(8,128)(2,1)S(1)}, bf16[6,32,256]{2,1,0:T(8,128)(2,1)S(1)}, u32[]{:S(2)}, u32[]{:S(2)}) collective-permute-start(bf16[6,32,256]{2,1,0:T(8,128)(2,1)S(1)} %get-tuple-element.28), channel_id=1, source_target_pairs={{0,4},{4,8},{8,12},{12,16},{16,20},{20,24},{24,28},{1,5},{5,9},{9,... | collective-permute-start | bytes 294920 | tf_op jit(solution)/shard_map/ppermute | solution.py:669
  92.0 1.3 %collective-permute-start.6 = (bf16[6,32,256]{2,1,0:T(8,128)(2,1)S(1)}, bf16[6,32,256]{2,1,0:T(8,128)(2,1)S(1)}, u32[]{:S(2)}, u32[]{:S(2)}) collective-permute-start(bf16[6,32,256]{2,1,0:T(8,128)(2,1)S(1)} %get-tuple-element.30), channel_id=1, source_target_pairs={{0,1},{1,2},{2,3},{4,5},{5,6},{6,7},{8,9},{9,10},{10,11},{12,13},{... | collective-permute-start | bytes 294920 | tf_op jit(solution)/shard_map/ppermute | solution.py:669
  94.6 8.9 %all-to-all-done.2.arrived.adjoint_two = bf16[8,512,128]{2,1,0:T(8,128)(2,1)} async-done(((bf16[8,512,128]{2,1,0:T(8,128)(2,1)}), bf16[8,512,128]{2,1,0:T(8,128)(2,1)}, u32[]{:S(2)}, u32[]{:S(2)}) %all-to-all-start.2) | async-done | bytes 1048608 | tf_op jit(solution)/shard_map/all_to_all | solution.py:674
  103.5 3.7 %all-to-all-start.3 = ((bf16[8,256,128]{2,1,0:T(8,128)(2,1)}), bf16[8,256,128]{2,1,0:T(8,128)(2,1)S(1)}, u32[]{:S(2)}, u32[]{:S(2)}) async-start(bf16[8,256,128]{2,1,0:T(8,128)(2,1)} %shard_map.96), calls=%async_computation.3 | async-start | bytes 1048576 | tf_op jit(solution)/shard_map/all_to_all | solution.py:674
  107.2 3.9 %shard_map.94.adjoint_one = bf16[8,256,128]{2,1,0:T(8,128)(2,1)S(1)} custom-call(bf16[3,32,256]{2,1,0:T(8,128)(2,1)} %get-tuple-element.27.tables_in, bf16[8,512,128]{2,1,0:T(8,128)(2,1)} %all-to-all-done.2.arrived.adjoint_two), custom_call_target="tpu_custom_call" | custom-call | flops 68719476736 | bytes 1048576 | tf_op jit(solution)/shard_map/pallas_call | solution.py:650
  111.2 7.0 %shard_map.95.gradient = f32[3,32,32,256]{3,2,1,0:T(8,128)} custom-call(bf16[32,32,256]{2,1,0:T(8,128)(2,1)S(1)} %copy-done.9, bf16[32,32,256]{2,1,0:T(8,128)(2,1)S(1)} %get-tuple-element.26.state, f32[32,32,256]{2,1,0:T(8,128)S(1)} %copy-done.11, bf16[8,512,128]{2,1,0:T(8,128)(2,1)} %all-to-all-done.2.arrived.adjoint_two, ...), custom_call_target="tpu_custom_call" | custom-call | flops 68719476736 | bytes 1048576 | tf_op jit(solution)/shard_map/pallas_call | solution.py:650
  118.2 2.4 %all-to-all-done.3.arrived = bf16[8,256,128]{2,1,0:T(8,128)(2,1)S(1)} async-done(((bf16[8,256,128]{2,1,0:T(8,128)(2,1)}), bf16[8,256,128]{2,1,0:T(8,128)(2,1)S(1)}, u32[]{:S(2)}, u32[]{:S(2)}) %all-to-all-start.3) | async-done | bytes 524320 | tf_op jit(solution)/shard_map/all_to_all | solution.py:674
  120.6 3.6 %shard_map.97 = bf16[32,32,256]{2,1,0:T(8,128)(2,1)} custom-call(bf16[3,32,256]{2,1,0:T(8,128)(2,1)S(1)} %copy-done.2, bf16[3,32,256]{2,1,0:T(8,128)(2,1)S(1)} %copy-done.1, f32[3,32,32,256]{3,2,1,0:T(8,128)} %shard_map.95.gradient, bf16[8,256,128]{2,1,0:T(8,128)(2,1)S(1)} %all-to-all-done.3.arrived), custom_call_target="tpu_custom_call" | custom-call | flops 1048576 | bytes 1048576 | tf_op jit(solution)/shard_map/pallas_call | solution.py:650
  (36 shorter events, 7.9 us)
Async XLA Ops:
  2.7 22.5 %all-to-all-start = ((bf16[8,272,128]{2,1,0:T(8,128)(2,1)}), bf16[8,272,128]{2,1,0:T(8,128)(2,1)S(1)}, u32[]{:S(2)}, u32[]{:S(2)}) async-start(bf16[8,272,128]{2,1,0:T(8,128)(2,1)} %shard_map.86.sent), calls=%async_computation | async-start | bytes 1114112 | tf_op jit(solution)/shard_map/all_to_all | solution.py:674
  10.0 0.7 copy-start.6
  10.7 14.5 %copy-start = (bf16[64,3,32,32]{0,3,2,1:T(8,128)(2,1)S(1)}, bf16[64,3,32,32]{0,3,2,1:T(8,128)(2,1)}, u32[]{:S(2)}) copy-start(bf16[64,3,32,32]{0,3,2,1:T(8,128)(2,1)} %param.10) | copy-start | bytes 1179652
  10.7 14.5 %copy-start.4 = (s32[2,1,1,8,1]{3,4,2,1,0:T(1,128)S(1)}, s32[2,1,1,8,1]{3,4,2,1,0:T(1,128)}, u32[]{:S(2)}) copy-start(s32[2,1,1,8,1]{3,4,2,1,0:T(1,128)} %param.11) | copy-start | bytes 196
  10.7 14.5 %copy-start.5 = (s32[2,1,1,8]{3,2,1,0:T(1,128)S(1)}, s32[2,1,1,8]{3,2,1,0:T(1,128)}, u32[]{:S(2)}) copy-start(s32[2,1,1,8]{3,2,1,0:T(1,128)} %landing.1) | copy-start | bytes 196
  28.8 41.9 %all-to-all-start.1 = ((bf16[8,768,128]{2,1,0:T(8,128)(2,1)}), bf16[8,768,128]{2,1,0:T(8,128)(2,1)S(1)}, u32[]{:S(2)}, u32[]{:S(2)}) async-start(bf16[8,768,128]{2,1,0:T(8,128)(2,1)} %get-tuple-element.20.sent), calls=%async_computation.1 | async-start | bytes 3145728 | tf_op jit(solution)/shard_map/all_to_all | solution.py:674
  32.4 10.4 %copy-start.7 = (s32[2,1,1,8]{3,2,1,0:T(1,128)S(1)}, s32[2,1,1,8]{3,2,1,0:T(1,128)}, u32[]{:S(2)}) copy-start(s32[2,1,1,8]{3,2,1,0:T(1,128)} %picks.3) | copy-start | bytes 196
  35.0 42.8 %collective-permute-start = (bf16[6,32,256]{2,1,0:T(8,128)(2,1)}, bf16[6,32,256]{2,1,0:T(8,128)(2,1)S(1)}, u32[]{:S(2)}, u32[]{:S(2)}) collective-permute-start(bf16[6,32,256]{2,1,0:T(8,128)(2,1)} %get-tuple-element.21), channel_id=1, source_target_pairs={{0,4},{4,8},{8,12},{12,16},{16,20},{20,24},{24,28},{1,5},{5,9},{9,... | collective-permute-start | bytes 294920 | tf_op jit(solution)/shard_map/ppermute | solution.py:669
  38.9 38.9 %collective-permute-start.2 = (bf16[6,32,256]{2,1,0:T(8,128)(2,1)}, bf16[6,32,256]{2,1,0:T(8,128)(2,1)S(1)}, u32[]{:S(2)}, u32[]{:S(2)}) collective-permute-start(bf16[6,32,256]{2,1,0:T(8,128)(2,1)} %get-tuple-element.23), channel_id=1, source_target_pairs={{0,1},{1,2},{2,3},{4,5},{5,6},{6,7},{8,9},{9,10},{10,11},{12,13},{... | collective-permute-start | bytes 294920 | tf_op jit(solution)/shard_map/ppermute | solution.py:669
  40.2 37.6 %collective-permute-start.3 = (bf16[6,32,256]{2,1,0:T(8,128)(2,1)S(1)}, bf16[6,32,256]{2,1,0:T(8,128)(2,1)S(1)}, u32[]{:S(2)}, u32[]{:S(2)}) collective-permute-start(bf16[6,32,256]{2,1,0:T(8,128)(2,1)S(1)} %get-tuple-element.24), channel_id=1, source_target_pairs={{1,0},{2,1},{3,2},{5,4},{6,5},{7,6},{9,8},{10,9},{11,10},{13,12},{... | collective-permute-start | bytes 294920 | tf_op jit(solution)/shard_map/ppermute | solution.py:669
  41.5 36.3 %collective-permute-start.1 = (bf16[6,32,256]{2,1,0:T(8,128)(2,1)S(1)}, bf16[6,32,256]{2,1,0:T(8,128)(2,1)S(1)}, u32[]{:S(2)}, u32[]{:S(2)}) collective-permute-start(bf16[6,32,256]{2,1,0:T(8,128)(2,1)S(1)} %get-tuple-element.22.edge), channel_id=1, source_target_pairs={{4,0},{8,4},{12,8},{16,12},{20,16},{24,20},{28,24},{5,1},{9,5},{13... | collective-permute-start | bytes 294920 | tf_op jit(solution)/shard_map/ppermute | solution.py:669
  70.7 0.7 copy-start.3
  73.6 29.9 %all-to-all-start.2 = ((bf16[8,512,128]{2,1,0:T(8,128)(2,1)}), bf16[8,512,128]{2,1,0:T(8,128)(2,1)}, u32[]{:S(2)}, u32[]{:S(2)}) async-start(bf16[8,512,128]{2,1,0:T(8,128)(2,1)} %shard_map.91.sent.shares), calls=%async_computation.2 | async-start | bytes 2097152 | tf_op jit(solution)/shard_map/all_to_all | solution.py:674
  77.9 1.9 %copy-start.8 = (f32[3,32,32,256]{3,2,1,0:T(8,128)S(1)}, f32[3,32,32,256]{3,2,1,0:T(8,128)}, u32[]{:S(2)}) copy-start(f32[3,32,32,256]{3,2,1,0:T(8,128)} %velocity.3) | copy-start | bytes 9437188
  81.3 2.7 %copy-start.10 = (f32[32,32,256]{2,1,0:T(8,128)}, f32[32,32,256]{2,1,0:T(8,128)S(1)}, u32[]{:S(2)}) copy-start(f32[32,32,256]{2,1,0:T(8,128)S(1)} %shard_map.92.divergence) | copy-start | bytes 3145732
  86.2 25.0 %collective-permute-start.5 = (bf16[6,32,256]{2,1,0:T(8,128)(2,1)S(1)}, bf16[6,32,256]{2,1,0:T(8,128)(2,1)S(1)}, u32[]{:S(2)}, u32[]{:S(2)}) collective-permute-start(bf16[6,32,256]{2,1,0:T(8,128)(2,1)S(1)} %get-tuple-element.29.edge), channel_id=1, source_target_pairs={{4,0},{8,4},{12,8},{16,12},{20,16},{24,20},{28,24},{5,1},{9,5},{13... | collective-permute-start | bytes 294920 | tf_op jit(solution)/shard_map/ppermute | solution.py:669
  87.5 23.6 %collective-permute-start.4 = (bf16[6,32,256]{2,1,0:T(8,128)(2,1)S(1)}, bf16[6,32,256]{2,1,0:T(8,128)(2,1)S(1)}, u32[]{:S(2)}, u32[]{:S(2)}) collective-permute-start(bf16[6,32,256]{2,1,0:T(8,128)(2,1)S(1)} %get-tuple-element.28), channel_id=1, source_target_pairs={{0,4},{4,8},{8,12},{12,16},{16,20},{20,24},{24,28},{1,5},{5,9},{9,... | collective-permute-start | bytes 294920 | tf_op jit(solution)/shard_map/ppermute | solution.py:669
  92.0 19.1 %collective-permute-start.6 = (bf16[6,32,256]{2,1,0:T(8,128)(2,1)S(1)}, bf16[6,32,256]{2,1,0:T(8,128)(2,1)S(1)}, u32[]{:S(2)}, u32[]{:S(2)}) collective-permute-start(bf16[6,32,256]{2,1,0:T(8,128)(2,1)S(1)} %get-tuple-element.30), channel_id=1, source_target_pairs={{0,1},{1,2},{2,3},{4,5},{5,6},{6,7},{8,9},{9,10},{10,11},{12,13},{... | collective-permute-start | bytes 294920 | tf_op jit(solution)/shard_map/ppermute | solution.py:669
  93.3 17.8 %collective-permute-start.7 = (bf16[6,32,256]{2,1,0:T(8,128)(2,1)S(1)}, bf16[6,32,256]{2,1,0:T(8,128)(2,1)S(1)}, u32[]{:S(2)}, u32[]{:S(2)}) collective-permute-start(bf16[6,32,256]{2,1,0:T(8,128)(2,1)S(1)} %get-tuple-element.31), channel_id=1, source_target_pairs={{1,0},{2,1},{3,2},{5,4},{6,5},{7,6},{9,8},{10,9},{11,10},{13,12},{... | collective-permute-start | bytes 294920 | tf_op jit(solution)/shard_map/ppermute | solution.py:669
  103.5 17.1 %all-to-all-start.3 = ((bf16[8,256,128]{2,1,0:T(8,128)(2,1)}), bf16[8,256,128]{2,1,0:T(8,128)(2,1)S(1)}, u32[]{:S(2)}, u32[]{:S(2)}) async-start(bf16[8,256,128]{2,1,0:T(8,128)(2,1)} %shard_map.96), calls=%async_computation.3 | async-start | bytes 1048576 | tf_op jit(solution)/shard_map/all_to_all | solution.py:674
  107.2 4.0 %copy-start.9 = (bf16[32,32,256]{2,1,0:T(8,128)(2,1)S(1)}, bf16[32,32,256]{2,1,0:T(8,128)(2,1)}, u32[]{:S(2)}) copy-start(bf16[32,32,256]{2,1,0:T(8,128)(2,1)} %template.3) | copy-start | bytes 1572868
  107.2 4.0 %copy-start.11 = (f32[32,32,256]{2,1,0:T(8,128)S(1)}, f32[32,32,256]{2,1,0:T(8,128)}, u32[]{:S(2)}) copy-start(f32[32,32,256]{2,1,0:T(8,128)} %copy-done.10) | copy-start | bytes 3145732
  111.2 9.4 %copy-start.1 = (bf16[3,32,256]{2,1,0:T(8,128)(2,1)S(1)}, bf16[3,32,256]{2,1,0:T(8,128)(2,1)}, u32[]{:S(2)}) copy-start(bf16[3,32,256]{2,1,0:T(8,128)(2,1)} %get-tuple-element.33.tables_zero) | copy-start | bytes 147460
  111.2 9.4 %copy-start.2 = (bf16[3,32,256]{2,1,0:T(8,128)(2,1)S(1)}, bf16[3,32,256]{2,1,0:T(8,128)(2,1)}, u32[]{:S(2)}) copy-start(bf16[3,32,256]{2,1,0:T(8,128)(2,1)} %get-tuple-element.32.tables_far) | copy-start | bytes 147460

commit v10 on v9

--- a/solution.py
+++ b/solution.py
@@ -205,11 +205,11 @@
 
 def target_kernel(picks_in, route_in, brick_in, target, send, *refs):
     picks, route, landing, field, stage, meta, meta_half, sems = refs
+    load = fetch(target, field, sems.at[3])
     told = [
         fetch(source, place, sems.at[index])
         for index, (source, place) in enumerate(((picks_in, picks), (route_in, route), (brick_in, landing)))
     ]
-    load = fetch(target, field, sems.at[3])
     for copy in told:
         copy.wait()
     lane = iota((1, 128), 1)
@@ -713,8 +713,8 @@
         [far((peers, 512 + shared, 128), BF16), far(TABLES, BF16), far((peers, 128), jnp.int32)],
         [SCALAR, SCALAR, WHOLE, WHOLE, WHOLE],
         [FAR] * 3,
-        [pltpu.VMEM((peers, 16, 128), F32), pltpu.VMEM((peers, 128), jnp.int32), pltpu.VMEM(FLAT, BF16)]
-        + turning[1:]
+        [pltpu.VMEM((peers, 16, 128), F32), pltpu.VMEM((peers, 128), jnp.int32)]
+        + turning
         + [stage, tables, sems, pltpu.SemaphoreType.DMA((8,))],
         SHORT,
     )(route, target_brick, listed, moved, targets)
@@ -781,7 +781,7 @@
         far(NATIVE, BF16),
         [WHOLE, WHOLE, FAR, NEAR],
         FAR,
-        [pltpu.VMEM(FLAT, BF16)] + turning[1:] + [form, pltpu.VMEM(NATIVE, BF16), quarter_sems],
+        turning + [form, pltpu.VMEM(NATIVE, BF16), quarter_sems],
         SHORT,
     )(tables_far, tables_zero, gradient, composed)
     return gradient, adjoint

time: 125 us -> 125 us (level)
  no operation moved by 1% of the time
where the time goes in v10:
time: 125 us; the launch traced here: 124 us
  waiting for transfers between devices  45.6 us (36%)
  Pallas kernels  39.2 us (31%)
  starting transfers between devices  35.1 us (28%)
  local copies, waits for them, and re-layouts  3.27 us (3%)
    all_to_all x4, waiting for transfers between devices, swap_slots(): return lax.all_to_all(send, 'gx', split_axis=0, concat_axis=0, tiled=True)  45.6 us
    pallas_call x12, Pallas kernels, apply(): made(*[pinned(value, spec) for value, spec in zip(values, in_specs, stric...  39.2 us
    all_to_all x4, starting transfers between devices, swap_slots(): return lax.all_to_all(send, 'gx', split_axis=0, concat_axis=0, tiled=True)  18.9 us
    ppermute x8, starting transfers between devices, neighbours(): moved += [lax.ppermute(high, axis, up), lax.ppermute(low, axis, down)]  16.2 us
    unnamed x24, local copies, waits for them, and re-layouts  3.27 us
  transfers between devices with their start and end apart: 12, of which 4 were waited for; matrix products, arithmetic and copies ran while one was open for 0% of the time, Pallas kernels for 24%

profile of v10, /device:TPU:0, one launch (start us, length us, event | category | flops | bytes accessed | tf_op | source)
XLA Modules:
  0.0 124.3 jit_solution(12347784715588812242)
XLA Ops:
  0.6 2.1 %shard_map.86.sent = bf16[8,272,128]{2,1,0:T(8,128)(2,1)} custom-call(s32[2,1,1,8]{3,2,1,0:T(1,128)} %picks.3, s32[2,1,1,8]{3,2,1,0:T(1,128)} %bitcast.9, s32[2,1,1,8]{3,2,1,0:T(1,128)} %landing.1, bf16[32,32,256]{2,1,0:T(8,128)(2,1)} %target.1), custom_call_target="tpu_custom_call" | custom-call | flops 1048576 | bytes 1048576 | tf_op jit(solution)/shard_map/pallas_call | solution.py:650
  2.7 7.3 %all-to-all-start = ((bf16[8,272,128]{2,1,0:T(8,128)(2,1)}), bf16[8,272,128]{2,1,0:T(8,128)(2,1)S(1)}, u32[]{:S(2)}, u32[]{:S(2)}) async-start(bf16[8,272,128]{2,1,0:T(8,128)(2,1)} %shard_map.86.sent), calls=%async_computation | async-start | bytes 1114112 | tf_op jit(solution)/shard_map/all_to_all | solution.py:674
  10.7 4.5 %shard_map.87 = (bf16[8,256,128]{2,1,0:T(8,128)(2,1)S(1)}, bf16[3,32,256]{2,1,0:T(8,128)(2,1)}) custom-call(s32[2,1,1,8]{3,2,1,0:T(1,128)S(1)} %copy-done.6, bf16[3072,64]{1,0:T(8,128)(2,1)} %bitcast.6, bf16[32,32,256]{2,1,0:T(8,128)(2,1)} %template.3, bf16[8,272,128]{2,1,0:T(8,128)(2,1)} %shard_map.86.sent), custom_call_target="tpu_custom_call" | custom-call | flops 68719476736 | bytes 1048576 | tf_op jit(solution)/shard_map/pallas_call | solution.py:650
  15.2 10.0 %all-to-all-done.arrived.targets = bf16[8,272,128]{2,1,0:T(8,128)(2,1)S(1)} async-done(((bf16[8,272,128]{2,1,0:T(8,128)(2,1)}), bf16[8,272,128]{2,1,0:T(8,128)(2,1)S(1)}, u32[]{:S(2)}, u32[]{:S(2)}) %all-to-all-start) | async-done | bytes 557088 | tf_op jit(solution)/shard_map/all_to_all | solution.py:674
  25.2 3.6 %shard_map.88 = (bf16[8,768,128]{2,1,0:T(8,128)(2,1)}, bf16[3,32,256]{2,1,0:T(8,128)(2,1)}, s32[8,128]{1,0:T(8,128)}) custom-call(s32[2,1,1,8]{3,2,1,0:T(1,128)S(1)} %bitcast.10, s32[2,1,1,8]{3,2,1,0:T(1,128)S(1)} %copy-done.5, bf16[3072,64]{1,0:T(8,128)(2,1)S(1)} %bitcast.7, bf16[8,256,128]{2,1,0:T(8,128)(2,1)S(1)} %get-tuple-element.18.moved, ...), custom_call_target="tpu_custom_call" | custom-call | flops 1048576 | bytes 1048576 | tf_op jit(solution)/shard_map/pallas_call | solution.py:650
  28.8 3.7 %all-to-all-start.1 = ((bf16[8,768,128]{2,1,0:T(8,128)(2,1)}), bf16[8,768,128]{2,1,0:T(8,128)(2,1)S(1)}, u32[]{:S(2)}, u32[]{:S(2)}) async-start(bf16[8,768,128]{2,1,0:T(8,128)(2,1)} %get-tuple-element.20.sent), calls=%async_computation.1 | async-start | bytes 3145728 | tf_op jit(solution)/shard_map/all_to_all | solution.py:674
  32.4 2.5 %shard_map.89 = (bf16[6,32,256]{2,1,0:T(8,128)(2,1)S(1)}, bf16[6,32,256]{2,1,0:T(8,128)(2,1)}, bf16[6,32,256]{2,1,0:T(8,128)(2,1)S(1)}, bf16[6,32,256]{2,1,0:T(8,128)(2,1)}) custom-call(bf16[32,32,256]{2,1,0:T(8,128)(2,1)} %template.3, f32[3,32,32,256]{3,2,1,0:T(8,128)} %velocity.3, bf16[8,768,128]{2,1,0:T(8,128)(2,1)} %get-tuple-element.20.sent), custom_call_target="tpu_custom_call" | custom-call | flops 68719476736 | bytes 1048576 | tf_op jit(solution)/shard_map/pallas_call | solution.py:650
  35.0 3.9 %collective-permute-start = (bf16[6,32,256]{2,1,0:T(8,128)(2,1)}, bf16[6,32,256]{2,1,0:T(8,128)(2,1)S(1)}, u32[]{:S(2)}, u32[]{:S(2)}) collective-permute-start(bf16[6,32,256]{2,1,0:T(8,128)(2,1)} %get-tuple-element.21), channel_id=1, source_target_pairs={{0,4},{4,8},{8,12},{12,16},{16,20},{20,24},{24,28},{1,5},{5,9},{9,... | collective-permute-start | bytes 294920 | tf_op jit(solution)/shard_map/ppermute | solution.py:669
  42.8 3.4 %shard_map.90 = (bf16[3,32,256]{2,1,0:T(8,128)(2,1)}, s32[8,128]{1,0:T(8,128)}) custom-call(s32[2,1,1,8]{3,2,1,0:T(1,128)S(1)} %copy-done.7, s32[8,128]{1,0:T(8,128)} %get-tuple-element.19.codes_in, bf16[3072,64]{1,0:T(8,128)(2,1)S(1)} %bitcast.8, bf16[6,32,256]{2,1,0:T(8,128)(2,1)S(1)} %get-tuple-element.22.edge), custom_call_target="tpu_custom_call" | custom-call | flops 68719476736 | bytes 1048576 | tf_op jit(solution)/shard_map/pallas_call | solution.py:650
  46.3 24.4 %all-to-all-done.1.arrived = bf16[8,768,128]{2,1,0:T(8,128)(2,1)S(1)} async-done(((bf16[8,768,128]{2,1,0:T(8,128)(2,1)}), bf16[8,768,128]{2,1,0:T(8,128)(2,1)S(1)}, u32[]{:S(2)}, u32[]{:S(2)}) %all-to-all-start.1) | async-done | bytes 1572896 | tf_op jit(solution)/shard_map/all_to_all | solution.py:674
  71.3 2.2 %shard_map.91.sent.shares = bf16[8,512,128]{2,1,0:T(8,128)(2,1)} custom-call(s32[8,128]{1,0:T(8,128)S(1)} %copy-done.3, bf16[8,768,128]{2,1,0:T(8,128)(2,1)S(1)} %all-to-all-done.1.arrived, bf16[8,272,128]{2,1,0:T(8,128)(2,1)S(1)} %all-to-all-done.arrived.targets), custom_call_target="tpu_custom_call" | custom-call | flops 1048576 | bytes 1048576 | tf_op jit(solution)/shard_map/pallas_call | solution.py:650
  73.6 4.3 %all-to-all-start.2 = ((bf16[8,512,128]{2,1,0:T(8,128)(2,1)}), bf16[8,512,128]{2,1,0:T(8,128)(2,1)}, u32[]{:S(2)}, u32[]{:S(2)}) async-start(bf16[8,512,128]{2,1,0:T(8,128)(2,1)} %shard_map.91.sent.shares), calls=%async_computation.2 | async-start | bytes 2097152 | tf_op jit(solution)/shard_map/all_to_all | solution.py:674
  77.9 1.9 %copy-done.8 = f32[3,32,32,256]{3,2,1,0:T(8,128)S(1)} copy-done((f32[3,32,32,256]{3,2,1,0:T(8,128)S(1)}, f32[3,32,32,256]{3,2,1,0:T(8,128)}, u32[]{:S(2)}) %copy-start.8) | copy-done | bytes 3145752
  79.8 1.5 %shard_map.92.divergence = f32[32,32,256]{2,1,0:T(8,128)S(1)} custom-call(f32[3,32,32,256]{3,2,1,0:T(8,128)S(1)} %copy-done.8, bf16[6,32,256]{2,1,0:T(8,128)(2,1)S(1)} %collective-permute-done.before_x.b0x, bf16[6,32,256]{2,1,0:T(8,128)(2,1)S(1)} %collective-permute-done.1.after_x.a0x, bf16[6,32,256]{2,1,0:T(8,128)(2,1)S(1)} %collective-permute-done.2.before_y.b0y, ...), custom_call_target="tpu_custom_call" | custom-call | flops 68719476736 | bytes 1048576 | tf_op jit(solution)/shard_map/pallas_call | solution.py:650
  81.2 2.7 %shard_map.93 = (bf16[32,32,256]{2,1,0:T(8,128)(2,1)S(1)}, bf16[6,32,256]{2,1,0:T(8,128)(2,1)S(1)}, bf16[6,32,256]{2,1,0:T(8,128)(2,1)S(1)}, bf16[6,32,256]{2,1,0:T(8,128)(2,1)S(1)}, bf16[6,32,256]{2,1,0:T(8,128)(2,1)S(1)}) custom-call(s32[8,128]{1,0:T(8,128)} %get-tuple-element.19.codes_in, bf16[8,768,128]{2,1,0:T(8,128)(2,1)S(1)} %all-to-all-done.1.arrived, ...), custom_call_target="tpu_custom_call" | custom-call | flops 68719476736 | bytes 1048576 | tf_op jit(solution)/shard_map/pallas_call | solution.py:650
  84.0 2.2 %shard_map.96 = bf16[8,256,128]{2,1,0:T(8,128)(2,1)} custom-call(s32[8,128]{1,0:T(8,128)} %get-tuple-element.25.plan.plan_in, bf16[8,512,128]{2,1,0:T(8,128)(2,1)} %shard_map.91.sent.shares, bf16[6,32,256]{2,1,0:T(8,128)(2,1)S(1)} %get-tuple-element.29.edge), custom_call_target="tpu_custom_call" | custom-call | flops 68719476736 | bytes 1048576 | tf_op jit(solution)/shard_map/pallas_call | solution.py:650
  87.4 4.6 %collective-permute-start.4 = (bf16[6,32,256]{2,1,0:T(8,128)(2,1)S(1)}, bf16[6,32,256]{2,1,0:T(8,128)(2,1)S(1)}, u32[]{:S(2)}, u32[]{:S(2)}) collective-permute-start(bf16[6,32,256]{2,1,0:T(8,128)(2,1)S(1)} %get-tuple-element.28), channel_id=1, source_target_pairs={{0,4},{4,8},{8,12},{12,16},{16,20},{20,24},{24,28},{1,5},{5,9},{9,... | collective-permute-start | bytes 294920 | tf_op jit(solution)/shard_map/ppermute | solution.py:669
  92.0 1.3 %collective-permute-start.6 = (bf16[6,32,256]{2,1,0:T(8,128)(2,1)S(1)}, bf16[6,32,256]{2,1,0:T(8,128)(2,1)S(1)}, u32[]{:S(2)}, u32[]{:S(2)}) collective-permute-start(bf16[6,32,256]{2,1,0:T(8,128)(2,1)S(1)} %get-tuple-element.30), channel_id=1, source_target_pairs={{0,1},{1,2},{2,3},{4,5},{5,6},{6,7},{8,9},{9,10},{10,11},{12,13},{... | collective-permute-start | bytes 294920 | tf_op jit(solution)/shard_map/ppermute | solution.py:669
  94.6 8.9 %all-to-all-done.2.arrived.adjoint_two = bf16[8,512,128]{2,1,0:T(8,128)(2,1)} async-done(((bf16[8,512,128]{2,1,0:T(8,128)(2,1)}), bf16[8,512,128]{2,1,0:T(8,128)(2,1)}, u32[]{:S(2)}, u32[]{:S(2)}) %all-to-all-start.2) | async-done | bytes 1048608 | tf_op jit(solution)/shard_map/all_to_all | solution.py:674
  103.5 3.7 %all-to-all-start.3 = ((bf16[8,256,128]{2,1,0:T(8,128)(2,1)}), bf16[8,256,128]{2,1,0:T(8,128)(2,1)S(1)}, u32[]{:S(2)}, u32[]{:S(2)}) async-start(bf16[8,256,128]{2,1,0:T(8,128)(2,1)} %shard_map.96), calls=%async_computation.3 | async-start | bytes 1048576 | tf_op jit(solution)/shard_map/all_to_all | solution.py:674
  107.2 3.9 %shard_map.94.adjoint_one = bf16[8,256,128]{2,1,0:T(8,128)(2,1)S(1)} custom-call(bf16[3,32,256]{2,1,0:T(8,128)(2,1)} %get-tuple-element.27.tables_in, bf16[8,512,128]{2,1,0:T(8,128)(2,1)} %all-to-all-done.2.arrived.adjoint_two), custom_call_target="tpu_custom_call" | custom-call | flops 68719476736 | bytes 1048576 | tf_op jit(solution)/shard_map/pallas_call | solution.py:650
  111.2 7.0 %shard_map.95.gradient = f32[3,32,32,256]{3,2,1,0:T(8,128)} custom-call(bf16[32,32,256]{2,1,0:T(8,128)(2,1)S(1)} %copy-done.9, bf16[32,32,256]{2,1,0:T(8,128)(2,1)S(1)} %get-tuple-element.26.state, f32[32,32,256]{2,1,0:T(8,128)S(1)} %copy-done.11, bf16[8,512,128]{2,1,0:T(8,128)(2,1)} %all-to-all-done.2.arrived.adjoint_two, ...), custom_call_target="tpu_custom_call" | custom-call | flops 68719476736 | bytes 1048576 | tf_op jit(solution)/shard_map/pallas_call | solution.py:650
  118.2 2.4 %all-to-all-done.3.arrived = bf16[8,256,128]{2,1,0:T(8,128)(2,1)S(1)} async-done(((bf16[8,256,128]{2,1,0:T(8,128)(2,1)}), bf16[8,256,128]{2,1,0:T(8,128)(2,1)S(1)}, u32[]{:S(2)}, u32[]{:S(2)}) %all-to-all-start.3) | async-done | bytes 524320 | tf_op jit(solution)/shard_map/all_to_all | solution.py:674
  120.6 3.6 %shard_map.97 = bf16[32,32,256]{2,1,0:T(8,128)(2,1)} custom-call(bf16[3,32,256]{2,1,0:T(8,128)(2,1)S(1)} %copy-done.2, bf16[3,32,256]{2,1,0:T(8,128)(2,1)S(1)} %copy-done.1, f32[3,32,32,256]{3,2,1,0:T(8,128)} %shard_map.95.gradient, bf16[8,256,128]{2,1,0:T(8,128)(2,1)S(1)} %all-to-all-done.3.arrived), custom_call_target="tpu_custom_call" | custom-call | flops 1048576 | bytes 1048576 | tf_op jit(solution)/shard_map/pallas_call | solution.py:650
  (36 shorter events, 7.9 us)
Async XLA Ops:
  2.7 22.5 %all-to-all-start = ((bf16[8,272,128]{2,1,0:T(8,128)(2,1)}), bf16[8,272,128]{2,1,0:T(8,128)(2,1)S(1)}, u32[]{:S(2)}, u32[]{:S(2)}) async-start(bf16[8,272,128]{2,1,0:T(8,128)(2,1)} %shard_map.86.sent), calls=%async_computation | async-start | bytes 1114112 | tf_op jit(solution)/shard_map/all_to_all | solution.py:674
  10.0 0.7 copy-start.6
  10.7 14.5 %copy-start = (bf16[64,3,32,32]{0,3,2,1:T(8,128)(2,1)S(1)}, bf16[64,3,32,32]{0,3,2,1:T(8,128)(2,1)}, u32[]{:S(2)}) copy-start(bf16[64,3,32,32]{0,3,2,1:T(8,128)(2,1)} %param.10) | copy-start | bytes 1179652
  10.7 14.5 %copy-start.4 = (s32[2,1,1,8,1]{3,4,2,1,0:T(1,128)S(1)}, s32[2,1,1,8,1]{3,4,2,1,0:T(1,128)}, u32[]{:S(2)}) copy-start(s32[2,1,1,8,1]{3,4,2,1,0:T(1,128)} %param.11) | copy-start | bytes 196
  10.7 14.5 %copy-start.5 = (s32[2,1,1,8]{3,2,1,0:T(1,128)S(1)}, s32[2,1,1,8]{3,2,1,0:T(1,128)}, u32[]{:S(2)}) copy-start(s32[2,1,1,8]{3,2,1,0:T(1,128)} %landing.1) | copy-start | bytes 196
  28.8 41.9 %all-to-all-start.1 = ((bf16[8,768,128]{2,1,0:T(8,128)(2,1)}), bf16[8,768,128]{2,1,0:T(8,128)(2,1)S(1)}, u32[]{:S(2)}, u32[]{:S(2)}) async-start(bf16[8,768,128]{2,1,0:T(8,128)(2,1)} %get-tuple-element.20.sent), calls=%async_computation.1 | async-start | bytes 3145728 | tf_op jit(solution)/shard_map/all_to_all | solution.py:674
  32.4 10.4 %copy-start.7 = (s32[2,1,1,8]{3,2,1,0:T(1,128)S(1)}, s32[2,1,1,8]{3,2,1,0:T(1,128)}, u32[]{:S(2)}) copy-start(s32[2,1,1,8]{3,2,1,0:T(1,128)} %picks.3) | copy-start | bytes 196
  35.0 42.8 %collective-permute-start = (bf16[6,32,256]{2,1,0:T(8,128)(2,1)}, bf16[6,32,256]{2,1,0:T(8,128)(2,1)S(1)}, u32[]{:S(2)}, u32[]{:S(2)}) collective-permute-start(bf16[6,32,256]{2,1,0:T(8,128)(2,1)} %get-tuple-element.21), channel_id=1, source_target_pairs={{0,4},{4,8},{8,12},{12,16},{16,20},{20,24},{24,28},{1,5},{5,9},{9,... | collective-permute-start | bytes 294920 | tf_op jit(solution)/shard_map/ppermute | solution.py:669
  38.9 38.9 %collective-permute-start.2 = (bf16[6,32,256]{2,1,0:T(8,128)(2,1)}, bf16[6,32,256]{2,1,0:T(8,128)(2,1)S(1)}, u32[]{:S(2)}, u32[]{:S(2)}) collective-permute-start(bf16[6,32,256]{2,1,0:T(8,128)(2,1)} %get-tuple-element.23), channel_id=1, source_target_pairs={{0,1},{1,2},{2,3},{4,5},{5,6},{6,7},{8,9},{9,10},{10,11},{12,13},{... | collective-permute-start | bytes 294920 | tf_op jit(solution)/shard_map/ppermute | solution.py:669
  40.2 37.6 %collective-permute-start.3 = (bf16[6,32,256]{2,1,0:T(8,128)(2,1)S(1)}, bf16[6,32,256]{2,1,0:T(8,128)(2,1)S(1)}, u32[]{:S(2)}, u32[]{:S(2)}) collective-permute-start(bf16[6,32,256]{2,1,0:T(8,128)(2,1)S(1)} %get-tuple-element.24), channel_id=1, source_target_pairs={{1,0},{2,1},{3,2},{5,4},{6,5},{7,6},{9,8},{10,9},{11,10},{13,12},{... | collective-permute-start | bytes 294920 | tf_op jit(solution)/shard_map/ppermute | solution.py:669
  41.5 36.3 %collective-permute-start.1 = (bf16[6,32,256]{2,1,0:T(8,128)(2,1)S(1)}, bf16[6,32,256]{2,1,0:T(8,128)(2,1)S(1)}, u32[]{:S(2)}, u32[]{:S(2)}) collective-permute-start(bf16[6,32,256]{2,1,0:T(8,128)(2,1)S(1)} %get-tuple-element.22.edge), channel_id=1, source_target_pairs={{4,0},{8,4},{12,8},{16,12},{20,16},{24,20},{28,24},{5,1},{9,5},{13... | collective-permute-start | bytes 294920 | tf_op jit(solution)/shard_map/ppermute | solution.py:669
  70.7 0.7 copy-start.3
  73.6 29.9 %all-to-all-start.2 = ((bf16[8,512,128]{2,1,0:T(8,128)(2,1)}), bf16[8,512,128]{2,1,0:T(8,128)(2,1)}, u32[]{:S(2)}, u32[]{:S(2)}) async-start(bf16[8,512,128]{2,1,0:T(8,128)(2,1)} %shard_map.91.sent.shares), calls=%async_computation.2 | async-start | bytes 2097152 | tf_op jit(solution)/shard_map/all_to_all | solution.py:674
  77.9 1.9 %copy-start.8 = (f32[3,32,32,256]{3,2,1,0:T(8,128)S(1)}, f32[3,32,32,256]{3,2,1,0:T(8,128)}, u32[]{:S(2)}) copy-start(f32[3,32,32,256]{3,2,1,0:T(8,128)} %velocity.3) | copy-start | bytes 9437188
  81.2 2.7 %copy-start.10 = (f32[32,32,256]{2,1,0:T(8,128)}, f32[32,32,256]{2,1,0:T(8,128)S(1)}, u32[]{:S(2)}) copy-start(f32[32,32,256]{2,1,0:T(8,128)S(1)} %shard_map.92.divergence) | copy-start | bytes 3145732
  86.1 25.0 %collective-permute-start.5 = (bf16[6,32,256]{2,1,0:T(8,128)(2,1)S(1)}, bf16[6,32,256]{2,1,0:T(8,128)(2,1)S(1)}, u32[]{:S(2)}, u32[]{:S(2)}) collective-permute-start(bf16[6,32,256]{2,1,0:T(8,128)(2,1)S(1)} %get-tuple-element.29.edge), channel_id=1, source_target_pairs={{4,0},{8,4},{12,8},{16,12},{20,16},{24,20},{28,24},{5,1},{9,5},{13... | collective-permute-start | bytes 294920 | tf_op jit(solution)/shard_map/ppermute | solution.py:669
  87.4 23.6 %collective-permute-start.4 = (bf16[6,32,256]{2,1,0:T(8,128)(2,1)S(1)}, bf16[6,32,256]{2,1,0:T(8,128)(2,1)S(1)}, u32[]{:S(2)}, u32[]{:S(2)}) collective-permute-start(bf16[6,32,256]{2,1,0:T(8,128)(2,1)S(1)} %get-tuple-element.28), channel_id=1, source_target_pairs={{0,4},{4,8},{8,12},{12,16},{16,20},{20,24},{24,28},{1,5},{5,9},{9,... | collective-permute-start | bytes 294920 | tf_op jit(solution)/shard_map/ppermute | solution.py:669
  92.0 19.1 %collective-permute-start.6 = (bf16[6,32,256]{2,1,0:T(8,128)(2,1)S(1)}, bf16[6,32,256]{2,1,0:T(8,128)(2,1)S(1)}, u32[]{:S(2)}, u32[]{:S(2)}) collective-permute-start(bf16[6,32,256]{2,1,0:T(8,128)(2,1)S(1)} %get-tuple-element.30), channel_id=1, source_target_pairs={{0,1},{1,2},{2,3},{4,5},{5,6},{6,7},{8,9},{9,10},{10,11},{12,13},{... | collective-permute-start | bytes 294920 | tf_op jit(solution)/shard_map/ppermute | solution.py:669
  93.3 17.8 %collective-permute-start.7 = (bf16[6,32,256]{2,1,0:T(8,128)(2,1)S(1)}, bf16[6,32,256]{2,1,0:T(8,128)(2,1)S(1)}, u32[]{:S(2)}, u32[]{:S(2)}) collective-permute-start(bf16[6,32,256]{2,1,0:T(8,128)(2,1)S(1)} %get-tuple-element.31), channel_id=1, source_target_pairs={{1,0},{2,1},{3,2},{5,4},{6,5},{7,6},{9,8},{10,9},{11,10},{13,12},{... | collective-permute-start | bytes 294920 | tf_op jit(solution)/shard_map/ppermute | solution.py:669
  103.5 17.1 %all-to-all-start.3 = ((bf16[8,256,128]{2,1,0:T(8,128)(2,1)}), bf16[8,256,128]{2,1,0:T(8,128)(2,1)S(1)}, u32[]{:S(2)}, u32[]{:S(2)}) async-start(bf16[8,256,128]{2,1,0:T(8,128)(2,1)} %shard_map.96), calls=%async_computation.3 | async-start | bytes 1048576 | tf_op jit(solution)/shard_map/all_to_all | solution.py:674
  107.2 4.0 %copy-start.9 = (bf16[32,32,256]{2,1,0:T(8,128)(2,1)S(1)}, bf16[32,32,256]{2,1,0:T(8,128)(2,1)}, u32[]{:S(2)}) copy-start(bf16[32,32,256]{2,1,0:T(8,128)(2,1)} %template.3) | copy-start | bytes 1572868
  107.2 4.0 %copy-start.11 = (f32[32,32,256]{2,1,0:T(8,128)S(1)}, f32[32,32,256]{2,1,0:T(8,128)}, u32[]{:S(2)}) copy-start(f32[32,32,256]{2,1,0:T(8,128)} %copy-done.10) | copy-start | bytes 3145732
  111.1 9.4 %copy-start.1 = (bf16[3,32,256]{2,1,0:T(8,128)(2,1)S(1)}, bf16[3,32,256]{2,1,0:T(8,128)(2,1)}, u32[]{:S(2)}) copy-start(bf16[3,32,256]{2,1,0:T(8,128)(2,1)} %get-tuple-element.33.tables_zero) | copy-start | bytes 147460
  111.1 9.4 %copy-start.2 = (bf16[3,32,256]{2,1,0:T(8,128)(2,1)S(1)}, bf16[3,32,256]{2,1,0:T(8,128)(2,1)}, u32[]{:S(2)}) copy-start(bf16[3,32,256]{2,1,0:T(8,128)(2,1)} %get-tuple-element.32.tables_far) | copy-start | bytes 147460
